TPU v7x, 32 devices: a whole 2x2x4 slice. The times are simulated.
32 devices in a mesh: groups: 2 (over y), dp: 4 (over z), mp: 4 (over x, core).
Axes of the slice: x: 2, y: 2, z: 4, core: 2. Of those that a mesh axis runs over, the one named last changes fastest.
Arguments:
- inputs: bfloat16 [4096, 6144], P(('groups', 'dp'), 'mp'), parts along dimension 0, may hold values from -6 to 6
- output_gradient: bfloat16 [4096, 1024], P(('groups', 'dp'), 'mp'), parts along dimension 0, may hold values from -1.5 to 1.5
- frozen_key_weight: bfloat16 [6144, 1024], P('mp'), may hold values from -0.1875 to 0.1875
- adapter_down_factors: bfloat16 [512, 16, 6144], P('dp', None, 'mp'), may hold values from -0.09375 to 0.09375
- adapter_up_factors: bfloat16 [512, 16, 1024], P('dp', None, 'mp'), may hold values from -0.3125 to 0.3125
- token_adapter_index: int32 [4096, 2], P(('groups', 'dp')), parts along dimension 0, may hold values from 0 to 511, as said below
- gates: bfloat16 [4096, 2], P(('groups', 'dp')), parts along dimension 0, may hold values from 0.099609375 to 0.8984375
Outputs:
- input_gradient: bfloat16 [4096, 6144], P(('groups', 'dp'), 'mp'), parts along dimension 0
- grad_gate: bfloat16 [4096, 2], P(('groups', 'dp')), parts along dimension 0
- grad_down: bfloat16 [1024, 16, 6144], P(('groups', 'dp'), None, 'mp'), parts along dimension 0
- grad_up: bfloat16 [1024, 16, 1024], P(('groups', 'dp'), None, 'mp'), parts along dimension 0
There are 2 independent parts, one for each index of `groups`. A program takes and returns all parts, laid end to end along the dimension named above; an argument that names none is the same for every part. Nothing has to cross between parts.
Inputs may be any that keep to these rules, and one draw needn't show every extreme that they name: `token_adapter_index`: each token names two different adapters; adapter e belongs to owner e // 128; the 1024 routes of one device's tokens name the adapters of one owner at most 512 times, and in every draw some owner is named exactly 512 times by the routes of every device.
All inputs are finite; a program needn't handle non-finite values.
Results may differ from a plain program's by a relative error of at most 0.005.
Values may be sent and summed in bfloat16 or wider, within the bound.
No kernel may reach another device: no remote copies, remote signals or barrier semaphores. Data moves between devices by JAX's collectives and lax.ppermute only.
A program may use at most 128 MiB of HBM per device.

v0:
```python
import jax
import jax.numpy as jnp
from jax import lax
from jax.sharding import PartitionSpec as P


def route_rows(flat_in, flat_out, gate_table, down_flattened, up_flattened):
    local_adapters = gate_table.shape[1]
    reduced_rank_output = down_flattened.shape[0] // local_adapters
    chosen = (gate_table != 0).astype(jnp.float32)
    gate_value = jnp.sum(gate_table.astype(jnp.float32), axis=1)
    dims = (((1,), (1,)), ((), ()))
    proj_in = lax.dot_general(flat_in, down_flattened, dims, preferred_element_type=jnp.float32)
    proj_out = lax.dot_general(flat_out, up_flattened, dims, preferred_element_type=jnp.float32)
    part_in = jnp.sum(
        chosen[:, :, None] * proj_in.reshape(-1, local_adapters, reduced_rank_output), axis=1
    )
    part_out = jnp.sum(
        chosen[:, :, None] * proj_out.reshape(-1, local_adapters, reduced_rank_output), axis=1
    )
    low_in, low_out = lax.psum((part_in, part_out), "mp")
    gate_gradient = jnp.sum(low_in * low_out, axis=1).astype(jnp.bfloat16)
    scaled_output = (gate_value[:, None] * low_out).astype(jnp.bfloat16)
    scaled_in = (gate_value[:, None] * low_in).astype(jnp.bfloat16)
    chosen_low = chosen.astype(jnp.bfloat16)
    spread_out = (chosen_low[:, :, None] * scaled_output[:, None, :]).reshape(
        -1, local_adapters * reduced_rank_output
    )
    spread_in = (chosen_low[:, :, None] * scaled_in[:, None, :]).reshape(
        -1, local_adapters * reduced_rank_output
    )
    back_rows = jnp.dot(spread_out, down_flattened, preferred_element_type=jnp.float32).astype(
        jnp.bfloat16
    )
    return (back_rows, gate_gradient, spread_out, spread_in)


def per_device(
    inputs,
    output_gradient,
    frozen_key_weight,
    adapter_down_factors,
    adapter_up_factors,
    token_adapter_index,
    gates,
):
    tok_count = inputs.shape[0]
    input_width = inputs.shape[1]
    output_width = output_gradient.shape[1]
    owners_count = lax.axis_size("dp")
    local_adapters = adapter_down_factors.shape[0]
    reduced_rank_output = adapter_down_factors.shape[1]
    capacity = 4 * tok_count // owners_count
    slot_total = owners_count * capacity
    full_out = lax.all_gather(output_gradient, "mp", axis=1, tiled=True)
    frozen_gradient = lax.dot_general(
        full_out, frozen_key_weight, (((1,), (1,)), ((), ())), preferred_element_type=jnp.float32
    )
    routes = token_adapter_index.reshape(-1)
    route_owner = routes // local_adapters
    local_id = routes % local_adapters
    owner_onehot = (route_owner[:, None] == jnp.arange(owners_count)[None, :]).astype(jnp.int32)
    before = jnp.cumsum(owner_onehot, axis=0) - owner_onehot
    position = jnp.sum(before * owner_onehot, axis=1)
    dest_slot = route_owner * capacity + position
    send_rows = (
        jnp.zeros((slot_total, input_width), jnp.bfloat16)
        .at[dest_slot]
        .set(jnp.repeat(inputs, 2, axis=0))
    )
    send_out = (
        jnp.zeros((slot_total, output_width), jnp.bfloat16)
        .at[dest_slot]
        .set(jnp.repeat(output_gradient, 2, axis=0))
    )
    send_gate = (
        jnp.zeros((slot_total, local_adapters), jnp.bfloat16)
        .at[dest_slot, local_id]
        .set(gates.reshape(-1))
    )
    send_rows = send_rows.reshape(owners_count, capacity, input_width)
    send_out = send_out.reshape(owners_count, capacity, output_width)
    send_gate = send_gate.reshape(owners_count, capacity, local_adapters)
    down_flattened = adapter_down_factors.reshape(local_adapters * reduced_rank_output, input_width)
    up_flattened = adapter_up_factors.reshape(local_adapters * reduced_rank_output, output_width)
    got_in, got_out, got_gate = (
        lax.all_to_all(send_rows, "dp", split_axis=0, concat_axis=0, tiled=True),
        lax.all_to_all(send_out, "dp", split_axis=0, concat_axis=0, tiled=True),
        lax.all_to_all(send_gate, "dp", split_axis=0, concat_axis=0, tiled=True),
    )
    flat_in = got_in.reshape(-1, input_width)
    flat_out = got_out.reshape(-1, output_width)
    back_rows, gate_gradient, spread_out, spread_in = route_rows(
        flat_in, flat_out, got_gate.reshape(-1, local_adapters), down_flattened, up_flattened
    )
    returned, returned_gate = (
        lax.all_to_all(
            back_rows.reshape(owners_count, capacity, input_width),
            "dp",
            split_axis=0,
            concat_axis=0,
            tiled=True,
        ),
        lax.all_to_all(
            gate_gradient.reshape(owners_count, capacity),
            "dp",
            split_axis=0,
            concat_axis=0,
            tiled=True,
        ),
    )
    rows_dims = (((0,), (0,)), ((), ()))
    down_grad = lax.dot_general(spread_out, flat_in, rows_dims, preferred_element_type=jnp.float32)
    up_grad = lax.dot_general(spread_in, flat_out, rows_dims, preferred_element_type=jnp.float32)
    down_grad = down_grad.astype(jnp.bfloat16).reshape(
        local_adapters, reduced_rank_output, input_width
    )
    up_grad = up_grad.astype(jnp.bfloat16).reshape(
        local_adapters, reduced_rank_output, output_width
    )
    adapter_rows = (
        returned.reshape(slot_total, input_width)[dest_slot]
        .reshape(tok_count, 2, input_width)
        .astype(jnp.float32)
    )
    input_gradient = (frozen_gradient + adapter_rows[:, 0] + adapter_rows[:, 1]).astype(
        jnp.bfloat16
    )
    grad_gate = returned_gate.reshape(-1)[dest_slot].reshape(tok_count, 2)
    return (input_gradient, grad_gate, down_grad, up_grad)


def solution(mesh):
    in_specs = (
        P(("groups", "dp"), "mp"),
        P(("groups", "dp"), "mp"),
        P("mp", None),
        P("dp", None, "mp"),
        P("dp", None, "mp"),
        P(("groups", "dp"), None),
        P(("groups", "dp"), None),
    )
    out_specs = (
        P(("groups", "dp"), "mp"),
        P(("groups", "dp"), None),
        P(("groups", "dp"), None, "mp"),
        P(("groups", "dp"), None, "mp"),
    )
    return jax.shard_map(
        per_device, mesh=mesh, in_specs=in_specs, out_specs=out_specs, check_vma=False
    )
```

profile of v0, /device:TPU:0, one launch (start us, length us, event | category | flops | bytes accessed | tf_op | source)
XLA Modules:
  0.0 479.1 jit_solution(17161447576793828018)
XLA Ops:
  7.2 0.0 copy-start
  7.2 1.0 copy.28
  8.2 0.2 reshape.291
  8.3 0.2 reshape.290
  8.5 0.2 reshape.289
  8.7 0.9 copy.31
  9.5 0.2 reshape.348
  9.8 1.1 reduce-window.6
  10.9 0.2 slice_reduce_fusion
  11.1 0.2 reduce-window.9
  11.3 0.1 add_bitcast_fusion
  11.5 0.8 and_reduce_fusion
  12.2 0.7 multiply_reduce_fusion.3
  13.0 8.5 %scatter_custom_fusion.2 = bf16[262144]{0:T(1024)(128)(2,1)} fusion(s32[1024]{0:T(1024)S(1)} %broadcast_select_fusion, bf16[1024]{0:T(1024)(128)(2,1)S(1)} %reshape.348, bf16[]{:T(256)} %constant.35.clone.1), kind=kCustom, calls=%fused_computation.25 | custom fusion | bytes 524290
  21.5 6.3 %all-to-all-start = ((bf16[4,512,128]{2,1,0:T(8,128)(2,1)}), bf16[4,512,128]{2,1,0:T(8,128)(2,1)}, u32[]{:S(2)}, u32[]{:S(2)}) async-start(bf16[4,512,128]{2,1,0:T(8,128)(2,1)} %bitcast.75), calls=%async_computation | async-start | bytes 1048576 | tf_op jit(solution)/shard_map/all_to_all | solution.py:89
  27.8 2.0 broadcast_in_dim.9
  29.8 2.0 reshape.334
  31.8 6.4 %scatter_custom_fusion = bf16[2048,256]{1,0:T(8,128)(2,1)} fusion(s32[1024]{0:T(1024)S(1)} %bitcast.76, bf16[1024,256]{1,0:T(8,128)(2,1)} %reshape.334, bf16[]{:T(256)} %constant.35.clone.1), kind=kCustom, calls=%fused_computation.23 | custom fusion | bytes 1049088 | tf_op jit(solution)/shard_map/scatter | solution.py:74
  38.2 4.1 all-to-all-done
  42.4 4.7 all-to-all-start.1
  47.1 4.7 broadcast_in_dim.11
  51.8 7.5 %reshape.342 = bf16[1024,1536]{1,0:T(8,128)(2,1)} reshape(bf16[512,2,1536]{2,1,0:T(2,128)(2,1)} %broadcast_in_dim.11) | data formatting | bytes 6291456 | tf_op jit(solution)/shard_map/reshape | solution.py:69
  59.3 10.1 %scatter_custom_fusion.1 = bf16[2048,1536]{1,0:T(8,128)(2,1)} fusion(s32[1024]{0:T(1024)S(1)} %bitcast.77, bf16[1024,1536]{1,0:T(8,128)(2,1)} %reshape.342, bf16[]{:T(256)} %constant.35.clone.1), kind=kCustom, calls=%fused_computation.16 | custom fusion | bytes 6291968 | tf_op jit(solution)/shard_map/scatter | solution.py:69
  69.4 3.0 all-to-all-done.1
  72.4 5.2 %all-to-all-start.3 = ((bf16[4,512,1536]{2,1,0:T(8,128)(2,1)}), bf16[4,512,1536]{2,1,0:T(8,128)(2,1)}, u32[]{:S(2)}, u32[]{:S(2)}) async-start(bf16[4,512,1536]{2,1,0:T(8,128)(2,1)} %bitcast.69), calls=%async_computation.3 | async-start | bytes 12582912 | tf_op jit(solution)/shard_map/all_to_all | solution.py:87
  77.6 0.2 all-reduce.3.cloned.1.call-start
  77.8 2.1 compare_convert_fusion
  80.0 2.5 copy.33
  82.5 2.1 bitcast_convert_fusion.1
  84.6 5.1 %multiply_reduce_fusion.1 = f32[2048,16]{0,1:T(8,128)} fusion(f32[2048,128]{0,1:T(8,128)} %copy.33, bf16[2048,256,1]{1,0,2:T(8,128)(2,1)} %bitcast.7, bf16[128,16,256]{2,1,0:T(8,128)(2,1)} %param.11), kind=kOutput, calls=%fused_computation.6 | convolution fusion | flops 2155839488 | bytes 3276800 | tf_op jit(solution)/shard_map/dot_general | solution.py:14
  89.7 125.6 %all-to-all-done.3 = bf16[4,512,1536]{2,1,0:T(8,128)(2,1)} async-done(((bf16[4,512,1536]{2,1,0:T(8,128)(2,1)}), bf16[4,512,1536]{2,1,0:T(8,128)(2,1)}, u32[]{:S(2)}, u32[]{:S(2)}) %all-to-all-start.3) | async-done | bytes 6291488 | tf_op jit(solution)/shard_map/all_to_all | solution.py:87
  215.3 20.8 %multiply_reduce_fusion = f32[2048,16]{0,1:T(8,128)} fusion(f32[2048,128]{0,1:T(8,128)} %copy.33, bf16[2048,1536,1]{1,0,2:T(8,128)(2,1)} %bitcast.15, bf16[128,16,1536]{2,1,0:T(8,128)(2,1)} %param.10), kind=kOutput, calls=%fused_computation.5 | convolution fusion | flops 12893257728 | bytes 13762560 | tf_op jit(solution)/shard_map/dot_general | solution.py:13
  236.0 0.0 all-reduce.3.cloned.1.call-update
  236.0 1.3 convert_reduce_fusion
  237.3 2.0 copy.32
  239.4 28.1 %all-reduce.3.cloned.1.call-done = (f32[2048,16]{0,1:T(8,128)}, f32[2048,16]{0,1:T(8,128)}) async-done(((f32[2048,16]{0,1:T(8,128)}, f32[2048,16]{0,1:T(8,128)}), (f32[2048,16]{0,1:T(8,128)}, f32[2048,16]{0,1:T(8,128)})) %all-reduce.3.cloned.1.call-update) | async-done | bytes 262160 | tf_op jit(solution)/shard_map/psum | solution.py:21
  267.4 1.0 multiply_convert_fusion
  268.4 0.5 broadcast.243
  269.0 0.7 reduce.8
  269.6 0.6 reshape.363
  270.2 4.6 all-to-all-start.4
  274.8 16.8 %bitcast_convert_fusion = bf16[2048,1536]{1,0:T(8,128)(2,1)} fusion(bf16[128,16,1536]{2,1,0:T(8,128)(2,1)} %param.10, bf16[2048,16]{0,1:T(8,128)(2,1)S(1)} %get-tuple-element.20, bf16[2048,128]{0,1:T(8,128)(2,1)} %copy.32), kind=kOutput, calls=%fused_computation.7 | convolution fusion | flops 12892241920 | bytes 13172736 | tf_op jit(solution)/shard_map/dot_general | solution.py:32
  291.6 0.0 all-to-all-done.4
  291.6 5.2 %all-to-all-start.2 = ((bf16[4,512,1536]{2,1,0:T(8,128)(2,1)}), bf16[4,512,1536]{2,1,0:T(8,128)(2,1)}, u32[]{:S(2)}, u32[]{:S(2)}) async-start(bf16[4,512,1536]{2,1,0:T(8,128)(2,1)} %bitcast.73), calls=%async_computation.2 | async-start | bytes 12582912 | tf_op jit(solution)/shard_map/all_to_all | solution.py:97
  296.8 0.3 all-gather.2.cloned.1.call-start
  297.1 0.5 all-gather.2.cloned.1.call-update
  297.6 7.9 %broadcast_multiply_fusion = (bf16[2048,128,16]{0,2,1:T(8,128)(2,1)}, bf16[2048,128,16]{0,2,1:T(8,128)(2,1)}) fusion(bf16[2048,16]{0,1:T(8,128)(2,1)S(1)} %get-tuple-element.18, bf16[2048,128]{0,1:T(8,128)(2,1)} %copy.32, bf16[2048,16]{0,1:T(8,128)(2,1)S(1)} %get-tuple-element.20), kind=kLoop, calls=%fused_computation.10 | loop fusion | flops 8388608 | bytes 17432576 | tf_op jit(solution)/shard_map/mul | solution.py:29
  305.5 0.0 copy-start.1
  305.5 7.3 %convolution_convert_fusion.1 = bf16[2048,256]{1,0:T(8,128)(2,1)} fusion(bf16[2048,2048]{0,1:T(8,128)(2,1)} %bitcast.72, bf16[2048,256]{1,0:T(8,128)(2,1)} %bitcast.6), kind=kOutput, calls=%fused_computation.19 | convolution fusion | flops 2148007936 | bytes 10485760 | tf_op jit(solution)/shard_map/dot_general | solution.py:114
  312.8 0.0 copy-done.1
  312.8 17.1 %convolution_convert_fusion = bf16[2048,1536]{1,0:T(8,128)(2,1)} fusion(bf16[2048,2048]{0,1:T(8,128)(2,1)S(1)} %bitcast.71, bf16[2048,1536]{1,0:T(8,128)(2,1)} %bitcast.14), kind=kOutput, calls=%fused_computation.8 | convolution fusion | flops 12888047616 | bytes 20971520 | tf_op jit(solution)/shard_map/dot_general | solution.py:113
  329.9 6.8 %gather_fusion.1 = bf16[1024]{0:T(1024)(128)(2,1)S(1)} fusion(bf16[2048]{0:T(1024)(128)(2,1)S(1)} %bitcast.68, s32[1024]{0:T(1024)S(1)} %broadcast_clamp_fusion), kind=kCustom, calls=%fused_computation.1 | custom fusion | bytes 8192 | tf_op jit(solution)/shard_map/gather | solution.py:129
  336.8 0.3 reshape.304
  337.0 0.7 copy.39
  337.7 96.3 %all-to-all-done.2 = bf16[4,512,1536]{2,1,0:T(8,128)(2,1)} async-done(((bf16[4,512,1536]{2,1,0:T(8,128)(2,1)}), bf16[4,512,1536]{2,1,0:T(8,128)(2,1)}, u32[]{:S(2)}, u32[]{:S(2)}) %all-to-all-start.2) | async-done | bytes 6291488 | tf_op jit(solution)/shard_map/all_to_all | solution.py:97
  434.0 10.9 %gather_fusion = bf16[1024,1536]{1,0:T(8,128)(2,1)} fusion(bf16[2048,1536]{1,0:T(8,128)(2,1)} %bitcast.10, s32[1024]{0:T(1024)S(1)} %broadcast_clamp_fusion), kind=kCustom, calls=%fused_computation | custom fusion | bytes 6295552 | tf_op jit(solution)/shard_map/gather | solution.py:122
  445.0 8.0 %reshape.313 = f32[512,2,1536]{2,1,0:T(2,128)} reshape(bf16[1024,1536]{1,0:T(8,128)(2,1)} %gather_fusion) | data formatting | bytes 9437184 | tf_op jit(solution)/shard_map/convert_element_type | solution.py:124
  453.0 12.7 %fusion.18 = (f32[512,1,1536]{2,1,0:T(1,128)}, f32[512,1,1536]{2,1,0:T(1,128)}) fusion(f32[512,2,1536]{2,1,0:T(2,128)} %reshape.313), kind=kLoop, calls=%fused_computation.66 | loop fusion | bytes 12582912 | tf_op jit(solution)/shard_map/slice | solution.py:126
  465.6 0.0 all-gather.2.cloned.1.call-done
  465.6 0.0 copy-done
  465.6 6.2 %fusion.4 = bf16[512,1536]{1,0:T(8,128)(2,1)} fusion(f32[512,1,1536]{2,1,0:T(1,128)} %get-tuple-element.15, f32[512,1,1536]{2,1,0:T(1,128)} %get-tuple-element.14, bf16[512,1024]{1,0:T(8,128)(2,1)} %all-gather.2.cloned.1.call-done, bf16[1536,1024]{1,0:T(8,128)(2,1)S(1)} %copy-done), kind=kOutput, calls=%fused_computation.18 | convolution fusion | flops 1612972032 | bytes 12058624 | tf_op jit(solution)/shard_map/dot_general | solution.py:56
  (12 shorter events, 0.2 us)
Async XLA Ops:
  7.2 458.5 %copy-start = (bf16[1536,1024]{1,0:T(8,128)(2,1)S(1)}, bf16[1536,1024]{1,0:T(8,128)(2,1)}, u32[]{:S(2)}) copy-start(bf16[1536,1024]{1,0:T(8,128)(2,1)} %param.9) | copy-start | bytes 9437188
  21.5 20.9 %all-to-all-start = ((bf16[4,512,128]{2,1,0:T(8,128)(2,1)}), bf16[4,512,128]{2,1,0:T(8,128)(2,1)}, u32[]{:S(2)}, u32[]{:S(2)}) async-start(bf16[4,512,128]{2,1,0:T(8,128)(2,1)} %bitcast.75), calls=%async_computation | async-start | bytes 1048576 | tf_op jit(solution)/shard_map/all_to_all | solution.py:89
  42.4 30.0 %all-to-all-start.1 = ((bf16[4,512,256]{2,1,0:T(8,128)(2,1)}), bf16[4,512,256]{2,1,0:T(8,128)(2,1)}, u32[]{:S(2)}, u32[]{:S(2)}) async-start(bf16[4,512,256]{2,1,0:T(8,128)(2,1)} %bitcast.74), calls=%async_computation.1 | async-start | bytes 2097152 | tf_op jit(solution)/shard_map/all_to_all | solution.py:88
  72.4 142.9 %all-to-all-start.3 = ((bf16[4,512,1536]{2,1,0:T(8,128)(2,1)}), bf16[4,512,1536]{2,1,0:T(8,128)(2,1)}, u32[]{:S(2)}, u32[]{:S(2)}) async-start(bf16[4,512,1536]{2,1,0:T(8,128)(2,1)} %bitcast.69), calls=%async_computation.3 | async-start | bytes 12582912 | tf_op jit(solution)/shard_map/all_to_all | solution.py:87
  77.6 189.8 %all-reduce.3.cloned.1.call-start = ((), (), s32[]{:S(2)}) async-start(), calls=%async_computation.6 | async-start | bytes 524288 | tf_op jit(solution)/shard_map/psum | solution.py:21
  270.2 21.4 %all-to-all-start.4 = ((bf16[4,2,256]{2,1,0:T(2,128)(2,1)}), bf16[4,2,256]{2,1,0:T(2,128)(2,1)S(1)}, u32[]{:S(2)}, u32[]{:S(2)}) async-start(bf16[4,2,256]{2,1,0:T(2,128)(2,1)} %reshape.363), calls=%async_computation.4 | async-start | bytes 8192 | tf_op jit(solution)/shard_map/all_to_all | solution.py:104
  291.6 142.4 %all-to-all-start.2 = ((bf16[4,512,1536]{2,1,0:T(8,128)(2,1)}), bf16[4,512,1536]{2,1,0:T(8,128)(2,1)}, u32[]{:S(2)}, u32[]{:S(2)}) async-start(bf16[4,512,1536]{2,1,0:T(8,128)(2,1)} %bitcast.73), calls=%async_computation.2 | async-start | bytes 12582912 | tf_op jit(solution)/shard_map/all_to_all | solution.py:97
  296.8 168.8 %all-gather.2.cloned.1.call-start = ((), (), s32[]{:S(2)}) async-start(), calls=%async_computation.5 | async-start | bytes 1310720 | tf_op jit(solution)/shard_map/all_gather | solution.py:55
  305.5 7.3 %copy-start.1 = (bf16[2048,128,16]{0,2,1:T(8,128)(2,1)S(1)}, bf16[2048,128,16]{0,2,1:T(8,128)(2,1)}, u32[]{:S(2)}) copy-start(bf16[2048,128,16]{0,2,1:T(8,128)(2,1)} %get-tuple-element.17) | copy-start | bytes 25165828
Sparse Core Ops, SparseCore 0:
  236.2 31.2 all-reduce.2
  299.3 17.3 all-gather.1
where the time goes:
time: 486 us; the launch traced here: 479 us
  waiting for transfers between devices  258 us (53%)
  local copies, waits for them, and re-layouts  89.1 us (18%)
  matrix products  73.2 us (15%)
  starting transfers between devices  26.6 us (5%)
  other arithmetic  18.1 us (4%)
  between operations  14.6 us (3%)
    all_to_all x1, waiting for transfers between devices, per_device(): lax.all_to_all(send_rows, 'dp', split_axis=0, concat_axis=0, tiled=True)  126 us
    all_to_all x1, waiting for transfers between devices, per_device(): lax.all_to_all(back_rows.reshape(owners_count, capacity, input_width), 'd...  96.3 us
    psum x1, waiting for transfers between devices, route_rows(): low_in, low_out = lax.psum((part_in, part_out), 'mp')  28.1 us
    dot_general x1, matrix products, route_rows(): lax.dot_general(flat_in, down_flattened, dims, preferred_element_type=jnp...  20.8 us
    dot_general x1, matrix products, per_device(): lax.dot_general(spread_out, flat_in, rows_dims, preferred_element_type=jn...  17.1 us
    dot_general x1, matrix products, route_rows(): jnp.dot(spread_out, down_flattened, preferred_element_type=jnp.float32)  16.8 us
    slice x1, local copies, waits for them, and re-layouts, per_device(): adapter_rows[:, 0]  12.7 us
    unnamed x12, local copies, waits for them, and re-layouts  11.6 us
  transfers between devices with their start and end apart: 7, of which 5 were waited for; matrix products, arithmetic and copies ran while one was open for 28% of the time, Pallas kernels for 0%

commit v1 on v0

v1 whole, which is shorter than its diff:
```python
import functools

import jax
import jax.numpy as jnp
from jax import lax
from jax.experimental import pallas as pl
from jax.experimental.pallas import tpu as pltpu
from jax.sharding import PartitionSpec as P

BF = jnp.bfloat16
F32 = jnp.float32
CHUNKS = 2
NT = (((1,), (1,)), ((), ()))


def call(body, out_shape, *, grid=None, in_specs=None, out_specs=None, scratch=(), prefetch=0,
         aliases=None, flops=0, moved=0, vmem=40):
    steps = len(grid) if grid else 0
    return pl.pallas_call(
        body,
        out_shape=out_shape,
        grid_spec=pltpu.PrefetchScalarGridSpec(
            num_scalar_prefetch=prefetch,
            grid=grid or (1,),
            in_specs=in_specs,
            out_specs=out_specs,
            scratch_shapes=list(scratch),
        ),
        input_output_aliases=aliases or {},
        compiler_params=pltpu.CompilerParams(
            vmem_limit_bytes=vmem << 20, dimension_semantics=("arbitrary",) * max(steps, 1)
        ),
        cost_estimate=pl.CostEstimate(flops=int(flops), bytes_accessed=int(moved), transcendentals=0),
    )


def whole(shape):
    return pl.BlockSpec(shape, lambda *_: (0,) * len(shape))


ANY = pl.BlockSpec(memory_space=pl.ANY)


def pack_body(index_ref, gate_ref, rows_ref, out_ref):
    count, width = rows_ref.shape
    out_ref[:count, :] = rows_ref[...]
    index = index_ref[...]
    gate = gate_ref[...].astype(F32)
    high, low = (index >> 4).astype(F32), (index & 15).astype(F32)
    pieces = []
    for vector in (high, low, gate):
        for slot in range(2):
            for part in range(count // width):
                pieces.append(vector[slot : slot + 1, part * width : (part + 1) * width])
    extra = out_ref.shape[0] - count
    if extra > len(pieces):
        pieces.append(jnp.zeros((extra - len(pieces), width), F32))
    out_ref[count:, :] = jnp.concatenate(pieces, axis=0).astype(BF)


def pack_rows(index, gate, rows):
    count, width = rows.shape
    extra = -(-6 * (count // width) // 16) * 16
    shape = (count + extra, width)
    return call(
        pack_body,
        jax.ShapeDtypeStruct(shape, BF),
        in_specs=[whole(index.shape), whole(gate.shape), whole(rows.shape)],
        out_specs=whole(shape),
        moved=4 * count * width,
    )(index, gate, rows)


def unpack_extra(block, count, width, base):
    per = count // width
    vectors = []
    for v in range(6):
        rows = block[v * per : (v + 1) * per, :].astype(F32)
        vectors.append(jnp.concatenate([rows[q : q + 1, :] for q in range(per)], axis=1))
    ids = [vectors[k] * 16.0 + vectors[2 + k] - base for k in range(2)]
    return jnp.concatenate(ids + vectors[4:6] + [jnp.zeros((4, count), F32)], axis=0)


def pick(product, ids, first, rank, kept):
    kept = list(kept)
    for a in range(product.shape[0] // rank):
        rows = product[a * rank : (a + 1) * rank, :]
        here = (first + a).astype(F32) if hasattr(first, "astype") else float(first + a)
        for k in range(2):
            kept[k] = jnp.where(ids[k : k + 1, :] == here, rows, kept[k])
    return kept


def project_out_body(rank, base_ref, up_ref, *refs):
    blocks, (part_ref, aux_ref) = refs[:-2], refs[-2:]
    count = part_ref.shape[1]
    width = up_ref.shape[1]
    total = up_ref.shape[0]
    step = min(1024, total)
    base = base_ref[0].astype(F32)
    for s, block in enumerate(blocks):
        aux = unpack_extra(block[count:, :], count, width, base)
        aux_ref[8 * s : 8 * s + 8, :] = aux
        ids = aux[0:2, :]

        def body(b, kept):
            product = lax.dot_general(
                up_ref[pl.ds(pl.multiple_of(b * step, step), step), :], block[:count, :], NT,
                preferred_element_type=F32,
            )
            return tuple(pick(product, ids, b * (step // rank), rank, kept))

        zero = jnp.zeros((rank, count), F32)
        kept = lax.fori_loop(0, total // step, body, (zero, zero))
        part_ref[2 * rank * s : 2 * rank * s + rank, :] = kept[0]
        part_ref[2 * rank * s + rank : 2 * rank * (s + 1), :] = kept[1]


def project_out(base, up, blocks, count, rank):
    slots = len(blocks)
    total, width = up.shape
    shapes = [(slots * 2 * rank, count), (slots * 8, count)]
    return call(
        functools.partial(project_out_body, rank),
        [jax.ShapeDtypeStruct(s, F32) for s in shapes],
        in_specs=[whole(up.shape)] + [whole(b.shape) for b in blocks],
        out_specs=[whole(s) for s in shapes],
        prefetch=1,
        flops=2 * slots * count * total * width,
        moved=2 * (slots * count * width + total * width),
        vmem=48,
    )(base, up, *blocks)


def project_in_body(rank, chunks, plan_ref, down_ref, aux_ref, before_ref, *refs):
    rows, (out_ref, kept_ref) = refs[:-2], refs[-2:]
    source, b = pl.program_id(0), pl.program_id(1)
    step = down_ref.shape[0]
    valid, slot = plan_ref[2 * source], plan_ref[2 * source + 1]

    @pl.when((source == 0) & (b == 0))
    def _():
        out_ref[...] = before_ref[...]

    @pl.when(valid == 1)
    def _():
        @pl.when(b == 0)
        def _():
            kept_ref[...] = jnp.zeros_like(kept_ref)

        for s in range(len(rows) // chunks):
            @pl.when(source == s)
            def _():
                at = 0
                for c in range(chunks):
                    ref = rows[s * chunks + c]
                    size = ref.shape[0]
                    ids = aux_ref[pl.ds(pl.multiple_of(slot * 8, 8), 8), at : at + size]
                    product = lax.dot_general(
                        down_ref[...], ref[...], NT, preferred_element_type=F32
                    )
                    kept = [kept_ref[:rank, at : at + size], kept_ref[rank:, at : at + size]]
                    kept = pick(product, ids, b * (step // rank), rank, kept)
                    kept_ref[:rank, at : at + size] = kept[0]
                    kept_ref[rank:, at : at + size] = kept[1]
                    at += size

        @pl.when(b == pl.num_programs(1) - 1)
        def _():
            out_ref[pl.ds(pl.multiple_of(slot * 2 * rank, 2 * rank), 2 * rank), :] = kept_ref[...]


def project_in(plan, down, aux, before, rows, chunks, rank):
    total, width = down.shape
    sources = len(rows) // chunks
    step = min(512, total)
    count = aux.shape[1]
    return call(
        functools.partial(project_in_body, rank, chunks),
        jax.ShapeDtypeStruct(before.shape, F32),
        grid=(sources, total // step),
        in_specs=[
            pl.BlockSpec((step, width), lambda s, b, plan: (b * plan[2 * s], 0)),
            whole(aux.shape),
            whole(before.shape),
        ]
        + [whole(r.shape) for r in rows],
        out_specs=whole(before.shape),
        scratch=[pltpu.VMEM((2 * rank, count), F32)],
        prefetch=1,
        aliases={3: 0},
        flops=2 * count * total * width,
        moved=2 * (count * width + total * width),
        vmem=48,
    )(plan, down, aux, before, *rows)


def adapter_rows_body(rank, parts, order_ref, *refs):
    part_refs, (aux_ref, down_ref, out_ref, spread_ref) = refs[:parts], refs[parts:]
    n, s = pl.program_id(0), pl.program_id(1)
    slot = order_ref[s]
    count = aux_ref.shape[1]
    total = down_ref.shape[0]
    here = pl.ds(pl.multiple_of(s * count, count), count)

    @pl.when(n == 0)
    def _():
        at = pl.ds(pl.multiple_of(slot * 2 * rank, 2 * rank), 2 * rank)
        low = part_refs[0][at, :]
        for ref in part_refs[1:]:
            low = low + ref[at, :]
        aux = aux_ref[pl.ds(pl.multiple_of(slot * 8, 8), 8), :]
        repeat = 128 // rank
        group = (lax.broadcasted_iota(jnp.int32, (128, count), 0) // rank).astype(F32)
        keys, values = [], []
        for k in range(2):
            scaled = (aux[2 + k : 3 + k, :] * low[k * rank : (k + 1) * rank, :]).astype(BF).astype(F32)
            values.append(jnp.concatenate([scaled] * repeat, axis=0).T)
            keys.append((aux[k : k + 1, :] - group).T)
        for g in range(total // 128):
            first = float(g * repeat)
            spread = jnp.where(keys[0] == first, values[0], jnp.where(keys[1] == first, values[1], 0.0))
            spread_ref[here, g * 128 : (g + 1) * 128] = spread.astype(BF)

    out_ref[0] = jnp.dot(spread_ref[here, :], down_ref[...], preferred_element_type=F32).astype(BF)


def adapter_rows(order, parts, aux, down, rank):
    slots = order.shape[0]
    total, width = down.shape
    count = aux.shape[1]
    step = 256
    return call(
        functools.partial(adapter_rows_body, rank, len(parts)),
        jax.ShapeDtypeStruct((slots, count, width), BF),
        grid=(width // step, slots),
        in_specs=[whole(p.shape) for p in parts]
        + [whole(aux.shape), pl.BlockSpec((total, step), lambda n, s, order: (0, n))],
        out_specs=pl.BlockSpec((1, count, step), lambda n, s, order: (s, 0, n)),
        scratch=[pltpu.VMEM((slots * count, total), BF)],
        prefetch=1,
        flops=2 * slots * count * total * width,
        moved=2 * (total * width + slots * count * width),
        vmem=48,
    )(order, *parts, aux, down)


def add_body(plan_ref, first_ref, second_ref, near_ref, far_ref, *refs):
    outs = refs[:2]
    held, terms, in_sem, term_sem, out_sem = refs[2:]
    size, width = held.shape[1:]
    pieces = in_sem.shape[1]
    piece = size // pieces
    row = plan_ref[4]
    for i, (source, out) in enumerate(zip((first_ref, second_ref), outs)):
        do, place = plan_ref[2 * i], plan_ref[2 * i + 1]

        def get(q):
            rows = pl.ds(q * piece, piece)
            return pltpu.make_async_copy(source.at[rows], held.at[i, rows], in_sem.at[i, q])

        def put(q):
            rows = pl.ds(q * piece, piece)
            return pltpu.make_async_copy(held.at[i, rows], out.at[rows], out_sem.at[i, q])

        def term(q, ref, index):
            rows = pl.ds(pl.multiple_of(row + q * piece, piece), piece)
            return pltpu.make_async_copy(
                ref.at[index, rows], terms.at[i, pl.ds(q * piece, piece)], term_sem.at[i, q]
            )

        @pl.when(do == 1)
        def _():
            for q in range(pieces):
                get(q).start()

                @pl.when(place == 0)
                def _():
                    term(q, near_ref, 0).start()

                @pl.when(place != 0)
                def _():
                    term(q, far_ref, jnp.maximum(place - 1, 0)).start()

            for q in range(pieces):
                get(q).wait()
                term(q, near_ref, 0).wait()
                rows = pl.ds(q * piece, piece)
                held[i, rows, :] = (held[i, rows, :].astype(F32) + terms[i, rows, :].astype(F32)).astype(BF)
                put(q).start()
            for q in range(pieces):
                put(q).wait()


def ring_add(plan, first, second, near, far):
    shape = first.shape
    pieces = 4 if shape[0] % 64 == 0 else 1
    return call(
        add_body,
        [jax.ShapeDtypeStruct(shape, BF)] * 2,
        in_specs=[ANY] * 4,
        out_specs=[ANY] * 2,
        scratch=[
            pltpu.VMEM((2,) + shape, BF),
            pltpu.VMEM((2,) + shape, BF),
            pltpu.SemaphoreType.DMA((2, pieces)),
            pltpu.SemaphoreType.DMA((2, pieces)),
            pltpu.SemaphoreType.DMA((2, pieces)),
        ],
        prefetch=1,
        aliases={1: 0, 2: 1},
        flops=2 * shape[0] * shape[1],
        moved=6 * shape[0] * shape[1],
    )(plan, first, second, near, far)


def spread_rows(values, ids, first, adapters):
    rows = []
    for a in range(adapters):
        here = (first + a).astype(F32)
        rows.append(
            jnp.where(ids[0:1, :] == here, values[0], jnp.where(ids[1:2, :] == here, values[1], 0.0)).astype(BF)
        )
    return jnp.concatenate(rows, axis=0)


def grad_down_body(rank, parts, where, plan_ref, *refs):
    part_refs, aux_ref = refs[:parts], refs[parts]
    row_refs = refs[parts + 1 : parts + 1 + len(where)]
    out_ref, rows_ref, scaled_ref, sem = refs[parts + 1 + len(where) :]
    b = pl.program_id(0)
    count = aux_ref.shape[1]
    slots = rows_ref.shape[0] // count
    step = out_ref.shape[0]

    def copies(act):
        for i, (source, offset) in enumerate(where):
            size = row_refs[i].shape[0]

            @pl.when(plan_ref[2 * source] == 1)
            def _():
                start = plan_ref[2 * source + 1] * count + offset
                act(
                    pltpu.make_async_copy(
                        row_refs[i], rows_ref.at[pl.ds(pl.multiple_of(start, size), size)], sem.at[i]
                    )
                )

    @pl.when(b == 0)
    def _():
        copies(lambda c: c.start())
        for s in range(slots):
            low = part_refs[0][2 * rank * s : 2 * rank * (s + 1), :]
            for ref in part_refs[1:]:
                low = low + ref[2 * rank * s : 2 * rank * (s + 1), :]
            for k in range(2):
                scaled = aux_ref[8 * s + 2 + k : 8 * s + 3 + k, :] * low[k * rank : (k + 1) * rank, :]
                scaled_ref[k, :, s * count : (s + 1) * count] = scaled.astype(BF).astype(F32)
        copies(lambda c: c.wait())

    spread = []
    for s in range(slots):
        values = [scaled_ref[k, :, s * count : (s + 1) * count] for k in range(2)]
        spread.append(
            spread_rows(values, aux_ref[8 * s : 8 * s + 2, :], b * (step // rank), step // rank)
        )
    out_ref[...] = jnp.dot(
        jnp.concatenate(spread, axis=1), rows_ref[...], preferred_element_type=F32
    ).astype(BF)


def grad_down(plan, parts, aux, rows, where, total, rank):
    count = aux.shape[1]
    slots = aux.shape[0] // 8
    width = rows[0].shape[1]
    step = min(256, total)
    return call(
        functools.partial(grad_down_body, rank, len(parts), where),
        jax.ShapeDtypeStruct((total, width), BF),
        grid=(total // step,),
        in_specs=[whole(p.shape) for p in parts] + [whole(aux.shape)] + [ANY] * len(rows),
        out_specs=pl.BlockSpec((step, width), lambda b, plan: (b, 0)),
        scratch=[
            pltpu.VMEM((slots * count, width), BF),
            pltpu.VMEM((2, rank, slots * count), F32),
            pltpu.SemaphoreType.DMA((len(rows),)),
        ],
        prefetch=1,
        flops=2 * slots * count * total * width,
        moved=2 * (total * width + slots * count * width),
        vmem=56,
    )(plan, *parts, aux, *rows)


def grad_up_body(rank, parts, slots, *refs):
    in_refs, out_refs, aux_ref = refs[:parts], refs[parts : 2 * parts], refs[2 * parts]
    blocks = refs[2 * parts + 1 : 2 * parts + 1 + slots]
    up_ref = refs[2 * parts + 1 + slots]
    gate_refs = refs[2 * parts + 2 + slots : 2 * parts + 2 + 2 * slots]
    rows_ref, scaled_ref = refs[-2:]
    b = pl.program_id(0)
    count = aux_ref.shape[1]
    step = up_ref.shape[0]

    @pl.when(b == 0)
    def _():
        for s in range(slots):
            rows_ref[s * count : (s + 1) * count, :] = blocks[s][:count, :]
            at = slice(2 * rank * s, 2 * rank * (s + 1))
            low_in, low_out = in_refs[0][at, :], out_refs[0][at, :]
            for ref in in_refs[1:]:
                low_in = low_in + ref[at, :]
            for ref in out_refs[1:]:
                low_out = low_out + ref[at, :]
            both = low_in * low_out
            gates = []
            for k in range(2):
                gates.append(jnp.sum(both[k * rank : (k + 1) * rank, :], axis=0, keepdims=True))
                scaled = aux_ref[8 * s + 2 + k : 8 * s + 3 + k, :] * low_in[k * rank : (k + 1) * rank, :]
                scaled_ref[k, :, s * count : (s + 1) * count] = scaled.astype(BF).astype(F32)
            gate_refs[s][...] = jnp.concatenate(gates, axis=0).astype(BF)

    spread = []
    for s in range(slots):
        values = [scaled_ref[k, :, s * count : (s + 1) * count] for k in range(2)]
        spread.append(
            spread_rows(values, aux_ref[8 * s : 8 * s + 2, :], b * (step // rank), step // rank)
        )
    up_ref[...] = jnp.dot(
        jnp.concatenate(spread, axis=1), rows_ref[...], preferred_element_type=F32
    ).astype(BF)


def grad_up(parts_in, parts_out, aux, blocks, total, rank):
    count = aux.shape[1]
    slots = len(blocks)
    width = blocks[0].shape[1]
    step = min(256, total)
    outs = [jax.ShapeDtypeStruct((total, width), BF)] + [jax.ShapeDtypeStruct((2, count), BF)] * slots
    arrays = [*parts_in, *parts_out, aux, *blocks]
    return call(
        functools.partial(grad_up_body, rank, len(parts_in), slots),
        outs,
        grid=(total // step,),
        in_specs=[whole(a.shape) for a in arrays],
        out_specs=[pl.BlockSpec((step, width), lambda b: (b, 0))] + [whole((2, count))] * slots,
        scratch=[pltpu.VMEM((slots * count, width), BF), pltpu.VMEM((2, rank, slots * count), F32)],
        flops=2 * slots * count * total * width,
        moved=2 * (total * width + slots * count * width),
    )(*arrays)


def finish_body(base_ref, first_ref, second_ref, *refs):
    out_ref = refs[-1]
    out_ref[...] = (
        base_ref[...] + first_ref[...].astype(F32) + second_ref[...].astype(F32)
    ).astype(BF)


def finish(base, first, second, chunk, before):
    size, width = first.shape
    step = min(64, size)
    blocks = size // step
    shift = pl.BlockSpec((step, width), lambda i: (i + chunk * blocks, 0))
    local = pl.BlockSpec((step, width), lambda i: (i, 0))
    arrays = [base, first, second] + ([] if before is None else [before])
    return call(
        finish_body,
        jax.ShapeDtypeStruct(base.shape, BF),
        grid=(blocks,),
        in_specs=[shift, local, local] + ([] if before is None else [ANY]),
        out_specs=shift,
        aliases=None if before is None else {3: 0},
        flops=2 * size * width,
        moved=10 * size * width,
    )(*arrays)


def per_device(inputs, output_gradient, frozen_key_weight, adapter_down_factors, adapter_up_factors,
               token_adapter_index, gates):
    count, width = inputs.shape
    out_width = output_gradient.shape[1]
    size = lax.axis_size("dp")
    shares = lax.axis_size("mp")
    local, rank = adapter_down_factors.shape[:2]
    total = local * rank
    d = lax.axis_index("dp")
    odd = d % 2
    half = count // CHUNKS
    down = adapter_down_factors.reshape(total, width)
    up = adapter_up_factors.reshape(total, out_width)
    pairs_a = [p for i in range(0, size - 1, 2) for p in ((i, i + 1), (i + 1, i))]
    pairs_b = [p for i in range(1, size - 1, 2) for p in ((i, i + 1), (i + 1, i))]
    i32 = jnp.int32

    block = pack_rows(token_adapter_index.T, gates.T, output_gradient)
    blocks = [block] + [
        lax.ppermute(block, "dp", [(i, (i + s) % size) for i in range(size)]) for s in range(1, size)
    ]
    full_out = lax.all_gather(output_gradient, "mp", axis=1, tiled=True)

    def exchange(part):
        if shares > 4:
            return [lax.psum(part, "mp")]
        return [part] + [
            lax.ppermute(part, "mp", [(i, (i + s) % shares) for i in range(shares)])
            for s in range(1, shares)
        ]

    base_id = (d * local).astype(i32).reshape(1)
    part_out, aux = project_out(base_id, up, blocks, count, rank)
    parts_out = exchange(part_out)

    ahead = d < (size + 1) // 2
    order = jnp.where(ahead, jnp.arange(1, size), jnp.arange(size - 1, 0, -1)).astype(i32)
    order = jnp.concatenate([order, jnp.zeros((1,), i32)])
    near = adapter_rows(order[:1], parts_out, aux, down, rank)
    far = adapter_rows(order[1:], parts_out, aux, down, rank)

    frozen = lax.dot_general(full_out, frozen_key_weight, NT, preferred_element_type=F32)
    frozen = frozen + far[size - 2].astype(F32)

    def arrival(j, a):
        left = (odd == 1) if a else (odd == 0)
        slot = jnp.where(left, j + 1, size - 1 - j)
        valid = jnp.where(left, d >= j + 1, d + j + 1 <= size - 1)
        return [valid.astype(i32), slot.astype(i32)]

    def departure(j, a):
        right = (odd == 0) if a else (odd == 1)
        slot = jnp.where(right, j, size - j)
        do = jnp.where(right, j > d, j > size - 1 - d)
        place = jnp.where(ahead, slot - 1, size - 1 - slot)
        return [do.astype(i32), place.astype(i32)]

    zero = jnp.zeros((), i32)
    low = jnp.zeros((size * 2 * rank, count), F32)
    low = project_in(
        jnp.stack([zero + 1, zero]), down, aux, low, [inputs], 1, rank
    )
    rows, where, plan = [inputs], [(0, 0)], [zero + 1, zero]
    send = [[inputs[c * half : (c + 1) * half]] * 2 for c in range(CHUNKS)]
    result = None
    for j in range(size):
        got = []
        for c in range(CHUNKS):
            to_a, to_b = send[c]
            if j > 0:
                steps = jnp.stack(departure(j, True) + departure(j, False) + [zero + c * half])
                to_a, to_b = ring_add(steps, to_a, to_b, near, far)
                rows += [to_b, to_a]
                where += [(2 * j - 1, c * half), (2 * j, c * half)]
            got.append((lax.ppermute(to_a, "dp", pairs_a), lax.ppermute(to_b, "dp", pairs_b)))
            send[c] = [got[c][1], got[c][0]]
        if j > 0:
            steps = arrival(j - 1, True) + arrival(j - 1, False)
            plan += steps
            last = rows[-2 * CHUNKS :]
            low = project_in(
                jnp.stack(steps), down, aux, low, last[0::2] + last[1::2], CHUNKS, rank
            )
        if j == size - 1:
            for c in range(CHUNKS):
                result = finish(frozen, got[c][0], got[c][1], c, result)

    parts_in = exchange(low)
    down_gradient = grad_down(jnp.stack(plan), parts_out, aux, rows, where, total, rank)
    up_gradient, *gate_rows = grad_up(parts_in, parts_out, aux, blocks, total, rank)
    gate_sum = gate_rows[0].astype(F32)
    for s in range(1, size):
        gate_sum = gate_sum + lax.ppermute(
            gate_rows[s], "dp", [(i, (i - s) % size) for i in range(size)]
        ).astype(F32)
    return (
        result,
        gate_sum.astype(BF).T,
        down_gradient.reshape(local, rank, width),
        up_gradient.reshape(local, rank, out_width),
    )


def solution(mesh):
    in_specs = (
        P(("groups", "dp"), "mp"),
        P(("groups", "dp"), "mp"),
        P("mp", None),
        P("dp", None, "mp"),
        P("dp", None, "mp"),
        P(("groups", "dp"), None),
        P(("groups", "dp"), None),
    )
    out_specs = (
        P(("groups", "dp"), "mp"),
        P(("groups", "dp"), None),
        P(("groups", "dp"), None, "mp"),
        P(("groups", "dp"), None, "mp"),
    )
    return jax.shard_map(
        per_device, mesh=mesh, in_specs=in_specs, out_specs=out_specs, check_vma=False
    )
```

time: 486 us -> 263 us (0.54); the launches traced: 479 us -> 262 us
  waiting for transfers between devices: 258 us -> 65.6 us
  Pallas kernels: 0 us -> 122 us
  local copies, waits for them, and re-layouts: 89.1 us -> 10.7 us
  matrix products: 73.2 us -> 3.55 us
  starting transfers between devices: 26.6 us -> 44.9 us
  other arithmetic: 18.1 us -> 0.9 us
    all_to_all x5 -> x0, waiting for transfers between devices: 229 us -> none  [the longest x1 126 us: per_device(): lax.all_to_all(send_rows, 'dp', split_axis=0, concat_axis=0, tiled=True)]
    pallas_call x0 -> x18, Pallas kernels: none -> 122 us  [the longest x4 33.8 us: project_in(): call(functools.partial(project_in_body, rank, chunks), jax.ShapeDtypeStru...]
    dot_general x6 -> x1, matrix products: 73.2 us -> 3.55 us  [per_device(): lax.dot_general(full_out, frozen_key_weight, NT, preferred_element_type=F32)]
    ppermute x0 -> x28, waiting for transfers between devices: none -> 65.6 us  [the longest x3 22.1 us: per_device(): lax.ppermute(block, 'dp', [(i, (i + s) % size) for i in range(size)])]
    ppermute x0 -> x28, starting transfers between devices: none -> 44.9 us  [the longest x8 15.8 us: per_device(): lax.ppermute(to_a, 'dp', pairs_a)]
    psum x1 -> x0, waiting for transfers between devices: 28.1 us -> none  [route_rows(): low_in, low_out = lax.psum((part_in, part_out), 'mp')]
    all_to_all x5 -> x0, starting transfers between devices: 26.1 us -> none  [the longest x1 6.32 us: per_device(): lax.all_to_all(send_gate, 'dp', split_axis=0, concat_axis=0, tiled=True)]
    gather x2 -> x0, local copies, waits for them, and re-layouts: 17.7 us -> none  [the longest x1 10.9 us: per_device(): returned.reshape(slot_total, input_width)[dest_slot]]
  transfers between devices with their start and end apart: 7 -> 29, of which waited for: 5 -> 10; matrix products, arithmetic and copies ran while one was open for 28% -> 3% of each run, Pallas kernels for 0% -> 43%
where the time goes in v1:
time: 263 us; the launch traced here: 262 us
  Pallas kernels  122 us (46%)
  waiting for transfers between devices  65.6 us (25%)
  starting transfers between devices  44.9 us (17%)
  between operations  14.4 us (5%)
  local copies, waits for them, and re-layouts  10.7 us (4%)
  matrix products  3.55 us (1%)
    pallas_call x4, Pallas kernels, project_in(): call(functools.partial(project_in_body, rank, chunks), jax.ShapeDtypeStru...  33.8 us
    pallas_call x2, Pallas kernels, adapter_rows(): call(functools.partial(adapter_rows_body, rank, len(parts)), jax.ShapeDty...  28.7 us
    ppermute x3, waiting for transfers between devices, per_device(): lax.ppermute(block, 'dp', [(i, (i + s) % size) for i in range(size)])  22.1 us
    pallas_call x1, Pallas kernels, grad_down(): call(functools.partial(grad_down_body, rank, len(parts), where), jax.Shap...  20.3 us
    pallas_call x6, Pallas kernels, ring_add(): call(add_body, [jax.ShapeDtypeStruct(shape, BF)] * 2, in_specs=[ANY] * 4,...  20 us
    ppermute x6, waiting for transfers between devices, exchange(): lax.ppermute(part, 'mp', [(i, (i + s) % shares) for i in range(shares)])  18.6 us
    ppermute x8, waiting for transfers between devices, per_device(): lax.ppermute(to_a, 'dp', pairs_a)  18.3 us
    ppermute x8, starting transfers between devices, per_device(): lax.ppermute(to_a, 'dp', pairs_a)  15.8 us
  transfers between devices with their start and end apart: 29, of which 10 were waited for; matrix products, arithmetic and copies ran while one was open for 3% of the time, Pallas kernels for 43%

profile of v1, /device:TPU:0, one launch (start us, length us, event | category | flops | bytes accessed | tf_op | source)
XLA Modules:
  0.0 261.8 jit_solution(4380406922219653645)
XLA Ops:
  7.2 1.1 copy-done.8
  8.3 0.7 copy-done.9
  9.0 0.7 copy-done.10
  9.7 5.1 %collective-permute-start.2 = (bf16[528,256]{1,0:T(8,128)(2,1)S(1)}, bf16[528,256]{1,0:T(8,128)(2,1)}, u32[]{:S(2)}, u32[]{:S(2)}) collective-permute-start(bf16[528,256]{1,0:T(8,128)(2,1)S(1)} %shard_map.102.refs_0_.refs_9_), channel_id=1, source_target_pairs={{0,12},{4,0},{8,4},{12,8},{1,13},{5,1},{9,5},{13,9},{2,14},{6,2},{... | collective-permute-start | bytes 811016 | tf_op jit(solution)/shard_map/ppermute | solution.py:498
  14.8 1.0 collective-permute-start
  15.8 5.9 %collective-permute-done.2.refs_3_.refs_12_ = bf16[528,256]{1,0:T(8,128)(2,1)} collective-permute-done((bf16[528,256]{1,0:T(8,128)(2,1)S(1)}, bf16[528,256]{1,0:T(8,128)(2,1)}, u32[]{:S(2)}, u32[]{:S(2)}) %collective-permute-start.2) | collective-permute-done | bytes 270368 | tf_op jit(solution)/shard_map/ppermute | solution.py:498
  21.8 16.2 %collective-permute-done.1.refs_2_.refs_11_ = bf16[528,256]{1,0:T(8,128)(2,1)} collective-permute-done((bf16[528,256]{1,0:T(8,128)(2,1)S(1)}, bf16[528,256]{1,0:T(8,128)(2,1)}, u32[]{:S(2)}, u32[]{:S(2)}) %collective-permute-start.1) | collective-permute-done | bytes 270368 | tf_op jit(solution)/shard_map/ppermute | solution.py:498
  38.0 1.2 copy-done.11
  39.2 6.6 %shard_map.103 = (f32[128,512]{1,0:T(8,128)}, f32[32,512]{1,0:T(8,128)S(1)}) custom-call(s32[1]{0:T(128)} %bitcast.base_ref, bf16[2048,256]{1,0:T(8,128)(2,1)S(1)} %bitcast.41, bf16[528,256]{1,0:T(8,128)(2,1)S(1)} %shard_map.102.refs_0_.refs_9_, bf16[528,256]{1,0:T(8,128)(2,1)} %collective-permute-done.refs_1_.refs_10_, ...), custom_call_target="tpu_custom_call" | custom-call | flops 2147483648 | bytes 2097152 | tf_op jit(solution)/shard_map/pallas_call | solution.py:123
  45.8 1.4 collective-permute-start.4
  47.2 0.2 collective-permute-start.3
  47.5 1.3 fusion.1
  48.7 0.8 collective-permute-start.15
  49.5 1.5 collective-permute-start.14
  51.3 0.1 stack.172.plan_ref
  51.4 0.5 collective-permute-done.5.refs_3_.refs_7_
  51.8 2.5 collective-permute-start.7
  54.4 5.9 %collective-permute-done.4.refs_2_.refs_6_ = f32[128,512]{1,0:T(8,128)} collective-permute-done((f32[128,512]{1,0:T(8,128)}, f32[128,512]{1,0:T(8,128)}, u32[]{:S(2)}, u32[]{:S(2)}) %collective-permute-start.4) | collective-permute-done | bytes 262176 | tf_op jit(solution)/shard_map/ppermute | solution.py:506
  60.3 1.5 collective-permute-start.6
  61.8 8.1 %shard_map.105.near_ref = bf16[1,512,1536]{2,1,0:T(8,128)(2,1)S(1)} custom-call(s32[1]{0:T(128)S(1)} %bitcast.42, f32[128,512]{1,0:T(8,128)} %get-tuple-element.23.refs_0_.refs_4_, f32[128,512]{1,0:T(8,128)} %collective-permute-done.3.refs_1_.refs_5_, f32[128,512]{1,0:T(8,128)} %collective-permute-done.4.refs_2_.refs_6_, ...), custom_call_target="tpu_custom_call" | custom-call | flops 3221225472 | bytes 7864320 | tf_op jit(solution)/shard_map/pallas_call | solution.py:233
  70.0 20.6 %shard_map.104.far_ref = bf16[3,512,1536]{2,1,0:T(8,128)(2,1)S(1)} custom-call(s32[3]{0:T(128)S(1)} %slice.15.order_ref, f32[128,512]{1,0:T(8,128)} %get-tuple-element.23.refs_0_.refs_4_, f32[128,512]{1,0:T(8,128)} %collective-permute-done.3.refs_1_.refs_5_, f32[128,512]{1,0:T(8,128)} %collective-permute-done.4.refs_2_.refs_6_, ...), custom_call_target="tpu_custom_call" | custom-call | flops 9663676416 | bytes 11010048 | tf_op jit(solution)/shard_map/pallas_call | solution.py:233
  90.6 3.6 %shard_map.109 = (bf16[256,1536]{1,0:T(8,128)(2,1)}, bf16[256,1536]{1,0:T(8,128)(2,1)}) custom-call(s32[5]{0:T(128)S(1)} %stack.175.plan_ref, bf16[256,1536]{1,0:T(8,128)(2,1)} %collective-permute-done.14.first_ref, bf16[256,1536]{1,0:T(8,128)(2,1)} %collective-permute-done.15.second_ref, ...), custom_call_target="tpu_custom_call", output_to_operand_aliasing={{0}: (1, {}), {1}: (2, {})} | custom-call | flops 786432 | bytes 2359296 | tf_op jit(solution)/shard_map/pallas_call | solution.py:298
  94.2 1.6 collective-permute-start.16
  95.7 1.3 collective-permute-start.17
  97.1 3.3 %shard_map.106 = (bf16[256,1536]{1,0:T(8,128)(2,1)}, bf16[256,1536]{1,0:T(8,128)(2,1)}) custom-call(s32[5]{0:T(128)S(1)} %stack.172.plan_ref, bf16[256,1536]{1,0:T(8,128)(2,1)} %collective-permute-done.6.first_ref, bf16[256,1536]{1,0:T(8,128)(2,1)} %collective-permute-done.7.second_ref, ...), custom_call_target="tpu_custom_call", output_to_operand_aliasing={{0}: (1, {}), {1}: (2, {})} | custom-call | flops 786432 | bytes 2359296 | tf_op jit(solution)/shard_map/pallas_call | solution.py:298
  100.4 1.6 collective-permute-start.8
  102.1 0.1 stack.173.plan_ref
  102.6 13.9 %collective-permute-done.17.second_ref = bf16[256,1536]{1,0:T(8,128)(2,1)} collective-permute-done((bf16[256,1536]{1,0:T(8,128)(2,1)}, bf16[256,1536]{1,0:T(8,128)(2,1)}, u32[]{:S(2)}, u32[]{:S(2)}) %collective-permute-start.17) | collective-permute-done | bytes 786464 | tf_op jit(solution)/shard_map/ppermute | solution.py:553
  116.5 2.3 copy-done.2
  118.9 1.4 copy-done.4
  120.3 3.3 %shard_map.110 = (bf16[256,1536]{1,0:T(8,128)(2,1)}, bf16[256,1536]{1,0:T(8,128)(2,1)}) custom-call(s32[5]{0:T(128)S(1)} %stack.174.plan_ref, bf16[256,1536]{1,0:T(8,128)(2,1)} %collective-permute-done.16.first_ref, bf16[256,1536]{1,0:T(8,128)(2,1)} %collective-permute-done.17.second_ref, ...), custom_call_target="tpu_custom_call", output_to_operand_aliasing={{0}: (1, {}), {1}: (2, {})} | custom-call | flops 786432 | bytes 2359296 | tf_op jit(solution)/shard_map/pallas_call | solution.py:298
  123.6 1.6 collective-permute-start.18
  125.1 3.8 %collective-permute-start.19 = (bf16[256,1536]{1,0:T(8,128)(2,1)}, bf16[256,1536]{1,0:T(8,128)(2,1)}, u32[]{:S(2)}, u32[]{:S(2)}) collective-permute-start(bf16[256,1536]{1,0:T(8,128)(2,1)} %get-tuple-element.34.refs_2_.refs_11_), channel_id=1, source_target_pairs={{0,4},{4,0},{8,12},{12,8},{1,5},{5,1},{9,13},{13,9},{2,6},{6,2},{1... | collective-permute-start | bytes 2359304 | tf_op jit(solution)/shard_map/ppermute | solution.py:553
  129.0 4.4 %collective-permute-done.9.second_ref = bf16[256,1536]{1,0:T(8,128)(2,1)} collective-permute-done((bf16[256,1536]{1,0:T(8,128)(2,1)}, bf16[256,1536]{1,0:T(8,128)(2,1)}, u32[]{:S(2)}, u32[]{:S(2)}) %collective-permute-start.9) | collective-permute-done | bytes 786464 | tf_op jit(solution)/shard_map/ppermute | solution.py:553
  133.4 3.3 %shard_map.107 = (bf16[256,1536]{1,0:T(8,128)(2,1)}, bf16[256,1536]{1,0:T(8,128)(2,1)}) custom-call(s32[5]{0:T(128)S(1)} %stack.165.plan_ref, bf16[256,1536]{1,0:T(8,128)(2,1)} %collective-permute-done.8.first_ref, bf16[256,1536]{1,0:T(8,128)(2,1)} %collective-permute-done.9.second_ref, ...), custom_call_target="tpu_custom_call", output_to_operand_aliasing={{0}: (1, {}), {1}: (2, {})} | custom-call | flops 786432 | bytes 2359296 | tf_op jit(solution)/shard_map/pallas_call | solution.py:298
  136.7 1.6 collective-permute-start.10
  138.2 3.9 %collective-permute-start.11 = (bf16[256,1536]{1,0:T(8,128)(2,1)}, bf16[256,1536]{1,0:T(8,128)(2,1)}, u32[]{:S(2)}, u32[]{:S(2)}) collective-permute-start(bf16[256,1536]{1,0:T(8,128)(2,1)} %get-tuple-element.28.refs_3_.refs_13_), channel_id=1, source_target_pairs={{0,4},{4,0},{8,12},{12,8},{1,5},{5,1},{9,13},{13,9},{2,6},{6,2},{1... | collective-permute-start | bytes 2359304 | tf_op jit(solution)/shard_map/ppermute | solution.py:553
  142.2 0.7 broadcast_in_dim.3.before_ref
  142.9 7.4 %shard_map.114.before_ref = f32[128,512]{1,0:T(8,128)} custom-call(s32[2]{0:T(128)S(1)} %copy-done.12, bf16[2048,1536]{1,0:T(8,128)(2,1)} %bitcast.45, f32[32,512]{1,0:T(8,128)S(1)} %get-tuple-element.24.refs_4_.aux_ref.refs_8_, f32[128,512]{1,0:T(8,128)} %broadcast_in_dim.3.before_ref, bf16[512,1536]{1,0:T(8,128)(2,1)S(1)} %copy-done.7), custom_call_target="tpu_custom_call", output_to_operand_aliasing={{}: (3, {})} | custom-call | flops 3221225472 | bytes 7864320 | tf_op jit(solution)/shard_map/pallas_call | solution.py:178
  150.3 9.0 %shard_map.115.before_ref = f32[128,512]{1,0:T(8,128)} custom-call(s32[4]{0:T(128)S(1)} %pad_add_fusion.3.plan_ref, bf16[2048,1536]{1,0:T(8,128)(2,1)} %bitcast.46, f32[32,512]{1,0:T(8,128)S(1)} %get-tuple-element.24.refs_4_.aux_ref.refs_8_, f32[128,512]{1,0:T(8,128)} %shard_map.114.before_ref, ...), custom_call_target="tpu_custom_call", output_to_operand_aliasing={{}: (3, {})} | custom-call | flops 3221225472 | bytes 7864320 | tf_op jit(solution)/shard_map/pallas_call | solution.py:178
  159.3 8.7 %shard_map.116.before_ref = f32[128,512]{1,0:T(8,128)} custom-call(s32[4]{0:T(128)S(1)} %pad_add_fusion.2.plan_ref, bf16[2048,1536]{1,0:T(8,128)(2,1)} %bitcast.47, f32[32,512]{1,0:T(8,128)S(1)} %get-tuple-element.24.refs_4_.aux_ref.refs_8_, f32[128,512]{1,0:T(8,128)} %shard_map.115.before_ref, ...), custom_call_target="tpu_custom_call", output_to_operand_aliasing={{}: (3, {})} | custom-call | flops 3221225472 | bytes 7864320 | tf_op jit(solution)/shard_map/pallas_call | solution.py:178
  168.1 3.3 %shard_map.111 = (bf16[256,1536]{1,0:T(8,128)(2,1)}, bf16[256,1536]{1,0:T(8,128)(2,1)}) custom-call(s32[5]{0:T(128)S(1)} %stack.173.plan_ref, bf16[256,1536]{1,0:T(8,128)(2,1)} %collective-permute-done.18.first_ref, bf16[256,1536]{1,0:T(8,128)(2,1)} %collective-permute-done.19.second_ref, ...), custom_call_target="tpu_custom_call", output_to_operand_aliasing={{0}: (1, {}), {1}: (2, {})} | custom-call | flops 786432 | bytes 2359296 | tf_op jit(solution)/shard_map/pallas_call | solution.py:298
  171.4 3.3 %shard_map.108 = (bf16[256,1536]{1,0:T(8,128)(2,1)}, bf16[256,1536]{1,0:T(8,128)(2,1)}) custom-call(s32[5]{0:T(128)S(1)} %stack.160.plan_ref, bf16[256,1536]{1,0:T(8,128)(2,1)} %collective-permute-done.10.first_ref, bf16[256,1536]{1,0:T(8,128)(2,1)} %collective-permute-done.11.second_ref, ...), custom_call_target="tpu_custom_call", output_to_operand_aliasing={{0}: (1, {}), {1}: (2, {})} | custom-call | flops 786432 | bytes 2359296 | tf_op jit(solution)/shard_map/pallas_call | solution.py:298
  174.7 8.7 %shard_map.117.refs_0_ = f32[128,512]{1,0:T(8,128)} custom-call(s32[4]{0:T(128)S(1)} %pad_add_fusion.1.plan_ref, bf16[2048,1536]{1,0:T(8,128)(2,1)} %bitcast.48, f32[32,512]{1,0:T(8,128)S(1)} %get-tuple-element.24.refs_4_.aux_ref.refs_8_, f32[128,512]{1,0:T(8,128)} %shard_map.116.before_ref, ...), custom_call_target="tpu_custom_call", output_to_operand_aliasing={{}: (3, {})} | custom-call | flops 3221225472 | bytes 7864320 | tf_op jit(solution)/shard_map/pallas_call | solution.py:178
  183.4 0.3 collective-permute-start.23
  183.7 0.2 collective-permute-start.22
  183.9 0.6 stack.195.plan_ref
  184.5 5.9 %collective-permute-done.24.refs_3_ = f32[128,512]{1,0:T(8,128)} collective-permute-done((f32[128,512]{1,0:T(8,128)}, f32[128,512]{1,0:T(8,128)}, u32[]{:S(2)}, u32[]{:S(2)}) %collective-permute-start.24) | collective-permute-done | bytes 262176 | tf_op jit(solution)/shard_map/ppermute | solution.py:506
  190.4 5.4 %collective-permute-done.23.refs_2_ = f32[128,512]{1,0:T(8,128)} collective-permute-done((f32[128,512]{1,0:T(8,128)}, f32[128,512]{1,0:T(8,128)}, u32[]{:S(2)}, u32[]{:S(2)}) %collective-permute-start.23) | collective-permute-done | bytes 262176 | tf_op jit(solution)/shard_map/ppermute | solution.py:506
  195.8 0.9 collective-permute-done.22.refs_1_
  196.8 7.3 %shard_map.118 = (bf16[2048,256]{1,0:T(8,128)(2,1)}, bf16[2,512]{1,0:T(2,128)(2,1)S(1)}, bf16[2,512]{1,0:T(2,128)(2,1)S(1)}, bf16[2,512]{1,0:T(2,128)(2,1)S(1)}, bf16[2,512]{1,0:T(2,128)(2,1)S(1)}) custom-call(f32[128,512]{1,0:T(8,128)} %shard_map.117.refs_0_, f32[128,512]{1,0:T(8,128)} %collective-permute-done.22.refs_1_, ...), custom_call_target="tpu_custom_call" | custom-call | flops 2147483648 | bytes 2097152 | tf_op jit(solution)/shard_map/pallas_call | solution.py:441
  204.0 0.9 collective-permute-start.25
  205.0 5.8 %collective-permute-start.26 = (bf16[2,512]{1,0:T(2,128)(2,1)S(1)}, bf16[2,512]{1,0:T(2,128)(2,1)S(1)}, u32[]{:S(2)}, u32[]{:S(2)}) collective-permute-start(bf16[2,512]{1,0:T(2,128)(2,1)S(1)} %get-tuple-element.39), channel_id=1, source_target_pairs={{0,8},{4,12},{8,0},{12,4},{1,9},{5,13},{9,1},{13,5},{2,10},{6,14},... | collective-permute-start | bytes 6152 | tf_op jit(solution)/shard_map/ppermute | solution.py:571
  210.8 3.6 %convert_add_fusion.base_ref = f32[512,1536]{1,0:T(8,128)S(1)} fusion(bf16[3,512,1536]{2,1,0:T(8,128)(2,1)} %copy-done.1, bf16[512,1024]{1,0:T(8,128)(2,1)} %all-gather.2.cloned.1.call-done, bf16[1536,1024]{1,0:T(8,128)(2,1)S(1)} %copy-done), kind=kOutput, calls=%fused_computation | convolution fusion | flops 1612185600 | bytes 8912896 | tf_op jit(solution)/shard_map/dot_general | solution.py:520
  214.3 0.1 collective-permute-start.20
  214.4 0.7 collective-permute-start.21
  215.1 3.3 %collective-permute-start.12 = (bf16[256,1536]{1,0:T(8,128)(2,1)}, bf16[256,1536]{1,0:T(8,128)(2,1)}, u32[]{:S(2)}, u32[]{:S(2)}) collective-permute-start(bf16[256,1536]{1,0:T(8,128)(2,1)} %get-tuple-element.29.refs_3_.refs_17_), channel_id=1, source_target_pairs={{0,4},{4,0},{8,12},{12,8},{1,5},{5,1},{9,13},{13,9},{2,6},{6,2},{1... | collective-permute-start | bytes 2359304 | tf_op jit(solution)/shard_map/ppermute | solution.py:553
  218.4 1.6 collective-permute-start.13
  220.0 2.5 collective-permute-start.27
  222.4 20.3 %shard_map.119 = bf16[2048,1536]{1,0:T(8,128)(2,1)} custom-call(s32[14]{0:T(128)} %stack.195.plan_ref, f32[128,512]{1,0:T(8,128)} %get-tuple-element.23.refs_0_.refs_4_, f32[128,512]{1,0:T(8,128)} %collective-permute-done.3.refs_1_.refs_5_, f32[128,512]{1,0:T(8,128)} %collective-permute-done.4.refs_2_.refs_6_, ...), custom_call_target="tpu_custom_call" | custom-call | flops 12884901888 | bytes 12582912 | tf_op jit(solution)/shard_map/pallas_call | solution.py:377
  242.8 6.5 %collective-permute-done.27 = bf16[2,512]{1,0:T(2,128)(2,1)S(1)} collective-permute-done((bf16[2,512]{1,0:T(2,128)(2,1)S(1)}, bf16[2,512]{1,0:T(2,128)(2,1)S(1)}, u32[]{:S(2)}, u32[]{:S(2)}) %collective-permute-start.27) | collective-permute-done | bytes 2080 | tf_op jit(solution)/shard_map/ppermute | solution.py:571
  249.3 0.6 fusion
  249.8 1.6 shard_map.112.refs_0_
  251.4 3.6 %shard_map.113 = bf16[512,1536]{1,0:T(8,128)(2,1)} custom-call(f32[512,1536]{1,0:T(8,128)S(1)} %convert_add_fusion.base_ref, bf16[256,1536]{1,0:T(8,128)(2,1)} %collective-permute-done.12.first_ref, bf16[256,1536]{1,0:T(8,128)(2,1)} %collective-permute-done.13.second_ref, bf16[512,1536]{1,0:T(8,128)(2,1)} %shard_map.112.refs_0_), custom_call_target="tpu_custom_call", output_to_operand_aliasing={{}: (3, {})} | custom-call | flops 786432 | bytes 3932160 | tf_op jit(solution)/shard_map/pallas_call | solution.py:467
  (63 shorter events, 1.0 us)
Async XLA Ops:
  7.2 203.6 %copy-start = (bf16[1536,1024]{1,0:T(8,128)(2,1)S(1)}, bf16[1536,1024]{1,0:T(8,128)(2,1)}, u32[]{:S(2)}) copy-start(bf16[1536,1024]{1,0:T(8,128)(2,1)} %param.9) | copy-start | bytes 9437188
  7.2 203.6 %all-gather.2.cloned.1.call-start = ((), (), s32[]{:S(2)}) async-start(), calls=%async_computation | async-start | bytes 1310720 | tf_op jit(solution)/shard_map/all_gather | solution.py:500
  7.2 1.1 copy-start.8
  8.3 0.7 copy-start.9
  9.0 0.7 copy-start.10
  9.7 12.0 %collective-permute-start.2 = (bf16[528,256]{1,0:T(8,128)(2,1)S(1)}, bf16[528,256]{1,0:T(8,128)(2,1)}, u32[]{:S(2)}, u32[]{:S(2)}) collective-permute-start(bf16[528,256]{1,0:T(8,128)(2,1)S(1)} %shard_map.102.refs_0_.refs_9_), channel_id=1, source_target_pairs={{0,12},{4,0},{8,4},{12,8},{1,13},{5,1},{9,5},{13,9},{2,14},{6,2},{... | collective-permute-start | bytes 811016 | tf_op jit(solution)/shard_map/ppermute | solution.py:498
  14.8 23.1 %collective-permute-start.1 = (bf16[528,256]{1,0:T(8,128)(2,1)S(1)}, bf16[528,256]{1,0:T(8,128)(2,1)}, u32[]{:S(2)}, u32[]{:S(2)}) collective-permute-start(bf16[528,256]{1,0:T(8,128)(2,1)S(1)} %shard_map.102.refs_0_.refs_9_), channel_id=1, source_target_pairs={{0,8},{4,12},{8,0},{12,4},{1,9},{5,13},{9,1},{13,5},{2,10},{6,14},... | collective-permute-start | bytes 811016 | tf_op jit(solution)/shard_map/ppermute | solution.py:498
  14.8 23.1 %collective-permute-start = (bf16[528,256]{1,0:T(8,128)(2,1)S(1)}, bf16[528,256]{1,0:T(8,128)(2,1)}, u32[]{:S(2)}, u32[]{:S(2)}) collective-permute-start(bf16[528,256]{1,0:T(8,128)(2,1)S(1)} %shard_map.102.refs_0_.refs_9_), channel_id=1, source_target_pairs={{0,4},{4,8},{8,12},{12,0},{1,5},{5,9},{9,13},{13,1},{2,6},{6,10},{... | collective-permute-start | bytes 811016 | tf_op jit(solution)/shard_map/ppermute | solution.py:498
  38.0 1.2 copy-start.11
  39.2 8.3 %copy-start.6 = (bf16[512,1536]{1,0:T(8,128)(2,1)S(1)}, bf16[512,1536]{1,0:T(8,128)(2,1)}, u32[]{:S(2)}) copy-start(bf16[512,1536]{1,0:T(8,128)(2,1)} %refs_5_.1) | copy-start | bytes 4718596
  45.7 151.0 %copy-start.13 = (f32[32,512]{1,0:T(8,128)}, f32[32,512]{1,0:T(8,128)S(1)}, u32[]{:S(2)}) copy-start(f32[32,512]{1,0:T(8,128)S(1)} %get-tuple-element.24.refs_4_.aux_ref.refs_8_) | copy-start | bytes 196612
  45.7 6.1 %collective-permute-start.5 = (f32[128,512]{1,0:T(8,128)}, f32[128,512]{1,0:T(8,128)}, u32[]{:S(2)}, u32[]{:S(2)}) collective-permute-start(f32[128,512]{1,0:T(8,128)} %get-tuple-element.23.refs_0_.refs_4_), channel_id=1, source_target_pairs={{0,3},{1,0},{2,1},{3,2},{4,7},{5,4},{6,5},{7,6},{8,11},{9,8},{10,9... | collective-permute-start | bytes 786440 | tf_op jit(solution)/shard_map/ppermute | solution.py:506
  45.8 14.5 %collective-permute-start.4 = (f32[128,512]{1,0:T(8,128)}, f32[128,512]{1,0:T(8,128)}, u32[]{:S(2)}, u32[]{:S(2)}) collective-permute-start(f32[128,512]{1,0:T(8,128)} %get-tuple-element.23.refs_0_.refs_4_), channel_id=1, source_target_pairs={{0,2},{1,3},{2,0},{3,1},{4,6},{5,7},{6,4},{7,5},{8,10},{9,11},{10,... | collective-permute-start | bytes 786440 | tf_op jit(solution)/shard_map/ppermute | solution.py:506
  47.2 14.6 %collective-permute-start.3 = (f32[128,512]{1,0:T(8,128)}, f32[128,512]{1,0:T(8,128)}, u32[]{:S(2)}, u32[]{:S(2)}) collective-permute-start(f32[128,512]{1,0:T(8,128)} %get-tuple-element.23.refs_0_.refs_4_), channel_id=1, source_target_pairs={{0,1},{1,2},{2,3},{3,0},{4,5},{5,6},{6,7},{7,4},{8,9},{9,10},{10,1... | collective-permute-start | bytes 786440 | tf_op jit(solution)/shard_map/ppermute | solution.py:506
  48.7 41.8 %collective-permute-start.15 = (bf16[256,1536]{1,0:T(8,128)(2,1)}, bf16[256,1536]{1,0:T(8,128)(2,1)}, u32[]{:S(2)}, u32[]{:S(2)}) collective-permute-start(bf16[256,1536]{1,0:T(8,128)(2,1)} %get-tuple-element.42), channel_id=1, source_target_pairs={{0,4},{4,0},{8,12},{12,8},{1,5},{5,1},{9,13},{13,9},{2,6},{6,2},{1... | collective-permute-start | bytes 2359304 | tf_op jit(solution)/shard_map/ppermute | solution.py:553
  49.5 41.1 %collective-permute-start.14 = (bf16[256,1536]{1,0:T(8,128)(2,1)}, bf16[256,1536]{1,0:T(8,128)(2,1)}, u32[]{:S(2)}, u32[]{:S(2)}) collective-permute-start(bf16[256,1536]{1,0:T(8,128)(2,1)} %get-tuple-element.42), channel_id=1, source_target_pairs={{4,8},{8,4},{5,9},{9,5},{6,10},{10,6},{7,11},{11,7},{20,24},{24,20... | collective-permute-start | bytes 2359304 | tf_op jit(solution)/shard_map/ppermute | solution.py:553
  51.8 45.2 %collective-permute-start.7 = (bf16[256,1536]{1,0:T(8,128)(2,1)}, bf16[256,1536]{1,0:T(8,128)(2,1)}, u32[]{:S(2)}, u32[]{:S(2)}) collective-permute-start(bf16[256,1536]{1,0:T(8,128)(2,1)} %get-tuple-element.43), channel_id=1, source_target_pairs={{0,4},{4,0},{8,12},{12,8},{1,5},{5,1},{9,13},{13,9},{2,6},{6,2},{1... | collective-permute-start | bytes 2359304 | tf_op jit(solution)/shard_map/ppermute | solution.py:553
  60.3 36.8 %collective-permute-start.6 = (bf16[256,1536]{1,0:T(8,128)(2,1)}, bf16[256,1536]{1,0:T(8,128)(2,1)}, u32[]{:S(2)}, u32[]{:S(2)}) collective-permute-start(bf16[256,1536]{1,0:T(8,128)(2,1)} %get-tuple-element.43), channel_id=1, source_target_pairs={{4,8},{8,4},{5,9},{9,5},{6,10},{10,6},{7,11},{11,7},{20,24},{24,20... | collective-permute-start | bytes 2359304 | tf_op jit(solution)/shard_map/ppermute | solution.py:553
  69.9 27.1 %copy-start.3 = (bf16[1,512,1536]{2,1,0:T(8,128)(2,1)}, bf16[1,512,1536]{2,1,0:T(8,128)(2,1)S(1)}, u32[]{:S(2)}) copy-start(bf16[1,512,1536]{2,1,0:T(8,128)(2,1)S(1)} %shard_map.105.near_ref) | copy-start | bytes 4718596
  90.6 6.5 %copy-start.1 = (bf16[3,512,1536]{2,1,0:T(8,128)(2,1)}, bf16[3,512,1536]{2,1,0:T(8,128)(2,1)S(1)}, u32[]{:S(2)}) copy-start(bf16[3,512,1536]{2,1,0:T(8,128)(2,1)S(1)} %shard_map.104.far_ref) | copy-start | bytes 14155780
  94.2 8.5 %collective-permute-start.16 = (bf16[256,1536]{1,0:T(8,128)(2,1)}, bf16[256,1536]{1,0:T(8,128)(2,1)}, u32[]{:S(2)}, u32[]{:S(2)}) collective-permute-start(bf16[256,1536]{1,0:T(8,128)(2,1)} %get-tuple-element.31.refs_0_.refs_6_), channel_id=1, source_target_pairs={{4,8},{8,4},{5,9},{9,5},{6,10},{10,6},{7,11},{11,7},{20,24},{24,20... | collective-permute-start | bytes 2359304 | tf_op jit(solution)/shard_map/ppermute | solution.py:553
  95.7 20.8 %collective-permute-start.17 = (bf16[256,1536]{1,0:T(8,128)(2,1)}, bf16[256,1536]{1,0:T(8,128)(2,1)}, u32[]{:S(2)}, u32[]{:S(2)}) collective-permute-start(bf16[256,1536]{1,0:T(8,128)(2,1)} %get-tuple-element.32.refs_2_.refs_7_), channel_id=1, source_target_pairs={{0,4},{4,0},{8,12},{12,8},{1,5},{5,1},{9,13},{13,9},{2,6},{6,2},{1... | collective-permute-start | bytes 2359304 | tf_op jit(solution)/shard_map/ppermute | solution.py:553
  100.4 28.6 %collective-permute-start.8 = (bf16[256,1536]{1,0:T(8,128)(2,1)}, bf16[256,1536]{1,0:T(8,128)(2,1)}, u32[]{:S(2)}, u32[]{:S(2)}) collective-permute-start(bf16[256,1536]{1,0:T(8,128)(2,1)} %get-tuple-element.25.refs_1_.refs_8_), channel_id=1, source_target_pairs={{4,8},{8,4},{5,9},{9,5},{6,10},{10,6},{7,11},{11,7},{20,24},{24,20... | collective-permute-start | bytes 2359304 | tf_op jit(solution)/shard_map/ppermute | solution.py:553
  102.0 31.4 %collective-permute-start.9 = (bf16[256,1536]{1,0:T(8,128)(2,1)}, bf16[256,1536]{1,0:T(8,128)(2,1)}, u32[]{:S(2)}, u32[]{:S(2)}) collective-permute-start(bf16[256,1536]{1,0:T(8,128)(2,1)} %get-tuple-element.26.refs_3_.refs_9_), channel_id=1, source_target_pairs={{0,4},{4,0},{8,12},{12,8},{1,5},{5,1},{9,13},{13,9},{2,6},{6,2},{1... | collective-permute-start | bytes 2359304 | tf_op jit(solution)/shard_map/ppermute | solution.py:553
  116.5 2.3 copy-start.2
  118.9 1.4 copy-start.4
  123.6 44.5 %collective-permute-start.18 = (bf16[256,1536]{1,0:T(8,128)(2,1)}, bf16[256,1536]{1,0:T(8,128)(2,1)}, u32[]{:S(2)}, u32[]{:S(2)}) collective-permute-start(bf16[256,1536]{1,0:T(8,128)(2,1)} %get-tuple-element.33.refs_0_.refs_10_), channel_id=1, source_target_pairs={{4,8},{8,4},{5,9},{9,5},{6,10},{10,6},{7,11},{11,7},{20,24},{24,20... | collective-permute-start | bytes 2359304 | tf_op jit(solution)/shard_map/ppermute | solution.py:553
  125.1 17.8 %copy-start.7 = (bf16[512,1536]{1,0:T(8,128)(2,1)S(1)}, bf16[512,1536]{1,0:T(8,128)(2,1)}, u32[]{:S(2)}) copy-start(bf16[512,1536]{1,0:T(8,128)(2,1)} %refs_5_.1) | copy-start | bytes 4718596
  125.1 17.8 %copy-start.12 = (s32[2]{0:T(128)S(1)}, s32[2]{0:T(128)}, u32[]{:S(2)}) copy-start(s32[2]{0:T(128)} %constant.50.clone.1.plan_ref) | copy-start | bytes 28
  125.1 42.9 %collective-permute-start.19 = (bf16[256,1536]{1,0:T(8,128)(2,1)}, bf16[256,1536]{1,0:T(8,128)(2,1)}, u32[]{:S(2)}, u32[]{:S(2)}) collective-permute-start(bf16[256,1536]{1,0:T(8,128)(2,1)} %get-tuple-element.34.refs_2_.refs_11_), channel_id=1, source_target_pairs={{0,4},{4,0},{8,12},{12,8},{1,5},{5,1},{9,13},{13,9},{2,6},{6,2},{1... | collective-permute-start | bytes 2359304 | tf_op jit(solution)/shard_map/ppermute | solution.py:553
  136.7 34.7 %collective-permute-start.10 = (bf16[256,1536]{1,0:T(8,128)(2,1)}, bf16[256,1536]{1,0:T(8,128)(2,1)}, u32[]{:S(2)}, u32[]{:S(2)}) collective-permute-start(bf16[256,1536]{1,0:T(8,128)(2,1)} %get-tuple-element.27.refs_1_.refs_12_), channel_id=1, source_target_pairs={{4,8},{8,4},{5,9},{9,5},{6,10},{10,6},{7,11},{11,7},{20,24},{24,20... | collective-permute-start | bytes 2359304 | tf_op jit(solution)/shard_map/ppermute | solution.py:553
  138.2 33.1 %collective-permute-start.11 = (bf16[256,1536]{1,0:T(8,128)(2,1)}, bf16[256,1536]{1,0:T(8,128)(2,1)}, u32[]{:S(2)}, u32[]{:S(2)}) collective-permute-start(bf16[256,1536]{1,0:T(8,128)(2,1)} %get-tuple-element.28.refs_3_.refs_13_), channel_id=1, source_target_pairs={{0,4},{4,0},{8,12},{12,8},{1,5},{5,1},{9,13},{13,9},{2,6},{6,2},{1... | collective-permute-start | bytes 2359304 | tf_op jit(solution)/shard_map/ppermute | solution.py:553
  150.3 17.7 %slice-start = ((s8[4718592]{0:T(1024)(128)(4,1)}), s8[4194304]{0:T(1024)(128)(4,1)S(1)}, s32[]{:S(2)}) async-start(s8[4718592]{0:T(1024)(128)(4,1)} %bitcast.37), calls=%async_computation.1 | async-start | bytes 8388608
  159.3 8.7 %slice-start.1 = ((s8[4718592]{0:T(1024)(128)(4,1)}), s8[524288]{0:T(1024)(128)(4,1)S(1)}, s32[]{:S(2)}) async-start(s8[4718592]{0:T(1024)(128)(4,1)} %bitcast.37), calls=%async_computation.2 | async-start | bytes 1048576
  159.3 8.7 %copy-start.5 = (bf16[1,512,1536]{2,1,0:T(8,128)(2,1)S(1)}, bf16[1,512,1536]{2,1,0:T(8,128)(2,1)}, u32[]{:S(2)}) copy-start(bf16[1,512,1536]{2,1,0:T(8,128)(2,1)} %copy-done.3) | copy-start | bytes 4718596
  183.4 7.0 %collective-permute-start.24 = (f32[128,512]{1,0:T(8,128)}, f32[128,512]{1,0:T(8,128)}, u32[]{:S(2)}, u32[]{:S(2)}) collective-permute-start(f32[128,512]{1,0:T(8,128)} %shard_map.117.refs_0_), channel_id=1, source_target_pairs={{0,3},{1,0},{2,1},{3,2},{4,7},{5,4},{6,5},{7,6},{8,11},{9,8},{10,9... | collective-permute-start | bytes 786440 | tf_op jit(solution)/shard_map/ppermute | solution.py:506
  183.4 12.5 %collective-permute-start.23 = (f32[128,512]{1,0:T(8,128)}, f32[128,512]{1,0:T(8,128)}, u32[]{:S(2)}, u32[]{:S(2)}) collective-permute-start(f32[128,512]{1,0:T(8,128)} %shard_map.117.refs_0_), channel_id=1, source_target_pairs={{0,2},{1,3},{2,0},{3,1},{4,6},{5,7},{6,4},{7,5},{8,10},{9,11},{10,... | collective-permute-start | bytes 786440 | tf_op jit(solution)/shard_map/ppermute | solution.py:506
  183.7 13.1 %collective-permute-start.22 = (f32[128,512]{1,0:T(8,128)}, f32[128,512]{1,0:T(8,128)}, u32[]{:S(2)}, u32[]{:S(2)}) collective-permute-start(f32[128,512]{1,0:T(8,128)} %shard_map.117.refs_0_), channel_id=1, source_target_pairs={{0,1},{1,2},{2,3},{3,0},{4,5},{5,6},{6,7},{7,4},{8,9},{9,10},{10,1... | collective-permute-start | bytes 786440 | tf_op jit(solution)/shard_map/ppermute | solution.py:506
  204.0 14.4 %collective-permute-start.25 = (bf16[2,512]{1,0:T(2,128)(2,1)S(1)}, bf16[2,512]{1,0:T(2,128)(2,1)S(1)}, u32[]{:S(2)}, u32[]{:S(2)}) collective-permute-start(bf16[2,512]{1,0:T(2,128)(2,1)S(1)} %get-tuple-element.38), channel_id=1, source_target_pairs={{0,12},{4,0},{8,4},{12,8},{1,13},{5,1},{9,5},{13,9},{2,14},{6,2},{... | collective-permute-start | bytes 6152 | tf_op jit(solution)/shard_map/ppermute | solution.py:571
  205.0 15.0 %collective-permute-start.26 = (bf16[2,512]{1,0:T(2,128)(2,1)S(1)}, bf16[2,512]{1,0:T(2,128)(2,1)S(1)}, u32[]{:S(2)}, u32[]{:S(2)}) collective-permute-start(bf16[2,512]{1,0:T(2,128)(2,1)S(1)} %get-tuple-element.39), channel_id=1, source_target_pairs={{0,8},{4,12},{8,0},{12,4},{1,9},{5,13},{9,1},{13,5},{2,10},{6,14},... | collective-permute-start | bytes 6152 | tf_op jit(solution)/shard_map/ppermute | solution.py:571
  214.3 35.5 %collective-permute-start.20 = (bf16[256,1536]{1,0:T(8,128)(2,1)}, bf16[256,1536]{1,0:T(8,128)(2,1)S(1)}, u32[]{:S(2)}, u32[]{:S(2)}) collective-permute-start(bf16[256,1536]{1,0:T(8,128)(2,1)} %get-tuple-element.35.refs_2_.refs_15_), channel_id=1, source_target_pairs={{0,4},{4,0},{8,12},{12,8},{1,5},{5,1},{9,13},{13,9},{2,6},{6,2},{1... | collective-permute-start | bytes 2359304 | tf_op jit(solution)/shard_map/ppermute | solution.py:553
  214.4 35.4 %collective-permute-start.21 = (bf16[256,1536]{1,0:T(8,128)(2,1)}, bf16[256,1536]{1,0:T(8,128)(2,1)S(1)}, u32[]{:S(2)}, u32[]{:S(2)}) collective-permute-start(bf16[256,1536]{1,0:T(8,128)(2,1)} %get-tuple-element.36.refs_0_.refs_14_), channel_id=1, source_target_pairs={{4,8},{8,4},{5,9},{9,5},{6,10},{10,6},{7,11},{11,7},{20,24},{24,20... | collective-permute-start | bytes 2359304 | tf_op jit(solution)/shard_map/ppermute | solution.py:553
  215.1 36.3 %collective-permute-start.12 = (bf16[256,1536]{1,0:T(8,128)(2,1)}, bf16[256,1536]{1,0:T(8,128)(2,1)}, u32[]{:S(2)}, u32[]{:S(2)}) collective-permute-start(bf16[256,1536]{1,0:T(8,128)(2,1)} %get-tuple-element.29.refs_3_.refs_17_), channel_id=1, source_target_pairs={{0,4},{4,0},{8,12},{12,8},{1,5},{5,1},{9,13},{13,9},{2,6},{6,2},{1... | collective-permute-start | bytes 2359304 | tf_op jit(solution)/shard_map/ppermute | solution.py:553
  218.4 33.0 %collective-permute-start.13 = (bf16[256,1536]{1,0:T(8,128)(2,1)}, bf16[256,1536]{1,0:T(8,128)(2,1)}, u32[]{:S(2)}, u32[]{:S(2)}) collective-permute-start(bf16[256,1536]{1,0:T(8,128)(2,1)} %get-tuple-element.30.refs_1_.refs_16_), channel_id=1, source_target_pairs={{4,8},{8,4},{5,9},{9,5},{6,10},{10,6},{7,11},{11,7},{20,24},{24,20... | collective-permute-start | bytes 2359304 | tf_op jit(solution)/shard_map/ppermute | solution.py:553
  220.0 29.3 %collective-permute-start.27 = (bf16[2,512]{1,0:T(2,128)(2,1)S(1)}, bf16[2,512]{1,0:T(2,128)(2,1)S(1)}, u32[]{:S(2)}, u32[]{:S(2)}) collective-permute-start(bf16[2,512]{1,0:T(2,128)(2,1)S(1)} %get-tuple-element.40), channel_id=1, source_target_pairs={{0,4},{4,8},{8,12},{12,0},{1,5},{5,9},{9,13},{13,1},{2,6},{6,10},{... | collective-permute-start | bytes 6152 | tf_op jit(solution)/shard_map/ppermute | solution.py:571
Sparse Core Ops, SparseCore 0:
  102.1 17.0 all-gather.1

commit v2 on v1

v2 whole, which is shorter than its diff:
```python
import functools

import jax
import jax.numpy as jnp
from jax import lax
from jax.experimental import pallas as pl
from jax.experimental.pallas import tpu as pltpu
from jax.sharding import PartitionSpec as P

BF = jnp.bfloat16
F32 = jnp.float32
CHUNKS = 2
NT = (((1,), (1,)), ((), ()))
ANY = pl.BlockSpec(memory_space=pl.ANY)
COST = 0.02


def call(body, out_shape, *, grid=None, in_specs=None, out_specs=None, scratch=(), prefetch=0,
         aliases=None, flops=0, moved=0, vmem=28, after=(), cost=COST):
    steps = len(grid) if grid else 0
    taken = prefetch + len(in_specs)
    skipped = len(after)

    def ordered(*refs):
        body(*refs[:taken], *refs[taken + skipped :])

    call_it = pl.pallas_call(
        ordered,
        out_shape=out_shape,
        grid_spec=pltpu.PrefetchScalarGridSpec(
            num_scalar_prefetch=prefetch,
            grid=grid or (1,),
            in_specs=list(in_specs) + [ANY] * skipped,
            out_specs=out_specs,
            scratch_shapes=list(scratch),
        ),
        input_output_aliases=aliases or {},
        compiler_params=pltpu.CompilerParams(
            vmem_limit_bytes=vmem << 20, dimension_semantics=("arbitrary",) * max(steps, 1)
        ),
        cost_estimate=pl.CostEstimate(
            flops=int(flops * cost), bytes_accessed=int(moved * cost), transcendentals=0
        ),
    )
    return lambda *arrays: call_it(*arrays, *after)


def whole(shape):
    return pl.BlockSpec(shape, lambda *_: (0,) * len(shape))


def arrival(d, size, j, a):
    if j < 0:
        return d >= 0, 0 * d
    left = d % 2 == (1 if a else 0)
    slot = jnp.where(left, j + 1, size - 1 - j)
    valid = jnp.where(left, d >= j + 1, d + j + 1 <= size - 1)
    return valid, slot


def departure(d, size, j, a):
    right = d % 2 == (0 if a else 1)
    slot = jnp.where(right, j, size - j)
    do = jnp.where(right, j > d, j > size - 1 - d)
    return do, slot


def place_of(d, size, slot):
    return jnp.where(d < (size + 1) // 2, jnp.where(slot == 0, size - 1, slot - 1), size - 1 - slot)


def slot_at(d, size, place):
    if place == size - 1:
        return 0 * d
    return jnp.where(d < (size + 1) // 2, place + 1, size - 1 - place)


def pack_body(local, pos_ref, index_ref, gate_ref, rows_ref, out_ref, aux_ref):
    count, width = rows_ref.shape
    out_ref[:count, :] = rows_ref[...]
    index = index_ref[...]
    gate = gate_ref[...].astype(F32)
    high, low = (index >> 4).astype(F32), (index & 15).astype(F32)
    pieces = []
    for vector in (high, low, gate):
        for slot in range(2):
            for part in range(count // width):
                pieces.append(vector[slot : slot + 1, part * width : (part + 1) * width])
    extra = out_ref.shape[0] - count
    if extra > len(pieces):
        pieces.append(jnp.zeros((extra - len(pieces), width), F32))
    out_ref[count:, :] = jnp.concatenate(pieces, axis=0).astype(BF)
    aux_ref[...] = jnp.concatenate(
        [(index - pos_ref[0] * local).astype(F32), gate, jnp.zeros((4, count), F32)], axis=0
    )


def pack_rows(pos, index, gate, rows, local):
    count, width = rows.shape
    extra = -(-6 * (count // width) // 16) * 16
    shape = (count + extra, width)
    return call(
        functools.partial(pack_body, local),
        [jax.ShapeDtypeStruct(shape, BF), jax.ShapeDtypeStruct((8, count), F32)],
        in_specs=[whole(index.shape), whole(gate.shape), whole(rows.shape)],
        out_specs=[whole(shape), whole((8, count))],
        prefetch=1,
        moved=4 * count * width,
        vmem=60,
    )(pos, index, gate, rows)


def pin_body(in_ref, out_ref):
    pass


def pin(array, after):
    return call(
        pin_body,
        jax.ShapeDtypeStruct(array.shape, array.dtype),
        in_specs=[ANY],
        out_specs=ANY,
        aliases={0: 0},
        after=after,
    )(array)


def unpack_extra(block, count, width, base):
    per = count // width
    vectors = []
    for v in range(6):
        rows = block[v * per : (v + 1) * per, :].astype(F32)
        vectors.append(jnp.concatenate([rows[q : q + 1, :] for q in range(per)], axis=1))
    ids = [vectors[k] * 16.0 + vectors[2 + k] - base for k in range(2)]
    return jnp.concatenate(ids + vectors[4:6] + [jnp.zeros((4, count), F32)], axis=0)


def pick(product, ids, first, rank, kept):
    kept = list(kept)
    for a in range(product.shape[0] // rank):
        rows = product[a * rank : (a + 1) * rank, :]
        here = (first + a).astype(F32) if hasattr(first, "astype") else float(first + a)
        for k in range(2):
            kept[k] = jnp.where(ids[k : k + 1, :] == here, rows, kept[k])
    return kept


def project_out_body(rank, pos_ref, up_ref, *refs):
    blocks, (part_ref, aux_ref) = refs[:-2], refs[-2:]
    count = part_ref.shape[1]
    width = up_ref.shape[1]
    total = up_ref.shape[0]
    step = min(1024, total)
    base = (pos_ref[0] * (total // rank)).astype(F32)
    for s, block in enumerate(blocks):
        aux = unpack_extra(block[count:, :], count, width, base)
        aux_ref[8 * s : 8 * s + 8, :] = aux
        ids = aux[0:2, :]

        def body(b, kept):
            product = lax.dot_general(
                up_ref[pl.ds(pl.multiple_of(b * step, step), step), :], block[:count, :], NT,
                preferred_element_type=F32,
            )
            return tuple(pick(product, ids, b * (step // rank), rank, kept))

        zero = jnp.zeros((rank, count), F32)
        kept = lax.fori_loop(0, total // step, body, (zero, zero))
        part_ref[2 * rank * s : 2 * rank * s + rank, :] = kept[0]
        part_ref[2 * rank * s + rank : 2 * rank * (s + 1), :] = kept[1]


def project_out(pos, up, blocks, count, rank, after):
    slots = len(blocks)
    total, width = up.shape
    shapes = [(slots * 2 * rank, count), (slots * 8, count)]
    return call(
        functools.partial(project_out_body, rank),
        [jax.ShapeDtypeStruct(s, F32) for s in shapes],
        in_specs=[whole(up.shape)] + [whole(b.shape) for b in blocks],
        out_specs=[whole(s) for s in shapes],
        prefetch=1,
        flops=2 * slots * count * total * width,
        moved=2 * (slots * count * width + total * width),
        cost=5,
        after=after,
    )(pos, up, *blocks)


def project_in_body(rank, chunks, size, step_index, pos_ref, down_ref, aux_ref, before_ref, *refs):
    rows, (out_ref, kept_ref) = refs[:-2], refs[-2:]
    source, b = pl.program_id(0), pl.program_id(1)
    step = down_ref.shape[0]

    @pl.when((source == 0) & (b == 0))
    def _():
        out_ref[...] = before_ref[...]

    for s in range(len(rows) // chunks):
        valid, slot = arrival(pos_ref[0], size, step_index, s == 0)

        @pl.when((source == s) & valid)
        def _():
            @pl.when(b == 0)
            def _():
                kept_ref[...] = jnp.zeros_like(kept_ref)

            at = 0
            for c in range(chunks):
                ref = rows[s * chunks + c]
                count = ref.shape[0]
                ids = aux_ref[pl.ds(pl.multiple_of(slot * 8, 8), 8), at : at + count]
                product = lax.dot_general(down_ref[...], ref[...], NT, preferred_element_type=F32)
                kept = [kept_ref[:rank, at : at + count], kept_ref[rank:, at : at + count]]
                kept = pick(product, ids, b * (step // rank), rank, kept)
                kept_ref[:rank, at : at + count] = kept[0]
                kept_ref[rank:, at : at + count] = kept[1]
                at += count

            @pl.when(b == pl.num_programs(1) - 1)
            def _():
                out_ref[pl.ds(pl.multiple_of(slot * 2 * rank, 2 * rank), 2 * rank), :] = kept_ref[...]


def project_in(pos, size, step_index, down, aux, before, rows, chunks, rank, after=()):
    total, width = down.shape
    sources = len(rows) // chunks
    step = min(512, total)
    count = aux.shape[1]

    def down_block(s, b, pos):
        use = b
        for i in range(sources):
            valid, _ = arrival(pos[0], size, step_index, i == 0)
            use = jnp.where((s == i) & jnp.logical_not(valid), 0, use)
        return use, 0

    return call(
        functools.partial(project_in_body, rank, chunks, size, step_index),
        jax.ShapeDtypeStruct(before.shape, F32),
        grid=(sources, total // step),
        in_specs=[pl.BlockSpec((step, width), down_block), whole(aux.shape), whole(before.shape)]
        + [whole(r.shape) for r in rows],
        out_specs=whole(before.shape),
        scratch=[pltpu.VMEM((2 * rank, count), F32)],
        prefetch=1,
        aliases={3: 0},
        flops=2 * count * total * width,
        moved=2 * (count * width + total * width),
        after=after,
    )(pos, down, aux, before, *rows)


def adapter_rows_body(rank, size, place, pos_ref, part_ref, aux_ref, down_ref, *refs):
    out_ref, spread_ref = refs[-2:]
    count = aux_ref.shape[1]
    total = down_ref.shape[0]

    @pl.when(pl.program_id(0) == 0)
    def _():
        slot = slot_at(pos_ref[0], size, place)
        low = part_ref[pl.ds(pl.multiple_of(slot * 2 * rank, 2 * rank), 2 * rank), :]
        aux = aux_ref[pl.ds(pl.multiple_of(slot * 8, 8), 8), :]
        repeat = 128 // rank
        group = (lax.broadcasted_iota(jnp.int32, (128, count), 0) // rank).astype(F32)
        keys, values = [], []
        for k in range(2):
            scaled = (aux[2 + k : 3 + k, :] * low[k * rank : (k + 1) * rank, :]).astype(BF).astype(F32)
            values.append(jnp.concatenate([scaled] * repeat, axis=0).T)
            keys.append((aux[k : k + 1, :] - group).T)
        tile = 32
        for t in range(count // tile):
            rows = slice(t * tile, (t + 1) * tile)
            key = [k[rows] for k in keys]
            value = [v[rows] for v in values]
            for g in range(total // 128):
                first = float(g * repeat)
                spread = jnp.where(key[0] == first, value[0], jnp.where(key[1] == first, value[1], 0.0))
                spread_ref[rows, g * 128 : (g + 1) * 128] = spread.astype(BF)

    rows = jnp.dot(spread_ref[...], down_ref[...], preferred_element_type=F32)
    if len(refs) == 4:
        rows = rows + lax.dot_general(refs[0][...], refs[1][...], NT, preferred_element_type=F32)
    out_ref[...] = rows.astype(out_ref.dtype)


def adapter_rows(pos, size, place, part, aux, down, rank, frozen=None, after=()):
    total, width = down.shape
    count = aux.shape[1]
    step = 256
    block = pl.BlockSpec((count, step), lambda n, pos: (0, n))
    more, specs = [], []
    if frozen is not None:
        more = list(frozen)
        specs = [whole(more[0].shape), pl.BlockSpec((step, more[1].shape[1]), lambda n, pos: (n, 0))]
    return call(
        functools.partial(adapter_rows_body, rank, size, place),
        jax.ShapeDtypeStruct((count, width), BF if frozen is None else F32),
        grid=(width // step,),
        in_specs=[
            whole(part.shape), whole(aux.shape), pl.BlockSpec((total, step), lambda n, pos: (0, n)),
        ]
        + specs,
        out_specs=block,
        scratch=[pltpu.VMEM((count, total), BF)],
        prefetch=1,
        flops=2 * count * total * width,
        moved=2 * (total * width + count * width),
        after=after,
    )(pos, part, aux, down, *more)


def add_body(size, step_index, row, pos_ref, first_ref, second_ref, near_ref, far_ref, *refs):
    outs = refs[:2]
    held, terms, in_sem, term_sem, out_sem = refs[2:]
    pieces = in_sem.shape[1]
    piece = held.shape[1] // pieces
    d = pos_ref[0]
    for i, (source, out) in enumerate(zip((first_ref, second_ref), outs)):
        do, slot = departure(d, size, step_index, i == 0)
        place = place_of(d, size, slot)

        def get(q):
            rows = pl.ds(q * piece, piece)
            return pltpu.make_async_copy(source.at[rows], held.at[i, rows], in_sem.at[i, q])

        def put(q):
            rows = pl.ds(q * piece, piece)
            return pltpu.make_async_copy(held.at[i, rows], out.at[rows], out_sem.at[i, q])

        def term(q, ref):
            rows = pl.ds(row + q * piece, piece)
            return pltpu.make_async_copy(
                ref.at[rows], terms.at[i, pl.ds(q * piece, piece)], term_sem.at[i, q]
            )

        @pl.when(do)
        def _():
            for q in range(pieces):
                get(q).start()

                @pl.when(place == 0)
                def _():
                    term(q, near_ref).start()

                @pl.when(place != 0)
                def _():
                    term(q, far_ref).start()

            for q in range(pieces):
                get(q).wait()
                term(q, near_ref).wait()
                rows = pl.ds(q * piece, piece)
                held[i, rows, :] = (held[i, rows, :].astype(F32) + terms[i, rows, :].astype(F32)).astype(BF)
                put(q).start()
            for q in range(pieces):
                put(q).wait()


def ring_add(pos, size, step_index, row, first, second, near, far, after):
    shape = first.shape
    pieces = 4 if shape[0] % 64 == 0 else 1
    return call(
        functools.partial(add_body, size, step_index, row),
        [jax.ShapeDtypeStruct(shape, BF)] * 2,
        in_specs=[ANY] * 4,
        out_specs=[ANY] * 2,
        scratch=[
            pltpu.VMEM((2,) + shape, BF),
            pltpu.VMEM((2,) + shape, BF),
            pltpu.SemaphoreType.DMA((2, pieces)),
            pltpu.SemaphoreType.DMA((2, pieces)),
            pltpu.SemaphoreType.DMA((2, pieces)),
        ],
        prefetch=1,
        aliases={1: 0, 2: 1},
        flops=2 * shape[0] * shape[1],
        moved=6 * shape[0] * shape[1],
        after=after,
    )(pos, first, second, near, far)


def spread_rows(values, ids, first, adapters):
    rows = []
    for a in range(adapters):
        here = (first + a).astype(F32)
        rows.append(
            jnp.where(ids[0:1, :] == here, values[0], jnp.where(ids[1:2, :] == here, values[1], 0.0)).astype(BF)
        )
    return jnp.concatenate(rows, axis=0)


def grad_down_body(rank, size, first, where, pos_ref, part_ref, aux_ref, *refs):
    row_refs = refs[: len(where)]
    before_ref = refs[len(where)] if len(refs) == len(where) + 6 else None
    out_ref, rows_ref, scaled_ref, ids_ref, sem = refs[-5:]
    b = pl.program_id(0)
    count = aux_ref.shape[1]
    places = rows_ref.shape[0] // count
    step = out_ref.shape[0]

    def copies(act):
        for i, (step_index, a, offset) in enumerate(where):
            height = row_refs[i].shape[0]
            valid, slot = arrival(pos_ref[0], size, step_index, a)
            place = place_of(pos_ref[0], size, slot)

            @pl.when(valid & (place >= first) & (place < first + places))
            def _():
                start = pl.multiple_of((place - first) * count + offset, height)
                act(pltpu.make_async_copy(row_refs[i], rows_ref.at[pl.ds(start, height)], sem.at[i]))

    @pl.when(b == 0)
    def _():
        copies(lambda c: c.start())
        for p in range(places):
            slot = slot_at(pos_ref[0], size, first + p)
            low = part_ref[pl.ds(pl.multiple_of(slot * 2 * rank, 2 * rank), 2 * rank), :]
            aux = aux_ref[pl.ds(pl.multiple_of(slot * 8, 8), 8), :]
            columns = slice(p * count, (p + 1) * count)
            ids_ref[:, columns] = aux
            for k in range(2):
                scaled = aux[2 + k : 3 + k, :] * low[k * rank : (k + 1) * rank, :]
                scaled_ref[k, :, columns] = scaled.astype(BF).astype(F32)
        copies(lambda c: c.wait())

    spread = []
    for p in range(places):
        columns = slice(p * count, (p + 1) * count)
        values = [scaled_ref[k, :, columns] for k in range(2)]
        spread.append(spread_rows(values, ids_ref[0:2, columns], b * (step // rank), step // rank))
    spread = spread[0] if places == 1 else jnp.concatenate(spread, axis=1)
    out = jnp.dot(spread, rows_ref[...], preferred_element_type=F32)
    if before_ref is not None:
        out = out + before_ref[...].astype(F32)
    out_ref[...] = out.astype(BF)


def grad_down(pos, size, part, aux, rows, where, first, places, total, rank, before=None, after=()):
    count = aux.shape[1]
    width = rows[0].shape[1]
    step = min(512, total)
    block = pl.BlockSpec((step, width), lambda b, pos: (b, 0))
    more = [] if before is None else [before]
    return call(
        functools.partial(grad_down_body, rank, size, first, where),
        jax.ShapeDtypeStruct((total, width), BF),
        grid=(total // step,),
        in_specs=[whole(part.shape), whole(aux.shape)] + [ANY] * len(rows) + [block] * len(more),
        out_specs=block,
        scratch=[
            pltpu.VMEM((places * count, width), BF),
            pltpu.VMEM((2, rank, places * count), F32),
            pltpu.VMEM((8, places * count), F32),
            pltpu.SemaphoreType.DMA((len(rows),)),
        ],
        prefetch=1,
        aliases={3 + len(rows): 0} if more else None,
        flops=2 * places * count * total * width,
        moved=2 * (total * width + places * count * width),
        vmem=28 if places * count * width <= 1 << 22 else 60,
        after=after,
    )(pos, part, aux, *rows, *more)


def grad_gates_body(rank, in_ref, out_ref, *gate_refs):
    for s, gate_ref in enumerate(gate_refs):
        at = slice(2 * rank * s, 2 * rank * (s + 1))
        both = in_ref[at, :] * out_ref[at, :]
        gates = [jnp.sum(both[k * rank : (k + 1) * rank, :], axis=0, keepdims=True) for k in range(2)]
        gate_ref[...] = jnp.concatenate(gates, axis=0).astype(BF)


def grad_gates(part_in, part_out, slots, rank):
    shape = part_in.shape
    return call(
        functools.partial(grad_gates_body, rank),
        [jax.ShapeDtypeStruct((2, shape[1]), BF)] * slots,
        in_specs=[whole(shape)] * 2,
        out_specs=[whole((2, shape[1]))] * slots,
        moved=8 * shape[0] * shape[1],
    )(part_in, part_out)


def grad_up_body(rank, slots, in_ref, aux_ref, *refs):
    blocks, (up_ref, rows_ref, scaled_ref) = refs[:slots], refs[slots:]
    b = pl.program_id(0)
    count = aux_ref.shape[1]
    step = up_ref.shape[0]

    @pl.when(b == 0)
    def _():
        for s in range(slots):
            rows_ref[s * count : (s + 1) * count, :] = blocks[s][:count, :]
            for k in range(2):
                at = slice(2 * rank * s + k * rank, 2 * rank * s + (k + 1) * rank)
                scaled = aux_ref[8 * s + 2 + k : 8 * s + 3 + k, :] * in_ref[at, :]
                scaled_ref[k, :, s * count : (s + 1) * count] = scaled.astype(BF).astype(F32)

    spread = []
    for s in range(slots):
        values = [scaled_ref[k, :, s * count : (s + 1) * count] for k in range(2)]
        spread.append(
            spread_rows(values, aux_ref[8 * s : 8 * s + 2, :], b * (step // rank), step // rank)
        )
    up_ref[...] = jnp.dot(
        jnp.concatenate(spread, axis=1), rows_ref[...], preferred_element_type=F32
    ).astype(BF)


def grad_up(part_in, aux, blocks, total, rank, after=()):
    count = aux.shape[1]
    slots = len(blocks)
    width = blocks[0].shape[1]
    step = min(256, total)
    arrays = [part_in, aux, *blocks]
    return call(
        functools.partial(grad_up_body, rank, slots),
        jax.ShapeDtypeStruct((total, width), BF),
        grid=(total // step,),
        in_specs=[whole(a.shape) for a in arrays],
        out_specs=pl.BlockSpec((step, width), lambda b: (b, 0)),
        scratch=[pltpu.VMEM((slots * count, width), BF), pltpu.VMEM((2, rank, slots * count), F32)],
        flops=2 * slots * count * total * width,
        moved=2 * (total * width + slots * count * width),
        after=after,
    )(*arrays)


def finish_body(base_ref, first_ref, second_ref, *refs):
    out_ref = refs[-1]
    out_ref[...] = (
        base_ref[...] + first_ref[...].astype(F32) + second_ref[...].astype(F32)
    ).astype(BF)


def finish(base, first, second, chunk, before, after):
    size, width = first.shape
    step = min(128, size)
    blocks = size // step
    shift = pl.BlockSpec((step, width), lambda i: (i + chunk * blocks, 0))
    local = pl.BlockSpec((step, width), lambda i: (i, 0))
    arrays = [base, first, second] + ([] if before is None else [before])
    return call(
        finish_body,
        jax.ShapeDtypeStruct(base.shape, BF),
        grid=(blocks,),
        in_specs=[shift, local, local] + ([] if before is None else [ANY]),
        out_specs=shift,
        aliases=None if before is None else {3: 0},
        flops=2 * size * width,
        moved=10 * size * width,
        after=after,
    )(*arrays)


def per_device(inputs, output_gradient, frozen_key_weight, adapter_down_factors, adapter_up_factors,
               token_adapter_index, gates):
    count, width = inputs.shape
    out_width = output_gradient.shape[1]
    size = lax.axis_size("dp")
    shares = lax.axis_size("mp")
    local, rank = adapter_down_factors.shape[:2]
    total = local * rank
    d = lax.axis_index("dp")
    odd = d % 2
    half = count // CHUNKS
    down = adapter_down_factors.reshape(total, width)
    up = adapter_up_factors.reshape(total, out_width)
    pairs_a = [p for i in range(0, size - 1, 2) for p in ((i, i + 1), (i + 1, i))]
    pairs_b = [p for i in range(1, size - 1, 2) for p in ((i, i + 1), (i + 1, i))]
    i32 = jnp.int32

    def exchange(part):
        bit = 1
        while bit < shares:
            part = part + lax.ppermute(part, "mp", [(i, i ^ bit) for i in range(shares)])
            bit *= 2
        return part

    pos = d.astype(jnp.int32).reshape(1)

    block, aux_own = pack_rows(pos, token_adapter_index.T, gates.T, output_gradient, local)
    blocks = [block] + [
        lax.ppermute(block, "dp", [(i, (i + s) % size) for i in range(size)]) for s in range(1, size)
    ]
    full_out = lax.all_gather(output_gradient, "mp", axis=1, tiled=True)
    low = jnp.zeros((size * 2 * rank, count), F32)
    low = project_in(pos, size, -1, down, aux_own, low, [inputs], 1, rank)

    sent = [pin(inputs[c * half : (c + 1) * half], blocks[1:]) for c in range(CHUNKS)]
    got = [[lax.ppermute(sent[c], "dp", p) for p in (pairs_a, pairs_b)] for c in range(CHUNKS)]

    part_out, aux = project_out(pos, up, blocks, count, rank, [low] + sent)
    part_out = exchange(part_out)
    near = far = adapter_rows(pos, size, 0, part_out, aux, down, rank)

    rows, where = [inputs], [(-1, True, 0)]
    early = result = None
    last = near
    for j in range(1, size):
        term = far
        for c in range(CHUNKS):
            to_a, to_b = ring_add(pos, size, j, c * half, got[c][1], got[c][0], near, term, [last])
            rows += [to_b, to_a]
            where += [(j - 1, True, c * half), (j - 1, False, c * half)]
            got[c] = [lax.ppermute(to_a, "dp", pairs_a), lax.ppermute(to_b, "dp", pairs_b)]
            last = to_a
            if c == 0:
                frozen = (full_out, frozen_key_weight) if j == size - 1 else None
                far = last = adapter_rows(pos, size, j, part_out, aux, down, rank, frozen, [to_a])
        newest = rows[-2 * CHUNKS :]
        low = last = project_in(
            pos, size, j - 1, down, aux, low, newest[0::2] + newest[1::2], CHUNKS, rank, [last]
        )
        if j == size - 2:
            early = last = grad_down(
                pos, size, part_out, aux, rows, where, 1, size - 1, total, rank, None, [last]
            )

    for c in range(CHUNKS):
        result = last = finish(far, got[c][0], got[c][1], c, result, [last])
        if c == 0:
            down_gradient = last = grad_down(
                pos, size, part_out, aux, rows, where, 0, 1, total, rank, early, [last]
            )
    part_in = exchange(pin(low, [result]))
    gate_rows = grad_gates(part_in, part_out, size, rank)
    up_gradient = grad_up(part_in, aux, blocks, total, rank, [gate_rows[0]])
    gate_sum = gate_rows[0].astype(F32)
    for s in range(1, size):
        gate_sum = gate_sum + lax.ppermute(
            gate_rows[s], "dp", [(i, (i - s) % size) for i in range(size)]
        ).astype(F32)
    return (
        result,
        gate_sum.astype(BF).T,
        down_gradient.reshape(local, rank, width),
        up_gradient.reshape(local, rank, out_width),
    )


def solution(mesh):
    in_specs = (
        P(("groups", "dp"), "mp"),
        P(("groups", "dp"), "mp"),
        P("mp", None),
        P("dp", None, "mp"),
        P("dp", None, "mp"),
        P(("groups", "dp"), None),
        P(("groups", "dp"), None),
    )
    out_specs = (
        P(("groups", "dp"), "mp"),
        P(("groups", "dp"), None),
        P(("groups", "dp"), None, "mp"),
        P(("groups", "dp"), None, "mp"),
    )
    return jax.shard_map(
        per_device, mesh=mesh, in_specs=in_specs, out_specs=out_specs, check_vma=False
    )
```

time: 263 us -> 224 us (0.85)
  waiting for transfers between devices: 65.6 us -> 29.4 us
  Pallas kernels: 122 us -> 104 us
  local copies, waits for them, and re-layouts: 10.7 us -> 25.8 us
  matrix products: 3.55 us -> 0 us
  starting transfers between devices: 44.9 us -> 48.2 us
    ppermute x8 -> x6, waiting for transfers between devices: 18.3 us -> 0.67 us  [per_device(): lax.ppermute(to_a, 'dp', pairs_a)]
    pallas_call x18 -> x25, Pallas kernels: 122 us -> 104 us  [call(): return lambda *arrays: call_it(*arrays, *after)]
    unnamed x32 -> x64, local copies, waits for them, and re-layouts: 7.49 us -> 24.8 us
    ppermute x3, waiting for transfers between devices: 22.1 us -> 11.9 us  [per_device(): lax.ppermute(block, 'dp', [(i, (i + s) % size) for i in range(size)])]
    ppermute x6 -> x8, starting transfers between devices: 2.24 us -> 10.3 us  [the longest x4 7.08 us: per_device(): lax.ppermute(sent[c], 'dp', p)]
    ppermute x3, waiting for transfers between devices: 6.49 us -> 0.01 us  [per_device(): lax.ppermute(gate_rows[s], 'dp', [(i, (i - s) % size) for i in range(size)])]
    ppermute x3, starting transfers between devices: 9.17 us -> 3.05 us  [per_device(): lax.ppermute(gate_rows[s], 'dp', [(i, (i - s) % size) for i in range(size)])]
    ppermute x8 -> x6, starting transfers between devices: 15.8 us -> 20.8 us  [per_device(): lax.ppermute(to_a, 'dp', pairs_a)]
  transfers between devices with their start and end apart: 29 -> 27, of which waited for: 10 -> 6; matrix products, arithmetic and copies ran while one was open for 3% -> 0% of each run, Pallas kernels for 43% -> 45%
where the time goes in v2:
time: 224 us; the launch traced here: 223 us
  Pallas kernels  104 us (46%)
  starting transfers between devices  48.2 us (22%)
  waiting for transfers between devices  29.4 us (13%)
  local copies, waits for them, and re-layouts  25.8 us (12%)
  between operations  14.6 us (7%)
    pallas_call x25, Pallas kernels, call(): return lambda *arrays: call_it(*arrays, *after)  104 us
    unnamed x64, local copies, waits for them, and re-layouts  24.8 us
    ppermute x6, starting transfers between devices, per_device(): lax.ppermute(to_a, 'dp', pairs_a)  20.8 us
    ppermute x4, waiting for transfers between devices, exchange(): lax.ppermute(part, 'mp', [(i, i ^ bit) for i in range(shares)])  16.8 us
    ppermute x3, waiting for transfers between devices, per_device(): lax.ppermute(block, 'dp', [(i, (i + s) % size) for i in range(size)])  11.9 us
    ppermute x6, starting transfers between devices, per_device(): lax.ppermute(to_b, 'dp', pairs_b)  7.91 us
    ppermute x4, starting transfers between devices, per_device(): lax.ppermute(sent[c], 'dp', p)  7.08 us
    ppermute x3, starting transfers between devices, per_device(): lax.ppermute(block, 'dp', [(i, (i + s) % size) for i in range(size)])  6.06 us
  transfers between devices with their start and end apart: 27, of which 6 were waited for; matrix products, arithmetic and copies ran while one was open for 0% of the time, Pallas kernels for 45%

profile of v2, /device:TPU:0, one launch (start us, length us, event | category | flops | bytes accessed | tf_op | source)
XLA Modules:
  0.0 223.1 jit_solution(4323919237706029966)
XLA Ops:
  7.2 1.7 shard_map.102
  9.0 5.0 %collective-permute-start.2 = (bf16[528,256]{1,0:T(8,128)(2,1)}, bf16[528,256]{1,0:T(8,128)(2,1)S(1)}, u32[]{:S(2)}, u32[]{:S(2)}) collective-permute-start(bf16[528,256]{1,0:T(8,128)(2,1)} %get-tuple-element.24.refs_2_), channel_id=1, source_target_pairs={{0,12},{4,0},{8,4},{12,8},{1,13},{5,1},{9,5},{13,9},{2,14},{6,2},{... | collective-permute-start | bytes 811016 | tf_op jit(solution)/shard_map/ppermute | solution.py:585
  14.0 1.0 collective-permute-start
  15.1 2.8 %copy-done = bf16[128,16,1536]{2,1,0:T(8,128)(2,1)S(1)} copy-done((bf16[128,16,1536]{2,1,0:T(8,128)(2,1)S(1)}, bf16[128,16,1536]{2,1,0:T(8,128)(2,1)}, u32[]{:S(2)}) %copy-start) | copy-done | bytes 6291480
  17.8 1.4 copy-done.9
  19.2 0.7 copy-done.26
  20.0 4.3 %shard_map.103.refs_6_.refs_3_ = f32[128,512]{1,0:T(8,128)S(1)} custom-call(s32[1]{0:T(128)} %bitcast.refs_0_, bf16[2048,1536]{1,0:T(8,128)(2,1)S(1)} %bitcast.9, f32[8,512]{1,0:T(8,128)S(1)} %copy-done.26, f32[128,512]{1,0:T(8,128)S(1)} %broadcast_in_dim.3.refs_3_, bf16[512,1536]{1,0:T(8,128)(2,1)S(1)} %copy-done.9), custom_call_target="tpu_custom_call", output_to_operand_aliasing={{}: (3, {})} | custom-call | flops 64424508 | bytes 157286 | tf_op jit(solution)/shard_map/pallas_call | solution.py:45
  24.3 1.0 fusion.1
  25.3 11.9 %collective-permute-done.1.refs_2_.refs_4_ = bf16[528,256]{1,0:T(8,128)(2,1)S(1)} collective-permute-done((bf16[528,256]{1,0:T(8,128)(2,1)}, bf16[528,256]{1,0:T(8,128)(2,1)S(1)}, u32[]{:S(2)}, u32[]{:S(2)}) %collective-permute-start.1) | collective-permute-done | bytes 270368 | tf_op jit(solution)/shard_map/ppermute | solution.py:585
  37.3 1.0 collective-permute-start.6
  38.2 0.7 collective-permute-start.5
  38.9 3.9 %collective-permute-start.10 = (bf16[256,1536]{1,0:T(8,128)(2,1)}, bf16[256,1536]{1,0:T(8,128)(2,1)}, u32[]{:S(2)}, u32[]{:S(2)}) collective-permute-start(bf16[256,1536]{1,0:T(8,128)(2,1)} %shard_map.105.refs_8_), channel_id=1, source_target_pairs={{0,4},{4,0},{8,12},{12,8},{1,5},{5,1},{9,13},{13,9},{2,6},{6,2},{1... | collective-permute-start | bytes 2359304 | tf_op jit(solution)/shard_map/ppermute | solution.py:592
  42.8 1.6 collective-permute-start.9
  44.4 4.6 %shard_map.106 = (f32[128,512]{1,0:T(8,128)S(1)}, f32[32,512]{1,0:T(8,128)S(1)}) custom-call(s32[1]{0:T(128)} %bitcast.refs_0_, bf16[2048,256]{1,0:T(8,128)(2,1)S(1)} %bitcast.22, bf16[528,256]{1,0:T(8,128)(2,1)S(1)} %copy-done.24, bf16[528,256]{1,0:T(8,128)(2,1)S(1)} %collective-permute-done.refs_1_.refs_3_, ...), custom_call_target="tpu_custom_call" | custom-call | flops 10737418240 | bytes 10485760 | tf_op jit(solution)/shard_map/pallas_call | solution.py:45
  49.0 0.1 collective-permute-start.3
  49.1 1.5 collective-permute-done.3
  50.7 1.6 collective-permute-start.4
  52.2 6.9 %collective-permute-done.4 = f32[128,512]{1,0:T(8,128)S(1)} collective-permute-done((f32[128,512]{1,0:T(8,128)S(1)}, f32[128,512]{1,0:T(8,128)S(1)}, u32[]{:S(2)}, u32[]{:S(2)}) %collective-permute-start.4) | collective-permute-done | bytes 262176 | tf_op jit(solution)/shard_map/ppermute | solution.py:577
  59.2 5.8 %shard_map.107.refs_3_.refs_4_.refs_5_ = bf16[512,1536]{1,0:T(8,128)(2,1)S(1)} custom-call(s32[1]{0:T(128)} %bitcast.refs_0_, f32[128,512]{1,0:T(8,128)S(1)} %add.22.refs_1_, f32[32,512]{1,0:T(8,128)S(1)} %get-tuple-element.27.refs_2_.refs_1_, bf16[2048,1536]{1,0:T(8,128)(2,1)S(1)} %bitcast.12), custom_call_target="tpu_custom_call" | custom-call | flops 64424508 | bytes 157286 | tf_op jit(solution)/shard_map/pallas_call | solution.py:45
  65.1 3.5 %shard_map.108 = (bf16[256,1536]{1,0:T(8,128)(2,1)S(1)}, bf16[256,1536]{1,0:T(8,128)(2,1)}) custom-call(s32[1]{0:T(128)} %bitcast.refs_0_, bf16[256,1536]{1,0:T(8,128)(2,1)S(1)} %collective-permute-done.5.refs_1_, bf16[256,1536]{1,0:T(8,128)(2,1)} %collective-permute-done.6.refs_2_, ...), custom_call_target="tpu_custom_call", output_to_operand_aliasing={{0}: (1, {}), {1}: (2, {})} | custom-call | flops 15728 | bytes 47185 | tf_op jit(solution)/shard_map/pallas_call | solution.py:45
  68.6 1.5 collective-permute-start.7
  70.1 0.6 collective-permute-start.8
  70.7 2.8 %copy-done.1 = bf16[128,16,1536]{2,1,0:T(8,128)(2,1)S(1)} copy-done((bf16[128,16,1536]{2,1,0:T(8,128)(2,1)S(1)}, bf16[128,16,1536]{2,1,0:T(8,128)(2,1)}, u32[]{:S(2)}) %copy-start.1) | copy-done | bytes 6291480
  73.5 5.8 %shard_map.109.refs_5_.refs_4_ = bf16[512,1536]{1,0:T(8,128)(2,1)S(1)} custom-call(s32[1]{0:T(128)} %bitcast.refs_0_, f32[128,512]{1,0:T(8,128)S(1)} %add.22.refs_1_, f32[32,512]{1,0:T(8,128)S(1)} %get-tuple-element.27.refs_2_.refs_1_, bf16[2048,1536]{1,0:T(8,128)(2,1)S(1)} %bitcast.13, bf16[256,1536]{1,0:T(8,128)(2,1)S(1)} %get-tuple-element.29.refs_4_.refs_6_.refs_5_), custom_call_target="tpu_custom_call" | custom-call | flops 64424508 | bytes 157286 | tf_op jit(solution)/shard_map/pallas_call | solution.py:45
  79.3 2.7 %shard_map.110 = (bf16[256,1536]{1,0:T(8,128)(2,1)}, bf16[256,1536]{1,0:T(8,128)(2,1)}) custom-call(s32[1]{0:T(128)} %bitcast.refs_0_, bf16[256,1536]{1,0:T(8,128)(2,1)} %collective-permute-done.9.refs_1_, bf16[256,1536]{1,0:T(8,128)(2,1)} %collective-permute-done.10.refs_2_, ...), custom_call_target="tpu_custom_call", output_to_operand_aliasing={{0}: (1, {}), {1}: (2, {})} | custom-call | flops 15728 | bytes 47185 | tf_op jit(solution)/shard_map/pallas_call | solution.py:45
  82.1 1.5 collective-permute-start.13
  83.6 6.4 %shard_map.111.refs_5_.refs_3_ = f32[128,512]{1,0:T(8,128)S(1)} custom-call(s32[1]{0:T(128)} %bitcast.refs_0_, bf16[2048,1536]{1,0:T(8,128)(2,1)S(1)} %bitcast.16, f32[32,512]{1,0:T(8,128)S(1)} %get-tuple-element.27.refs_2_.refs_1_, f32[128,512]{1,0:T(8,128)S(1)} %shard_map.103.refs_6_.refs_3_, ...), custom_call_target="tpu_custom_call", output_to_operand_aliasing={{}: (3, {})} | custom-call | flops 64424508 | bytes 157286 | tf_op jit(solution)/shard_map/pallas_call | solution.py:45
  90.0 0.7 collective-permute-done.8.refs_2_
  90.7 2.7 %shard_map.112 = (bf16[256,1536]{1,0:T(8,128)(2,1)}, bf16[256,1536]{1,0:T(8,128)(2,1)}) custom-call(s32[1]{0:T(128)} %bitcast.refs_0_, bf16[256,1536]{1,0:T(8,128)(2,1)} %collective-permute-done.7.refs_1_, bf16[256,1536]{1,0:T(8,128)(2,1)} %collective-permute-done.8.refs_2_, ...), custom_call_target="tpu_custom_call", output_to_operand_aliasing={{0}: (1, {}), {1}: (2, {})} | custom-call | flops 15728 | bytes 47185 | tf_op jit(solution)/shard_map/pallas_call | solution.py:45
  93.4 1.6 collective-permute-start.11
  94.9 6.9 %collective-permute-start.12 = (bf16[256,1536]{1,0:T(8,128)(2,1)}, bf16[256,1536]{1,0:T(8,128)(2,1)}, u32[]{:S(2)}, u32[]{:S(2)}) collective-permute-start(bf16[256,1536]{1,0:T(8,128)(2,1)} %get-tuple-element.33.refs_4_.refs_6_.refs_9_), channel_id=1, source_target_pairs={{0,4},{4,0},{8,12},{12,8},{1,5},{5,1},{9,13},{13,9},{2,6},{6,2},{1... | collective-permute-start | bytes 2359304 | tf_op jit(solution)/shard_map/ppermute | solution.py:607
  101.8 5.8 %shard_map.113.refs_5_.refs_4_ = bf16[512,1536]{1,0:T(8,128)(2,1)S(1)} custom-call(s32[1]{0:T(128)} %bitcast.refs_0_, f32[128,512]{1,0:T(8,128)S(1)} %add.22.refs_1_, f32[32,512]{1,0:T(8,128)S(1)} %get-tuple-element.27.refs_2_.refs_1_, bf16[2048,1536]{1,0:T(8,128)(2,1)S(1)} %bitcast.17, bf16[256,1536]{1,0:T(8,128)(2,1)} %get-tuple-element.33.refs_4_.refs_6_.refs_9_), custom_call_target="tpu_custom_call" | custom-call | flops 64424508 | bytes 157286 | tf_op jit(solution)/shard_map/pallas_call | solution.py:45
  107.7 2.8 %shard_map.114 = (bf16[256,1536]{1,0:T(8,128)(2,1)}, bf16[256,1536]{1,0:T(8,128)(2,1)}) custom-call(s32[1]{0:T(128)} %bitcast.refs_0_, bf16[256,1536]{1,0:T(8,128)(2,1)} %collective-permute-done.13.refs_1_, bf16[256,1536]{1,0:T(8,128)(2,1)} %collective-permute-done.14.refs_2_, ...), custom_call_target="tpu_custom_call", output_to_operand_aliasing={{0}: (1, {}), {1}: (2, {})} | custom-call | flops 15728 | bytes 47185 | tf_op jit(solution)/shard_map/pallas_call | solution.py:45
  110.5 1.6 collective-permute-start.15
  112.1 6.5 %collective-permute-start.16 = (bf16[256,1536]{1,0:T(8,128)(2,1)}, bf16[256,1536]{1,0:T(8,128)(2,1)}, u32[]{:S(2)}, u32[]{:S(2)}) collective-permute-start(bf16[256,1536]{1,0:T(8,128)(2,1)} %get-tuple-element.35.refs_7_.refs_8_.refs_11_), channel_id=1, source_target_pairs={{0,4},{4,0},{8,12},{12,8},{1,5},{5,1},{9,13},{13,9},{2,6},{6,2},{1... | collective-permute-start | bytes 2359304 | tf_op jit(solution)/shard_map/ppermute | solution.py:607
  118.6 6.6 %shard_map.115.refs_12_.refs_3_ = f32[128,512]{1,0:T(8,128)S(1)} custom-call(s32[1]{0:T(128)} %bitcast.refs_0_, bf16[2048,1536]{1,0:T(8,128)(2,1)S(1)} %bitcast.18, f32[32,512]{1,0:T(8,128)S(1)} %get-tuple-element.27.refs_2_.refs_1_, f32[128,512]{1,0:T(8,128)S(1)} %shard_map.111.refs_5_.refs_3_, ...), custom_call_target="tpu_custom_call", output_to_operand_aliasing={{}: (3, {})} | custom-call | flops 64424508 | bytes 157286 | tf_op jit(solution)/shard_map/pallas_call | solution.py:45
  125.2 13.8 %shard_map.116.refs_5_.refs_16_ = bf16[2048,1536]{1,0:T(8,128)(2,1)} custom-call(s32[1]{0:T(128)} %bitcast.refs_0_, f32[128,512]{1,0:T(8,128)S(1)} %add.22.refs_1_, f32[32,512]{1,0:T(8,128)S(1)} %get-tuple-element.27.refs_2_.refs_1_, bf16[512,1536]{1,0:T(8,128)(2,1)S(1)} %copy-done.10, bf16[256,1536]{1,0:T(8,128)(2,1)} %get-tuple-element.28.refs_4_, ...), custom_call_target="tpu_custom_call" | custom-call | flops 193273536 | bytes 220200 | tf_op jit(solution)/shard_map/pallas_call | solution.py:45
  139.0 2.8 %copy-done.7 = bf16[2048,1536]{1,0:T(8,128)(2,1)S(1)} copy-done((bf16[2048,1536]{1,0:T(8,128)(2,1)S(1)}, bf16[2048,1536]{1,0:T(8,128)(2,1)}, u32[]{:S(2)}) %copy-start.7) | copy-done | bytes 6291480
  141.8 2.7 %shard_map.117 = (bf16[256,1536]{1,0:T(8,128)(2,1)}, bf16[256,1536]{1,0:T(8,128)(2,1)}) custom-call(s32[1]{0:T(128)} %bitcast.refs_0_, bf16[256,1536]{1,0:T(8,128)(2,1)} %collective-permute-done.11.refs_1_, bf16[256,1536]{1,0:T(8,128)(2,1)} %collective-permute-done.12.refs_2_, ...), custom_call_target="tpu_custom_call", output_to_operand_aliasing={{0}: (1, {}), {1}: (2, {})} | custom-call | flops 15728 | bytes 47185 | tf_op jit(solution)/shard_map/pallas_call | solution.py:45
  144.5 0.7 collective-permute-start.20
  145.2 4.3 %collective-permute-start.19 = (bf16[256,1536]{1,0:T(8,128)(2,1)}, bf16[256,1536]{1,0:T(8,128)(2,1)}, u32[]{:S(2)}, u32[]{:S(2)}) collective-permute-start(bf16[256,1536]{1,0:T(8,128)(2,1)} %get-tuple-element.36.refs_6_.refs_13_), channel_id=1, source_target_pairs={{0,4},{4,0},{8,12},{12,8},{1,5},{5,1},{9,13},{13,9},{2,6},{6,2},{1... | collective-permute-start | bytes 2359304 | tf_op jit(solution)/shard_map/ppermute | solution.py:607
  149.5 2.8 %copy-done.2 = bf16[128,16,1536]{2,1,0:T(8,128)(2,1)S(1)} copy-done((bf16[128,16,1536]{2,1,0:T(8,128)(2,1)S(1)}, bf16[128,16,1536]{2,1,0:T(8,128)(2,1)}, u32[]{:S(2)}) %copy-start.2) | copy-done | bytes 6291480
  152.2 1.9 copy-done.16
  154.1 1.2 copy-done.23
  155.4 7.8 %shard_map.118.refs_5_.refs_0_ = f32[512,1536]{1,0:T(8,128)S(1)} custom-call(s32[1]{0:T(128)} %bitcast.refs_0_, f32[128,512]{1,0:T(8,128)S(1)} %add.22.refs_1_, f32[32,512]{1,0:T(8,128)S(1)} %get-tuple-element.27.refs_2_.refs_1_, bf16[2048,1536]{1,0:T(8,128)(2,1)S(1)} %bitcast.19, bf16[512,1024]{1,0:T(8,128)(2,1)S(1)} %copy-done.23, ...), custom_call_target="tpu_custom_call" | custom-call | flops 64424508 | bytes 157286 | tf_op jit(solution)/shard_map/pallas_call | solution.py:45
  163.2 2.7 %shard_map.119 = (bf16[256,1536]{1,0:T(8,128)(2,1)}, bf16[256,1536]{1,0:T(8,128)(2,1)}) custom-call(s32[1]{0:T(128)} %bitcast.refs_0_, bf16[256,1536]{1,0:T(8,128)(2,1)} %collective-permute-done.15.refs_1_, bf16[256,1536]{1,0:T(8,128)(2,1)} %collective-permute-done.16.refs_2_, ...), custom_call_target="tpu_custom_call", output_to_operand_aliasing={{0}: (1, {}), {1}: (2, {})} | custom-call | flops 15728 | bytes 47185 | tf_op jit(solution)/shard_map/pallas_call | solution.py:45
  165.9 2.6 %collective-permute-start.17 = (bf16[256,1536]{1,0:T(8,128)(2,1)}, bf16[256,1536]{1,0:T(8,128)(2,1)S(1)}, u32[]{:S(2)}, u32[]{:S(2)}) collective-permute-start(bf16[256,1536]{1,0:T(8,128)(2,1)} %get-tuple-element.37.refs_7_.refs_8_.refs_15_), channel_id=1, source_target_pairs={{0,4},{4,0},{8,12},{12,8},{1,5},{5,1},{9,13},{13,9},{2,6},{6,2},{1... | collective-permute-start | bytes 2359304 | tf_op jit(solution)/shard_map/ppermute | solution.py:607
  168.5 0.9 collective-permute-start.18
  169.4 2.8 %copy-done.3 = bf16[128,16,1536]{2,1,0:T(8,128)(2,1)S(1)} copy-done((bf16[128,16,1536]{2,1,0:T(8,128)(2,1)S(1)}, bf16[128,16,1536]{2,1,0:T(8,128)(2,1)}, u32[]{:S(2)}) %copy-start.3) | copy-done | bytes 6291480
  172.2 6.6 %shard_map.120.refs_3_.refs_0_ = f32[128,512]{1,0:T(8,128)S(1)} custom-call(s32[1]{0:T(128)} %bitcast.refs_0_, bf16[2048,1536]{1,0:T(8,128)(2,1)S(1)} %bitcast.20, f32[32,512]{1,0:T(8,128)S(1)} %get-tuple-element.27.refs_2_.refs_1_, f32[128,512]{1,0:T(8,128)S(1)} %shard_map.115.refs_12_.refs_3_, ...), custom_call_target="tpu_custom_call", output_to_operand_aliasing={{}: (3, {})} | custom-call | flops 64424508 | bytes 157286 | tf_op jit(solution)/shard_map/pallas_call | solution.py:45
  178.8 2.2 shard_map.121.refs_17_.refs_3_
  181.0 1.4 copy-done.12
  182.4 9.3 %shard_map.122.refs_4_ = bf16[2048,1536]{1,0:T(8,128)(2,1)} custom-call(s32[1]{0:T(128)} %bitcast.refs_0_, f32[128,512]{1,0:T(8,128)S(1)} %add.22.refs_1_, f32[32,512]{1,0:T(8,128)S(1)} %get-tuple-element.27.refs_2_.refs_1_, bf16[512,1536]{1,0:T(8,128)(2,1)S(1)} %copy-done.11, ...), custom_call_target="tpu_custom_call", output_to_operand_aliasing={{}: (16, {})} | custom-call | flops 64424508 | bytes 157286 | tf_op jit(solution)/shard_map/pallas_call | solution.py:45
  191.8 2.8 %copy-done.8 = bf16[2048,1536]{1,0:T(8,128)(2,1)S(1)} copy-done((bf16[2048,1536]{1,0:T(8,128)(2,1)S(1)}, bf16[2048,1536]{1,0:T(8,128)(2,1)}, u32[]{:S(2)}) %copy-start.8) | copy-done | bytes 6291480
  194.6 1.1 shard_map.123.refs_1_
  195.6 1.4 copy-done.13
  197.1 0.1 collective-permute-start.21
  197.1 1.5 collective-permute-done.21
  198.7 1.6 collective-permute-start.22
  200.3 6.9 %collective-permute-done.22 = f32[128,512]{1,0:T(8,128)S(1)} collective-permute-done((f32[128,512]{1,0:T(8,128)S(1)}, f32[128,512]{1,0:T(8,128)S(1)}, u32[]{:S(2)}, u32[]{:S(2)}) %collective-permute-start.22) | collective-permute-done | bytes 262176 | tf_op jit(solution)/shard_map/ppermute | solution.py:577
  207.2 2.4 %collective-permute-start.23 = (bf16[2,512]{1,0:T(2,128)(2,1)S(1)}, bf16[2,512]{1,0:T(2,128)(2,1)S(1)}, u32[]{:S(2)}, u32[]{:S(2)}) collective-permute-start(bf16[2,512]{1,0:T(2,128)(2,1)S(1)} %get-tuple-element.41), channel_id=1, source_target_pairs={{0,12},{4,0},{8,4},{12,8},{1,13},{5,1},{9,5},{13,9},{2,14},{6,2},{... | collective-permute-start | bytes 6152 | tf_op jit(solution)/shard_map/ppermute | solution.py:632
  209.6 0.6 collective-permute-start.25
  210.3 5.4 %shard_map.126 = bf16[2048,256]{1,0:T(8,128)(2,1)} custom-call(f32[128,512]{1,0:T(8,128)S(1)} %add.24.refs_0_, f32[32,512]{1,0:T(8,128)S(1)} %get-tuple-element.27.refs_2_.refs_1_, bf16[528,256]{1,0:T(8,128)(2,1)S(1)} %copy-done.25, bf16[528,256]{1,0:T(8,128)(2,1)S(1)} %copy-done.22, bf16[528,256]{1,0:T(8,128)(2,1)S(1)} %copy-done.20, ...), custom_call_target="tpu_custom_call" | custom-call | flops 42949672 | bytes 41943 | tf_op jit(solution)/shard_map/pallas_call | solution.py:45
  215.7 0.6 fusion
  (89 shorter events, 0.5 us)
Async XLA Ops:
  7.2 142.3 %all-gather.2.cloned.1.call-start = ((), (), s32[]{:S(2)}) async-start(), calls=%async_computation | async-start | bytes 1310720 | tf_op jit(solution)/shard_map/all_gather | solution.py:587
  9.0 16.3 %collective-permute-start.2 = (bf16[528,256]{1,0:T(8,128)(2,1)}, bf16[528,256]{1,0:T(8,128)(2,1)S(1)}, u32[]{:S(2)}, u32[]{:S(2)}) collective-permute-start(bf16[528,256]{1,0:T(8,128)(2,1)} %get-tuple-element.24.refs_2_), channel_id=1, source_target_pairs={{0,12},{4,0},{8,4},{12,8},{1,13},{5,1},{9,5},{13,9},{2,14},{6,2},{... | collective-permute-start | bytes 811016 | tf_op jit(solution)/shard_map/ppermute | solution.py:585
  14.0 23.2 %collective-permute-start.1 = (bf16[528,256]{1,0:T(8,128)(2,1)}, bf16[528,256]{1,0:T(8,128)(2,1)S(1)}, u32[]{:S(2)}, u32[]{:S(2)}) collective-permute-start(bf16[528,256]{1,0:T(8,128)(2,1)} %get-tuple-element.24.refs_2_), channel_id=1, source_target_pairs={{0,8},{4,12},{8,0},{12,4},{1,9},{5,13},{9,1},{13,5},{2,10},{6,14},... | collective-permute-start | bytes 811016 | tf_op jit(solution)/shard_map/ppermute | solution.py:585
  14.0 23.2 %collective-permute-start = (bf16[528,256]{1,0:T(8,128)(2,1)}, bf16[528,256]{1,0:T(8,128)(2,1)S(1)}, u32[]{:S(2)}, u32[]{:S(2)}) collective-permute-start(bf16[528,256]{1,0:T(8,128)(2,1)} %get-tuple-element.24.refs_2_), channel_id=1, source_target_pairs={{0,4},{4,8},{8,12},{12,0},{1,5},{5,9},{9,13},{13,1},{2,6},{6,10},{... | collective-permute-start | bytes 811016 | tf_op jit(solution)/shard_map/ppermute | solution.py:585
  15.0 2.8 %copy-start = (bf16[128,16,1536]{2,1,0:T(8,128)(2,1)S(1)}, bf16[128,16,1536]{2,1,0:T(8,128)(2,1)}, u32[]{:S(2)}) copy-start(bf16[128,16,1536]{2,1,0:T(8,128)(2,1)} %param.10) | copy-start | bytes 18874372
  17.8 1.4 copy-start.9
  19.2 0.7 copy-start.26
  25.3 19.1 %copy-start.17 = (bf16[528,256]{1,0:T(8,128)(2,1)}, bf16[528,256]{1,0:T(8,128)(2,1)S(1)}, u32[]{:S(2)}) copy-start(bf16[528,256]{1,0:T(8,128)(2,1)S(1)} %collective-permute-done.2.refs_3_.refs_5_) | copy-start | bytes 811012
  37.2 7.1 %copy-start.19 = (bf16[528,256]{1,0:T(8,128)(2,1)}, bf16[528,256]{1,0:T(8,128)(2,1)S(1)}, u32[]{:S(2)}) copy-start(bf16[528,256]{1,0:T(8,128)(2,1)S(1)} %collective-permute-done.1.refs_2_.refs_4_) | copy-start | bytes 811012
  37.2 7.1 %copy-start.21 = (bf16[528,256]{1,0:T(8,128)(2,1)}, bf16[528,256]{1,0:T(8,128)(2,1)S(1)}, u32[]{:S(2)}) copy-start(bf16[528,256]{1,0:T(8,128)(2,1)S(1)} %collective-permute-done.refs_1_.refs_3_) | copy-start | bytes 811012
  37.2 7.1 %copy-start.24 = (bf16[528,256]{1,0:T(8,128)(2,1)S(1)}, bf16[528,256]{1,0:T(8,128)(2,1)}, u32[]{:S(2)}) copy-start(bf16[528,256]{1,0:T(8,128)(2,1)} %get-tuple-element.24.refs_2_) | copy-start | bytes 811012
  37.2 7.1 %copy-start.27 = (bf16[128,16,256]{2,1,0:T(8,128)(2,1)S(1)}, bf16[128,16,256]{2,1,0:T(8,128)(2,1)}, u32[]{:S(2)}) copy-start(bf16[128,16,256]{2,1,0:T(8,128)(2,1)} %param.11) | copy-start | bytes 3145732
  37.3 27.8 %collective-permute-start.6 = (bf16[256,1536]{1,0:T(8,128)(2,1)S(1)}, bf16[256,1536]{1,0:T(8,128)(2,1)}, u32[]{:S(2)}, u32[]{:S(2)}) collective-permute-start(bf16[256,1536]{1,0:T(8,128)(2,1)S(1)} %shard_map.104.refs_7_), channel_id=1, source_target_pairs={{0,4},{4,0},{8,12},{12,8},{1,5},{5,1},{9,13},{13,9},{2,6},{6,2},{1... | collective-permute-start | bytes 2359304 | tf_op jit(solution)/shard_map/ppermute | solution.py:592
  38.2 26.8 %collective-permute-start.5 = (bf16[256,1536]{1,0:T(8,128)(2,1)S(1)}, bf16[256,1536]{1,0:T(8,128)(2,1)S(1)}, u32[]{:S(2)}, u32[]{:S(2)}) collective-permute-start(bf16[256,1536]{1,0:T(8,128)(2,1)S(1)} %shard_map.104.refs_7_), channel_id=1, source_target_pairs={{4,8},{8,4},{5,9},{9,5},{6,10},{10,6},{7,11},{11,7},{20,24},{24,20... | collective-permute-start | bytes 2359304 | tf_op jit(solution)/shard_map/ppermute | solution.py:592
  38.9 40.4 %collective-permute-start.10 = (bf16[256,1536]{1,0:T(8,128)(2,1)}, bf16[256,1536]{1,0:T(8,128)(2,1)}, u32[]{:S(2)}, u32[]{:S(2)}) collective-permute-start(bf16[256,1536]{1,0:T(8,128)(2,1)} %shard_map.105.refs_8_), channel_id=1, source_target_pairs={{0,4},{4,0},{8,12},{12,8},{1,5},{5,1},{9,13},{13,9},{2,6},{6,2},{1... | collective-permute-start | bytes 2359304 | tf_op jit(solution)/shard_map/ppermute | solution.py:592
  42.8 36.5 %collective-permute-start.9 = (bf16[256,1536]{1,0:T(8,128)(2,1)}, bf16[256,1536]{1,0:T(8,128)(2,1)}, u32[]{:S(2)}, u32[]{:S(2)}) collective-permute-start(bf16[256,1536]{1,0:T(8,128)(2,1)} %shard_map.105.refs_8_), channel_id=1, source_target_pairs={{4,8},{8,4},{5,9},{9,5},{6,10},{10,6},{7,11},{11,7},{20,24},{24,20... | collective-permute-start | bytes 2359304 | tf_op jit(solution)/shard_map/ppermute | solution.py:592
  44.4 14.8 %slice-start = ((s8[6291456]{0:T(1024)(128)(4,1)}), s8[4194304]{0:T(1024)(128)(4,1)S(1)}, s32[]{:S(2)}) async-start(s8[6291456]{0:T(1024)(128)(4,1)} %bitcast.10), calls=%async_computation.1 | async-start | bytes 8388608
  44.4 14.8 %slice-start.1 = ((s8[6291456]{0:T(1024)(128)(4,1)}), s8[2097152]{0:T(1024)(128)(4,1)S(1)}, s32[]{:S(2)}) async-start(s8[6291456]{0:T(1024)(128)(4,1)} %bitcast.10), calls=%async_computation.2 | async-start | bytes 4194304
  49.0 1.6 collective-permute-start.3
  50.7 8.4 %collective-permute-start.4 = (f32[128,512]{1,0:T(8,128)S(1)}, f32[128,512]{1,0:T(8,128)S(1)}, u32[]{:S(2)}, u32[]{:S(2)}) collective-permute-start(f32[128,512]{1,0:T(8,128)S(1)} %add.21), channel_id=1, source_target_pairs={{0,2},{1,3},{2,0},{3,1},{4,6},{5,7},{6,4},{7,5},{8,10},{9,11},{10,... | collective-permute-start | bytes 786440 | tf_op jit(solution)/shard_map/ppermute | solution.py:577
  65.0 3.5 %copy-start.4 = (bf16[512,1536]{1,0:T(8,128)(2,1)}, bf16[512,1536]{1,0:T(8,128)(2,1)S(1)}, u32[]{:S(2)}) copy-start(bf16[512,1536]{1,0:T(8,128)(2,1)S(1)} %shard_map.107.refs_3_.refs_4_.refs_5_) | copy-start | bytes 4718596
  65.0 18.6 %slice-start.2 = ((s8[6291456]{0:T(1024)(128)(4,1)}), s8[2097152]{0:T(1024)(128)(4,1)S(1)}, s32[]{:S(2)}) async-start(s8[6291456]{0:T(1024)(128)(4,1)} %bitcast.14), calls=%async_computation.3 | async-start | bytes 4194304
  68.6 21.5 %collective-permute-start.7 = (bf16[256,1536]{1,0:T(8,128)(2,1)}, bf16[256,1536]{1,0:T(8,128)(2,1)}, u32[]{:S(2)}, u32[]{:S(2)}) collective-permute-start(bf16[256,1536]{1,0:T(8,128)(2,1)} %get-tuple-element.28.refs_4_), channel_id=1, source_target_pairs={{4,8},{8,4},{5,9},{9,5},{6,10},{10,6},{7,11},{11,7},{20,24},{24,20... | collective-permute-start | bytes 2359304 | tf_op jit(solution)/shard_map/ppermute | solution.py:607
  70.1 20.6 %collective-permute-start.8 = (bf16[256,1536]{1,0:T(8,128)(2,1)S(1)}, bf16[256,1536]{1,0:T(8,128)(2,1)}, u32[]{:S(2)}, u32[]{:S(2)}) collective-permute-start(bf16[256,1536]{1,0:T(8,128)(2,1)S(1)} %get-tuple-element.29.refs_4_.refs_6_.refs_5_), channel_id=1, source_target_pairs={{0,4},{4,0},{8,12},{12,8},{1,5},{5,1},{9,13},{13,9},{2,6},{6,2},{1... | collective-permute-start | bytes 2359304 | tf_op jit(solution)/shard_map/ppermute | solution.py:607
  70.7 2.8 %copy-start.1 = (bf16[128,16,1536]{2,1,0:T(8,128)(2,1)S(1)}, bf16[128,16,1536]{2,1,0:T(8,128)(2,1)}, u32[]{:S(2)}) copy-start(bf16[128,16,1536]{2,1,0:T(8,128)(2,1)} %param.10) | copy-start | bytes 18874372
  73.5 5.8 %copy-start.5 = (bf16[512,1536]{1,0:T(8,128)(2,1)S(1)}, bf16[512,1536]{1,0:T(8,128)(2,1)}, u32[]{:S(2)}) copy-start(bf16[512,1536]{1,0:T(8,128)(2,1)} %copy-done.4) | copy-start | bytes 4718596
  73.5 10.1 %slice-start.3 = ((s8[6291456]{0:T(1024)(128)(4,1)}), s8[4194304]{0:T(1024)(128)(4,1)S(1)}, s32[]{:S(2)}) async-start(s8[6291456]{0:T(1024)(128)(4,1)} %bitcast.14), calls=%async_computation.4 | async-start | bytes 8388608
  82.1 25.6 %collective-permute-start.13 = (bf16[256,1536]{1,0:T(8,128)(2,1)}, bf16[256,1536]{1,0:T(8,128)(2,1)}, u32[]{:S(2)}, u32[]{:S(2)}) collective-permute-start(bf16[256,1536]{1,0:T(8,128)(2,1)} %get-tuple-element.30.refs_5_.refs_6_), channel_id=1, source_target_pairs={{4,8},{8,4},{5,9},{9,5},{6,10},{10,6},{7,11},{11,7},{20,24},{24,20... | collective-permute-start | bytes 2359304 | tf_op jit(solution)/shard_map/ppermute | solution.py:607
  83.6 24.1 %collective-permute-start.14 = (bf16[256,1536]{1,0:T(8,128)(2,1)}, bf16[256,1536]{1,0:T(8,128)(2,1)}, u32[]{:S(2)}, u32[]{:S(2)}) collective-permute-start(bf16[256,1536]{1,0:T(8,128)(2,1)} %get-tuple-element.31.refs_7_.refs_8_), channel_id=1, source_target_pairs={{0,4},{4,0},{8,12},{12,8},{1,5},{5,1},{9,13},{13,9},{2,6},{6,2},{1... | collective-permute-start | bytes 2359304 | tf_op jit(solution)/shard_map/ppermute | solution.py:607
  93.4 45.6 %collective-permute-start.11 = (bf16[256,1536]{1,0:T(8,128)(2,1)}, bf16[256,1536]{1,0:T(8,128)(2,1)}, u32[]{:S(2)}, u32[]{:S(2)}) collective-permute-start(bf16[256,1536]{1,0:T(8,128)(2,1)} %get-tuple-element.32.refs_4_.refs_8_), channel_id=1, source_target_pairs={{4,8},{8,4},{5,9},{9,5},{6,10},{10,6},{7,11},{11,7},{20,24},{24,20... | collective-permute-start | bytes 2359304 | tf_op jit(solution)/shard_map/ppermute | solution.py:607
  94.9 44.0 %collective-permute-start.12 = (bf16[256,1536]{1,0:T(8,128)(2,1)}, bf16[256,1536]{1,0:T(8,128)(2,1)}, u32[]{:S(2)}, u32[]{:S(2)}) collective-permute-start(bf16[256,1536]{1,0:T(8,128)(2,1)} %get-tuple-element.33.refs_4_.refs_6_.refs_9_), channel_id=1, source_target_pairs={{0,4},{4,0},{8,12},{12,8},{1,5},{5,1},{9,13},{13,9},{2,6},{6,2},{1... | collective-permute-start | bytes 2359304 | tf_op jit(solution)/shard_map/ppermute | solution.py:607
  107.7 31.3 %copy-start.14 = (bf16[512,1536]{1,0:T(8,128)(2,1)}, bf16[512,1536]{1,0:T(8,128)(2,1)S(1)}, u32[]{:S(2)}) copy-start(bf16[512,1536]{1,0:T(8,128)(2,1)S(1)} %shard_map.113.refs_5_.refs_4_) | copy-start | bytes 4718596
  110.5 52.7 %collective-permute-start.15 = (bf16[256,1536]{1,0:T(8,128)(2,1)}, bf16[256,1536]{1,0:T(8,128)(2,1)}, u32[]{:S(2)}, u32[]{:S(2)}) collective-permute-start(bf16[256,1536]{1,0:T(8,128)(2,1)} %get-tuple-element.34.refs_5_.refs_10_), channel_id=1, source_target_pairs={{4,8},{8,4},{5,9},{9,5},{6,10},{10,6},{7,11},{11,7},{20,24},{24,20... | collective-permute-start | bytes 2359304 | tf_op jit(solution)/shard_map/ppermute | solution.py:607
  112.1 13.1 %copy-start.10 = (bf16[512,1536]{1,0:T(8,128)(2,1)S(1)}, bf16[512,1536]{1,0:T(8,128)(2,1)}, u32[]{:S(2)}) copy-start(bf16[512,1536]{1,0:T(8,128)(2,1)} %refs_3_.5) | copy-start | bytes 4718596
  112.1 51.1 %collective-permute-start.16 = (bf16[256,1536]{1,0:T(8,128)(2,1)}, bf16[256,1536]{1,0:T(8,128)(2,1)}, u32[]{:S(2)}, u32[]{:S(2)}) collective-permute-start(bf16[256,1536]{1,0:T(8,128)(2,1)} %get-tuple-element.35.refs_7_.refs_8_.refs_11_), channel_id=1, source_target_pairs={{0,4},{4,0},{8,12},{12,8},{1,5},{5,1},{9,13},{13,9},{2,6},{6,2},{1... | collective-permute-start | bytes 2359304 | tf_op jit(solution)/shard_map/ppermute | solution.py:607
  139.0 2.8 %copy-start.7 = (bf16[2048,1536]{1,0:T(8,128)(2,1)S(1)}, bf16[2048,1536]{1,0:T(8,128)(2,1)}, u32[]{:S(2)}) copy-start(bf16[2048,1536]{1,0:T(8,128)(2,1)} %shard_map.116.refs_5_.refs_16_) | copy-start | bytes 18874372
  144.5 34.4 %collective-permute-start.20 = (bf16[256,1536]{1,0:T(8,128)(2,1)}, bf16[256,1536]{1,0:T(8,128)(2,1)S(1)}, u32[]{:S(2)}, u32[]{:S(2)}) collective-permute-start(bf16[256,1536]{1,0:T(8,128)(2,1)} %get-tuple-element.39.refs_4_.refs_12_), channel_id=1, source_target_pairs={{4,8},{8,4},{5,9},{9,5},{6,10},{10,6},{7,11},{11,7},{20,24},{24,20... | collective-permute-start | bytes 2359304 | tf_op jit(solution)/shard_map/ppermute | solution.py:607
  145.2 33.6 %collective-permute-start.19 = (bf16[256,1536]{1,0:T(8,128)(2,1)}, bf16[256,1536]{1,0:T(8,128)(2,1)}, u32[]{:S(2)}, u32[]{:S(2)}) collective-permute-start(bf16[256,1536]{1,0:T(8,128)(2,1)} %get-tuple-element.36.refs_6_.refs_13_), channel_id=1, source_target_pairs={{0,4},{4,0},{8,12},{12,8},{1,5},{5,1},{9,13},{13,9},{2,6},{6,2},{1... | collective-permute-start | bytes 2359304 | tf_op jit(solution)/shard_map/ppermute | solution.py:607
  149.4 2.8 %copy-start.2 = (bf16[128,16,1536]{2,1,0:T(8,128)(2,1)S(1)}, bf16[128,16,1536]{2,1,0:T(8,128)(2,1)}, u32[]{:S(2)}) copy-start(bf16[128,16,1536]{2,1,0:T(8,128)(2,1)} %param.10) | copy-start | bytes 18874372
  152.2 1.9 copy-start.16
  154.1 1.2 copy-start.23
  155.4 7.8 %copy-start.6 = (bf16[512,1536]{1,0:T(8,128)(2,1)S(1)}, bf16[512,1536]{1,0:T(8,128)(2,1)}, u32[]{:S(2)}) copy-start(bf16[512,1536]{1,0:T(8,128)(2,1)} %copy-done.4) | copy-start | bytes 4718596
  155.4 7.8 %copy-start.15 = (bf16[512,1536]{1,0:T(8,128)(2,1)S(1)}, bf16[512,1536]{1,0:T(8,128)(2,1)}, u32[]{:S(2)}) copy-start(bf16[512,1536]{1,0:T(8,128)(2,1)} %copy-done.14) | copy-start | bytes 4718596
  165.9 25.8 %collective-permute-start.17 = (bf16[256,1536]{1,0:T(8,128)(2,1)}, bf16[256,1536]{1,0:T(8,128)(2,1)S(1)}, u32[]{:S(2)}, u32[]{:S(2)}) collective-permute-start(bf16[256,1536]{1,0:T(8,128)(2,1)} %get-tuple-element.37.refs_7_.refs_8_.refs_15_), channel_id=1, source_target_pairs={{0,4},{4,0},{8,12},{12,8},{1,5},{5,1},{9,13},{13,9},{2,6},{6,2},{1... | collective-permute-start | bytes 2359304 | tf_op jit(solution)/shard_map/ppermute | solution.py:607
  168.5 23.3 %collective-permute-start.18 = (bf16[256,1536]{1,0:T(8,128)(2,1)}, bf16[256,1536]{1,0:T(8,128)(2,1)S(1)}, u32[]{:S(2)}, u32[]{:S(2)}) collective-permute-start(bf16[256,1536]{1,0:T(8,128)(2,1)} %get-tuple-element.38.refs_5_.refs_14_), channel_id=1, source_target_pairs={{4,8},{8,4},{5,9},{9,5},{6,10},{10,6},{7,11},{11,7},{20,24},{24,20... | collective-permute-start | bytes 2359304 | tf_op jit(solution)/shard_map/ppermute | solution.py:607
  169.4 2.8 %copy-start.3 = (bf16[128,16,1536]{2,1,0:T(8,128)(2,1)S(1)}, bf16[128,16,1536]{2,1,0:T(8,128)(2,1)}, u32[]{:S(2)}) copy-start(bf16[128,16,1536]{2,1,0:T(8,128)(2,1)} %param.10) | copy-start | bytes 18874372
  178.8 2.2 copy-start.11
  181.0 1.4 copy-start.12
  191.8 2.8 %copy-start.8 = (bf16[2048,1536]{1,0:T(8,128)(2,1)S(1)}, bf16[2048,1536]{1,0:T(8,128)(2,1)}, u32[]{:S(2)}) copy-start(bf16[2048,1536]{1,0:T(8,128)(2,1)} %shard_map.122.refs_4_) | copy-start | bytes 18874372
  195.6 1.4 copy-start.13
  197.0 13.2 %copy-start.18 = (bf16[528,256]{1,0:T(8,128)(2,1)S(1)}, bf16[528,256]{1,0:T(8,128)(2,1)}, u32[]{:S(2)}) copy-start(bf16[528,256]{1,0:T(8,128)(2,1)} %copy-done.17) | copy-start | bytes 811012
  197.0 13.2 %copy-start.20 = (bf16[528,256]{1,0:T(8,128)(2,1)S(1)}, bf16[528,256]{1,0:T(8,128)(2,1)}, u32[]{:S(2)}) copy-start(bf16[528,256]{1,0:T(8,128)(2,1)} %copy-done.19) | copy-start | bytes 811012
  197.0 13.2 %copy-start.22 = (bf16[528,256]{1,0:T(8,128)(2,1)S(1)}, bf16[528,256]{1,0:T(8,128)(2,1)}, u32[]{:S(2)}) copy-start(bf16[528,256]{1,0:T(8,128)(2,1)} %copy-done.21) | copy-start | bytes 811012
  197.0 13.2 %copy-start.25 = (bf16[528,256]{1,0:T(8,128)(2,1)S(1)}, bf16[528,256]{1,0:T(8,128)(2,1)}, u32[]{:S(2)}) copy-start(bf16[528,256]{1,0:T(8,128)(2,1)} %get-tuple-element.24.refs_2_) | copy-start | bytes 811012
  197.1 1.6 collective-permute-start.21
  198.7 8.4 %collective-permute-start.22 = (f32[128,512]{1,0:T(8,128)S(1)}, f32[128,512]{1,0:T(8,128)S(1)}, u32[]{:S(2)}, u32[]{:S(2)}) collective-permute-start(f32[128,512]{1,0:T(8,128)S(1)} %add.23), channel_id=1, source_target_pairs={{0,2},{1,3},{2,0},{3,1},{4,6},{5,7},{6,4},{7,5},{8,10},{9,11},{10,... | collective-permute-start | bytes 786440 | tf_op jit(solution)/shard_map/ppermute | solution.py:577
  207.2 8.5 %collective-permute-start.23 = (bf16[2,512]{1,0:T(2,128)(2,1)S(1)}, bf16[2,512]{1,0:T(2,128)(2,1)S(1)}, u32[]{:S(2)}, u32[]{:S(2)}) collective-permute-start(bf16[2,512]{1,0:T(2,128)(2,1)S(1)} %get-tuple-element.41), channel_id=1, source_target_pairs={{0,12},{4,0},{8,4},{12,8},{1,13},{5,1},{9,5},{13,9},{2,14},{6,2},{... | collective-permute-start | bytes 6152 | tf_op jit(solution)/shard_map/ppermute | solution.py:632
  209.6 6.1 %collective-permute-start.24 = (bf16[2,512]{1,0:T(2,128)(2,1)S(1)}, bf16[2,512]{1,0:T(2,128)(2,1)S(1)}, u32[]{:S(2)}, u32[]{:S(2)}) collective-permute-start(bf16[2,512]{1,0:T(2,128)(2,1)S(1)} %get-tuple-element.42), channel_id=1, source_target_pairs={{0,8},{4,12},{8,0},{12,4},{1,9},{5,13},{9,1},{13,5},{2,10},{6,14},... | collective-permute-start | bytes 6152 | tf_op jit(solution)/shard_map/ppermute | solution.py:632
  209.6 6.1 %collective-permute-start.25 = (bf16[2,512]{1,0:T(2,128)(2,1)S(1)}, bf16[2,512]{1,0:T(2,128)(2,1)S(1)}, u32[]{:S(2)}, u32[]{:S(2)}) collective-permute-start(bf16[2,512]{1,0:T(2,128)(2,1)S(1)} %get-tuple-element.43), channel_id=1, source_target_pairs={{0,4},{4,8},{8,12},{12,0},{1,5},{5,9},{9,13},{13,1},{2,6},{6,10},{... | collective-permute-start | bytes 6152 | tf_op jit(solution)/shard_map/ppermute | solution.py:632
Sparse Core Ops, SparseCore 0:
  70.8 16.0 all-gather.1

commit v3 on v2

--- a/solution.py
+++ b/solution.py
@@ -16,22 +16,26 @@
 
 
 def call(body, out_shape, *, grid=None, in_specs=None, out_specs=None, scratch=(), prefetch=0,
-         aliases=None, flops=0, moved=0, vmem=28, after=(), cost=COST):
+         aliases=None, flops=0, moved=0, vmem=16, after=(), cost=COST):
     steps = len(grid) if grid else 0
+    several = isinstance(out_shape, (list, tuple))
+    shapes = list(out_shape) if several else [out_shape]
+    specs = list(out_specs) if several else [out_specs]
     taken = prefetch + len(in_specs)
     skipped = len(after)
+    given = taken + skipped + len(shapes)
 
     def ordered(*refs):
-        body(*refs[:taken], *refs[taken + skipped :])
+        body(*refs[:taken], *refs[taken + skipped : given], *refs[given + 1 :])
 
     call_it = pl.pallas_call(
         ordered,
-        out_shape=out_shape,
+        out_shape=shapes + [jax.ShapeDtypeStruct((8, 128), F32)],
         grid_spec=pltpu.PrefetchScalarGridSpec(
             num_scalar_prefetch=prefetch,
             grid=grid or (1,),
             in_specs=list(in_specs) + [ANY] * skipped,
-            out_specs=out_specs,
+            out_specs=specs + [ANY],
             scratch_shapes=list(scratch),
         ),
         input_output_aliases=aliases or {},
@@ -458,7 +462,7 @@
         aliases={3 + len(rows): 0} if more else None,
         flops=2 * places * count * total * width,
         moved=2 * (total * width + places * count * width),
-        vmem=28 if places * count * width <= 1 << 22 else 60,
+        vmem=24 if places * count * width <= 1 << 22 else 60,
         after=after,
     )(pos, part, aux, *rows, *more)
 
@@ -471,7 +475,7 @@
         gate_ref[...] = jnp.concatenate(gates, axis=0).astype(BF)
 
 
-def grad_gates(part_in, part_out, slots, rank):
+def grad_gates(part_in, part_out, slots, rank, after):
     shape = part_in.shape
     return call(
         functools.partial(grad_gates_body, rank),
@@ -479,6 +483,7 @@
         in_specs=[whole(shape)] * 2,
         out_specs=[whole((2, shape[1]))] * slots,
         moved=8 * shape[0] * shape[1],
+        after=after,
     )(part_in, part_out)
 
 
@@ -580,53 +585,55 @@
 
     pos = d.astype(jnp.int32).reshape(1)
 
-    block, aux_own = pack_rows(pos, token_adapter_index.T, gates.T, output_gradient, local)
+    block, aux_own, _ = pack_rows(pos, token_adapter_index.T, gates.T, output_gradient, local)
     blocks = [block] + [
         lax.ppermute(block, "dp", [(i, (i + s) % size) for i in range(size)]) for s in range(1, size)
     ]
     full_out = lax.all_gather(output_gradient, "mp", axis=1, tiled=True)
     low = jnp.zeros((size * 2 * rank, count), F32)
-    low = project_in(pos, size, -1, down, aux_own, low, [inputs], 1, rank)
-
-    sent = [pin(inputs[c * half : (c + 1) * half], blocks[1:]) for c in range(CHUNKS)]
+    low, token = project_in(pos, size, -1, down, aux_own, low, [inputs], 1, rank)
+
+    sent, tokens = zip(*[pin(inputs[c * half : (c + 1) * half], blocks[1:]) for c in range(CHUNKS)])
     got = [[lax.ppermute(sent[c], "dp", p) for p in (pairs_a, pairs_b)] for c in range(CHUNKS)]
 
-    part_out, aux = project_out(pos, up, blocks, count, rank, [low] + sent)
+    part_out, aux, _ = project_out(pos, up, blocks, count, rank, [token, *tokens])
     part_out = exchange(part_out)
-    near = far = adapter_rows(pos, size, 0, part_out, aux, down, rank)
+    near, token = adapter_rows(pos, size, 0, part_out, aux, down, rank)
+    far = near
 
     rows, where = [inputs], [(-1, True, 0)]
     early = result = None
-    last = near
     for j in range(1, size):
         term = far
         for c in range(CHUNKS):
-            to_a, to_b = ring_add(pos, size, j, c * half, got[c][1], got[c][0], near, term, [last])
+            to_a, to_b, token = ring_add(
+                pos, size, j, c * half, got[c][1], got[c][0], near, term, [token]
+            )
             rows += [to_b, to_a]
             where += [(j - 1, True, c * half), (j - 1, False, c * half)]
             got[c] = [lax.ppermute(to_a, "dp", pairs_a), lax.ppermute(to_b, "dp", pairs_b)]
-            last = to_a
             if c == 0:
                 frozen = (full_out, frozen_key_weight) if j == size - 1 else None
-                far = last = adapter_rows(pos, size, j, part_out, aux, down, rank, frozen, [to_a])
+                far, token = adapter_rows(pos, size, j, part_out, aux, down, rank, frozen, [token])
         newest = rows[-2 * CHUNKS :]
-        low = last = project_in(
-            pos, size, j - 1, down, aux, low, newest[0::2] + newest[1::2], CHUNKS, rank, [last]
+        low, token = project_in(
+            pos, size, j - 1, down, aux, low, newest[0::2] + newest[1::2], CHUNKS, rank, [token]
         )
         if j == size - 2:
-            early = last = grad_down(
-                pos, size, part_out, aux, rows, where, 1, size - 1, total, rank, None, [last]
+            early, token = grad_down(
+                pos, size, part_out, aux, rows, where, 1, size - 1, total, rank, None, [token]
             )
 
-    for c in range(CHUNKS):
-        result = last = finish(far, got[c][0], got[c][1], c, result, [last])
-        if c == 0:
-            down_gradient = last = grad_down(
-                pos, size, part_out, aux, rows, where, 0, 1, total, rank, early, [last]
-            )
-    part_in = exchange(pin(low, [result]))
-    gate_rows = grad_gates(part_in, part_out, size, rank)
-    up_gradient = grad_up(part_in, aux, blocks, total, rank, [gate_rows[0]])
+    result, token = finish(far, got[0][0], got[0][1], 0, None, [token])
+    low, _ = pin(low, [token])
+    part_in = exchange(low)
+    down_gradient, token = grad_down(
+        pos, size, part_out, aux, rows, where, 0, 1, total, rank, early, [token]
+    )
+    for c in range(1, CHUNKS):
+        result, token = finish(far, got[c][0], got[c][1], c, result, [token])
+    *gate_rows, token = grad_gates(part_in, part_out, size, rank, [token])
+    up_gradient, _ = grad_up(part_in, aux, blocks, total, rank, [token])
     gate_sum = gate_rows[0].astype(F32)
     for s in range(1, size):
         gate_sum = gate_sum + lax.ppermute(

time: 224 us -> 206 us (0.920)
  local copies, waits for them, and re-layouts: 25.8 us -> 14.7 us
  waiting for transfers between devices: 29.4 us -> 21 us
  starting transfers between devices: 48.2 us -> 50.8 us
    ppermute x4, waiting for transfers between devices: 16.8 us -> 5.36 us  [exchange(): lax.ppermute(part, 'mp', [(i, i ^ bit) for i in range(shares)])]
    unnamed x64 -> x58, local copies, waits for them, and re-layouts: 24.8 us -> 13.7 us
    ppermute x6, waiting for transfers between devices: 0.67 us -> 3.7 us  [per_device(): lax.ppermute(to_a, 'dp', pairs_a)]
  transfers between devices with their start and end apart: 27 -> 27, of which waited for: 6 -> 6; matrix products, arithmetic and copies ran while one was open for 0% -> 1% of each run, Pallas kernels for 45% -> 50%
where the time goes in v3:
time: 206 us
  Pallas kernels  104 us (50%)
  starting transfers between devices  50.8 us (25%)
  waiting for transfers between devices  21 us (10%)
  local copies, waits for them, and re-layouts  14.7 us (7%)
  between operations  14.6 us (7%)
    pallas_call x25, Pallas kernels, call(): return lambda *arrays: call_it(*arrays, *after)  104 us
    ppermute x6, starting transfers between devices, per_device(): lax.ppermute(to_a, 'dp', pairs_a)  22.5 us
    unnamed x58, local copies, waits for them, and re-layouts  13.7 us
    ppermute x3, waiting for transfers between devices, per_device(): lax.ppermute(block, 'dp', [(i, (i + s) % size) for i in range(size)])  11.9 us
    ppermute x6, starting transfers between devices, per_device(): lax.ppermute(to_b, 'dp', pairs_b)  8.83 us
    ppermute x4, starting transfers between devices, per_device(): lax.ppermute(sent[c], 'dp', p)  7.06 us
    ppermute x3, starting transfers between devices, per_device(): lax.ppermute(block, 'dp', [(i, (i + s) % size) for i in range(size)])  6.06 us
    ppermute x4, waiting for transfers between devices, exchange(): lax.ppermute(part, 'mp', [(i, i ^ bit) for i in range(shares)])  5.36 us
  transfers between devices with their start and end apart: 27, of which 6 were waited for; matrix products, arithmetic and copies ran while one was open for 1% of the time, Pallas kernels for 50%

profile of v3, /device:TPU:0, one launch (start us, length us, event | category | flops | bytes accessed | tf_op | source)
XLA Modules:
  0.0 205.5 jit_solution(10635201260711424105)
XLA Ops:
  7.2 0.0 all-gather.2.cloned.1.call-start
  7.2 1.7 shard_map.102
  8.9 5.0 %collective-permute-start.2 = (bf16[528,256]{1,0:T(8,128)(2,1)}, bf16[528,256]{1,0:T(8,128)(2,1)S(1)}, u32[]{:S(2)}, u32[]{:S(2)}) collective-permute-start(bf16[528,256]{1,0:T(8,128)(2,1)} %get-tuple-element.61.refs_2_), channel_id=1, source_target_pairs={{0,12},{4,0},{8,4},{12,8},{1,13},{5,1},{9,5},{13,9},{2,14},{6,2},{... | collective-permute-start | bytes 811016 | tf_op jit(solution)/shard_map/ppermute | solution.py:590
  14.0 1.0 collective-permute-start
  15.0 2.8 %copy-done = bf16[128,16,1536]{2,1,0:T(8,128)(2,1)S(1)} copy-done((bf16[128,16,1536]{2,1,0:T(8,128)(2,1)S(1)}, bf16[128,16,1536]{2,1,0:T(8,128)(2,1)}, u32[]{:S(2)}) %copy-start) | copy-done | bytes 6291480
  17.8 1.4 copy-done.6
  19.2 0.7 copy-done.21
  19.9 4.3 %shard_map.103 = (f32[128,512]{1,0:T(8,128)S(1)}, f32[8,128]{1,0:T(8,128)S(1)}) custom-call(s32[1]{0:T(128)} %bitcast.refs_0_, bf16[2048,1536]{1,0:T(8,128)(2,1)S(1)} %bitcast.9, f32[8,512]{1,0:T(8,128)S(1)} %copy-done.21, f32[128,512]{1,0:T(8,128)S(1)} %broadcast_in_dim.3.refs_3_, bf16[512,1536]{1,0:T(8,128)(2,1)S(1)} %copy-done.6), custom_call_target="tpu_custom_call", output_to_operand_aliasing={{0}: (3, {})} | custom-call | flops 64424508 | bytes 157286 | tf_op jit(solution)/shard_map/pallas_call | solution.py:49
  24.3 1.0 fusion.1
  25.3 11.9 %collective-permute-done.1.refs_2_.refs_4_ = bf16[528,256]{1,0:T(8,128)(2,1)S(1)} collective-permute-done((bf16[528,256]{1,0:T(8,128)(2,1)}, bf16[528,256]{1,0:T(8,128)(2,1)S(1)}, u32[]{:S(2)}, u32[]{:S(2)}) %collective-permute-start.1) | collective-permute-done | bytes 270368 | tf_op jit(solution)/shard_map/ppermute | solution.py:590
  37.2 1.0 collective-permute-start.6
  38.2 1.5 collective-permute-start.5
  39.8 4.6 %shard_map.106 = (f32[128,512]{1,0:T(8,128)S(1)}, f32[32,512]{1,0:T(8,128)S(1)}, f32[8,128]{1,0:T(8,128)}) custom-call(s32[1]{0:T(128)} %bitcast.refs_0_, bf16[2048,256]{1,0:T(8,128)(2,1)S(1)} %bitcast.23, bf16[528,256]{1,0:T(8,128)(2,1)S(1)} %copy-done.19, bf16[528,256]{1,0:T(8,128)(2,1)S(1)} %collective-permute-done.refs_1_.refs_3_, ...), custom_call_target="tpu_custom_call" | custom-call | flops 10737418240 | bytes 10485760 | tf_op jit(solution)/shard_map/pallas_call | solution.py:49
  44.4 0.1 collective-permute-start.3
  44.5 1.5 collective-permute-done.3
  46.1 1.6 collective-permute-start.4
  47.6 3.0 %collective-permute-start.10 = (bf16[256,1536]{1,0:T(8,128)(2,1)}, bf16[256,1536]{1,0:T(8,128)(2,1)}, u32[]{:S(2)}, u32[]{:S(2)}) collective-permute-start(bf16[256,1536]{1,0:T(8,128)(2,1)} %get-tuple-element.76), channel_id=1, source_target_pairs={{0,4},{4,0},{8,12},{12,8},{1,5},{5,1},{9,13},{13,9},{2,6},{6,2},{1... | collective-permute-start | bytes 2359304 | tf_op jit(solution)/shard_map/ppermute | solution.py:597
  50.6 1.6 collective-permute-start.9
  52.2 2.3 %collective-permute-done.4 = f32[128,512]{1,0:T(8,128)S(1)} collective-permute-done((f32[128,512]{1,0:T(8,128)S(1)}, f32[128,512]{1,0:T(8,128)S(1)}, u32[]{:S(2)}, u32[]{:S(2)}) %collective-permute-start.4) | collective-permute-done | bytes 262176 | tf_op jit(solution)/shard_map/ppermute | solution.py:582
  54.6 5.8 %shard_map.107 = (bf16[512,1536]{1,0:T(8,128)(2,1)S(1)}, f32[8,128]{1,0:T(8,128)S(1)}) custom-call(s32[1]{0:T(128)} %bitcast.refs_0_, f32[128,512]{1,0:T(8,128)S(1)} %add.22.refs_1_, f32[32,512]{1,0:T(8,128)S(1)} %get-tuple-element.67.refs_2_.refs_1_, bf16[2048,1536]{1,0:T(8,128)(2,1)S(1)} %bitcast.12), custom_call_target="tpu_custom_call" | custom-call | flops 64424508 | bytes 157286 | tf_op jit(solution)/shard_map/pallas_call | solution.py:49
  60.4 0.0 slice-start.2
  60.4 2.8 %shard_map.108 = (bf16[256,1536]{1,0:T(8,128)(2,1)}, bf16[256,1536]{1,0:T(8,128)(2,1)S(1)}, f32[8,128]{1,0:T(8,128)S(1)}) custom-call(s32[1]{0:T(128)} %bitcast.refs_0_, bf16[256,1536]{1,0:T(8,128)(2,1)} %collective-permute-done.5.refs_1_, bf16[256,1536]{1,0:T(8,128)(2,1)S(1)} %collective-permute-done.6.refs_2_, ...), custom_call_target="tpu_custom_call", output_to_operand_aliasing={{0}: (1, {}), {1}: (2, {})} | custom-call | flops 15728 | bytes 47185 | tf_op jit(solution)/shard_map/pallas_call | solution.py:49
  63.2 1.6 collective-permute-start.7
  64.8 2.4 %collective-permute-start.8 = (bf16[256,1536]{1,0:T(8,128)(2,1)}, bf16[256,1536]{1,0:T(8,128)(2,1)}, u32[]{:S(2)}, u32[]{:S(2)}) collective-permute-start(bf16[256,1536]{1,0:T(8,128)(2,1)} %get-tuple-element.72.refs_6_.refs_5_), channel_id=1, source_target_pairs={{0,4},{4,0},{8,12},{12,8},{1,5},{5,1},{9,13},{13,9},{2,6},{6,2},{1... | collective-permute-start | bytes 2359304 | tf_op jit(solution)/shard_map/ppermute | solution.py:614
  67.2 0.0 all-gather.2.cloned.1.call-update
  67.2 2.8 %copy-done.1 = bf16[128,16,1536]{2,1,0:T(8,128)(2,1)S(1)} copy-done((bf16[128,16,1536]{2,1,0:T(8,128)(2,1)S(1)}, bf16[128,16,1536]{2,1,0:T(8,128)(2,1)}, u32[]{:S(2)}) %copy-start.1) | copy-done | bytes 6291480
  70.0 5.8 %shard_map.109 = (bf16[512,1536]{1,0:T(8,128)(2,1)S(1)}, f32[8,128]{1,0:T(8,128)S(1)}) custom-call(s32[1]{0:T(128)} %bitcast.refs_0_, f32[128,512]{1,0:T(8,128)S(1)} %add.22.refs_1_, f32[32,512]{1,0:T(8,128)S(1)} %get-tuple-element.67.refs_2_.refs_1_, bf16[2048,1536]{1,0:T(8,128)(2,1)S(1)} %bitcast.13, f32[8,128]{1,0:T(8,128)S(1)} %get-tuple-element.73.refs_4_), custom_call_target="tpu_custom_call" | custom-call | flops 64424508 | bytes 157286 | tf_op jit(solution)/shard_map/pallas_call | solution.py:49
  75.8 2.7 %shard_map.110 = (bf16[256,1536]{1,0:T(8,128)(2,1)}, bf16[256,1536]{1,0:T(8,128)(2,1)}, f32[8,128]{1,0:T(8,128)S(1)}) custom-call(s32[1]{0:T(128)} %bitcast.refs_0_, bf16[256,1536]{1,0:T(8,128)(2,1)} %collective-permute-done.9.refs_1_, bf16[256,1536]{1,0:T(8,128)(2,1)} %collective-permute-done.10.refs_2_, ...), custom_call_target="tpu_custom_call", output_to_operand_aliasing={{0}: (1, {}), {1}: (2, {})} | custom-call | flops 15728 | bytes 47185 | tf_op jit(solution)/shard_map/pallas_call | solution.py:49
  78.6 1.6 collective-permute-start.13
  80.2 2.1 %collective-permute-start.14 = (bf16[256,1536]{1,0:T(8,128)(2,1)}, bf16[256,1536]{1,0:T(8,128)(2,1)}, u32[]{:S(2)}, u32[]{:S(2)}) collective-permute-start(bf16[256,1536]{1,0:T(8,128)(2,1)} %get-tuple-element.79.refs_7_), channel_id=1, source_target_pairs={{0,4},{4,0},{8,12},{12,8},{1,5},{5,1},{9,13},{13,9},{2,6},{6,2},{1... | collective-permute-start | bytes 2359304 | tf_op jit(solution)/shard_map/ppermute | solution.py:614
  82.3 6.4 %shard_map.111 = (f32[128,512]{1,0:T(8,128)S(1)}, f32[8,128]{1,0:T(8,128)S(1)}) custom-call(s32[1]{0:T(128)} %bitcast.refs_0_, bf16[2048,1536]{1,0:T(8,128)(2,1)S(1)} %bitcast.16, f32[32,512]{1,0:T(8,128)S(1)} %get-tuple-element.67.refs_2_.refs_1_, f32[128,512]{1,0:T(8,128)S(1)} %get-tuple-element.75.refs_3_, ...), custom_call_target="tpu_custom_call", output_to_operand_aliasing={{0}: (3, {})} | custom-call | flops 64424508 | bytes 157286 | tf_op jit(solution)/shard_map/pallas_call | solution.py:49
  88.7 2.9 %collective-permute-done.8.refs_2_ = bf16[256,1536]{1,0:T(8,128)(2,1)} collective-permute-done((bf16[256,1536]{1,0:T(8,128)(2,1)}, bf16[256,1536]{1,0:T(8,128)(2,1)}, u32[]{:S(2)}, u32[]{:S(2)}) %collective-permute-start.8) | collective-permute-done | bytes 786464 | tf_op jit(solution)/shard_map/ppermute | solution.py:614
  91.6 2.7 %shard_map.112 = (bf16[256,1536]{1,0:T(8,128)(2,1)}, bf16[256,1536]{1,0:T(8,128)(2,1)}, f32[8,128]{1,0:T(8,128)S(1)}) custom-call(s32[1]{0:T(128)} %bitcast.refs_0_, bf16[256,1536]{1,0:T(8,128)(2,1)} %collective-permute-done.7.refs_1_, bf16[256,1536]{1,0:T(8,128)(2,1)} %collective-permute-done.8.refs_2_, ...), custom_call_target="tpu_custom_call", output_to_operand_aliasing={{0}: (1, {}), {1}: (2, {})} | custom-call | flops 15728 | bytes 47185 | tf_op jit(solution)/shard_map/pallas_call | solution.py:49
  94.3 1.6 collective-permute-start.11
  95.8 6.0 %collective-permute-start.12 = (bf16[256,1536]{1,0:T(8,128)(2,1)}, bf16[256,1536]{1,0:T(8,128)(2,1)}, u32[]{:S(2)}, u32[]{:S(2)}) collective-permute-start(bf16[256,1536]{1,0:T(8,128)(2,1)} %get-tuple-element.83.refs_6_.refs_9_), channel_id=1, source_target_pairs={{0,4},{4,0},{8,12},{12,8},{1,5},{5,1},{9,13},{13,9},{2,6},{6,2},{1... | collective-permute-start | bytes 2359304 | tf_op jit(solution)/shard_map/ppermute | solution.py:614
  101.8 5.8 %shard_map.113 = (bf16[512,1536]{1,0:T(8,128)(2,1)S(1)}, f32[8,128]{1,0:T(8,128)S(1)}) custom-call(s32[1]{0:T(128)} %bitcast.refs_0_, f32[128,512]{1,0:T(8,128)S(1)} %add.22.refs_1_, f32[32,512]{1,0:T(8,128)S(1)} %get-tuple-element.67.refs_2_.refs_1_, bf16[2048,1536]{1,0:T(8,128)(2,1)S(1)} %bitcast.17, f32[8,128]{1,0:T(8,128)S(1)} %get-tuple-element.84.refs_4_), custom_call_target="tpu_custom_call" | custom-call | flops 64424508 | bytes 157286 | tf_op jit(solution)/shard_map/pallas_call | solution.py:49
  107.6 0.8 collective-permute-done.14.refs_2_
  108.5 2.7 %shard_map.114 = (bf16[256,1536]{1,0:T(8,128)(2,1)}, bf16[256,1536]{1,0:T(8,128)(2,1)}, f32[8,128]{1,0:T(8,128)S(1)}) custom-call(s32[1]{0:T(128)} %bitcast.refs_0_, bf16[256,1536]{1,0:T(8,128)(2,1)} %collective-permute-done.13.refs_1_, bf16[256,1536]{1,0:T(8,128)(2,1)} %collective-permute-done.14.refs_2_, ...), custom_call_target="tpu_custom_call", output_to_operand_aliasing={{0}: (1, {}), {1}: (2, {})} | custom-call | flops 15728 | bytes 47185 | tf_op jit(solution)/shard_map/pallas_call | solution.py:49
  111.1 1.6 collective-permute-start.15
  112.7 5.8 %collective-permute-start.16 = (bf16[256,1536]{1,0:T(8,128)(2,1)}, bf16[256,1536]{1,0:T(8,128)(2,1)}, u32[]{:S(2)}, u32[]{:S(2)}) collective-permute-start(bf16[256,1536]{1,0:T(8,128)(2,1)} %get-tuple-element.88.refs_7_.refs_11_), channel_id=1, source_target_pairs={{0,4},{4,0},{8,12},{12,8},{1,5},{5,1},{9,13},{13,9},{2,6},{6,2},{1... | collective-permute-start | bytes 2359304 | tf_op jit(solution)/shard_map/ppermute | solution.py:614
  118.5 6.7 %shard_map.115 = (f32[128,512]{1,0:T(8,128)S(1)}, f32[8,128]{1,0:T(8,128)S(1)}) custom-call(s32[1]{0:T(128)} %bitcast.refs_0_, bf16[2048,1536]{1,0:T(8,128)(2,1)S(1)} %bitcast.18, f32[32,512]{1,0:T(8,128)S(1)} %get-tuple-element.67.refs_2_.refs_1_, f32[128,512]{1,0:T(8,128)S(1)} %get-tuple-element.89.refs_3_, ...), custom_call_target="tpu_custom_call", output_to_operand_aliasing={{0}: (3, {})} | custom-call | flops 64424508 | bytes 157286 | tf_op jit(solution)/shard_map/pallas_call | solution.py:49
  125.2 13.6 %shard_map.116 = (bf16[2048,1536]{1,0:T(8,128)(2,1)}, f32[8,128]{1,0:T(8,128)S(1)}) custom-call(s32[1]{0:T(128)} %bitcast.refs_0_, f32[128,512]{1,0:T(8,128)S(1)} %add.22.refs_1_, f32[32,512]{1,0:T(8,128)S(1)} %get-tuple-element.67.refs_2_.refs_1_, bf16[512,1536]{1,0:T(8,128)(2,1)S(1)} %copy-done.7, bf16[256,1536]{1,0:T(8,128)(2,1)S(1)} %get-tuple-element.71.refs_4_, ...), custom_call_target="tpu_custom_call" | custom-call | flops 193273536 | bytes 220200 | tf_op jit(solution)/shard_map/pallas_call | solution.py:49
  138.9 0.0 slice-start.4
  138.9 2.8 %shard_map.117 = (bf16[256,1536]{1,0:T(8,128)(2,1)}, bf16[256,1536]{1,0:T(8,128)(2,1)}, f32[8,128]{1,0:T(8,128)S(1)}) custom-call(s32[1]{0:T(128)} %bitcast.refs_0_, bf16[256,1536]{1,0:T(8,128)(2,1)} %collective-permute-done.11.refs_1_, bf16[256,1536]{1,0:T(8,128)(2,1)} %collective-permute-done.12.refs_2_, ...), custom_call_target="tpu_custom_call", output_to_operand_aliasing={{0}: (1, {}), {1}: (2, {})} | custom-call | flops 15728 | bytes 47185 | tf_op jit(solution)/shard_map/pallas_call | solution.py:49
  141.7 2.8 %collective-permute-start.19 = (bf16[256,1536]{1,0:T(8,128)(2,1)}, bf16[256,1536]{1,0:T(8,128)(2,1)}, u32[]{:S(2)}, u32[]{:S(2)}) collective-permute-start(bf16[256,1536]{1,0:T(8,128)(2,1)} %get-tuple-element.98.refs_6_.refs_13_), channel_id=1, source_target_pairs={{0,4},{4,0},{8,12},{12,8},{1,5},{5,1},{9,13},{13,9},{2,6},{6,2},{1... | collective-permute-start | bytes 2359304 | tf_op jit(solution)/shard_map/ppermute | solution.py:614
  144.4 1.6 collective-permute-start.20
  146.0 2.8 %copy-done.2 = bf16[128,16,1536]{2,1,0:T(8,128)(2,1)S(1)} copy-done((bf16[128,16,1536]{2,1,0:T(8,128)(2,1)S(1)}, bf16[128,16,1536]{2,1,0:T(8,128)(2,1)}, u32[]{:S(2)}) %copy-start.2) | copy-done | bytes 6291480
  148.8 1.9 copy-done.11
  150.7 1.2 copy-done.18
  151.9 7.7 %shard_map.118 = (f32[512,1536]{1,0:T(8,128)S(1)}, f32[8,128]{1,0:T(8,128)S(1)}) custom-call(s32[1]{0:T(128)} %bitcast.refs_0_, f32[128,512]{1,0:T(8,128)S(1)} %add.22.refs_1_, f32[32,512]{1,0:T(8,128)S(1)} %get-tuple-element.67.refs_2_.refs_1_, bf16[2048,1536]{1,0:T(8,128)(2,1)S(1)} %bitcast.19, bf16[512,1024]{1,0:T(8,128)(2,1)S(1)} %copy-done.18, ...), custom_call_target="tpu_custom_call" | custom-call | flops 64424508 | bytes 157286 | tf_op jit(solution)/shard_map/pallas_call | solution.py:49
  159.7 2.7 %shard_map.119 = (bf16[256,1536]{1,0:T(8,128)(2,1)}, bf16[256,1536]{1,0:T(8,128)(2,1)}, f32[8,128]{1,0:T(8,128)S(1)}) custom-call(s32[1]{0:T(128)} %bitcast.refs_0_, bf16[256,1536]{1,0:T(8,128)(2,1)} %collective-permute-done.15.refs_1_, bf16[256,1536]{1,0:T(8,128)(2,1)} %collective-permute-done.16.refs_2_, ...), custom_call_target="tpu_custom_call", output_to_operand_aliasing={{0}: (1, {}), {1}: (2, {})} | custom-call | flops 15728 | bytes 47185 | tf_op jit(solution)/shard_map/pallas_call | solution.py:49
  162.4 3.5 %collective-permute-start.17 = (bf16[256,1536]{1,0:T(8,128)(2,1)}, bf16[256,1536]{1,0:T(8,128)(2,1)S(1)}, u32[]{:S(2)}, u32[]{:S(2)}) collective-permute-start(bf16[256,1536]{1,0:T(8,128)(2,1)} %get-tuple-element.96.refs_7_.refs_15_), channel_id=1, source_target_pairs={{0,4},{4,0},{8,12},{12,8},{1,5},{5,1},{9,13},{13,9},{2,6},{6,2},{1... | collective-permute-start | bytes 2359304 | tf_op jit(solution)/shard_map/ppermute | solution.py:614
  165.9 0.9 collective-permute-start.18
  166.9 6.6 %shard_map.120 = (f32[128,512]{1,0:T(8,128)S(1)}, f32[8,128]{1,0:T(8,128)S(1)}) custom-call(s32[1]{0:T(128)} %bitcast.refs_0_, bf16[2048,1536]{1,0:T(8,128)(2,1)S(1)} %bitcast.22, f32[32,512]{1,0:T(8,128)S(1)} %get-tuple-element.67.refs_2_.refs_1_, f32[128,512]{1,0:T(8,128)S(1)} %get-tuple-element.100.refs_3_, ...), custom_call_target="tpu_custom_call", output_to_operand_aliasing={{0}: (3, {})} | custom-call | flops 64424508 | bytes 157286 | tf_op jit(solution)/shard_map/pallas_call | solution.py:49
  173.5 2.4 %shard_map.121 = (bf16[512,1536]{1,0:T(8,128)(2,1)}, f32[8,128]{1,0:T(8,128)S(1)}) custom-call(f32[512,1536]{1,0:T(8,128)S(1)} %get-tuple-element.94.refs_0_, bf16[256,1536]{1,0:T(8,128)(2,1)} %collective-permute-done.19.refs_1_, bf16[256,1536]{1,0:T(8,128)(2,1)} %collective-permute-done.20.refs_2_, f32[8,128]{1,0:T(8,128)S(1)} %get-tuple-element.102.refs_3_), custom_call_target="tpu_custom_call" | custom-call | flops 15728 | bytes 78643 | tf_op jit(solution)/shard_map/pallas_call | solution.py:49
  175.9 1.5 collective-permute-done.21
  177.5 1.6 collective-permute-start.22
  179.0 9.3 %shard_map.122 = (bf16[2048,1536]{1,0:T(8,128)(2,1)}, f32[8,128]{1,0:T(8,128)S(1)}) custom-call(s32[1]{0:T(128)} %bitcast.refs_0_, f32[128,512]{1,0:T(8,128)S(1)} %add.22.refs_1_, f32[32,512]{1,0:T(8,128)S(1)} %get-tuple-element.67.refs_2_.refs_1_, bf16[512,1536]{1,0:T(8,128)(2,1)S(1)} %copy-done.8, ...), custom_call_target="tpu_custom_call", output_to_operand_aliasing={{0}: (16, {})} | custom-call | flops 64424508 | bytes 157286 | tf_op jit(solution)/shard_map/pallas_call | solution.py:49
  188.4 1.1 shard_map.123
  189.5 0.1 shard_map.125
  189.6 2.4 %collective-permute-start.23 = (bf16[2,512]{1,0:T(2,128)(2,1)S(1)}, bf16[2,512]{1,0:T(2,128)(2,1)S(1)}, u32[]{:S(2)}, u32[]{:S(2)}) collective-permute-start(bf16[2,512]{1,0:T(2,128)(2,1)S(1)} %get-tuple-element.112), channel_id=1, source_target_pairs={{0,12},{4,0},{8,4},{12,8},{1,13},{5,1},{9,5},{13,9},{2,14},{6,2},{... | collective-permute-start | bytes 6152 | tf_op jit(solution)/shard_map/ppermute | solution.py:639
  192.0 0.6 collective-permute-start.25
  192.7 5.4 %shard_map.126 = (bf16[2048,256]{1,0:T(8,128)(2,1)}, f32[8,128]{1,0:T(8,128)}) custom-call(f32[128,512]{1,0:T(8,128)S(1)} %add.24.refs_0_, f32[32,512]{1,0:T(8,128)S(1)} %get-tuple-element.67.refs_2_.refs_1_, bf16[528,256]{1,0:T(8,128)(2,1)S(1)} %copy-done.20, bf16[528,256]{1,0:T(8,128)(2,1)S(1)} %copy-done.17, bf16[528,256]{1,0:T(8,128)(2,1)S(1)} %copy-done.15, ...), custom_call_target="tpu_custom_call" | custom-call | flops 42949672 | bytes 41943 | tf_op jit(solution)/shard_map/pallas_call | solution.py:49
  198.1 0.6 fusion
  (84 shorter events, 0.4 us)
Async XLA Ops:
  7.2 138.8 %all-gather.2.cloned.1.call-start = ((), (), s32[]{:S(2)}) async-start(), calls=%async_computation | async-start | bytes 1310720 | tf_op jit(solution)/shard_map/all_gather | solution.py:592
  8.9 16.3 %collective-permute-start.2 = (bf16[528,256]{1,0:T(8,128)(2,1)}, bf16[528,256]{1,0:T(8,128)(2,1)S(1)}, u32[]{:S(2)}, u32[]{:S(2)}) collective-permute-start(bf16[528,256]{1,0:T(8,128)(2,1)} %get-tuple-element.61.refs_2_), channel_id=1, source_target_pairs={{0,12},{4,0},{8,4},{12,8},{1,13},{5,1},{9,5},{13,9},{2,14},{6,2},{... | collective-permute-start | bytes 811016 | tf_op jit(solution)/shard_map/ppermute | solution.py:590
  14.0 23.2 %collective-permute-start.1 = (bf16[528,256]{1,0:T(8,128)(2,1)}, bf16[528,256]{1,0:T(8,128)(2,1)S(1)}, u32[]{:S(2)}, u32[]{:S(2)}) collective-permute-start(bf16[528,256]{1,0:T(8,128)(2,1)} %get-tuple-element.61.refs_2_), channel_id=1, source_target_pairs={{0,8},{4,12},{8,0},{12,4},{1,9},{5,13},{9,1},{13,5},{2,10},{6,14},... | collective-permute-start | bytes 811016 | tf_op jit(solution)/shard_map/ppermute | solution.py:590
  14.0 23.2 %collective-permute-start = (bf16[528,256]{1,0:T(8,128)(2,1)}, bf16[528,256]{1,0:T(8,128)(2,1)S(1)}, u32[]{:S(2)}, u32[]{:S(2)}) collective-permute-start(bf16[528,256]{1,0:T(8,128)(2,1)} %get-tuple-element.61.refs_2_), channel_id=1, source_target_pairs={{0,4},{4,8},{8,12},{12,0},{1,5},{5,9},{9,13},{13,1},{2,6},{6,10},{... | collective-permute-start | bytes 811016 | tf_op jit(solution)/shard_map/ppermute | solution.py:590
  15.0 2.8 %copy-start = (bf16[128,16,1536]{2,1,0:T(8,128)(2,1)S(1)}, bf16[128,16,1536]{2,1,0:T(8,128)(2,1)}, u32[]{:S(2)}) copy-start(bf16[128,16,1536]{2,1,0:T(8,128)(2,1)} %param.10) | copy-start | bytes 18874372
  17.8 1.4 copy-start.6
  19.2 0.7 copy-start.21
  25.3 14.5 %copy-start.12 = (bf16[528,256]{1,0:T(8,128)(2,1)}, bf16[528,256]{1,0:T(8,128)(2,1)S(1)}, u32[]{:S(2)}) copy-start(bf16[528,256]{1,0:T(8,128)(2,1)S(1)} %collective-permute-done.2.refs_3_.refs_5_) | copy-start | bytes 811012
  37.2 2.5 %copy-start.14 = (bf16[528,256]{1,0:T(8,128)(2,1)}, bf16[528,256]{1,0:T(8,128)(2,1)S(1)}, u32[]{:S(2)}) copy-start(bf16[528,256]{1,0:T(8,128)(2,1)S(1)} %collective-permute-done.1.refs_2_.refs_4_) | copy-start | bytes 811012
  37.2 2.5 %copy-start.16 = (bf16[528,256]{1,0:T(8,128)(2,1)}, bf16[528,256]{1,0:T(8,128)(2,1)S(1)}, u32[]{:S(2)}) copy-start(bf16[528,256]{1,0:T(8,128)(2,1)S(1)} %collective-permute-done.refs_1_.refs_3_) | copy-start | bytes 811012
  37.2 2.5 %copy-start.19 = (bf16[528,256]{1,0:T(8,128)(2,1)S(1)}, bf16[528,256]{1,0:T(8,128)(2,1)}, u32[]{:S(2)}) copy-start(bf16[528,256]{1,0:T(8,128)(2,1)} %get-tuple-element.61.refs_2_) | copy-start | bytes 811012
  37.2 2.6 %copy-start.22 = (bf16[128,16,256]{2,1,0:T(8,128)(2,1)S(1)}, bf16[128,16,256]{2,1,0:T(8,128)(2,1)}, u32[]{:S(2)}) copy-start(bf16[128,16,256]{2,1,0:T(8,128)(2,1)} %param.11) | copy-start | bytes 3145732
  37.2 23.2 %collective-permute-start.6 = (bf16[256,1536]{1,0:T(8,128)(2,1)S(1)}, bf16[256,1536]{1,0:T(8,128)(2,1)S(1)}, u32[]{:S(2)}, u32[]{:S(2)}) collective-permute-start(bf16[256,1536]{1,0:T(8,128)(2,1)S(1)} %get-tuple-element.68), channel_id=1, source_target_pairs={{0,4},{4,0},{8,12},{12,8},{1,5},{5,1},{9,13},{13,9},{2,6},{6,2},{1... | collective-permute-start | bytes 2359304 | tf_op jit(solution)/shard_map/ppermute | solution.py:597
  38.2 22.2 %collective-permute-start.5 = (bf16[256,1536]{1,0:T(8,128)(2,1)S(1)}, bf16[256,1536]{1,0:T(8,128)(2,1)}, u32[]{:S(2)}, u32[]{:S(2)}) collective-permute-start(bf16[256,1536]{1,0:T(8,128)(2,1)S(1)} %get-tuple-element.68), channel_id=1, source_target_pairs={{4,8},{8,4},{5,9},{9,5},{6,10},{10,6},{7,11},{11,7},{20,24},{24,20... | collective-permute-start | bytes 2359304 | tf_op jit(solution)/shard_map/ppermute | solution.py:597
  39.7 14.8 %slice-start = ((s8[6291456]{0:T(1024)(128)(4,1)}), s8[4194304]{0:T(1024)(128)(4,1)S(1)}, s32[]{:S(2)}) async-start(s8[6291456]{0:T(1024)(128)(4,1)} %bitcast.10), calls=%async_computation.1 | async-start | bytes 8388608
  39.8 14.8 %slice-start.1 = ((s8[6291456]{0:T(1024)(128)(4,1)}), s8[2097152]{0:T(1024)(128)(4,1)S(1)}, s32[]{:S(2)}) async-start(s8[6291456]{0:T(1024)(128)(4,1)} %bitcast.10), calls=%async_computation.2 | async-start | bytes 4194304
  44.4 1.6 collective-permute-start.3
  46.1 8.4 %collective-permute-start.4 = (f32[128,512]{1,0:T(8,128)S(1)}, f32[128,512]{1,0:T(8,128)S(1)}, u32[]{:S(2)}, u32[]{:S(2)}) collective-permute-start(f32[128,512]{1,0:T(8,128)S(1)} %add.21), channel_id=1, source_target_pairs={{0,2},{1,3},{2,0},{3,1},{4,6},{5,7},{6,4},{7,5},{8,10},{9,11},{10,... | collective-permute-start | bytes 786440 | tf_op jit(solution)/shard_map/ppermute | solution.py:582
  47.6 28.2 %collective-permute-start.10 = (bf16[256,1536]{1,0:T(8,128)(2,1)}, bf16[256,1536]{1,0:T(8,128)(2,1)}, u32[]{:S(2)}, u32[]{:S(2)}) collective-permute-start(bf16[256,1536]{1,0:T(8,128)(2,1)} %get-tuple-element.76), channel_id=1, source_target_pairs={{0,4},{4,0},{8,12},{12,8},{1,5},{5,1},{9,13},{13,9},{2,6},{6,2},{1... | collective-permute-start | bytes 2359304 | tf_op jit(solution)/shard_map/ppermute | solution.py:597
  50.6 25.2 %collective-permute-start.9 = (bf16[256,1536]{1,0:T(8,128)(2,1)}, bf16[256,1536]{1,0:T(8,128)(2,1)}, u32[]{:S(2)}, u32[]{:S(2)}) collective-permute-start(bf16[256,1536]{1,0:T(8,128)(2,1)} %get-tuple-element.76), channel_id=1, source_target_pairs={{4,8},{8,4},{5,9},{9,5},{6,10},{10,6},{7,11},{11,7},{20,24},{24,20... | collective-permute-start | bytes 2359304 | tf_op jit(solution)/shard_map/ppermute | solution.py:597
  60.4 2.8 %copy-start.3 = (bf16[512,1536]{1,0:T(8,128)(2,1)}, bf16[512,1536]{1,0:T(8,128)(2,1)S(1)}, u32[]{:S(2)}) copy-start(bf16[512,1536]{1,0:T(8,128)(2,1)S(1)} %get-tuple-element.69.refs_3_.refs_4_) | copy-start | bytes 4718596
  60.4 21.9 %slice-start.2 = ((s8[6291456]{0:T(1024)(128)(4,1)}), s8[2097152]{0:T(1024)(128)(4,1)S(1)}, s32[]{:S(2)}) async-start(s8[6291456]{0:T(1024)(128)(4,1)} %bitcast.14), calls=%async_computation.3 | async-start | bytes 4194304
  63.2 25.5 %collective-permute-start.7 = (bf16[256,1536]{1,0:T(8,128)(2,1)S(1)}, bf16[256,1536]{1,0:T(8,128)(2,1)}, u32[]{:S(2)}, u32[]{:S(2)}) collective-permute-start(bf16[256,1536]{1,0:T(8,128)(2,1)S(1)} %get-tuple-element.71.refs_4_), channel_id=1, source_target_pairs={{4,8},{8,4},{5,9},{9,5},{6,10},{10,6},{7,11},{11,7},{20,24},{24,20... | collective-permute-start | bytes 2359304 | tf_op jit(solution)/shard_map/ppermute | solution.py:614
  64.8 26.8 %collective-permute-start.8 = (bf16[256,1536]{1,0:T(8,128)(2,1)}, bf16[256,1536]{1,0:T(8,128)(2,1)}, u32[]{:S(2)}, u32[]{:S(2)}) collective-permute-start(bf16[256,1536]{1,0:T(8,128)(2,1)} %get-tuple-element.72.refs_6_.refs_5_), channel_id=1, source_target_pairs={{0,4},{4,0},{8,12},{12,8},{1,5},{5,1},{9,13},{13,9},{2,6},{6,2},{1... | collective-permute-start | bytes 2359304 | tf_op jit(solution)/shard_map/ppermute | solution.py:614
  67.2 2.8 %copy-start.1 = (bf16[128,16,1536]{2,1,0:T(8,128)(2,1)S(1)}, bf16[128,16,1536]{2,1,0:T(8,128)(2,1)}, u32[]{:S(2)}) copy-start(bf16[128,16,1536]{2,1,0:T(8,128)(2,1)} %param.10) | copy-start | bytes 18874372
  70.0 5.8 %copy-start.4 = (bf16[512,1536]{1,0:T(8,128)(2,1)S(1)}, bf16[512,1536]{1,0:T(8,128)(2,1)}, u32[]{:S(2)}) copy-start(bf16[512,1536]{1,0:T(8,128)(2,1)} %copy-done.3) | copy-start | bytes 4718596
  70.0 12.3 %slice-start.3 = ((s8[6291456]{0:T(1024)(128)(4,1)}), s8[4194304]{0:T(1024)(128)(4,1)S(1)}, s32[]{:S(2)}) async-start(s8[6291456]{0:T(1024)(128)(4,1)} %bitcast.14), calls=%async_computation.4 | async-start | bytes 8388608
  78.6 29.1 %collective-permute-start.13 = (bf16[256,1536]{1,0:T(8,128)(2,1)}, bf16[256,1536]{1,0:T(8,128)(2,1)}, u32[]{:S(2)}, u32[]{:S(2)}) collective-permute-start(bf16[256,1536]{1,0:T(8,128)(2,1)} %get-tuple-element.78.refs_5_.refs_6_), channel_id=1, source_target_pairs={{4,8},{8,4},{5,9},{9,5},{6,10},{10,6},{7,11},{11,7},{20,24},{24,20... | collective-permute-start | bytes 2359304 | tf_op jit(solution)/shard_map/ppermute | solution.py:614
  80.2 28.2 %collective-permute-start.14 = (bf16[256,1536]{1,0:T(8,128)(2,1)}, bf16[256,1536]{1,0:T(8,128)(2,1)}, u32[]{:S(2)}, u32[]{:S(2)}) collective-permute-start(bf16[256,1536]{1,0:T(8,128)(2,1)} %get-tuple-element.79.refs_7_), channel_id=1, source_target_pairs={{0,4},{4,0},{8,12},{12,8},{1,5},{5,1},{9,13},{13,9},{2,6},{6,2},{1... | collective-permute-start | bytes 2359304 | tf_op jit(solution)/shard_map/ppermute | solution.py:614
  94.3 44.6 %collective-permute-start.11 = (bf16[256,1536]{1,0:T(8,128)(2,1)}, bf16[256,1536]{1,0:T(8,128)(2,1)}, u32[]{:S(2)}, u32[]{:S(2)}) collective-permute-start(bf16[256,1536]{1,0:T(8,128)(2,1)} %get-tuple-element.82.refs_4_.refs_8_), channel_id=1, source_target_pairs={{4,8},{8,4},{5,9},{9,5},{6,10},{10,6},{7,11},{11,7},{20,24},{24,20... | collective-permute-start | bytes 2359304 | tf_op jit(solution)/shard_map/ppermute | solution.py:614
  95.8 43.0 %collective-permute-start.12 = (bf16[256,1536]{1,0:T(8,128)(2,1)}, bf16[256,1536]{1,0:T(8,128)(2,1)}, u32[]{:S(2)}, u32[]{:S(2)}) collective-permute-start(bf16[256,1536]{1,0:T(8,128)(2,1)} %get-tuple-element.83.refs_6_.refs_9_), channel_id=1, source_target_pairs={{0,4},{4,0},{8,12},{12,8},{1,5},{5,1},{9,13},{13,9},{2,6},{6,2},{1... | collective-permute-start | bytes 2359304 | tf_op jit(solution)/shard_map/ppermute | solution.py:614
  107.6 31.2 %copy-start.9 = (bf16[512,1536]{1,0:T(8,128)(2,1)}, bf16[512,1536]{1,0:T(8,128)(2,1)S(1)}, u32[]{:S(2)}) copy-start(bf16[512,1536]{1,0:T(8,128)(2,1)S(1)} %get-tuple-element.85.refs_4_) | copy-start | bytes 4718596
  111.1 48.5 %collective-permute-start.15 = (bf16[256,1536]{1,0:T(8,128)(2,1)}, bf16[256,1536]{1,0:T(8,128)(2,1)}, u32[]{:S(2)}, u32[]{:S(2)}) collective-permute-start(bf16[256,1536]{1,0:T(8,128)(2,1)} %get-tuple-element.87.refs_5_.refs_10_), channel_id=1, source_target_pairs={{4,8},{8,4},{5,9},{9,5},{6,10},{10,6},{7,11},{11,7},{20,24},{24,20... | collective-permute-start | bytes 2359304 | tf_op jit(solution)/shard_map/ppermute | solution.py:614
  112.7 47.0 %collective-permute-start.16 = (bf16[256,1536]{1,0:T(8,128)(2,1)}, bf16[256,1536]{1,0:T(8,128)(2,1)}, u32[]{:S(2)}, u32[]{:S(2)}) collective-permute-start(bf16[256,1536]{1,0:T(8,128)(2,1)} %get-tuple-element.88.refs_7_.refs_11_), channel_id=1, source_target_pairs={{0,4},{4,0},{8,12},{12,8},{1,5},{5,1},{9,13},{13,9},{2,6},{6,2},{1... | collective-permute-start | bytes 2359304 | tf_op jit(solution)/shard_map/ppermute | solution.py:614
  118.5 6.7 %copy-start.7 = (bf16[512,1536]{1,0:T(8,128)(2,1)S(1)}, bf16[512,1536]{1,0:T(8,128)(2,1)}, u32[]{:S(2)}) copy-start(bf16[512,1536]{1,0:T(8,128)(2,1)} %refs_3_.5) | copy-start | bytes 4718596
  138.9 28.0 %slice-start.4 = ((s8[6291456]{0:T(1024)(128)(4,1)}), s8[2097152]{0:T(1024)(128)(4,1)S(1)}, s32[]{:S(2)}) async-start(s8[6291456]{0:T(1024)(128)(4,1)} %bitcast.20), calls=%async_computation.5 | async-start | bytes 4194304
  141.7 31.9 %collective-permute-start.19 = (bf16[256,1536]{1,0:T(8,128)(2,1)}, bf16[256,1536]{1,0:T(8,128)(2,1)}, u32[]{:S(2)}, u32[]{:S(2)}) collective-permute-start(bf16[256,1536]{1,0:T(8,128)(2,1)} %get-tuple-element.98.refs_6_.refs_13_), channel_id=1, source_target_pairs={{0,4},{4,0},{8,12},{12,8},{1,5},{5,1},{9,13},{13,9},{2,6},{6,2},{1... | collective-permute-start | bytes 2359304 | tf_op jit(solution)/shard_map/ppermute | solution.py:614
  144.4 29.1 %collective-permute-start.20 = (bf16[256,1536]{1,0:T(8,128)(2,1)}, bf16[256,1536]{1,0:T(8,128)(2,1)}, u32[]{:S(2)}, u32[]{:S(2)}) collective-permute-start(bf16[256,1536]{1,0:T(8,128)(2,1)} %get-tuple-element.99.refs_4_.refs_12_), channel_id=1, source_target_pairs={{4,8},{8,4},{5,9},{9,5},{6,10},{10,6},{7,11},{11,7},{20,24},{24,20... | collective-permute-start | bytes 2359304 | tf_op jit(solution)/shard_map/ppermute | solution.py:614
  146.0 2.8 %copy-start.2 = (bf16[128,16,1536]{2,1,0:T(8,128)(2,1)S(1)}, bf16[128,16,1536]{2,1,0:T(8,128)(2,1)}, u32[]{:S(2)}) copy-start(bf16[128,16,1536]{2,1,0:T(8,128)(2,1)} %param.10) | copy-start | bytes 18874372
  148.8 1.9 copy-start.11
  150.7 1.2 copy-start.18
  151.9 7.8 %copy-start.5 = (bf16[512,1536]{1,0:T(8,128)(2,1)S(1)}, bf16[512,1536]{1,0:T(8,128)(2,1)}, u32[]{:S(2)}) copy-start(bf16[512,1536]{1,0:T(8,128)(2,1)} %copy-done.3) | copy-start | bytes 4718596
  151.9 7.8 %copy-start.10 = (bf16[512,1536]{1,0:T(8,128)(2,1)S(1)}, bf16[512,1536]{1,0:T(8,128)(2,1)}, u32[]{:S(2)}) copy-start(bf16[512,1536]{1,0:T(8,128)(2,1)} %copy-done.9) | copy-start | bytes 4718596
  151.9 14.9 %slice-start.5 = ((s8[6291456]{0:T(1024)(128)(4,1)}), s8[4194304]{0:T(1024)(128)(4,1)S(1)}, s32[]{:S(2)}) async-start(s8[6291456]{0:T(1024)(128)(4,1)} %bitcast.20), calls=%async_computation.6 | async-start | bytes 8388608
  162.4 25.9 %collective-permute-start.17 = (bf16[256,1536]{1,0:T(8,128)(2,1)}, bf16[256,1536]{1,0:T(8,128)(2,1)S(1)}, u32[]{:S(2)}, u32[]{:S(2)}) collective-permute-start(bf16[256,1536]{1,0:T(8,128)(2,1)} %get-tuple-element.96.refs_7_.refs_15_), channel_id=1, source_target_pairs={{0,4},{4,0},{8,12},{12,8},{1,5},{5,1},{9,13},{13,9},{2,6},{6,2},{1... | collective-permute-start | bytes 2359304 | tf_op jit(solution)/shard_map/ppermute | solution.py:614
  165.9 22.5 %collective-permute-start.18 = (bf16[256,1536]{1,0:T(8,128)(2,1)}, bf16[256,1536]{1,0:T(8,128)(2,1)S(1)}, u32[]{:S(2)}, u32[]{:S(2)}) collective-permute-start(bf16[256,1536]{1,0:T(8,128)(2,1)} %get-tuple-element.97.refs_5_.refs_14_), channel_id=1, source_target_pairs={{4,8},{8,4},{5,9},{9,5},{6,10},{10,6},{7,11},{11,7},{20,24},{24,20... | collective-permute-start | bytes 2359304 | tf_op jit(solution)/shard_map/ppermute | solution.py:614
  173.5 5.5 %copy-start.8 = (bf16[512,1536]{1,0:T(8,128)(2,1)S(1)}, bf16[512,1536]{1,0:T(8,128)(2,1)}, u32[]{:S(2)}) copy-start(bf16[512,1536]{1,0:T(8,128)(2,1)} %refs_3_.5) | copy-start | bytes 4718596
  175.9 1.5 collective-permute-start.21
  177.5 12.0 %collective-permute-start.22 = (f32[128,512]{1,0:T(8,128)S(1)}, f32[128,512]{1,0:T(8,128)S(1)}, u32[]{:S(2)}, u32[]{:S(2)}) collective-permute-start(f32[128,512]{1,0:T(8,128)S(1)} %add.23), channel_id=1, source_target_pairs={{0,2},{1,3},{2,0},{3,1},{4,6},{5,7},{6,4},{7,5},{8,10},{9,11},{10,... | collective-permute-start | bytes 786440 | tf_op jit(solution)/shard_map/ppermute | solution.py:582
  188.4 4.3 %copy-start.13 = (bf16[528,256]{1,0:T(8,128)(2,1)S(1)}, bf16[528,256]{1,0:T(8,128)(2,1)}, u32[]{:S(2)}) copy-start(bf16[528,256]{1,0:T(8,128)(2,1)} %copy-done.12) | copy-start | bytes 811012
  188.4 4.3 %copy-start.15 = (bf16[528,256]{1,0:T(8,128)(2,1)S(1)}, bf16[528,256]{1,0:T(8,128)(2,1)}, u32[]{:S(2)}) copy-start(bf16[528,256]{1,0:T(8,128)(2,1)} %copy-done.14) | copy-start | bytes 811012
  188.4 4.3 %copy-start.17 = (bf16[528,256]{1,0:T(8,128)(2,1)S(1)}, bf16[528,256]{1,0:T(8,128)(2,1)}, u32[]{:S(2)}) copy-start(bf16[528,256]{1,0:T(8,128)(2,1)} %copy-done.16) | copy-start | bytes 811012
  188.4 4.3 %copy-start.20 = (bf16[528,256]{1,0:T(8,128)(2,1)S(1)}, bf16[528,256]{1,0:T(8,128)(2,1)}, u32[]{:S(2)}) copy-start(bf16[528,256]{1,0:T(8,128)(2,1)} %get-tuple-element.61.refs_2_) | copy-start | bytes 811012
  189.6 8.5 %collective-permute-start.23 = (bf16[2,512]{1,0:T(2,128)(2,1)S(1)}, bf16[2,512]{1,0:T(2,128)(2,1)S(1)}, u32[]{:S(2)}, u32[]{:S(2)}) collective-permute-start(bf16[2,512]{1,0:T(2,128)(2,1)S(1)} %get-tuple-element.112), channel_id=1, source_target_pairs={{0,12},{4,0},{8,4},{12,8},{1,13},{5,1},{9,5},{13,9},{2,14},{6,2},{... | collective-permute-start | bytes 6152 | tf_op jit(solution)/shard_map/ppermute | solution.py:639
  192.0 6.1 %collective-permute-start.24 = (bf16[2,512]{1,0:T(2,128)(2,1)S(1)}, bf16[2,512]{1,0:T(2,128)(2,1)S(1)}, u32[]{:S(2)}, u32[]{:S(2)}) collective-permute-start(bf16[2,512]{1,0:T(2,128)(2,1)S(1)} %get-tuple-element.113), channel_id=1, source_target_pairs={{0,8},{4,12},{8,0},{12,4},{1,9},{5,13},{9,1},{13,5},{2,10},{6,14},... | collective-permute-start | bytes 6152 | tf_op jit(solution)/shard_map/ppermute | solution.py:639
  192.0 6.1 %collective-permute-start.25 = (bf16[2,512]{1,0:T(2,128)(2,1)S(1)}, bf16[2,512]{1,0:T(2,128)(2,1)S(1)}, u32[]{:S(2)}, u32[]{:S(2)}) collective-permute-start(bf16[2,512]{1,0:T(2,128)(2,1)S(1)} %get-tuple-element.114), channel_id=1, source_target_pairs={{0,4},{4,8},{8,12},{12,0},{1,5},{5,9},{9,13},{13,1},{2,6},{6,10},{... | collective-permute-start | bytes 6152 | tf_op jit(solution)/shard_map/ppermute | solution.py:639
Sparse Core Ops, SparseCore 0:
  67.3 16.8 all-gather.1

commit v4 on v3

--- a/solution.py
+++ b/solution.py
@@ -13,6 +13,10 @@
 NT = (((1,), (1,)), ((), ()))
 ANY = pl.BlockSpec(memory_space=pl.ANY)
 COST = 0.02
+STEP_IN = 1024
+STEP_ROWS = 512
+STEP_DOWN = 1024
+STEP_UP = 512
 
 
 def call(body, out_shape, *, grid=None, in_specs=None, out_specs=None, scratch=(), prefetch=0,
@@ -191,7 +195,7 @@
     )(pos, up, *blocks)
 
 
-def project_in_body(rank, chunks, size, step_index, pos_ref, down_ref, aux_ref, before_ref, *refs):
+def project_in_body(rank, chunks, size, sources, pos_ref, down_ref, aux_ref, before_ref, *refs):
     rows, (out_ref, kept_ref) = refs[:-2], refs[-2:]
     source, b = pl.program_id(0), pl.program_id(1)
     step = down_ref.shape[0]
@@ -200,8 +204,8 @@
     def _():
         out_ref[...] = before_ref[...]
 
-    for s in range(len(rows) // chunks):
-        valid, slot = arrival(pos_ref[0], size, step_index, s == 0)
+    for s, (step_index, a) in enumerate(sources):
+        valid, slot = arrival(pos_ref[0], size, step_index, a)
 
         @pl.when((source == s) & valid)
         def _():
@@ -226,23 +230,22 @@
                 out_ref[pl.ds(pl.multiple_of(slot * 2 * rank, 2 * rank), 2 * rank), :] = kept_ref[...]
 
 
-def project_in(pos, size, step_index, down, aux, before, rows, chunks, rank, after=()):
+def project_in(pos, size, sources, down, aux, before, rows, chunks, rank, after=()):
     total, width = down.shape
-    sources = len(rows) // chunks
-    step = min(512, total)
+    step = min(STEP_IN, total)
     count = aux.shape[1]
 
     def down_block(s, b, pos):
         use = b
-        for i in range(sources):
-            valid, _ = arrival(pos[0], size, step_index, i == 0)
+        for i, (step_index, a) in enumerate(sources):
+            valid, _ = arrival(pos[0], size, step_index, a)
             use = jnp.where((s == i) & jnp.logical_not(valid), 0, use)
         return use, 0
 
     return call(
-        functools.partial(project_in_body, rank, chunks, size, step_index),
+        functools.partial(project_in_body, rank, chunks, size, sources),
         jax.ShapeDtypeStruct(before.shape, F32),
-        grid=(sources, total // step),
+        grid=(len(sources), total // step),
         in_specs=[pl.BlockSpec((step, width), down_block), whole(aux.shape), whole(before.shape)]
         + [whole(r.shape) for r in rows],
         out_specs=whole(before.shape),
@@ -283,20 +286,17 @@
                 spread_ref[rows, g * 128 : (g + 1) * 128] = spread.astype(BF)
 
     rows = jnp.dot(spread_ref[...], down_ref[...], preferred_element_type=F32)
-    if len(refs) == 4:
-        rows = rows + lax.dot_general(refs[0][...], refs[1][...], NT, preferred_element_type=F32)
+    if len(refs) == 3:
+        rows = rows + refs[0][...]
     out_ref[...] = rows.astype(out_ref.dtype)
 
 
 def adapter_rows(pos, size, place, part, aux, down, rank, frozen=None, after=()):
     total, width = down.shape
     count = aux.shape[1]
-    step = 256
+    step = STEP_ROWS if width % STEP_ROWS == 0 else 256
     block = pl.BlockSpec((count, step), lambda n, pos: (0, n))
-    more, specs = [], []
-    if frozen is not None:
-        more = list(frozen)
-        specs = [whole(more[0].shape), pl.BlockSpec((step, more[1].shape[1]), lambda n, pos: (n, 0))]
+    more = [] if frozen is None else [frozen]
     return call(
         functools.partial(adapter_rows_body, rank, size, place),
         jax.ShapeDtypeStruct((count, width), BF if frozen is None else F32),
@@ -304,7 +304,7 @@
         in_specs=[
             whole(part.shape), whole(aux.shape), pl.BlockSpec((total, step), lambda n, pos: (0, n)),
         ]
-        + specs,
+        + [block] * len(more),
         out_specs=block,
         scratch=[pltpu.VMEM((count, total), BF)],
         prefetch=1,
@@ -314,51 +314,93 @@
     )(pos, part, aux, down, *more)
 
 
+def frozen_body(count, share_ref, own_ref, near_ref, far_ref, weight_ref, out_ref):
+    width = own_ref.shape[1]
+    blocks = [own_ref[...], near_ref[...]]
+    blocks += [far_ref[i * count : (i + 1) * count, :] for i in range(far_ref.shape[0] // count)]
+    total = 0.0
+    for i, block in enumerate(blocks):
+        start = pl.multiple_of((share_ref[0] ^ i) * width, width)
+        total = total + lax.dot_general(
+            block, weight_ref[:, pl.ds(start, width)], NT, preferred_element_type=F32
+        )
+    out_ref[...] = total
+
+
+def frozen_product(share, own, near, far, weight, after):
+    count = own.shape[0]
+    total, width = weight.shape
+    step = 512 if total % 512 == 0 else 256
+    return call(
+        functools.partial(frozen_body, count),
+        jax.ShapeDtypeStruct((count, total), F32),
+        grid=(total // step,),
+        in_specs=[whole(own.shape), whole(near.shape), whole(far.shape)]
+        + [pl.BlockSpec((step, width), lambda n, share: (n, 0))],
+        out_specs=pl.BlockSpec((count, step), lambda n, share: (0, n)),
+        prefetch=1,
+        flops=2 * count * width * total,
+        moved=4 * count * total,
+        after=after,
+    )(share, own, near, far, weight)
+
+
 def add_body(size, step_index, row, pos_ref, first_ref, second_ref, near_ref, far_ref, *refs):
     outs = refs[:2]
     held, terms, in_sem, term_sem, out_sem = refs[2:]
+    sources = (first_ref, second_ref)
     pieces = in_sem.shape[1]
     piece = held.shape[1] // pieces
     d = pos_ref[0]
-    for i, (source, out) in enumerate(zip((first_ref, second_ref), outs)):
-        do, slot = departure(d, size, step_index, i == 0)
+
+    def get(i, q):
+        rows = pl.ds(q * piece, piece)
+        return pltpu.make_async_copy(sources[i].at[rows], held.at[i, rows], in_sem.at[i, q])
+
+    def put(i, q):
+        rows = pl.ds(q * piece, piece)
+        return pltpu.make_async_copy(held.at[i, rows], outs[i].at[rows], out_sem.at[i, q])
+
+    def term(i, q, ref):
+        rows = pl.ds(q * piece, piece)
+        return pltpu.make_async_copy(
+            ref.at[pl.ds(row + q * piece, piece)], terms.at[i, rows], term_sem.at[i, q]
+        )
+
+    plans = [departure(d, size, step_index, i == 0) for i in range(2)]
+    for i, (do, slot) in enumerate(plans):
         place = place_of(d, size, slot)
-
-        def get(q):
-            rows = pl.ds(q * piece, piece)
-            return pltpu.make_async_copy(source.at[rows], held.at[i, rows], in_sem.at[i, q])
-
-        def put(q):
-            rows = pl.ds(q * piece, piece)
-            return pltpu.make_async_copy(held.at[i, rows], out.at[rows], out_sem.at[i, q])
-
-        def term(q, ref):
-            rows = pl.ds(row + q * piece, piece)
-            return pltpu.make_async_copy(
-                ref.at[rows], terms.at[i, pl.ds(q * piece, piece)], term_sem.at[i, q]
-            )
 
         @pl.when(do)
         def _():
             for q in range(pieces):
-                get(q).start()
+                get(i, q).start()
 
                 @pl.when(place == 0)
                 def _():
-                    term(q, near_ref).start()
+                    term(i, q, near_ref).start()
 
                 @pl.when(place != 0)
                 def _():
-                    term(q, far_ref).start()
-
+                    term(i, q, far_ref).start()
+
+    for i, (do, _) in enumerate(plans):
+
+        @pl.when(do)
+        def _():
             for q in range(pieces):
-                get(q).wait()
-                term(q, near_ref).wait()
+                get(i, q).wait()
+                term(i, q, near_ref).wait()
                 rows = pl.ds(q * piece, piece)
                 held[i, rows, :] = (held[i, rows, :].astype(F32) + terms[i, rows, :].astype(F32)).astype(BF)
-                put(q).start()
+                put(i, q).start()
+
+    for i, (do, _) in enumerate(plans):
+
+        @pl.when(do)
+        def _():
             for q in range(pieces):
-                put(q).wait()
+                put(i, q).wait()
 
 
 def ring_add(pos, size, step_index, row, first, second, near, far, after):
@@ -394,9 +436,8 @@
     return jnp.concatenate(rows, axis=0)
 
 
-def grad_down_body(rank, size, first, where, pos_ref, part_ref, aux_ref, *refs):
+def grad_down_body(rank, size, where, pos_ref, part_ref, aux_ref, *refs):
     row_refs = refs[: len(where)]
-    before_ref = refs[len(where)] if len(refs) == len(where) + 6 else None
     out_ref, rows_ref, scaled_ref, ids_ref, sem = refs[-5:]
     b = pl.program_id(0)
     count = aux_ref.shape[1]
@@ -409,16 +450,16 @@
             valid, slot = arrival(pos_ref[0], size, step_index, a)
             place = place_of(pos_ref[0], size, slot)
 
-            @pl.when(valid & (place >= first) & (place < first + places))
+            @pl.when(valid)
             def _():
-                start = pl.multiple_of((place - first) * count + offset, height)
+                start = pl.multiple_of(place * count + offset, height)
                 act(pltpu.make_async_copy(row_refs[i], rows_ref.at[pl.ds(start, height)], sem.at[i]))
 
     @pl.when(b == 0)
     def _():
         copies(lambda c: c.start())
         for p in range(places):
-            slot = slot_at(pos_ref[0], size, first + p)
+            slot = slot_at(pos_ref[0], size, p)
             low = part_ref[pl.ds(pl.multiple_of(slot * 2 * rank, 2 * rank), 2 * rank), :]
             aux = aux_ref[pl.ds(pl.multiple_of(slot * 8, 8), 8), :]
             columns = slice(p * count, (p + 1) * count)
@@ -435,22 +476,20 @@
         spread.append(spread_rows(values, ids_ref[0:2, columns], b * (step // rank), step // rank))
     spread = spread[0] if places == 1 else jnp.concatenate(spread, axis=1)
     out = jnp.dot(spread, rows_ref[...], preferred_element_type=F32)
-    if before_ref is not None:
-        out = out + before_ref[...].astype(F32)
     out_ref[...] = out.astype(BF)
 
 
-def grad_down(pos, size, part, aux, rows, where, first, places, total, rank, before=None, after=()):
+def grad_down(pos, size, part, aux, rows, where, total, rank, after):
+    places = size
     count = aux.shape[1]
     width = rows[0].shape[1]
-    step = min(512, total)
+    step = min(STEP_DOWN, total)
     block = pl.BlockSpec((step, width), lambda b, pos: (b, 0))
-    more = [] if before is None else [before]
-    return call(
-        functools.partial(grad_down_body, rank, size, first, where),
+    return call(
+        functools.partial(grad_down_body, rank, size, where),
         jax.ShapeDtypeStruct((total, width), BF),
         grid=(total // step,),
-        in_specs=[whole(part.shape), whole(aux.shape)] + [ANY] * len(rows) + [block] * len(more),
+        in_specs=[whole(part.shape), whole(aux.shape)] + [ANY] * len(rows),
         out_specs=block,
         scratch=[
             pltpu.VMEM((places * count, width), BF),
@@ -459,12 +498,11 @@
             pltpu.SemaphoreType.DMA((len(rows),)),
         ],
         prefetch=1,
-        aliases={3 + len(rows): 0} if more else None,
         flops=2 * places * count * total * width,
         moved=2 * (total * width + places * count * width),
-        vmem=24 if places * count * width <= 1 << 22 else 60,
-        after=after,
-    )(pos, part, aux, *rows, *more)
+        vmem=34 if places * count * width <= 1 << 22 else 60,
+        after=after,
+    )(pos, part, aux, *rows)
 
 
 def grad_gates_body(rank, in_ref, out_ref, *gate_refs):
@@ -517,7 +555,7 @@
     count = aux.shape[1]
     slots = len(blocks)
     width = blocks[0].shape[1]
-    step = min(256, total)
+    step = min(STEP_UP, total)
     arrays = [part_in, aux, *blocks]
     return call(
         functools.partial(grad_up_body, rank, slots),
@@ -589,47 +627,61 @@
     blocks = [block] + [
         lax.ppermute(block, "dp", [(i, (i + s) % size) for i in range(size)]) for s in range(1, size)
     ]
-    full_out = lax.all_gather(output_gradient, "mp", axis=1, tiled=True)
+    share = lax.axis_index("mp").astype(jnp.int32).reshape(1)
+    swap = lambda rows, bit: lax.ppermute(rows, "mp", [(i, i ^ bit) for i in range(shares)])
+    next_out = swap(output_gradient, 1)
+    held_out = jnp.concatenate([output_gradient, next_out], axis=0)
+    bit = 2
+    while bit < shares:
+        held_out = jnp.concatenate([held_out, swap(held_out, bit)], axis=0)
+        bit *= 2
+    far_out = held_out[2 * count :]
     low = jnp.zeros((size * 2 * rank, count), F32)
-    low, token = project_in(pos, size, -1, down, aux_own, low, [inputs], 1, rank)
+    low, token = project_in(pos, size, [(-1, True)], down, aux_own, low, [inputs], 1, rank)
 
     sent, tokens = zip(*[pin(inputs[c * half : (c + 1) * half], blocks[1:]) for c in range(CHUNKS)])
     got = [[lax.ppermute(sent[c], "dp", p) for p in (pairs_a, pairs_b)] for c in range(CHUNKS)]
 
+    frozen, token = frozen_product(share, output_gradient, next_out, far_out, frozen_key_weight, [token])
     part_out, aux, _ = project_out(pos, up, blocks, count, rank, [token, *tokens])
     part_out = exchange(part_out)
     near, token = adapter_rows(pos, size, 0, part_out, aux, down, rank)
     far = near
 
+    def add_projection(low, sources, token):
+        return project_in(
+            pos, size, [k for k, _ in sources], down, aux, low, sum([v for _, v in sources], []), CHUNKS,
+            rank, [token],
+        )
+
     rows, where = [inputs], [(-1, True, 0)]
-    early = result = None
+    result, waiting = None, []
     for j in range(1, size):
         term = far
+        arrived = {True: [], False: []}
         for c in range(CHUNKS):
             to_a, to_b, token = ring_add(
                 pos, size, j, c * half, got[c][1], got[c][0], near, term, [token]
             )
             rows += [to_b, to_a]
             where += [(j - 1, True, c * half), (j - 1, False, c * half)]
+            arrived[True].append(to_b)
+            arrived[False].append(to_a)
             got[c] = [lax.ppermute(to_a, "dp", pairs_a), lax.ppermute(to_b, "dp", pairs_b)]
             if c == 0:
-                frozen = (full_out, frozen_key_weight) if j == size - 1 else None
-                far, token = adapter_rows(pos, size, j, part_out, aux, down, rank, frozen, [token])
-        newest = rows[-2 * CHUNKS :]
-        low, token = project_in(
-            pos, size, j - 1, down, aux, low, newest[0::2] + newest[1::2], CHUNKS, rank, [token]
-        )
-        if j == size - 2:
-            early, token = grad_down(
-                pos, size, part_out, aux, rows, where, 1, size - 1, total, rank, None, [token]
-            )
+                far, token = adapter_rows(
+                    pos, size, j, part_out, aux, down, rank, frozen if j == size - 1 else None, [token]
+                )
+        ready = [((j - 1, True), arrived[True])] + waiting
+        waiting = [((j - 1, False), arrived[False])]
+        if j == size - 1:
+            ready += waiting if size % 2 else []
+        low, token = add_projection(low, ready, token)
 
     result, token = finish(far, got[0][0], got[0][1], 0, None, [token])
     low, _ = pin(low, [token])
     part_in = exchange(low)
-    down_gradient, token = grad_down(
-        pos, size, part_out, aux, rows, where, 0, 1, total, rank, early, [token]
-    )
+    down_gradient, token = grad_down(pos, size, part_out, aux, rows, where, total, rank, [token])
     for c in range(1, CHUNKS):
         result, token = finish(far, got[c][0], got[c][1], c, result, [token])
     *gate_rows, token = grad_gates(part_in, part_out, size, rank, [token])

time: 206 us -> 187 us (0.908)
  Pallas kernels: 104 us -> 89.5 us
  between operations: 14.6 us -> 1.07 us
  starting transfers between devices: 50.8 us -> 62.3 us
  local copies, waits for them, and re-layouts: 14.7 us -> 5.23 us
  waiting for transfers between devices: 21 us -> 27.5 us
    pallas_call x25, Pallas kernels: 104 us -> 89.5 us  [call(): return lambda *arrays: call_it(*arrays, *after)]
    ppermute x6, starting transfers between devices: 22.5 us -> 33.6 us  [per_device(): lax.ppermute(to_a, 'dp', pairs_a)]
    unnamed x58 -> x20, local copies, waits for them, and re-layouts: 13.7 us -> 5.11 us
    ppermute x6, waiting for transfers between devices: 3.7 us -> 8.44 us  [per_device(): lax.ppermute(to_a, 'dp', pairs_a)]
    ppermute x6, starting transfers between devices: 8.83 us -> 4.64 us  [per_device(): lax.ppermute(to_b, 'dp', pairs_b)]
    ppermute x3, starting transfers between devices: 3.06 us -> 7.05 us  [per_device(): lax.ppermute(gate_rows[s], 'dp', [(i, (i - s) % size) for i in range(size)])]
    ppermute x0 -> x2, starting transfers between devices: none -> 2.07 us  [per_device(): lax.ppermute(rows, 'mp', [(i, i ^ bit) for i in range(shares)])]
  transfers between devices with their start and end apart: 27 -> 28, of which waited for: 6 -> 9; matrix products, arithmetic and copies ran while one was open for 1% -> 0% of each run, Pallas kernels for 50% -> 48%
where the time goes in v4:
time: 187 us; the launch traced here: 186 us
  Pallas kernels  89.5 us (48%)
  starting transfers between devices  62.3 us (33%)
  waiting for transfers between devices  27.5 us (15%)
  local copies, waits for them, and re-layouts  5.23 us (3%)
    pallas_call x25, Pallas kernels, call(): return lambda *arrays: call_it(*arrays, *after)  89.5 us
    ppermute x6, starting transfers between devices, per_device(): lax.ppermute(to_a, 'dp', pairs_a)  33.6 us
    ppermute x3, waiting for transfers between devices, per_device(): lax.ppermute(block, 'dp', [(i, (i + s) % size) for i in range(size)])  12.3 us
    ppermute x6, waiting for transfers between devices, per_device(): lax.ppermute(to_a, 'dp', pairs_a)  8.44 us
    ppermute x3, starting transfers between devices, per_device(): lax.ppermute(gate_rows[s], 'dp', [(i, (i - s) % size) for i in range(size)])  7.05 us
    ppermute x4, starting transfers between devices, per_device(): lax.ppermute(sent[c], 'dp', p)  6.12 us
    ppermute x3, starting transfers between devices, per_device(): lax.ppermute(block, 'dp', [(i, (i + s) % size) for i in range(size)])  5.63 us
    ppermute x4, waiting for transfers between devices, exchange(): lax.ppermute(part, 'mp', [(i, i ^ bit) for i in range(shares)])  5.48 us
  transfers between devices with their start and end apart: 28, of which 9 were waited for; matrix products, arithmetic and copies ran while one was open for 0% of the time, Pallas kernels for 48%

profile of v4, /device:TPU:0, one launch (start us, length us, event | category | flops | bytes accessed | tf_op | source)
XLA Modules:
  0.0 186.4 jit_solution(12656606940436132455)
XLA Ops:
  0.6 0.5 collective-permute-start.3
  1.1 1.7 shard_map.102
  2.9 4.6 %collective-permute-start.2 = (bf16[528,256]{1,0:T(8,128)(2,1)}, bf16[528,256]{1,0:T(8,128)(2,1)S(1)}, u32[]{:S(2)}, u32[]{:S(2)}) collective-permute-start(bf16[528,256]{1,0:T(8,128)(2,1)} %get-tuple-element.61.refs_2_), channel_id=1, source_target_pairs={{0,12},{4,0},{8,4},{12,8},{1,13},{5,1},{9,5},{13,9},{2,14},{6,2},{... | collective-permute-start | bytes 811016 | tf_op jit(solution)/shard_map/ppermute | solution.py:628
  7.5 1.0 collective-permute-start
  8.5 2.8 %copy-done = bf16[128,16,1536]{2,1,0:T(8,128)(2,1)S(1)} copy-done((bf16[128,16,1536]{2,1,0:T(8,128)(2,1)S(1)}, bf16[128,16,1536]{2,1,0:T(8,128)(2,1)}, u32[]{:S(2)}) %copy-start) | copy-done | bytes 6291480
  11.3 1.4 copy-done.1
  12.7 0.7 copy-done.6
  13.4 3.9 %shard_map.103 = (f32[128,512]{1,0:T(8,128)S(1)}, f32[8,128]{1,0:T(8,128)S(1)}) custom-call(s32[1]{0:T(128)} %bitcast.refs_0_, bf16[2048,1536]{1,0:T(8,128)(2,1)S(1)} %bitcast.10, f32[8,512]{1,0:T(8,128)S(1)} %copy-done.6, f32[128,512]{1,0:T(8,128)S(1)} %broadcast_in_dim.3.refs_3_, bf16[512,1536]{1,0:T(8,128)(2,1)S(1)} %copy-done.1), custom_call_target="tpu_custom_call", output_to_operand_aliasing={{0}: (3, {})} | custom-call | flops 64424508 | bytes 157286 | tf_op jit(solution)/shard_map/pallas_call | solution.py:53
  17.4 1.6 collective-permute-start.4
  19.0 0.1 fusion.1
  19.1 12.3 %collective-permute-done.1.refs_2_.refs_4_ = bf16[528,256]{1,0:T(8,128)(2,1)S(1)} collective-permute-done((bf16[528,256]{1,0:T(8,128)(2,1)}, bf16[528,256]{1,0:T(8,128)(2,1)S(1)}, u32[]{:S(2)}, u32[]{:S(2)}) %collective-permute-start.1) | collective-permute-done | bytes 270368 | tf_op jit(solution)/shard_map/ppermute | solution.py:628
  31.4 1.0 collective-permute-start.8
  32.4 0.7 collective-permute-start.7
  33.1 0.2 copy-done.3
  33.3 2.4 %shard_map.104 = (f32[512,1536]{1,0:T(8,128)S(1)}, f32[8,128]{1,0:T(8,128)S(1)}) custom-call(s32[1]{0:T(128)} %bitcast.4.refs_0_, bf16[512,256]{1,0:T(8,128)(2,1)S(1)} %copy-done.4, bf16[512,256]{1,0:T(8,128)(2,1)S(1)} %collective-permute-done.3.refs_2_, bf16[1024,256]{1,0:T(8,128)(2,1)S(1)} %collective-permute-done.4.refs_3_, ...), custom_call_target="tpu_custom_call" | custom-call | flops 32212254 | bytes 62914 | tf_op jit(solution)/shard_map/pallas_call | solution.py:53
  35.7 0.0 slice-start
  35.8 4.6 %shard_map.107 = (f32[128,512]{1,0:T(8,128)S(1)}, f32[32,512]{1,0:T(8,128)S(1)}, f32[8,128]{1,0:T(8,128)}) custom-call(s32[1]{0:T(128)} %bitcast.refs_0_, bf16[2048,256]{1,0:T(8,128)(2,1)S(1)} %bitcast.20, bf16[528,256]{1,0:T(8,128)(2,1)S(1)} %copy-done.5, bf16[528,256]{1,0:T(8,128)(2,1)S(1)} %collective-permute-done.refs_1_.refs_3_, ...), custom_call_target="tpu_custom_call" | custom-call | flops 10737418240 | bytes 10485760 | tf_op jit(solution)/shard_map/pallas_call | solution.py:53
  40.4 0.1 collective-permute-start.5
  40.5 1.5 collective-permute-done.5
  42.0 1.5 collective-permute-start.6
  43.6 3.7 %collective-permute-start.12 = (bf16[256,1536]{1,0:T(8,128)(2,1)S(1)}, bf16[256,1536]{1,0:T(8,128)(2,1)S(1)}, u32[]{:S(2)}, u32[]{:S(2)}) collective-permute-start(bf16[256,1536]{1,0:T(8,128)(2,1)S(1)} %get-tuple-element.78), channel_id=1, source_target_pairs={{0,4},{4,0},{8,12},{12,8},{1,5},{5,1},{9,13},{13,9},{2,6},{6,2},{1... | collective-permute-start | bytes 2359304 | tf_op jit(solution)/shard_map/ppermute | solution.py:643
  47.3 0.7 collective-permute-start.11
  48.0 2.4 %collective-permute-done.6 = f32[128,512]{1,0:T(8,128)S(1)} collective-permute-done((f32[128,512]{1,0:T(8,128)S(1)}, f32[128,512]{1,0:T(8,128)S(1)}, u32[]{:S(2)}, u32[]{:S(2)}) %collective-permute-start.6) | collective-permute-done | bytes 262176 | tf_op jit(solution)/shard_map/ppermute | solution.py:620
  50.5 5.3 %shard_map.108 = (bf16[512,1536]{1,0:T(8,128)(2,1)S(1)}, f32[8,128]{1,0:T(8,128)S(1)}) custom-call(s32[1]{0:T(128)} %bitcast.refs_0_, f32[128,512]{1,0:T(8,128)S(1)} %add.22.refs_1_, f32[32,512]{1,0:T(8,128)S(1)} %get-tuple-element.68.refs_2_.refs_1_, bf16[2048,1536]{1,0:T(8,128)(2,1)S(1)} %bitcast.13), custom_call_target="tpu_custom_call" | custom-call | flops 64424508 | bytes 157286 | tf_op jit(solution)/shard_map/pallas_call | solution.py:53
  55.8 3.5 %shard_map.109 = (bf16[256,1536]{1,0:T(8,128)(2,1)S(1)}, bf16[256,1536]{1,0:T(8,128)(2,1)S(1)}, f32[8,128]{1,0:T(8,128)S(1)}) custom-call(s32[1]{0:T(128)} %bitcast.refs_0_, bf16[256,1536]{1,0:T(8,128)(2,1)S(1)} %collective-permute-done.7.refs_1_, ...), custom_call_target="tpu_custom_call", output_to_operand_aliasing={{0}: (1, {}), {1}: (2, {})} | custom-call | flops 15728 | bytes 47185 | tf_op jit(solution)/shard_map/pallas_call | solution.py:53
  59.3 0.7 collective-permute-start.9
  60.0 2.2 %collective-permute-start.10 = (bf16[256,1536]{1,0:T(8,128)(2,1)S(1)}, bf16[256,1536]{1,0:T(8,128)(2,1)S(1)}, u32[]{:S(2)}, u32[]{:S(2)}) collective-permute-start(bf16[256,1536]{1,0:T(8,128)(2,1)S(1)} %get-tuple-element.74.refs_6_.refs_5_), channel_id=1, source_target_pairs={{0,4},{4,0},{8,12},{12,8},{1,5},{5,1},{9,13},{13,9},{2,6},{6,2},{1... | collective-permute-start | bytes 2359304 | tf_op jit(solution)/shard_map/ppermute | solution.py:670
  62.2 5.2 %shard_map.110 = (bf16[512,1536]{1,0:T(8,128)(2,1)S(1)}, f32[8,128]{1,0:T(8,128)S(1)}) custom-call(s32[1]{0:T(128)} %bitcast.refs_0_, f32[128,512]{1,0:T(8,128)S(1)} %add.22.refs_1_, f32[32,512]{1,0:T(8,128)S(1)} %get-tuple-element.68.refs_2_.refs_1_, bf16[2048,1536]{1,0:T(8,128)(2,1)S(1)} %bitcast.14, f32[8,128]{1,0:T(8,128)S(1)} %get-tuple-element.75.refs_4_), custom_call_target="tpu_custom_call" | custom-call | flops 64424508 | bytes 157286 | tf_op jit(solution)/shard_map/pallas_call | solution.py:53
  67.4 1.2 collective-permute-done.12.refs_2_
  68.7 3.5 %shard_map.111 = (bf16[256,1536]{1,0:T(8,128)(2,1)S(1)}, bf16[256,1536]{1,0:T(8,128)(2,1)S(1)}, f32[8,128]{1,0:T(8,128)S(1)}) custom-call(s32[1]{0:T(128)} %bitcast.refs_0_, bf16[256,1536]{1,0:T(8,128)(2,1)S(1)} %collective-permute-done.11.refs_1_, ...), custom_call_target="tpu_custom_call", output_to_operand_aliasing={{0}: (1, {}), {1}: (2, {})} | custom-call | flops 15728 | bytes 47185 | tf_op jit(solution)/shard_map/pallas_call | solution.py:53
  72.1 0.9 collective-permute-start.15
  73.0 3.6 %collective-permute-start.16 = (bf16[256,1536]{1,0:T(8,128)(2,1)S(1)}, bf16[256,1536]{1,0:T(8,128)(2,1)S(1)}, u32[]{:S(2)}, u32[]{:S(2)}) collective-permute-start(bf16[256,1536]{1,0:T(8,128)(2,1)S(1)} %get-tuple-element.88.refs_7_), channel_id=1, source_target_pairs={{0,4},{4,0},{8,12},{12,8},{1,5},{5,1},{9,13},{13,9},{2,6},{6,2},{1... | collective-permute-start | bytes 2359304 | tf_op jit(solution)/shard_map/ppermute | solution.py:670
  76.6 3.9 %shard_map.112 = (f32[128,512]{1,0:T(8,128)S(1)}, f32[8,128]{1,0:T(8,128)S(1)}) custom-call(s32[1]{0:T(128)} %bitcast.refs_0_, bf16[2048,1536]{1,0:T(8,128)(2,1)S(1)} %bitcast.15, f32[32,512]{1,0:T(8,128)S(1)} %get-tuple-element.68.refs_2_.refs_1_, f32[128,512]{1,0:T(8,128)S(1)} %get-tuple-element.77.refs_3_, ...), custom_call_target="tpu_custom_call", output_to_operand_aliasing={{0}: (3, {})} | custom-call | flops 64424508 | bytes 157286 | tf_op jit(solution)/shard_map/pallas_call | solution.py:53
  80.5 5.0 %collective-permute-done.10.refs_2_ = bf16[256,1536]{1,0:T(8,128)(2,1)S(1)} collective-permute-done((bf16[256,1536]{1,0:T(8,128)(2,1)S(1)}, bf16[256,1536]{1,0:T(8,128)(2,1)S(1)}, u32[]{:S(2)}, u32[]{:S(2)}) %collective-permute-start.10) | collective-permute-done | bytes 786464 | tf_op jit(solution)/shard_map/ppermute | solution.py:670
  85.5 3.4 %shard_map.113 = (bf16[256,1536]{1,0:T(8,128)(2,1)S(1)}, bf16[256,1536]{1,0:T(8,128)(2,1)S(1)}, f32[8,128]{1,0:T(8,128)S(1)}) custom-call(s32[1]{0:T(128)} %bitcast.refs_0_, bf16[256,1536]{1,0:T(8,128)(2,1)S(1)} %collective-permute-done.9.refs_1_, ...), custom_call_target="tpu_custom_call", output_to_operand_aliasing={{0}: (1, {}), {1}: (2, {})} | custom-call | flops 15728 | bytes 47185 | tf_op jit(solution)/shard_map/pallas_call | solution.py:53
  89.0 0.7 collective-permute-start.13
  89.7 6.8 %collective-permute-start.14 = (bf16[256,1536]{1,0:T(8,128)(2,1)S(1)}, bf16[256,1536]{1,0:T(8,128)(2,1)S(1)}, u32[]{:S(2)}, u32[]{:S(2)}) collective-permute-start(bf16[256,1536]{1,0:T(8,128)(2,1)S(1)} %get-tuple-element.84.refs_6_.refs_9_), channel_id=1, source_target_pairs={{0,4},{4,0},{8,12},{12,8},{1,5},{5,1},{9,13},{13,9},{2,6},{6,2},{1... | collective-permute-start | bytes 2359304 | tf_op jit(solution)/shard_map/ppermute | solution.py:670
  96.5 5.2 %shard_map.114 = (bf16[512,1536]{1,0:T(8,128)(2,1)S(1)}, f32[8,128]{1,0:T(8,128)S(1)}) custom-call(s32[1]{0:T(128)} %bitcast.refs_0_, f32[128,512]{1,0:T(8,128)S(1)} %add.22.refs_1_, f32[32,512]{1,0:T(8,128)S(1)} %get-tuple-element.68.refs_2_.refs_1_, bf16[2048,1536]{1,0:T(8,128)(2,1)S(1)} %bitcast.16, f32[8,128]{1,0:T(8,128)S(1)} %get-tuple-element.85.refs_4_), custom_call_target="tpu_custom_call" | custom-call | flops 64424508 | bytes 157286 | tf_op jit(solution)/shard_map/pallas_call | solution.py:53
  101.8 0.6 collective-permute-done.16.refs_2_
  102.4 3.4 %shard_map.115 = (bf16[256,1536]{1,0:T(8,128)(2,1)S(1)}, bf16[256,1536]{1,0:T(8,128)(2,1)S(1)}, f32[8,128]{1,0:T(8,128)S(1)}) custom-call(s32[1]{0:T(128)} %bitcast.refs_0_, bf16[256,1536]{1,0:T(8,128)(2,1)S(1)} %collective-permute-done.15.refs_1_, ...), custom_call_target="tpu_custom_call", output_to_operand_aliasing={{0}: (1, {}), {1}: (2, {})} | custom-call | flops 15728 | bytes 47185 | tf_op jit(solution)/shard_map/pallas_call | solution.py:53
  105.8 0.7 collective-permute-start.17
  106.5 6.8 %collective-permute-start.18 = (bf16[256,1536]{1,0:T(8,128)(2,1)S(1)}, bf16[256,1536]{1,0:T(8,128)(2,1)S(1)}, u32[]{:S(2)}, u32[]{:S(2)}) collective-permute-start(bf16[256,1536]{1,0:T(8,128)(2,1)S(1)} %get-tuple-element.95.refs_7_.refs_11_), channel_id=1, source_target_pairs={{0,4},{4,0},{8,12},{12,8},{1,5},{5,1},{9,13},{13,9},{2,6},{6,2},{1... | collective-permute-start | bytes 2359304 | tf_op jit(solution)/shard_map/ppermute | solution.py:670
  113.3 4.1 %shard_map.116 = (f32[128,512]{1,0:T(8,128)S(1)}, f32[8,128]{1,0:T(8,128)S(1)}) custom-call(s32[1]{0:T(128)} %bitcast.refs_0_, bf16[2048,1536]{1,0:T(8,128)(2,1)S(1)} %bitcast.17, f32[32,512]{1,0:T(8,128)S(1)} %get-tuple-element.68.refs_2_.refs_1_, f32[128,512]{1,0:T(8,128)S(1)} %get-tuple-element.87.refs_3_, ...), custom_call_target="tpu_custom_call", output_to_operand_aliasing={{0}: (3, {})} | custom-call | flops 64424508 | bytes 157286 | tf_op jit(solution)/shard_map/pallas_call | solution.py:53
  117.4 1.8 collective-permute-done.14.refs_2_
  119.2 3.5 %shard_map.117 = (bf16[256,1536]{1,0:T(8,128)(2,1)S(1)}, bf16[256,1536]{1,0:T(8,128)(2,1)S(1)}, f32[8,128]{1,0:T(8,128)S(1)}) custom-call(s32[1]{0:T(128)} %bitcast.refs_0_, bf16[256,1536]{1,0:T(8,128)(2,1)S(1)} %collective-permute-done.13.refs_1_, ...), custom_call_target="tpu_custom_call", output_to_operand_aliasing={{0}: (1, {}), {1}: (2, {})} | custom-call | flops 15728 | bytes 47185 | tf_op jit(solution)/shard_map/pallas_call | solution.py:53
  122.7 7.3 %collective-permute-start.21 = (bf16[256,1536]{1,0:T(8,128)(2,1)S(1)}, bf16[256,1536]{1,0:T(8,128)(2,1)S(1)}, u32[]{:S(2)}, u32[]{:S(2)}) collective-permute-start(bf16[256,1536]{1,0:T(8,128)(2,1)S(1)} %get-tuple-element.99.refs_13_), channel_id=1, source_target_pairs={{0,4},{4,0},{8,12},{12,8},{1,5},{5,1},{9,13},{13,9},{2,6},{6,2},{1... | collective-permute-start | bytes 2359304 | tf_op jit(solution)/shard_map/ppermute | solution.py:670
  130.0 0.7 collective-permute-start.22
  130.7 5.6 %shard_map.118 = (f32[512,1536]{1,0:T(8,128)S(1)}, f32[8,128]{1,0:T(8,128)S(1)}) custom-call(s32[1]{0:T(128)} %bitcast.refs_0_, f32[128,512]{1,0:T(8,128)S(1)} %add.22.refs_1_, f32[32,512]{1,0:T(8,128)S(1)} %get-tuple-element.68.refs_2_.refs_1_, bf16[2048,1536]{1,0:T(8,128)(2,1)S(1)} %bitcast.18, f32[512,1536]{1,0:T(8,128)S(1)} %get-tuple-element.69.refs_4_, ...), custom_call_target="tpu_custom_call" | custom-call | flops 64424508 | bytes 157286 | tf_op jit(solution)/shard_map/pallas_call | solution.py:53
  136.3 3.5 %shard_map.119 = (bf16[256,1536]{1,0:T(8,128)(2,1)S(1)}, bf16[256,1536]{1,0:T(8,128)(2,1)S(1)}, f32[8,128]{1,0:T(8,128)S(1)}) custom-call(s32[1]{0:T(128)} %bitcast.refs_0_, bf16[256,1536]{1,0:T(8,128)(2,1)S(1)} %collective-permute-done.17.refs_1_, ...), custom_call_target="tpu_custom_call", output_to_operand_aliasing={{0}: (1, {}), {1}: (2, {})} | custom-call | flops 15728 | bytes 47185 | tf_op jit(solution)/shard_map/pallas_call | solution.py:53
  139.8 7.0 %collective-permute-start.19 = (bf16[256,1536]{1,0:T(8,128)(2,1)S(1)}, bf16[256,1536]{1,0:T(8,128)(2,1)S(1)}, u32[]{:S(2)}, u32[]{:S(2)}) collective-permute-start(bf16[256,1536]{1,0:T(8,128)(2,1)S(1)} %get-tuple-element.97.refs_15_), channel_id=1, source_target_pairs={{0,4},{4,0},{8,12},{12,8},{1,5},{5,1},{9,13},{13,9},{2,6},{6,2},{1... | collective-permute-start | bytes 2359304 | tf_op jit(solution)/shard_map/ppermute | solution.py:670
  146.8 0.9 collective-permute-start.20
  147.7 4.1 %shard_map.120 = (f32[128,512]{1,0:T(8,128)S(1)}, f32[8,128]{1,0:T(8,128)S(1)}) custom-call(s32[1]{0:T(128)} %bitcast.refs_0_, bf16[2048,1536]{1,0:T(8,128)(2,1)S(1)} %bitcast.19, f32[32,512]{1,0:T(8,128)S(1)} %get-tuple-element.68.refs_2_.refs_1_, f32[128,512]{1,0:T(8,128)S(1)} %get-tuple-element.101.refs_3_, ...), custom_call_target="tpu_custom_call", output_to_operand_aliasing={{0}: (3, {})} | custom-call | flops 64424508 | bytes 157286 | tf_op jit(solution)/shard_map/pallas_call | solution.py:53
  151.9 1.1 collective-permute-done.21.refs_1_
  152.9 1.0 shard_map.121
  154.0 1.5 collective-permute-done.23
  155.5 1.6 collective-permute-start.24
  157.1 15.9 %shard_map.122 = (bf16[2048,1536]{1,0:T(8,128)(2,1)}, f32[8,128]{1,0:T(8,128)S(1)}) custom-call(s32[1]{0:T(128)} %bitcast.refs_0_, f32[128,512]{1,0:T(8,128)S(1)} %add.22.refs_1_, f32[32,512]{1,0:T(8,128)S(1)} %get-tuple-element.68.refs_2_.refs_1_, bf16[512,1536]{1,0:T(8,128)(2,1)S(1)} %copy-done.2, bf16[256,1536]{1,0:T(8,128)(2,1)S(1)} %get-tuple-element.73.refs_4_, ...), custom_call_target="tpu_custom_call" | custom-call | flops 257698032 | bytes 251658 | tf_op jit(solution)/shard_map/pallas_call | solution.py:53
  173.0 1.1 shard_map.123
  174.1 0.1 shard_map.125
  174.2 2.3 %collective-permute-start.25 = (bf16[2,512]{1,0:T(2,128)(2,1)S(1)}, bf16[2,512]{1,0:T(2,128)(2,1)S(1)}, u32[]{:S(2)}, u32[]{:S(2)}) collective-permute-start(bf16[2,512]{1,0:T(2,128)(2,1)S(1)} %get-tuple-element.112), channel_id=1, source_target_pairs={{0,12},{4,0},{8,4},{12,8},{1,13},{5,1},{9,5},{13,9},{2,14},{6,2},{... | collective-permute-start | bytes 6152 | tf_op jit(solution)/shard_map/ppermute | solution.py:691
  176.5 3.2 %collective-permute-start.26 = (bf16[2,512]{1,0:T(2,128)(2,1)S(1)}, bf16[2,512]{1,0:T(2,128)(2,1)S(1)}, u32[]{:S(2)}, u32[]{:S(2)}) collective-permute-start(bf16[2,512]{1,0:T(2,128)(2,1)S(1)} %get-tuple-element.113), channel_id=1, source_target_pairs={{0,8},{4,12},{8,0},{12,4},{1,9},{5,13},{9,1},{13,5},{2,10},{6,14},... | collective-permute-start | bytes 6152 | tf_op jit(solution)/shard_map/ppermute | solution.py:691
  179.6 1.6 collective-permute-start.27
  181.2 4.5 %shard_map.126 = (bf16[2048,256]{1,0:T(8,128)(2,1)}, f32[8,128]{1,0:T(8,128)}) custom-call(f32[128,512]{1,0:T(8,128)S(1)} %add.24.refs_0_, f32[32,512]{1,0:T(8,128)S(1)} %get-tuple-element.68.refs_2_.refs_1_, bf16[528,256]{1,0:T(8,128)(2,1)S(1)} %copy-done.5, bf16[528,256]{1,0:T(8,128)(2,1)S(1)} %collective-permute-done.refs_1_.refs_3_, ...), custom_call_target="tpu_custom_call" | custom-call | flops 42949672 | bytes 41943 | tf_op jit(solution)/shard_map/pallas_call | solution.py:53
  185.8 0.6 fusion
  (46 shorter events, 0.3 us)
Async XLA Ops:
  0.6 16.7 %collective-permute-start.3 = (bf16[512,256]{1,0:T(8,128)(2,1)}, bf16[512,256]{1,0:T(8,128)(2,1)S(1)}, u32[]{:S(2)}, u32[]{:S(2)}) collective-permute-start(bf16[512,256]{1,0:T(8,128)(2,1)} %refs_1_.1), channel_id=1, source_target_pairs={{0,1},{1,0},{2,3},{3,2},{4,5},{5,4},{6,7},{7,6},{8,9},{9,8},{10,11... | collective-permute-start | bytes 786440 | tf_op jit(solution)/shard_map/ppermute | solution.py:631
  2.9 16.2 %collective-permute-start.2 = (bf16[528,256]{1,0:T(8,128)(2,1)}, bf16[528,256]{1,0:T(8,128)(2,1)S(1)}, u32[]{:S(2)}, u32[]{:S(2)}) collective-permute-start(bf16[528,256]{1,0:T(8,128)(2,1)} %get-tuple-element.61.refs_2_), channel_id=1, source_target_pairs={{0,12},{4,0},{8,4},{12,8},{1,13},{5,1},{9,5},{13,9},{2,14},{6,2},{... | collective-permute-start | bytes 811016 | tf_op jit(solution)/shard_map/ppermute | solution.py:628
  7.5 23.9 %collective-permute-start.1 = (bf16[528,256]{1,0:T(8,128)(2,1)}, bf16[528,256]{1,0:T(8,128)(2,1)S(1)}, u32[]{:S(2)}, u32[]{:S(2)}) collective-permute-start(bf16[528,256]{1,0:T(8,128)(2,1)} %get-tuple-element.61.refs_2_), channel_id=1, source_target_pairs={{0,8},{4,12},{8,0},{12,4},{1,9},{5,13},{9,1},{13,5},{2,10},{6,14},... | collective-permute-start | bytes 811016 | tf_op jit(solution)/shard_map/ppermute | solution.py:628
  7.5 23.9 %collective-permute-start = (bf16[528,256]{1,0:T(8,128)(2,1)}, bf16[528,256]{1,0:T(8,128)(2,1)S(1)}, u32[]{:S(2)}, u32[]{:S(2)}) collective-permute-start(bf16[528,256]{1,0:T(8,128)(2,1)} %get-tuple-element.61.refs_2_), channel_id=1, source_target_pairs={{0,4},{4,8},{8,12},{12,0},{1,5},{5,9},{9,13},{13,1},{2,6},{6,10},{... | collective-permute-start | bytes 811016 | tf_op jit(solution)/shard_map/ppermute | solution.py:628
  8.5 2.8 %copy-start = (bf16[128,16,1536]{2,1,0:T(8,128)(2,1)S(1)}, bf16[128,16,1536]{2,1,0:T(8,128)(2,1)}, u32[]{:S(2)}) copy-start(bf16[128,16,1536]{2,1,0:T(8,128)(2,1)} %param.10) | copy-start | bytes 18874372
  11.3 1.4 copy-start.1
  12.7 0.7 copy-start.6
  13.4 3.9 %copy-start.4 = (bf16[512,256]{1,0:T(8,128)(2,1)S(1)}, bf16[512,256]{1,0:T(8,128)(2,1)}, u32[]{:S(2)}) copy-start(bf16[512,256]{1,0:T(8,128)(2,1)} %refs_1_.1) | copy-start | bytes 786436
  17.4 15.7 %collective-permute-start.4 = (bf16[1024,256]{1,0:T(8,128)(2,1)S(1)}, bf16[1024,256]{1,0:T(8,128)(2,1)S(1)}, u32[]{:S(2)}, u32[]{:S(2)}) collective-permute-start(bf16[1024,256]{1,0:T(8,128)(2,1)S(1)} %pad_maximum_fusion), channel_id=1, source_target_pairs={{0,2},{1,3},{2,0},{3,1},{4,6},{5,7},{6,4},{7,5},{8,10},{9,11},{10,... | collective-permute-start | bytes 1572872 | tf_op jit(solution)/shard_map/ppermute | solution.py:631
  31.4 1.9 %copy-start.3 = (bf16[1536,1024]{1,0:T(8,128)(2,1)S(1)}, bf16[1536,1024]{1,0:T(8,128)(2,1)}, u32[]{:S(2)}) copy-start(bf16[1536,1024]{1,0:T(8,128)(2,1)} %refs_4_.3) | copy-start | bytes 9437188
  31.4 24.4 %collective-permute-start.8 = (bf16[256,1536]{1,0:T(8,128)(2,1)S(1)}, bf16[256,1536]{1,0:T(8,128)(2,1)S(1)}, u32[]{:S(2)}, u32[]{:S(2)}) collective-permute-start(bf16[256,1536]{1,0:T(8,128)(2,1)S(1)} %get-tuple-element.70), channel_id=1, source_target_pairs={{0,4},{4,0},{8,12},{12,8},{1,5},{5,1},{9,13},{13,9},{2,6},{6,2},{1... | collective-permute-start | bytes 2359304 | tf_op jit(solution)/shard_map/ppermute | solution.py:643
  32.4 23.4 %collective-permute-start.7 = (bf16[256,1536]{1,0:T(8,128)(2,1)S(1)}, bf16[256,1536]{1,0:T(8,128)(2,1)S(1)}, u32[]{:S(2)}, u32[]{:S(2)}) collective-permute-start(bf16[256,1536]{1,0:T(8,128)(2,1)S(1)} %get-tuple-element.70), channel_id=1, source_target_pairs={{4,8},{8,4},{5,9},{9,5},{6,10},{10,6},{7,11},{11,7},{20,24},{24,20... | collective-permute-start | bytes 2359304 | tf_op jit(solution)/shard_map/ppermute | solution.py:643
  33.3 2.5 %copy-start.5 = (bf16[528,256]{1,0:T(8,128)(2,1)S(1)}, bf16[528,256]{1,0:T(8,128)(2,1)}, u32[]{:S(2)}) copy-start(bf16[528,256]{1,0:T(8,128)(2,1)} %get-tuple-element.61.refs_2_) | copy-start | bytes 811012
  33.3 2.5 %copy-start.7 = (bf16[128,16,256]{2,1,0:T(8,128)(2,1)S(1)}, bf16[128,16,256]{2,1,0:T(8,128)(2,1)}, u32[]{:S(2)}) copy-start(bf16[128,16,256]{2,1,0:T(8,128)(2,1)} %param.11) | copy-start | bytes 3145732
  35.7 14.8 %slice-start = ((s8[6291456]{0:T(1024)(128)(4,1)}), s8[4194304]{0:T(1024)(128)(4,1)S(1)}, s32[]{:S(2)}) async-start(s8[6291456]{0:T(1024)(128)(4,1)} %bitcast.11), calls=%async_computation | async-start | bytes 8388608
  35.7 14.7 %slice-start.1 = ((s8[6291456]{0:T(1024)(128)(4,1)}), s8[2097152]{0:T(1024)(128)(4,1)S(1)}, s32[]{:S(2)}) async-start(s8[6291456]{0:T(1024)(128)(4,1)} %bitcast.11), calls=%async_computation.1 | async-start | bytes 4194304
  40.4 1.6 collective-permute-start.5
  42.0 8.4 %collective-permute-start.6 = (f32[128,512]{1,0:T(8,128)S(1)}, f32[128,512]{1,0:T(8,128)S(1)}, u32[]{:S(2)}, u32[]{:S(2)}) collective-permute-start(f32[128,512]{1,0:T(8,128)S(1)} %add.21), channel_id=1, source_target_pairs={{0,2},{1,3},{2,0},{3,1},{4,6},{5,7},{6,4},{7,5},{8,10},{9,11},{10,... | collective-permute-start | bytes 786440 | tf_op jit(solution)/shard_map/ppermute | solution.py:620
  43.6 25.1 %collective-permute-start.12 = (bf16[256,1536]{1,0:T(8,128)(2,1)S(1)}, bf16[256,1536]{1,0:T(8,128)(2,1)S(1)}, u32[]{:S(2)}, u32[]{:S(2)}) collective-permute-start(bf16[256,1536]{1,0:T(8,128)(2,1)S(1)} %get-tuple-element.78), channel_id=1, source_target_pairs={{0,4},{4,0},{8,12},{12,8},{1,5},{5,1},{9,13},{13,9},{2,6},{6,2},{1... | collective-permute-start | bytes 2359304 | tf_op jit(solution)/shard_map/ppermute | solution.py:643
  47.3 21.4 %collective-permute-start.11 = (bf16[256,1536]{1,0:T(8,128)(2,1)S(1)}, bf16[256,1536]{1,0:T(8,128)(2,1)S(1)}, u32[]{:S(2)}, u32[]{:S(2)}) collective-permute-start(bf16[256,1536]{1,0:T(8,128)(2,1)S(1)} %get-tuple-element.78), channel_id=1, source_target_pairs={{4,8},{8,4},{5,9},{9,5},{6,10},{10,6},{7,11},{11,7},{20,24},{24,20... | collective-permute-start | bytes 2359304 | tf_op jit(solution)/shard_map/ppermute | solution.py:643
  59.3 21.2 %collective-permute-start.9 = (bf16[256,1536]{1,0:T(8,128)(2,1)S(1)}, bf16[256,1536]{1,0:T(8,128)(2,1)S(1)}, u32[]{:S(2)}, u32[]{:S(2)}) collective-permute-start(bf16[256,1536]{1,0:T(8,128)(2,1)S(1)} %get-tuple-element.73.refs_4_), channel_id=1, source_target_pairs={{4,8},{8,4},{5,9},{9,5},{6,10},{10,6},{7,11},{11,7},{20,24},{24,20... | collective-permute-start | bytes 2359304 | tf_op jit(solution)/shard_map/ppermute | solution.py:670
  60.0 25.5 %collective-permute-start.10 = (bf16[256,1536]{1,0:T(8,128)(2,1)S(1)}, bf16[256,1536]{1,0:T(8,128)(2,1)S(1)}, u32[]{:S(2)}, u32[]{:S(2)}) collective-permute-start(bf16[256,1536]{1,0:T(8,128)(2,1)S(1)} %get-tuple-element.74.refs_6_.refs_5_), channel_id=1, source_target_pairs={{0,4},{4,0},{8,12},{12,8},{1,5},{5,1},{9,13},{13,9},{2,6},{6,2},{1... | collective-permute-start | bytes 2359304 | tf_op jit(solution)/shard_map/ppermute | solution.py:670
  72.1 29.6 %collective-permute-start.15 = (bf16[256,1536]{1,0:T(8,128)(2,1)S(1)}, bf16[256,1536]{1,0:T(8,128)(2,1)S(1)}, u32[]{:S(2)}, u32[]{:S(2)}) collective-permute-start(bf16[256,1536]{1,0:T(8,128)(2,1)S(1)} %get-tuple-element.80.refs_5_.refs_6_), channel_id=1, source_target_pairs={{4,8},{8,4},{5,9},{9,5},{6,10},{10,6},{7,11},{11,7},{20,24},{24,20... | collective-permute-start | bytes 2359304 | tf_op jit(solution)/shard_map/ppermute | solution.py:670
  73.0 29.3 %collective-permute-start.16 = (bf16[256,1536]{1,0:T(8,128)(2,1)S(1)}, bf16[256,1536]{1,0:T(8,128)(2,1)S(1)}, u32[]{:S(2)}, u32[]{:S(2)}) collective-permute-start(bf16[256,1536]{1,0:T(8,128)(2,1)S(1)} %get-tuple-element.88.refs_7_), channel_id=1, source_target_pairs={{0,4},{4,0},{8,12},{12,8},{1,5},{5,1},{9,13},{13,9},{2,6},{6,2},{1... | collective-permute-start | bytes 2359304 | tf_op jit(solution)/shard_map/ppermute | solution.py:670
  89.0 28.5 %collective-permute-start.13 = (bf16[256,1536]{1,0:T(8,128)(2,1)S(1)}, bf16[256,1536]{1,0:T(8,128)(2,1)S(1)}, u32[]{:S(2)}, u32[]{:S(2)}) collective-permute-start(bf16[256,1536]{1,0:T(8,128)(2,1)S(1)} %get-tuple-element.83.refs_4_.refs_8_), channel_id=1, source_target_pairs={{4,8},{8,4},{5,9},{9,5},{6,10},{10,6},{7,11},{11,7},{20,24},{24,20... | collective-permute-start | bytes 2359304 | tf_op jit(solution)/shard_map/ppermute | solution.py:670
  89.7 29.5 %collective-permute-start.14 = (bf16[256,1536]{1,0:T(8,128)(2,1)S(1)}, bf16[256,1536]{1,0:T(8,128)(2,1)S(1)}, u32[]{:S(2)}, u32[]{:S(2)}) collective-permute-start(bf16[256,1536]{1,0:T(8,128)(2,1)S(1)} %get-tuple-element.84.refs_6_.refs_9_), channel_id=1, source_target_pairs={{0,4},{4,0},{8,12},{12,8},{1,5},{5,1},{9,13},{13,9},{2,6},{6,2},{1... | collective-permute-start | bytes 2359304 | tf_op jit(solution)/shard_map/ppermute | solution.py:670
  105.8 30.5 %collective-permute-start.17 = (bf16[256,1536]{1,0:T(8,128)(2,1)S(1)}, bf16[256,1536]{1,0:T(8,128)(2,1)S(1)}, u32[]{:S(2)}, u32[]{:S(2)}) collective-permute-start(bf16[256,1536]{1,0:T(8,128)(2,1)S(1)} %get-tuple-element.90.refs_5_.refs_10_), channel_id=1, source_target_pairs={{4,8},{8,4},{5,9},{9,5},{6,10},{10,6},{7,11},{11,7},{20,24},{24,20... | collective-permute-start | bytes 2359304 | tf_op jit(solution)/shard_map/ppermute | solution.py:670
  106.5 29.8 %collective-permute-start.18 = (bf16[256,1536]{1,0:T(8,128)(2,1)S(1)}, bf16[256,1536]{1,0:T(8,128)(2,1)S(1)}, u32[]{:S(2)}, u32[]{:S(2)}) collective-permute-start(bf16[256,1536]{1,0:T(8,128)(2,1)S(1)} %get-tuple-element.95.refs_7_.refs_11_), channel_id=1, source_target_pairs={{0,4},{4,0},{8,12},{12,8},{1,5},{5,1},{9,13},{13,9},{2,6},{6,2},{1... | collective-permute-start | bytes 2359304 | tf_op jit(solution)/shard_map/ppermute | solution.py:670
  122.7 30.2 %collective-permute-start.21 = (bf16[256,1536]{1,0:T(8,128)(2,1)S(1)}, bf16[256,1536]{1,0:T(8,128)(2,1)S(1)}, u32[]{:S(2)}, u32[]{:S(2)}) collective-permute-start(bf16[256,1536]{1,0:T(8,128)(2,1)S(1)} %get-tuple-element.99.refs_13_), channel_id=1, source_target_pairs={{0,4},{4,0},{8,12},{12,8},{1,5},{5,1},{9,13},{13,9},{2,6},{6,2},{1... | collective-permute-start | bytes 2359304 | tf_op jit(solution)/shard_map/ppermute | solution.py:670
  130.0 23.0 %collective-permute-start.22 = (bf16[256,1536]{1,0:T(8,128)(2,1)S(1)}, bf16[256,1536]{1,0:T(8,128)(2,1)S(1)}, u32[]{:S(2)}, u32[]{:S(2)}) collective-permute-start(bf16[256,1536]{1,0:T(8,128)(2,1)S(1)} %get-tuple-element.100.refs_4_.refs_12_), channel_id=1, source_target_pairs={{4,8},{8,4},{5,9},{9,5},{6,10},{10,6},{7,11},{11,7},{20,24},{24,20... | collective-permute-start | bytes 2359304 | tf_op jit(solution)/shard_map/ppermute | solution.py:670
  139.8 33.2 %collective-permute-start.19 = (bf16[256,1536]{1,0:T(8,128)(2,1)S(1)}, bf16[256,1536]{1,0:T(8,128)(2,1)S(1)}, u32[]{:S(2)}, u32[]{:S(2)}) collective-permute-start(bf16[256,1536]{1,0:T(8,128)(2,1)S(1)} %get-tuple-element.97.refs_15_), channel_id=1, source_target_pairs={{0,4},{4,0},{8,12},{12,8},{1,5},{5,1},{9,13},{13,9},{2,6},{6,2},{1... | collective-permute-start | bytes 2359304 | tf_op jit(solution)/shard_map/ppermute | solution.py:670
  146.8 26.2 %collective-permute-start.20 = (bf16[256,1536]{1,0:T(8,128)(2,1)S(1)}, bf16[256,1536]{1,0:T(8,128)(2,1)S(1)}, u32[]{:S(2)}, u32[]{:S(2)}) collective-permute-start(bf16[256,1536]{1,0:T(8,128)(2,1)S(1)} %get-tuple-element.98.refs_5_.refs_14_), channel_id=1, source_target_pairs={{4,8},{8,4},{5,9},{9,5},{6,10},{10,6},{7,11},{11,7},{20,24},{24,20... | collective-permute-start | bytes 2359304 | tf_op jit(solution)/shard_map/ppermute | solution.py:670
  152.9 4.2 %copy-start.2 = (bf16[512,1536]{1,0:T(8,128)(2,1)S(1)}, bf16[512,1536]{1,0:T(8,128)(2,1)}, u32[]{:S(2)}) copy-start(bf16[512,1536]{1,0:T(8,128)(2,1)} %refs_3_.3) | copy-start | bytes 4718596
  154.0 1.5 collective-permute-start.23
  155.5 18.5 %collective-permute-start.24 = (f32[128,512]{1,0:T(8,128)S(1)}, f32[128,512]{1,0:T(8,128)S(1)}, u32[]{:S(2)}, u32[]{:S(2)}) collective-permute-start(f32[128,512]{1,0:T(8,128)S(1)} %add.23), channel_id=1, source_target_pairs={{0,2},{1,3},{2,0},{3,1},{4,6},{5,7},{6,4},{7,5},{8,10},{9,11},{10,... | collective-permute-start | bytes 786440 | tf_op jit(solution)/shard_map/ppermute | solution.py:620
  174.2 11.6 %collective-permute-start.25 = (bf16[2,512]{1,0:T(2,128)(2,1)S(1)}, bf16[2,512]{1,0:T(2,128)(2,1)S(1)}, u32[]{:S(2)}, u32[]{:S(2)}) collective-permute-start(bf16[2,512]{1,0:T(2,128)(2,1)S(1)} %get-tuple-element.112), channel_id=1, source_target_pairs={{0,12},{4,0},{8,4},{12,8},{1,13},{5,1},{9,5},{13,9},{2,14},{6,2},{... | collective-permute-start | bytes 6152 | tf_op jit(solution)/shard_map/ppermute | solution.py:691
  176.5 9.3 %collective-permute-start.26 = (bf16[2,512]{1,0:T(2,128)(2,1)S(1)}, bf16[2,512]{1,0:T(2,128)(2,1)S(1)}, u32[]{:S(2)}, u32[]{:S(2)}) collective-permute-start(bf16[2,512]{1,0:T(2,128)(2,1)S(1)} %get-tuple-element.113), channel_id=1, source_target_pairs={{0,8},{4,12},{8,0},{12,4},{1,9},{5,13},{9,1},{13,5},{2,10},{6,14},... | collective-permute-start | bytes 6152 | tf_op jit(solution)/shard_map/ppermute | solution.py:691
  179.6 6.1 %collective-permute-start.27 = (bf16[2,512]{1,0:T(2,128)(2,1)S(1)}, bf16[2,512]{1,0:T(2,128)(2,1)S(1)}, u32[]{:S(2)}, u32[]{:S(2)}) collective-permute-start(bf16[2,512]{1,0:T(2,128)(2,1)S(1)} %get-tuple-element.114), channel_id=1, source_target_pairs={{0,4},{4,8},{8,12},{12,0},{1,5},{5,9},{9,13},{13,1},{2,6},{6,10},{... | collective-permute-start | bytes 6152 | tf_op jit(solution)/shard_map/ppermute | solution.py:691

commit v5 on v4

--- a/solution.py
+++ b/solution.py
@@ -405,7 +405,7 @@
 
 def ring_add(pos, size, step_index, row, first, second, near, far, after):
     shape = first.shape
-    pieces = 4 if shape[0] % 64 == 0 else 1
+    pieces = 1
     return call(
         functools.partial(add_body, size, step_index, row),
         [jax.ShapeDtypeStruct(shape, BF)] * 2,
@@ -639,7 +639,9 @@
     low = jnp.zeros((size * 2 * rank, count), F32)
     low, token = project_in(pos, size, [(-1, True)], down, aux_own, low, [inputs], 1, rank)
 
-    sent, tokens = zip(*[pin(inputs[c * half : (c + 1) * half], blocks[1:]) for c in range(CHUNKS)])
+    sent, tokens = zip(
+        *[pin(inputs[c * half : (c + 1) * half], [token] if c == 0 else blocks[1:]) for c in range(CHUNKS)]
+    )
     got = [[lax.ppermute(sent[c], "dp", p) for p in (pairs_a, pairs_b)] for c in range(CHUNKS)]
 
     frozen, token = frozen_product(share, output_gradient, next_out, far_out, frozen_key_weight, [token])
@@ -679,13 +681,12 @@
         low, token = add_projection(low, ready, token)
 
     result, token = finish(far, got[0][0], got[0][1], 0, None, [token])
-    low, _ = pin(low, [token])
     part_in = exchange(low)
+    *gate_rows, token = grad_gates(part_in, part_out, size, rank, [token])
     down_gradient, token = grad_down(pos, size, part_out, aux, rows, where, total, rank, [token])
+    up_gradient, token = grad_up(part_in, aux, blocks, total, rank, [token])
     for c in range(1, CHUNKS):
         result, token = finish(far, got[c][0], got[c][1], c, result, [token])
-    *gate_rows, token = grad_gates(part_in, part_out, size, rank, [token])
-    up_gradient, _ = grad_up(part_in, aux, blocks, total, rank, [token])
     gate_sum = gate_rows[0].astype(F32)
     for s in range(1, size):
         gate_sum = gate_sum + lax.ppermute(

time: 187 us -> 183 us (0.979)
  Pallas kernels: 89.5 us -> 74.8 us
  waiting for transfers between devices: 27.5 us -> 34.6 us
    pallas_call x25 -> x24, Pallas kernels: 89.5 us -> 74.8 us  [call(): return lambda *arrays: call_it(*arrays, *after)]
    ppermute x4, waiting for transfers between devices: 5.48 us -> 16.8 us  [exchange(): lax.ppermute(part, 'mp', [(i, i ^ bit) for i in range(shares)])]
    ppermute x3, waiting for transfers between devices: 12.3 us -> 1.27 us  [per_device(): lax.ppermute(block, 'dp', [(i, (i + s) % size) for i in range(size)])]
    ppermute x6, waiting for transfers between devices: 8.44 us -> 16.5 us  [per_device(): lax.ppermute(to_a, 'dp', pairs_a)]
    ppermute x4, starting transfers between devices: 6.12 us -> 12.9 us  [per_device(): lax.ppermute(sent[c], 'dp', p)]
    ppermute x6, starting transfers between devices: 33.6 us -> 29.2 us  [per_device(): lax.ppermute(to_a, 'dp', pairs_a)]
    ppermute x3, starting transfers between devices: 7.05 us -> 4.98 us  [per_device(): lax.ppermute(gate_rows[s], 'dp', [(i, (i - s) % size) for i in range(size)])]
    unnamed x20 -> x24, local copies, waits for them, and re-layouts: 5.11 us -> 6.84 us
  transfers between devices with their start and end apart: 28 -> 28, of which waited for: 9 -> 9; matrix products, arithmetic and copies ran while one was open for 0% -> 1% of each run, Pallas kernels for 48% -> 41%
where the time goes in v5:
time: 183 us; the launch traced here: 182 us
  Pallas kernels  74.8 us (41%)
  starting transfers between devices  63.1 us (34%)
  waiting for transfers between devices  34.6 us (19%)
  local copies, waits for them, and re-layouts  6.96 us (4%)
    pallas_call x24, Pallas kernels, call(): return lambda *arrays: call_it(*arrays, *after)  74.8 us
    ppermute x6, starting transfers between devices, per_device(): lax.ppermute(to_a, 'dp', pairs_a)  29.2 us
    ppermute x4, waiting for transfers between devices, exchange(): lax.ppermute(part, 'mp', [(i, i ^ bit) for i in range(shares)])  16.8 us
    ppermute x6, waiting for transfers between devices, per_device(): lax.ppermute(to_a, 'dp', pairs_a)  16.5 us
    ppermute x4, starting transfers between devices, per_device(): lax.ppermute(sent[c], 'dp', p)  12.9 us
    unnamed x24, local copies, waits for them, and re-layouts  6.84 us
    ppermute x3, starting transfers between devices, per_device(): lax.ppermute(block, 'dp', [(i, (i + s) % size) for i in range(size)])  6.53 us
    ppermute x3, starting transfers between devices, per_device(): lax.ppermute(gate_rows[s], 'dp', [(i, (i - s) % size) for i in range(size)])  4.98 us
  transfers between devices with their start and end apart: 28, of which 9 were waited for; matrix products, arithmetic and copies ran while one was open for 1% of the time, Pallas kernels for 41%

profile of v5, /device:TPU:0, one launch (start us, length us, event | category | flops | bytes accessed | tf_op | source)
XLA Modules:
  0.0 182.2 jit_solution(16423448555062379983)
XLA Ops:
  0.6 0.5 collective-permute-start.3
  1.1 1.7 shard_map.102
  2.9 2.6 %collective-permute-start = (bf16[528,256]{1,0:T(8,128)(2,1)}, bf16[528,256]{1,0:T(8,128)(2,1)S(1)}, u32[]{:S(2)}, u32[]{:S(2)}) collective-permute-start(bf16[528,256]{1,0:T(8,128)(2,1)} %get-tuple-element.60.refs_2_), channel_id=1, source_target_pairs={{0,4},{4,8},{8,12},{12,0},{1,5},{5,9},{9,13},{13,1},{2,6},{6,10},{... | collective-permute-start | bytes 811016 | tf_op jit(solution)/shard_map/ppermute | solution.py:628
  5.5 2.6 %collective-permute-start.1 = (bf16[528,256]{1,0:T(8,128)(2,1)}, bf16[528,256]{1,0:T(8,128)(2,1)S(1)}, u32[]{:S(2)}, u32[]{:S(2)}) collective-permute-start(bf16[528,256]{1,0:T(8,128)(2,1)} %get-tuple-element.60.refs_2_), channel_id=1, source_target_pairs={{0,8},{4,12},{8,0},{12,4},{1,9},{5,13},{9,1},{13,5},{2,10},{6,14},... | collective-permute-start | bytes 811016 | tf_op jit(solution)/shard_map/ppermute | solution.py:628
  8.0 1.3 collective-permute-start.2
  9.4 2.8 %copy-done = bf16[128,16,1536]{2,1,0:T(8,128)(2,1)S(1)} copy-done((bf16[128,16,1536]{2,1,0:T(8,128)(2,1)S(1)}, bf16[128,16,1536]{2,1,0:T(8,128)(2,1)}, u32[]{:S(2)}) %copy-start) | copy-done | bytes 6291480
  12.2 1.4 copy-done.1
  13.6 0.7 copy-done.8
  14.3 3.9 %shard_map.103 = (f32[128,512]{1,0:T(8,128)S(1)}, f32[8,128]{1,0:T(8,128)S(1)}) custom-call(s32[1]{0:T(128)} %bitcast.refs_0_, bf16[2048,1536]{1,0:T(8,128)(2,1)S(1)} %bitcast.10, f32[8,512]{1,0:T(8,128)S(1)} %copy-done.8, f32[128,512]{1,0:T(8,128)S(1)} %broadcast_in_dim.3.refs_3_, bf16[512,1536]{1,0:T(8,128)(2,1)S(1)} %copy-done.1), custom_call_target="tpu_custom_call", output_to_operand_aliasing={{0}: (3, {})} | custom-call | flops 64424508 | bytes 157286 | tf_op jit(solution)/shard_map/pallas_call | solution.py:53
  18.3 0.9 pad_maximum_fusion
  19.2 1.5 collective-permute-start.4
  20.6 0.1 fusion.1
  20.8 0.7 collective-permute-start.7
  21.5 3.8 %collective-permute-start.8 = (bf16[256,1536]{1,0:T(8,128)(2,1)S(1)}, bf16[256,1536]{1,0:T(8,128)(2,1)S(1)}, u32[]{:S(2)}, u32[]{:S(2)}) collective-permute-start(bf16[256,1536]{1,0:T(8,128)(2,1)S(1)} %get-tuple-element.69), channel_id=1, source_target_pairs={{0,4},{4,0},{8,12},{12,8},{1,5},{5,1},{9,13},{13,9},{2,6},{6,2},{1... | collective-permute-start | bytes 2359304 | tf_op jit(solution)/shard_map/ppermute | solution.py:645
  25.3 1.3 collective-permute-done.1.refs_2_.refs_4_
  26.6 0.7 collective-permute-start.11
  27.3 7.7 %collective-permute-start.12 = (bf16[256,1536]{1,0:T(8,128)(2,1)S(1)}, bf16[256,1536]{1,0:T(8,128)(2,1)S(1)}, u32[]{:S(2)}, u32[]{:S(2)}) collective-permute-start(bf16[256,1536]{1,0:T(8,128)(2,1)S(1)} %get-tuple-element.77), channel_id=1, source_target_pairs={{0,4},{4,0},{8,12},{12,8},{1,5},{5,1},{9,13},{13,9},{2,6},{6,2},{1... | collective-permute-start | bytes 2359304 | tf_op jit(solution)/shard_map/ppermute | solution.py:645
  35.0 1.9 %copy-done.3 = bf16[1536,1024]{1,0:T(8,128)(2,1)S(1)} copy-done((bf16[1536,1024]{1,0:T(8,128)(2,1)S(1)}, bf16[1536,1024]{1,0:T(8,128)(2,1)}, u32[]{:S(2)}) %copy-start.3) | copy-done | bytes 3145752
  36.9 3.6 %shard_map.104 = (f32[512,1536]{1,0:T(8,128)S(1)}, f32[8,128]{1,0:T(8,128)S(1)}) custom-call(s32[1]{0:T(128)} %bitcast.4.refs_0_, bf16[512,256]{1,0:T(8,128)(2,1)S(1)} %copy-done.4, bf16[512,256]{1,0:T(8,128)(2,1)S(1)} %copy-done.6, bf16[1024,256]{1,0:T(8,128)(2,1)} %collective-permute-done.4.refs_3_, bf16[1536,1024]{1,0:T(8,128)(2,1)S(1)} %copy-done.3, ...), custom_call_target="tpu_custom_call" | custom-call | flops 32212254 | bytes 62914 | tf_op jit(solution)/shard_map/pallas_call | solution.py:53
  40.6 5.7 %shard_map.107 = (f32[128,512]{1,0:T(8,128)S(1)}, f32[32,512]{1,0:T(8,128)S(1)}, f32[8,128]{1,0:T(8,128)}) custom-call(s32[1]{0:T(128)} %bitcast.refs_0_, bf16[2048,256]{1,0:T(8,128)(2,1)S(1)} %bitcast.20, bf16[528,256]{1,0:T(8,128)(2,1)S(1)} %copy-done.7, bf16[528,256]{1,0:T(8,128)(2,1)S(1)} %collective-permute-done.refs_1_.refs_3_, ...), custom_call_target="tpu_custom_call" | custom-call | flops 10737418240 | bytes 10485760 | tf_op jit(solution)/shard_map/pallas_call | solution.py:53
  46.3 0.1 collective-permute-start.5
  46.4 1.5 collective-permute-done.5
  47.9 1.5 collective-permute-start.6
  49.5 6.9 %collective-permute-done.6 = f32[128,512]{1,0:T(8,128)S(1)} collective-permute-done((f32[128,512]{1,0:T(8,128)S(1)}, f32[128,512]{1,0:T(8,128)S(1)}, u32[]{:S(2)}, u32[]{:S(2)}) %collective-permute-start.6) | collective-permute-done | bytes 262176 | tf_op jit(solution)/shard_map/ppermute | solution.py:620
  56.4 5.3 %shard_map.108 = (bf16[512,1536]{1,0:T(8,128)(2,1)S(1)}, f32[8,128]{1,0:T(8,128)S(1)}) custom-call(s32[1]{0:T(128)} %bitcast.refs_0_, f32[128,512]{1,0:T(8,128)S(1)} %add.22.refs_1_, f32[32,512]{1,0:T(8,128)S(1)} %get-tuple-element.67.refs_2_.refs_1_, bf16[2048,1536]{1,0:T(8,128)(2,1)S(1)} %bitcast.13), custom_call_target="tpu_custom_call" | custom-call | flops 64424508 | bytes 157286 | tf_op jit(solution)/shard_map/pallas_call | solution.py:53
  61.7 0.4 shard_map.109
  62.2 0.1 collective-permute-start.10
  62.2 0.7 collective-permute-start.9
  63.0 5.3 %shard_map.110 = (bf16[512,1536]{1,0:T(8,128)(2,1)S(1)}, f32[8,128]{1,0:T(8,128)S(1)}) custom-call(s32[1]{0:T(128)} %bitcast.refs_0_, f32[128,512]{1,0:T(8,128)S(1)} %add.22.refs_1_, f32[32,512]{1,0:T(8,128)S(1)} %get-tuple-element.67.refs_2_.refs_1_, bf16[2048,1536]{1,0:T(8,128)(2,1)S(1)} %bitcast.14, f32[8,128]{1,0:T(8,128)S(1)} %get-tuple-element.74.refs_4_), custom_call_target="tpu_custom_call" | custom-call | flops 64424508 | bytes 157286 | tf_op jit(solution)/shard_map/pallas_call | solution.py:53
  68.2 0.4 shard_map.111
  68.7 0.7 collective-permute-start.15
  69.4 6.1 %collective-permute-start.16 = (bf16[256,1536]{1,0:T(8,128)(2,1)S(1)}, bf16[256,1536]{1,0:T(8,128)(2,1)S(1)}, u32[]{:S(2)}, u32[]{:S(2)}) collective-permute-start(bf16[256,1536]{1,0:T(8,128)(2,1)S(1)} %get-tuple-element.87.refs_7_), channel_id=1, source_target_pairs={{0,4},{4,0},{8,12},{12,8},{1,5},{5,1},{9,13},{13,9},{2,6},{6,2},{1... | collective-permute-start | bytes 2359304 | tf_op jit(solution)/shard_map/ppermute | solution.py:672
  75.6 3.9 %shard_map.112 = (f32[128,512]{1,0:T(8,128)S(1)}, f32[8,128]{1,0:T(8,128)S(1)}) custom-call(s32[1]{0:T(128)} %bitcast.refs_0_, bf16[2048,1536]{1,0:T(8,128)(2,1)S(1)} %bitcast.15, f32[32,512]{1,0:T(8,128)S(1)} %get-tuple-element.67.refs_2_.refs_1_, f32[128,512]{1,0:T(8,128)S(1)} %get-tuple-element.76.refs_3_, ...), custom_call_target="tpu_custom_call", output_to_operand_aliasing={{0}: (3, {})} | custom-call | flops 64424508 | bytes 157286 | tf_op jit(solution)/shard_map/pallas_call | solution.py:53
  79.5 3.2 %collective-permute-done.10.refs_2_ = bf16[256,1536]{1,0:T(8,128)(2,1)S(1)} collective-permute-done((bf16[256,1536]{1,0:T(8,128)(2,1)S(1)}, bf16[256,1536]{1,0:T(8,128)(2,1)S(1)}, u32[]{:S(2)}, u32[]{:S(2)}) %collective-permute-start.10) | collective-permute-done | bytes 786464 | tf_op jit(solution)/shard_map/ppermute | solution.py:672
  82.7 0.6 shard_map.113
  83.3 0.7 collective-permute-start.13
  84.0 7.2 %collective-permute-start.14 = (bf16[256,1536]{1,0:T(8,128)(2,1)S(1)}, bf16[256,1536]{1,0:T(8,128)(2,1)S(1)}, u32[]{:S(2)}, u32[]{:S(2)}) collective-permute-start(bf16[256,1536]{1,0:T(8,128)(2,1)S(1)} %get-tuple-element.83.refs_6_.refs_9_), channel_id=1, source_target_pairs={{0,4},{4,0},{8,12},{12,8},{1,5},{5,1},{9,13},{13,9},{2,6},{6,2},{1... | collective-permute-start | bytes 2359304 | tf_op jit(solution)/shard_map/ppermute | solution.py:672
  91.2 5.2 %shard_map.114 = (bf16[512,1536]{1,0:T(8,128)(2,1)S(1)}, f32[8,128]{1,0:T(8,128)S(1)}) custom-call(s32[1]{0:T(128)} %bitcast.refs_0_, f32[128,512]{1,0:T(8,128)S(1)} %add.22.refs_1_, f32[32,512]{1,0:T(8,128)S(1)} %get-tuple-element.67.refs_2_.refs_1_, bf16[2048,1536]{1,0:T(8,128)(2,1)S(1)} %bitcast.16, f32[8,128]{1,0:T(8,128)S(1)} %get-tuple-element.84.refs_4_), custom_call_target="tpu_custom_call" | custom-call | flops 64424508 | bytes 157286 | tf_op jit(solution)/shard_map/pallas_call | solution.py:53
  96.5 3.1 %collective-permute-done.16.refs_2_ = bf16[256,1536]{1,0:T(8,128)(2,1)S(1)} collective-permute-done((bf16[256,1536]{1,0:T(8,128)(2,1)S(1)}, bf16[256,1536]{1,0:T(8,128)(2,1)S(1)}, u32[]{:S(2)}, u32[]{:S(2)}) %collective-permute-start.16) | collective-permute-done | bytes 786464 | tf_op jit(solution)/shard_map/ppermute | solution.py:672
  99.6 0.4 shard_map.115
  100.0 0.7 collective-permute-start.17
  100.7 7.2 %collective-permute-start.18 = (bf16[256,1536]{1,0:T(8,128)(2,1)S(1)}, bf16[256,1536]{1,0:T(8,128)(2,1)S(1)}, u32[]{:S(2)}, u32[]{:S(2)}) collective-permute-start(bf16[256,1536]{1,0:T(8,128)(2,1)S(1)} %get-tuple-element.94.refs_7_.refs_11_), channel_id=1, source_target_pairs={{0,4},{4,0},{8,12},{12,8},{1,5},{5,1},{9,13},{13,9},{2,6},{6,2},{1... | collective-permute-start | bytes 2359304 | tf_op jit(solution)/shard_map/ppermute | solution.py:672
  107.9 4.1 %shard_map.116 = (f32[128,512]{1,0:T(8,128)S(1)}, f32[8,128]{1,0:T(8,128)S(1)}) custom-call(s32[1]{0:T(128)} %bitcast.refs_0_, bf16[2048,1536]{1,0:T(8,128)(2,1)S(1)} %bitcast.17, f32[32,512]{1,0:T(8,128)S(1)} %get-tuple-element.67.refs_2_.refs_1_, f32[128,512]{1,0:T(8,128)S(1)} %get-tuple-element.86.refs_3_, ...), custom_call_target="tpu_custom_call", output_to_operand_aliasing={{0}: (3, {})} | custom-call | flops 64424508 | bytes 157286 | tf_op jit(solution)/shard_map/pallas_call | solution.py:53
  112.0 4.4 %collective-permute-done.14.refs_2_ = bf16[256,1536]{1,0:T(8,128)(2,1)S(1)} collective-permute-done((bf16[256,1536]{1,0:T(8,128)(2,1)S(1)}, bf16[256,1536]{1,0:T(8,128)(2,1)S(1)}, u32[]{:S(2)}, u32[]{:S(2)}) %collective-permute-start.14) | collective-permute-done | bytes 786464 | tf_op jit(solution)/shard_map/ppermute | solution.py:672
  116.4 0.4 shard_map.117
  116.8 4.3 %collective-permute-start.21 = (bf16[256,1536]{1,0:T(8,128)(2,1)S(1)}, bf16[256,1536]{1,0:T(8,128)(2,1)S(1)}, u32[]{:S(2)}, u32[]{:S(2)}) collective-permute-start(bf16[256,1536]{1,0:T(8,128)(2,1)S(1)} %get-tuple-element.98.refs_13_), channel_id=1, source_target_pairs={{0,4},{4,0},{8,12},{12,8},{1,5},{5,1},{9,13},{13,9},{2,6},{6,2},{1... | collective-permute-start | bytes 2359304 | tf_op jit(solution)/shard_map/ppermute | solution.py:672
  121.2 0.7 collective-permute-start.22
  121.9 5.6 %shard_map.118 = (f32[512,1536]{1,0:T(8,128)S(1)}, f32[8,128]{1,0:T(8,128)S(1)}) custom-call(s32[1]{0:T(128)} %bitcast.refs_0_, f32[128,512]{1,0:T(8,128)S(1)} %add.22.refs_1_, f32[32,512]{1,0:T(8,128)S(1)} %get-tuple-element.67.refs_2_.refs_1_, bf16[2048,1536]{1,0:T(8,128)(2,1)S(1)} %bitcast.18, f32[512,1536]{1,0:T(8,128)S(1)} %get-tuple-element.68.refs_4_, ...), custom_call_target="tpu_custom_call" | custom-call | flops 64424508 | bytes 157286 | tf_op jit(solution)/shard_map/pallas_call | solution.py:53
  127.5 5.8 %collective-permute-done.18.refs_2_ = bf16[256,1536]{1,0:T(8,128)(2,1)S(1)} collective-permute-done((bf16[256,1536]{1,0:T(8,128)(2,1)S(1)}, bf16[256,1536]{1,0:T(8,128)(2,1)S(1)}, u32[]{:S(2)}, u32[]{:S(2)}) %collective-permute-start.18) | collective-permute-done | bytes 786464 | tf_op jit(solution)/shard_map/ppermute | solution.py:672
  133.3 0.4 shard_map.119
  133.7 4.3 %collective-permute-start.19 = (bf16[256,1536]{1,0:T(8,128)(2,1)S(1)}, bf16[256,1536]{1,0:T(8,128)(2,1)S(1)}, u32[]{:S(2)}, u32[]{:S(2)}) collective-permute-start(bf16[256,1536]{1,0:T(8,128)(2,1)S(1)} %get-tuple-element.96.refs_15_), channel_id=1, source_target_pairs={{0,4},{4,0},{8,12},{12,8},{1,5},{5,1},{9,13},{13,9},{2,6},{6,2},{1... | collective-permute-start | bytes 2359304 | tf_op jit(solution)/shard_map/ppermute | solution.py:672
  138.0 0.7 collective-permute-start.20
  138.7 4.1 %shard_map.120 = (f32[128,512]{1,0:T(8,128)S(1)}, f32[8,128]{1,0:T(8,128)S(1)}) custom-call(s32[1]{0:T(128)} %bitcast.refs_0_, bf16[2048,1536]{1,0:T(8,128)(2,1)S(1)} %bitcast.19, f32[32,512]{1,0:T(8,128)S(1)} %get-tuple-element.67.refs_2_.refs_1_, f32[128,512]{1,0:T(8,128)S(1)} %get-tuple-element.100.refs_3_, ...), custom_call_target="tpu_custom_call", output_to_operand_aliasing={{0}: (3, {})} | custom-call | flops 64424508 | bytes 157286 | tf_op jit(solution)/shard_map/pallas_call | solution.py:53
  142.9 0.1 collective-permute-start.23
  142.9 1.5 collective-permute-done.23
  144.5 1.5 collective-permute-start.24
  146.0 6.9 %collective-permute-done.24 = f32[128,512]{1,0:T(8,128)S(1)} collective-permute-done((f32[128,512]{1,0:T(8,128)S(1)}, f32[128,512]{1,0:T(8,128)S(1)}, u32[]{:S(2)}, u32[]{:S(2)}) %collective-permute-start.24) | collective-permute-done | bytes 262176 | tf_op jit(solution)/shard_map/ppermute | solution.py:620
  153.0 1.1 shard_map.121
  154.2 3.2 %collective-permute-start.25 = (bf16[2,512]{1,0:T(2,128)(2,1)S(1)}, bf16[2,512]{1,0:T(2,128)(2,1)S(1)}, u32[]{:S(2)}, u32[]{:S(2)}) collective-permute-start(bf16[2,512]{1,0:T(2,128)(2,1)S(1)} %get-tuple-element.111), channel_id=1, source_target_pairs={{0,12},{4,0},{8,4},{12,8},{1,13},{5,1},{9,5},{13,9},{2,14},{6,2},{... | collective-permute-start | bytes 6152 | tf_op jit(solution)/shard_map/ppermute | solution.py:692
  157.4 1.8 collective-permute-start.26
  159.2 15.9 %shard_map.123 = (bf16[2048,1536]{1,0:T(8,128)(2,1)}, f32[8,128]{1,0:T(8,128)S(1)}) custom-call(s32[1]{0:T(128)} %bitcast.refs_0_, f32[128,512]{1,0:T(8,128)S(1)} %add.22.refs_1_, f32[32,512]{1,0:T(8,128)S(1)} %get-tuple-element.67.refs_2_.refs_1_, bf16[512,1536]{1,0:T(8,128)(2,1)S(1)} %copy-done.2, bf16[256,1536]{1,0:T(8,128)(2,1)S(1)} %get-tuple-element.72.refs_4_, ...), custom_call_target="tpu_custom_call" | custom-call | flops 257698032 | bytes 251658 | tf_op jit(solution)/shard_map/pallas_call | solution.py:53
  175.1 5.5 %shard_map.124 = (bf16[2048,256]{1,0:T(8,128)(2,1)}, f32[8,128]{1,0:T(8,128)S(1)}) custom-call(f32[128,512]{1,0:T(8,128)S(1)} %add.24.refs_0_, f32[32,512]{1,0:T(8,128)S(1)} %get-tuple-element.67.refs_2_.refs_1_, bf16[528,256]{1,0:T(8,128)(2,1)S(1)} %copy-done.7, bf16[528,256]{1,0:T(8,128)(2,1)S(1)} %collective-permute-done.refs_1_.refs_3_, ...), custom_call_target="tpu_custom_call" | custom-call | flops 42949672 | bytes 41943 | tf_op jit(solution)/shard_map/pallas_call | solution.py:53
  180.6 1.0 shard_map.125
  181.7 0.6 fusion
  (49 shorter events, 0.4 us)
Async XLA Ops:
  0.6 17.6 %collective-permute-start.3 = (bf16[512,256]{1,0:T(8,128)(2,1)}, bf16[512,256]{1,0:T(8,128)(2,1)S(1)}, u32[]{:S(2)}, u32[]{:S(2)}) collective-permute-start(bf16[512,256]{1,0:T(8,128)(2,1)} %refs_1_.1), channel_id=1, source_target_pairs={{0,1},{1,0},{2,3},{3,2},{4,5},{5,4},{6,7},{7,6},{8,9},{9,8},{10,11... | collective-permute-start | bytes 786440 | tf_op jit(solution)/shard_map/ppermute | solution.py:631
  2.9 18.6 %collective-permute-start = (bf16[528,256]{1,0:T(8,128)(2,1)}, bf16[528,256]{1,0:T(8,128)(2,1)S(1)}, u32[]{:S(2)}, u32[]{:S(2)}) collective-permute-start(bf16[528,256]{1,0:T(8,128)(2,1)} %get-tuple-element.60.refs_2_), channel_id=1, source_target_pairs={{0,4},{4,8},{8,12},{12,0},{1,5},{5,9},{9,13},{13,1},{2,6},{6,10},{... | collective-permute-start | bytes 811016 | tf_op jit(solution)/shard_map/ppermute | solution.py:628
  5.5 21.1 %collective-permute-start.1 = (bf16[528,256]{1,0:T(8,128)(2,1)}, bf16[528,256]{1,0:T(8,128)(2,1)S(1)}, u32[]{:S(2)}, u32[]{:S(2)}) collective-permute-start(bf16[528,256]{1,0:T(8,128)(2,1)} %get-tuple-element.60.refs_2_), channel_id=1, source_target_pairs={{0,8},{4,12},{8,0},{12,4},{1,9},{5,13},{9,1},{13,5},{2,10},{6,14},... | collective-permute-start | bytes 811016 | tf_op jit(solution)/shard_map/ppermute | solution.py:628
  8.0 18.5 %collective-permute-start.2 = (bf16[528,256]{1,0:T(8,128)(2,1)}, bf16[528,256]{1,0:T(8,128)(2,1)}, u32[]{:S(2)}, u32[]{:S(2)}) collective-permute-start(bf16[528,256]{1,0:T(8,128)(2,1)} %get-tuple-element.60.refs_2_), channel_id=1, source_target_pairs={{0,12},{4,0},{8,4},{12,8},{1,13},{5,1},{9,5},{13,9},{2,14},{6,2},{... | collective-permute-start | bytes 811016 | tf_op jit(solution)/shard_map/ppermute | solution.py:628
  9.4 2.8 %copy-start = (bf16[128,16,1536]{2,1,0:T(8,128)(2,1)S(1)}, bf16[128,16,1536]{2,1,0:T(8,128)(2,1)}, u32[]{:S(2)}) copy-start(bf16[128,16,1536]{2,1,0:T(8,128)(2,1)} %param.10) | copy-start | bytes 18874372
  12.2 1.4 copy-start.1
  13.6 0.7 copy-start.8
  14.3 3.9 %copy-start.4 = (bf16[512,256]{1,0:T(8,128)(2,1)S(1)}, bf16[512,256]{1,0:T(8,128)(2,1)}, u32[]{:S(2)}) copy-start(bf16[512,256]{1,0:T(8,128)(2,1)} %refs_1_.1) | copy-start | bytes 786436
  18.3 2.5 %copy-start.5 = (bf16[512,256]{1,0:T(8,128)(2,1)}, bf16[512,256]{1,0:T(8,128)(2,1)S(1)}, u32[]{:S(2)}) copy-start(bf16[512,256]{1,0:T(8,128)(2,1)S(1)} %collective-permute-done.3.refs_2_) | copy-start | bytes 786436
  19.2 15.9 %collective-permute-start.4 = (bf16[1024,256]{1,0:T(8,128)(2,1)}, bf16[1024,256]{1,0:T(8,128)(2,1)}, u32[]{:S(2)}, u32[]{:S(2)}) collective-permute-start(bf16[1024,256]{1,0:T(8,128)(2,1)} %pad_maximum_fusion), channel_id=1, source_target_pairs={{0,2},{1,3},{2,0},{3,1},{4,6},{5,7},{6,4},{7,5},{8,10},{9,11},{10,... | collective-permute-start | bytes 1572872 | tf_op jit(solution)/shard_map/ppermute | solution.py:631
  20.8 40.9 %collective-permute-start.7 = (bf16[256,1536]{1,0:T(8,128)(2,1)S(1)}, bf16[256,1536]{1,0:T(8,128)(2,1)S(1)}, u32[]{:S(2)}, u32[]{:S(2)}) collective-permute-start(bf16[256,1536]{1,0:T(8,128)(2,1)S(1)} %get-tuple-element.69), channel_id=1, source_target_pairs={{4,8},{8,4},{5,9},{9,5},{6,10},{10,6},{7,11},{11,7},{20,24},{24,20... | collective-permute-start | bytes 2359304 | tf_op jit(solution)/shard_map/ppermute | solution.py:645
  21.5 13.5 %copy-start.6 = (bf16[512,256]{1,0:T(8,128)(2,1)S(1)}, bf16[512,256]{1,0:T(8,128)(2,1)}, u32[]{:S(2)}) copy-start(bf16[512,256]{1,0:T(8,128)(2,1)} %copy-done.5) | copy-start | bytes 786436
  21.5 40.2 %collective-permute-start.8 = (bf16[256,1536]{1,0:T(8,128)(2,1)S(1)}, bf16[256,1536]{1,0:T(8,128)(2,1)S(1)}, u32[]{:S(2)}, u32[]{:S(2)}) collective-permute-start(bf16[256,1536]{1,0:T(8,128)(2,1)S(1)} %get-tuple-element.69), channel_id=1, source_target_pairs={{0,4},{4,0},{8,12},{12,8},{1,5},{5,1},{9,13},{13,9},{2,6},{6,2},{1... | collective-permute-start | bytes 2359304 | tf_op jit(solution)/shard_map/ppermute | solution.py:645
  26.6 41.7 %collective-permute-start.11 = (bf16[256,1536]{1,0:T(8,128)(2,1)S(1)}, bf16[256,1536]{1,0:T(8,128)(2,1)S(1)}, u32[]{:S(2)}, u32[]{:S(2)}) collective-permute-start(bf16[256,1536]{1,0:T(8,128)(2,1)S(1)} %get-tuple-element.77), channel_id=1, source_target_pairs={{4,8},{8,4},{5,9},{9,5},{6,10},{10,6},{7,11},{11,7},{20,24},{24,20... | collective-permute-start | bytes 2359304 | tf_op jit(solution)/shard_map/ppermute | solution.py:645
  27.3 41.0 %collective-permute-start.12 = (bf16[256,1536]{1,0:T(8,128)(2,1)S(1)}, bf16[256,1536]{1,0:T(8,128)(2,1)S(1)}, u32[]{:S(2)}, u32[]{:S(2)}) collective-permute-start(bf16[256,1536]{1,0:T(8,128)(2,1)S(1)} %get-tuple-element.77), channel_id=1, source_target_pairs={{0,4},{4,0},{8,12},{12,8},{1,5},{5,1},{9,13},{13,9},{2,6},{6,2},{1... | collective-permute-start | bytes 2359304 | tf_op jit(solution)/shard_map/ppermute | solution.py:645
  35.0 1.9 %copy-start.3 = (bf16[1536,1024]{1,0:T(8,128)(2,1)S(1)}, bf16[1536,1024]{1,0:T(8,128)(2,1)}, u32[]{:S(2)}) copy-start(bf16[1536,1024]{1,0:T(8,128)(2,1)} %refs_4_.3) | copy-start | bytes 9437188
  36.9 3.6 %copy-start.7 = (bf16[528,256]{1,0:T(8,128)(2,1)S(1)}, bf16[528,256]{1,0:T(8,128)(2,1)}, u32[]{:S(2)}) copy-start(bf16[528,256]{1,0:T(8,128)(2,1)} %get-tuple-element.60.refs_2_) | copy-start | bytes 811012
  36.9 3.6 %copy-start.9 = (bf16[128,16,256]{2,1,0:T(8,128)(2,1)S(1)}, bf16[128,16,256]{2,1,0:T(8,128)(2,1)}, u32[]{:S(2)}) copy-start(bf16[128,16,256]{2,1,0:T(8,128)(2,1)} %param.11) | copy-start | bytes 3145732
  40.5 15.9 %slice-start = ((s8[6291456]{0:T(1024)(128)(4,1)}), s8[4194304]{0:T(1024)(128)(4,1)S(1)}, s32[]{:S(2)}) async-start(s8[6291456]{0:T(1024)(128)(4,1)} %bitcast.11), calls=%async_computation | async-start | bytes 8388608
  40.5 15.9 %slice-start.1 = ((s8[6291456]{0:T(1024)(128)(4,1)}), s8[2097152]{0:T(1024)(128)(4,1)S(1)}, s32[]{:S(2)}) async-start(s8[6291456]{0:T(1024)(128)(4,1)} %bitcast.11), calls=%async_computation.1 | async-start | bytes 4194304
  46.3 1.6 collective-permute-start.5
  47.9 8.4 %collective-permute-start.6 = (f32[128,512]{1,0:T(8,128)S(1)}, f32[128,512]{1,0:T(8,128)S(1)}, u32[]{:S(2)}, u32[]{:S(2)}) collective-permute-start(f32[128,512]{1,0:T(8,128)S(1)} %add.21), channel_id=1, source_target_pairs={{0,2},{1,3},{2,0},{3,1},{4,6},{5,7},{6,4},{7,5},{8,10},{9,11},{10,... | collective-permute-start | bytes 786440 | tf_op jit(solution)/shard_map/ppermute | solution.py:620
  62.2 20.5 %collective-permute-start.10 = (bf16[256,1536]{1,0:T(8,128)(2,1)S(1)}, bf16[256,1536]{1,0:T(8,128)(2,1)S(1)}, u32[]{:S(2)}, u32[]{:S(2)}) collective-permute-start(bf16[256,1536]{1,0:T(8,128)(2,1)S(1)} %get-tuple-element.73.refs_6_.refs_5_), channel_id=1, source_target_pairs={{0,4},{4,0},{8,12},{12,8},{1,5},{5,1},{9,13},{13,9},{2,6},{6,2},{1... | collective-permute-start | bytes 2359304 | tf_op jit(solution)/shard_map/ppermute | solution.py:672
  62.2 20.5 %collective-permute-start.9 = (bf16[256,1536]{1,0:T(8,128)(2,1)S(1)}, bf16[256,1536]{1,0:T(8,128)(2,1)S(1)}, u32[]{:S(2)}, u32[]{:S(2)}) collective-permute-start(bf16[256,1536]{1,0:T(8,128)(2,1)S(1)} %get-tuple-element.72.refs_4_), channel_id=1, source_target_pairs={{4,8},{8,4},{5,9},{9,5},{6,10},{10,6},{7,11},{11,7},{20,24},{24,20... | collective-permute-start | bytes 2359304 | tf_op jit(solution)/shard_map/ppermute | solution.py:672
  68.7 27.8 %collective-permute-start.15 = (bf16[256,1536]{1,0:T(8,128)(2,1)S(1)}, bf16[256,1536]{1,0:T(8,128)(2,1)S(1)}, u32[]{:S(2)}, u32[]{:S(2)}) collective-permute-start(bf16[256,1536]{1,0:T(8,128)(2,1)S(1)} %get-tuple-element.79.refs_5_.refs_6_), channel_id=1, source_target_pairs={{4,8},{8,4},{5,9},{9,5},{6,10},{10,6},{7,11},{11,7},{20,24},{24,20... | collective-permute-start | bytes 2359304 | tf_op jit(solution)/shard_map/ppermute | solution.py:672
  69.4 30.1 %collective-permute-start.16 = (bf16[256,1536]{1,0:T(8,128)(2,1)S(1)}, bf16[256,1536]{1,0:T(8,128)(2,1)S(1)}, u32[]{:S(2)}, u32[]{:S(2)}) collective-permute-start(bf16[256,1536]{1,0:T(8,128)(2,1)S(1)} %get-tuple-element.87.refs_7_), channel_id=1, source_target_pairs={{0,4},{4,0},{8,12},{12,8},{1,5},{5,1},{9,13},{13,9},{2,6},{6,2},{1... | collective-permute-start | bytes 2359304 | tf_op jit(solution)/shard_map/ppermute | solution.py:672
  83.3 28.6 %collective-permute-start.13 = (bf16[256,1536]{1,0:T(8,128)(2,1)S(1)}, bf16[256,1536]{1,0:T(8,128)(2,1)S(1)}, u32[]{:S(2)}, u32[]{:S(2)}) collective-permute-start(bf16[256,1536]{1,0:T(8,128)(2,1)S(1)} %get-tuple-element.82.refs_4_.refs_8_), channel_id=1, source_target_pairs={{4,8},{8,4},{5,9},{9,5},{6,10},{10,6},{7,11},{11,7},{20,24},{24,20... | collective-permute-start | bytes 2359304 | tf_op jit(solution)/shard_map/ppermute | solution.py:672
  84.0 32.4 %collective-permute-start.14 = (bf16[256,1536]{1,0:T(8,128)(2,1)S(1)}, bf16[256,1536]{1,0:T(8,128)(2,1)S(1)}, u32[]{:S(2)}, u32[]{:S(2)}) collective-permute-start(bf16[256,1536]{1,0:T(8,128)(2,1)S(1)} %get-tuple-element.83.refs_6_.refs_9_), channel_id=1, source_target_pairs={{0,4},{4,0},{8,12},{12,8},{1,5},{5,1},{9,13},{13,9},{2,6},{6,2},{1... | collective-permute-start | bytes 2359304 | tf_op jit(solution)/shard_map/ppermute | solution.py:672
  100.0 27.5 %collective-permute-start.17 = (bf16[256,1536]{1,0:T(8,128)(2,1)S(1)}, bf16[256,1536]{1,0:T(8,128)(2,1)S(1)}, u32[]{:S(2)}, u32[]{:S(2)}) collective-permute-start(bf16[256,1536]{1,0:T(8,128)(2,1)S(1)} %get-tuple-element.89.refs_5_.refs_10_), channel_id=1, source_target_pairs={{4,8},{8,4},{5,9},{9,5},{6,10},{10,6},{7,11},{11,7},{20,24},{24,20... | collective-permute-start | bytes 2359304 | tf_op jit(solution)/shard_map/ppermute | solution.py:672
  100.7 32.6 %collective-permute-start.18 = (bf16[256,1536]{1,0:T(8,128)(2,1)S(1)}, bf16[256,1536]{1,0:T(8,128)(2,1)S(1)}, u32[]{:S(2)}, u32[]{:S(2)}) collective-permute-start(bf16[256,1536]{1,0:T(8,128)(2,1)S(1)} %get-tuple-element.94.refs_7_.refs_11_), channel_id=1, source_target_pairs={{0,4},{4,0},{8,12},{12,8},{1,5},{5,1},{9,13},{13,9},{2,6},{6,2},{1... | collective-permute-start | bytes 2359304 | tf_op jit(solution)/shard_map/ppermute | solution.py:672
  116.8 36.1 %collective-permute-start.21 = (bf16[256,1536]{1,0:T(8,128)(2,1)S(1)}, bf16[256,1536]{1,0:T(8,128)(2,1)S(1)}, u32[]{:S(2)}, u32[]{:S(2)}) collective-permute-start(bf16[256,1536]{1,0:T(8,128)(2,1)S(1)} %get-tuple-element.98.refs_13_), channel_id=1, source_target_pairs={{0,4},{4,0},{8,12},{12,8},{1,5},{5,1},{9,13},{13,9},{2,6},{6,2},{1... | collective-permute-start | bytes 2359304 | tf_op jit(solution)/shard_map/ppermute | solution.py:672
  121.2 31.8 %collective-permute-start.22 = (bf16[256,1536]{1,0:T(8,128)(2,1)S(1)}, bf16[256,1536]{1,0:T(8,128)(2,1)S(1)}, u32[]{:S(2)}, u32[]{:S(2)}) collective-permute-start(bf16[256,1536]{1,0:T(8,128)(2,1)S(1)} %get-tuple-element.99.refs_4_.refs_12_), channel_id=1, source_target_pairs={{4,8},{8,4},{5,9},{9,5},{6,10},{10,6},{7,11},{11,7},{20,24},{24,20... | collective-permute-start | bytes 2359304 | tf_op jit(solution)/shard_map/ppermute | solution.py:672
  133.7 46.9 %collective-permute-start.19 = (bf16[256,1536]{1,0:T(8,128)(2,1)S(1)}, bf16[256,1536]{1,0:T(8,128)(2,1)S(1)}, u32[]{:S(2)}, u32[]{:S(2)}) collective-permute-start(bf16[256,1536]{1,0:T(8,128)(2,1)S(1)} %get-tuple-element.96.refs_15_), channel_id=1, source_target_pairs={{0,4},{4,0},{8,12},{12,8},{1,5},{5,1},{9,13},{13,9},{2,6},{6,2},{1... | collective-permute-start | bytes 2359304 | tf_op jit(solution)/shard_map/ppermute | solution.py:672
  138.0 42.6 %collective-permute-start.20 = (bf16[256,1536]{1,0:T(8,128)(2,1)S(1)}, bf16[256,1536]{1,0:T(8,128)(2,1)S(1)}, u32[]{:S(2)}, u32[]{:S(2)}) collective-permute-start(bf16[256,1536]{1,0:T(8,128)(2,1)S(1)} %get-tuple-element.97.refs_5_.refs_14_), channel_id=1, source_target_pairs={{4,8},{8,4},{5,9},{9,5},{6,10},{10,6},{7,11},{11,7},{20,24},{24,20... | collective-permute-start | bytes 2359304 | tf_op jit(solution)/shard_map/ppermute | solution.py:672
  142.9 1.6 collective-permute-start.23
  144.5 8.4 %collective-permute-start.24 = (f32[128,512]{1,0:T(8,128)S(1)}, f32[128,512]{1,0:T(8,128)S(1)}, u32[]{:S(2)}, u32[]{:S(2)}) collective-permute-start(f32[128,512]{1,0:T(8,128)S(1)} %add.23), channel_id=1, source_target_pairs={{0,2},{1,3},{2,0},{3,1},{4,6},{5,7},{6,4},{7,5},{8,10},{9,11},{10,... | collective-permute-start | bytes 786440 | tf_op jit(solution)/shard_map/ppermute | solution.py:620
  153.0 6.2 %copy-start.2 = (bf16[512,1536]{1,0:T(8,128)(2,1)S(1)}, bf16[512,1536]{1,0:T(8,128)(2,1)}, u32[]{:S(2)}) copy-start(bf16[512,1536]{1,0:T(8,128)(2,1)} %refs_3_.3) | copy-start | bytes 4718596
  154.2 27.5 %collective-permute-start.25 = (bf16[2,512]{1,0:T(2,128)(2,1)S(1)}, bf16[2,512]{1,0:T(2,128)(2,1)S(1)}, u32[]{:S(2)}, u32[]{:S(2)}) collective-permute-start(bf16[2,512]{1,0:T(2,128)(2,1)S(1)} %get-tuple-element.111), channel_id=1, source_target_pairs={{0,12},{4,0},{8,4},{12,8},{1,13},{5,1},{9,5},{13,9},{2,14},{6,2},{... | collective-permute-start | bytes 6152 | tf_op jit(solution)/shard_map/ppermute | solution.py:692
  157.4 24.3 %collective-permute-start.26 = (bf16[2,512]{1,0:T(2,128)(2,1)S(1)}, bf16[2,512]{1,0:T(2,128)(2,1)S(1)}, u32[]{:S(2)}, u32[]{:S(2)}) collective-permute-start(bf16[2,512]{1,0:T(2,128)(2,1)S(1)} %get-tuple-element.112), channel_id=1, source_target_pairs={{0,8},{4,12},{8,0},{12,4},{1,9},{5,13},{9,1},{13,5},{2,10},{6,14},... | collective-permute-start | bytes 6152 | tf_op jit(solution)/shard_map/ppermute | solution.py:692
  159.1 22.5 %collective-permute-start.27 = (bf16[2,512]{1,0:T(2,128)(2,1)S(1)}, bf16[2,512]{1,0:T(2,128)(2,1)S(1)}, u32[]{:S(2)}, u32[]{:S(2)}) collective-permute-start(bf16[2,512]{1,0:T(2,128)(2,1)S(1)} %get-tuple-element.113), channel_id=1, source_target_pairs={{0,4},{4,8},{8,12},{12,0},{1,5},{5,9},{9,13},{13,1},{2,6},{6,10},{... | collective-permute-start | bytes 6152 | tf_op jit(solution)/shard_map/ppermute | solution.py:692

commit v6 on v5

--- a/solution.py
+++ b/solution.py
@@ -680,10 +680,10 @@
             ready += waiting if size % 2 else []
         low, token = add_projection(low, ready, token)
 
+    part_in = exchange(low)
+    down_gradient, token = grad_down(pos, size, part_out, aux, rows, where, total, rank, [token])
     result, token = finish(far, got[0][0], got[0][1], 0, None, [token])
-    part_in = exchange(low)
     *gate_rows, token = grad_gates(part_in, part_out, size, rank, [token])
-    down_gradient, token = grad_down(pos, size, part_out, aux, rows, where, total, rank, [token])
     up_gradient, token = grad_up(part_in, aux, blocks, total, rank, [token])
     for c in range(1, CHUNKS):
         result, token = finish(far, got[c][0], got[c][1], c, result, [token])

time: 183 us -> 176 us (0.962)
  waiting for transfers between devices: 34.6 us -> 27.8 us
    ppermute x4, waiting for transfers between devices: 16.8 us -> 9.92 us  [exchange(): lax.ppermute(part, 'mp', [(i, i ^ bit) for i in range(shares)])]
  transfers between devices with their start and end apart: 28 -> 28, of which waited for: 9 -> 8; matrix products, arithmetic and copies ran while one was open for 1% -> 1% of each run, Pallas kernels for 41% -> 43%
where the time goes in v6:
time: 176 us; the launch traced here: 175 us
  Pallas kernels  74.7 us (42%)
  starting transfers between devices  63.1 us (36%)
  waiting for transfers between devices  27.8 us (16%)
  local copies, waits for them, and re-layouts  6.96 us (4%)
    pallas_call x24, Pallas kernels, call(): return lambda *arrays: call_it(*arrays, *after)  74.7 us
    ppermute x6, starting transfers between devices, per_device(): lax.ppermute(to_a, 'dp', pairs_a)  29.2 us
    ppermute x6, waiting for transfers between devices, per_device(): lax.ppermute(to_a, 'dp', pairs_a)  16.6 us
    ppermute x4, starting transfers between devices, per_device(): lax.ppermute(sent[c], 'dp', p)  12.9 us
    ppermute x4, waiting for transfers between devices, exchange(): lax.ppermute(part, 'mp', [(i, i ^ bit) for i in range(shares)])  9.92 us
    unnamed x24, local copies, waits for them, and re-layouts  6.84 us
    ppermute x3, starting transfers between devices, per_device(): lax.ppermute(block, 'dp', [(i, (i + s) % size) for i in range(size)])  6.53 us
    ppermute x3, starting transfers between devices, per_device(): lax.ppermute(gate_rows[s], 'dp', [(i, (i - s) % size) for i in range(size)])  4.78 us
  transfers between devices with their start and end apart: 28, of which 8 were waited for; matrix products, arithmetic and copies ran while one was open for 1% of the time, Pallas kernels for 43%

profile of v6, /device:TPU:0, one launch (start us, length us, event | category | flops | bytes accessed | tf_op | source)
XLA Modules:
  0.0 175.3 jit_solution(11226628084145248145)
XLA Ops:
  0.6 0.5 collective-permute-start.3
  1.1 1.7 shard_map.102
  2.9 2.6 %collective-permute-start = (bf16[528,256]{1,0:T(8,128)(2,1)}, bf16[528,256]{1,0:T(8,128)(2,1)S(1)}, u32[]{:S(2)}, u32[]{:S(2)}) collective-permute-start(bf16[528,256]{1,0:T(8,128)(2,1)} %get-tuple-element.60.refs_2_), channel_id=1, source_target_pairs={{0,4},{4,8},{8,12},{12,0},{1,5},{5,9},{9,13},{13,1},{2,6},{6,10},{... | collective-permute-start | bytes 811016 | tf_op jit(solution)/shard_map/ppermute | solution.py:628
  5.5 2.6 %collective-permute-start.1 = (bf16[528,256]{1,0:T(8,128)(2,1)}, bf16[528,256]{1,0:T(8,128)(2,1)S(1)}, u32[]{:S(2)}, u32[]{:S(2)}) collective-permute-start(bf16[528,256]{1,0:T(8,128)(2,1)} %get-tuple-element.60.refs_2_), channel_id=1, source_target_pairs={{0,8},{4,12},{8,0},{12,4},{1,9},{5,13},{9,1},{13,5},{2,10},{6,14},... | collective-permute-start | bytes 811016 | tf_op jit(solution)/shard_map/ppermute | solution.py:628
  8.0 1.3 collective-permute-start.2
  9.4 2.8 %copy-done = bf16[128,16,1536]{2,1,0:T(8,128)(2,1)S(1)} copy-done((bf16[128,16,1536]{2,1,0:T(8,128)(2,1)S(1)}, bf16[128,16,1536]{2,1,0:T(8,128)(2,1)}, u32[]{:S(2)}) %copy-start) | copy-done | bytes 6291480
  12.2 1.4 copy-done.1
  13.6 0.7 copy-done.8
  14.3 3.9 %shard_map.103 = (f32[128,512]{1,0:T(8,128)S(1)}, f32[8,128]{1,0:T(8,128)S(1)}) custom-call(s32[1]{0:T(128)} %bitcast.refs_0_, bf16[2048,1536]{1,0:T(8,128)(2,1)S(1)} %bitcast.10, f32[8,512]{1,0:T(8,128)S(1)} %copy-done.8, f32[128,512]{1,0:T(8,128)S(1)} %broadcast_in_dim.3.refs_3_, bf16[512,1536]{1,0:T(8,128)(2,1)S(1)} %copy-done.1), custom_call_target="tpu_custom_call", output_to_operand_aliasing={{0}: (3, {})} | custom-call | flops 64424508 | bytes 157286 | tf_op jit(solution)/shard_map/pallas_call | solution.py:53
  18.3 0.9 pad_maximum_fusion
  19.2 1.5 collective-permute-start.4
  20.6 0.1 fusion.1
  20.8 0.7 collective-permute-start.7
  21.5 3.8 %collective-permute-start.8 = (bf16[256,1536]{1,0:T(8,128)(2,1)S(1)}, bf16[256,1536]{1,0:T(8,128)(2,1)S(1)}, u32[]{:S(2)}, u32[]{:S(2)}) collective-permute-start(bf16[256,1536]{1,0:T(8,128)(2,1)S(1)} %get-tuple-element.69), channel_id=1, source_target_pairs={{0,4},{4,0},{8,12},{12,8},{1,5},{5,1},{9,13},{13,9},{2,6},{6,2},{1... | collective-permute-start | bytes 2359304 | tf_op jit(solution)/shard_map/ppermute | solution.py:645
  25.3 1.3 collective-permute-done.1.refs_2_.refs_4_
  26.6 0.7 collective-permute-start.11
  27.3 7.7 %collective-permute-start.12 = (bf16[256,1536]{1,0:T(8,128)(2,1)S(1)}, bf16[256,1536]{1,0:T(8,128)(2,1)S(1)}, u32[]{:S(2)}, u32[]{:S(2)}) collective-permute-start(bf16[256,1536]{1,0:T(8,128)(2,1)S(1)} %get-tuple-element.77), channel_id=1, source_target_pairs={{0,4},{4,0},{8,12},{12,8},{1,5},{5,1},{9,13},{13,9},{2,6},{6,2},{1... | collective-permute-start | bytes 2359304 | tf_op jit(solution)/shard_map/ppermute | solution.py:645
  35.0 1.9 %copy-done.3 = bf16[1536,1024]{1,0:T(8,128)(2,1)S(1)} copy-done((bf16[1536,1024]{1,0:T(8,128)(2,1)S(1)}, bf16[1536,1024]{1,0:T(8,128)(2,1)}, u32[]{:S(2)}) %copy-start.3) | copy-done | bytes 3145752
  36.9 3.6 %shard_map.104 = (f32[512,1536]{1,0:T(8,128)S(1)}, f32[8,128]{1,0:T(8,128)S(1)}) custom-call(s32[1]{0:T(128)} %bitcast.4.refs_0_, bf16[512,256]{1,0:T(8,128)(2,1)S(1)} %copy-done.4, bf16[512,256]{1,0:T(8,128)(2,1)S(1)} %copy-done.6, bf16[1024,256]{1,0:T(8,128)(2,1)} %collective-permute-done.4.refs_3_, bf16[1536,1024]{1,0:T(8,128)(2,1)S(1)} %copy-done.3, ...), custom_call_target="tpu_custom_call" | custom-call | flops 32212254 | bytes 62914 | tf_op jit(solution)/shard_map/pallas_call | solution.py:53
  40.6 5.7 %shard_map.107 = (f32[128,512]{1,0:T(8,128)S(1)}, f32[32,512]{1,0:T(8,128)S(1)}, f32[8,128]{1,0:T(8,128)}) custom-call(s32[1]{0:T(128)} %bitcast.refs_0_, bf16[2048,256]{1,0:T(8,128)(2,1)S(1)} %bitcast.20, bf16[528,256]{1,0:T(8,128)(2,1)S(1)} %copy-done.7, bf16[528,256]{1,0:T(8,128)(2,1)S(1)} %collective-permute-done.refs_1_.refs_3_, ...), custom_call_target="tpu_custom_call" | custom-call | flops 10737418240 | bytes 10485760 | tf_op jit(solution)/shard_map/pallas_call | solution.py:53
  46.3 0.1 collective-permute-start.5
  46.4 1.5 collective-permute-done.5
  48.0 1.5 collective-permute-start.6
  49.5 6.9 %collective-permute-done.6 = f32[128,512]{1,0:T(8,128)S(1)} collective-permute-done((f32[128,512]{1,0:T(8,128)S(1)}, f32[128,512]{1,0:T(8,128)S(1)}, u32[]{:S(2)}, u32[]{:S(2)}) %collective-permute-start.6) | collective-permute-done | bytes 262176 | tf_op jit(solution)/shard_map/ppermute | solution.py:620
  56.4 5.3 %shard_map.108 = (bf16[512,1536]{1,0:T(8,128)(2,1)S(1)}, f32[8,128]{1,0:T(8,128)S(1)}) custom-call(s32[1]{0:T(128)} %bitcast.refs_0_, f32[128,512]{1,0:T(8,128)S(1)} %add.22.refs_1_, f32[32,512]{1,0:T(8,128)S(1)} %get-tuple-element.67.refs_2_.refs_1_, bf16[2048,1536]{1,0:T(8,128)(2,1)S(1)} %bitcast.13), custom_call_target="tpu_custom_call" | custom-call | flops 64424508 | bytes 157286 | tf_op jit(solution)/shard_map/pallas_call | solution.py:53
  61.7 0.4 shard_map.109
  62.2 0.1 collective-permute-start.10
  62.3 0.7 collective-permute-start.9
  63.0 5.3 %shard_map.110 = (bf16[512,1536]{1,0:T(8,128)(2,1)S(1)}, f32[8,128]{1,0:T(8,128)S(1)}) custom-call(s32[1]{0:T(128)} %bitcast.refs_0_, f32[128,512]{1,0:T(8,128)S(1)} %add.22.refs_1_, f32[32,512]{1,0:T(8,128)S(1)} %get-tuple-element.67.refs_2_.refs_1_, bf16[2048,1536]{1,0:T(8,128)(2,1)S(1)} %bitcast.14, f32[8,128]{1,0:T(8,128)S(1)} %get-tuple-element.74.refs_4_), custom_call_target="tpu_custom_call" | custom-call | flops 64424508 | bytes 157286 | tf_op jit(solution)/shard_map/pallas_call | solution.py:53
  68.3 0.4 shard_map.111
  68.7 0.7 collective-permute-start.15
  69.4 6.1 %collective-permute-start.16 = (bf16[256,1536]{1,0:T(8,128)(2,1)S(1)}, bf16[256,1536]{1,0:T(8,128)(2,1)S(1)}, u32[]{:S(2)}, u32[]{:S(2)}) collective-permute-start(bf16[256,1536]{1,0:T(8,128)(2,1)S(1)} %get-tuple-element.87.refs_7_), channel_id=1, source_target_pairs={{0,4},{4,0},{8,12},{12,8},{1,5},{5,1},{9,13},{13,9},{2,6},{6,2},{1... | collective-permute-start | bytes 2359304 | tf_op jit(solution)/shard_map/ppermute | solution.py:672
  75.6 3.9 %shard_map.112 = (f32[128,512]{1,0:T(8,128)S(1)}, f32[8,128]{1,0:T(8,128)S(1)}) custom-call(s32[1]{0:T(128)} %bitcast.refs_0_, bf16[2048,1536]{1,0:T(8,128)(2,1)S(1)} %bitcast.15, f32[32,512]{1,0:T(8,128)S(1)} %get-tuple-element.67.refs_2_.refs_1_, f32[128,512]{1,0:T(8,128)S(1)} %get-tuple-element.76.refs_3_, ...), custom_call_target="tpu_custom_call", output_to_operand_aliasing={{0}: (3, {})} | custom-call | flops 64424508 | bytes 157286 | tf_op jit(solution)/shard_map/pallas_call | solution.py:53
  79.5 3.2 %collective-permute-done.10.refs_2_ = bf16[256,1536]{1,0:T(8,128)(2,1)S(1)} collective-permute-done((bf16[256,1536]{1,0:T(8,128)(2,1)S(1)}, bf16[256,1536]{1,0:T(8,128)(2,1)S(1)}, u32[]{:S(2)}, u32[]{:S(2)}) %collective-permute-start.10) | collective-permute-done | bytes 786464 | tf_op jit(solution)/shard_map/ppermute | solution.py:672
  82.7 0.6 shard_map.113
  83.3 0.7 collective-permute-start.13
  84.1 7.1 %collective-permute-start.14 = (bf16[256,1536]{1,0:T(8,128)(2,1)S(1)}, bf16[256,1536]{1,0:T(8,128)(2,1)S(1)}, u32[]{:S(2)}, u32[]{:S(2)}) collective-permute-start(bf16[256,1536]{1,0:T(8,128)(2,1)S(1)} %get-tuple-element.83.refs_6_.refs_9_), channel_id=1, source_target_pairs={{0,4},{4,0},{8,12},{12,8},{1,5},{5,1},{9,13},{13,9},{2,6},{6,2},{1... | collective-permute-start | bytes 2359304 | tf_op jit(solution)/shard_map/ppermute | solution.py:672
  91.2 5.2 %shard_map.114 = (bf16[512,1536]{1,0:T(8,128)(2,1)S(1)}, f32[8,128]{1,0:T(8,128)S(1)}) custom-call(s32[1]{0:T(128)} %bitcast.refs_0_, f32[128,512]{1,0:T(8,128)S(1)} %add.22.refs_1_, f32[32,512]{1,0:T(8,128)S(1)} %get-tuple-element.67.refs_2_.refs_1_, bf16[2048,1536]{1,0:T(8,128)(2,1)S(1)} %bitcast.16, f32[8,128]{1,0:T(8,128)S(1)} %get-tuple-element.84.refs_4_), custom_call_target="tpu_custom_call" | custom-call | flops 64424508 | bytes 157286 | tf_op jit(solution)/shard_map/pallas_call | solution.py:53
  96.5 3.1 %collective-permute-done.16.refs_2_ = bf16[256,1536]{1,0:T(8,128)(2,1)S(1)} collective-permute-done((bf16[256,1536]{1,0:T(8,128)(2,1)S(1)}, bf16[256,1536]{1,0:T(8,128)(2,1)S(1)}, u32[]{:S(2)}, u32[]{:S(2)}) %collective-permute-start.16) | collective-permute-done | bytes 786464 | tf_op jit(solution)/shard_map/ppermute | solution.py:672
  99.6 0.4 shard_map.115
  100.0 0.7 collective-permute-start.17
  100.7 7.2 %collective-permute-start.18 = (bf16[256,1536]{1,0:T(8,128)(2,1)S(1)}, bf16[256,1536]{1,0:T(8,128)(2,1)S(1)}, u32[]{:S(2)}, u32[]{:S(2)}) collective-permute-start(bf16[256,1536]{1,0:T(8,128)(2,1)S(1)} %get-tuple-element.94.refs_7_.refs_11_), channel_id=1, source_target_pairs={{0,4},{4,0},{8,12},{12,8},{1,5},{5,1},{9,13},{13,9},{2,6},{6,2},{1... | collective-permute-start | bytes 2359304 | tf_op jit(solution)/shard_map/ppermute | solution.py:672
  107.9 4.1 %shard_map.116 = (f32[128,512]{1,0:T(8,128)S(1)}, f32[8,128]{1,0:T(8,128)S(1)}) custom-call(s32[1]{0:T(128)} %bitcast.refs_0_, bf16[2048,1536]{1,0:T(8,128)(2,1)S(1)} %bitcast.17, f32[32,512]{1,0:T(8,128)S(1)} %get-tuple-element.67.refs_2_.refs_1_, f32[128,512]{1,0:T(8,128)S(1)} %get-tuple-element.86.refs_3_, ...), custom_call_target="tpu_custom_call", output_to_operand_aliasing={{0}: (3, {})} | custom-call | flops 64424508 | bytes 157286 | tf_op jit(solution)/shard_map/pallas_call | solution.py:53
  112.0 4.5 %collective-permute-done.14.refs_2_ = bf16[256,1536]{1,0:T(8,128)(2,1)S(1)} collective-permute-done((bf16[256,1536]{1,0:T(8,128)(2,1)S(1)}, bf16[256,1536]{1,0:T(8,128)(2,1)S(1)}, u32[]{:S(2)}, u32[]{:S(2)}) %collective-permute-start.14) | collective-permute-done | bytes 786464 | tf_op jit(solution)/shard_map/ppermute | solution.py:672
  116.4 0.4 shard_map.117
  116.9 4.3 %collective-permute-start.21 = (bf16[256,1536]{1,0:T(8,128)(2,1)S(1)}, bf16[256,1536]{1,0:T(8,128)(2,1)S(1)}, u32[]{:S(2)}, u32[]{:S(2)}) collective-permute-start(bf16[256,1536]{1,0:T(8,128)(2,1)S(1)} %get-tuple-element.98.refs_13_), channel_id=1, source_target_pairs={{0,4},{4,0},{8,12},{12,8},{1,5},{5,1},{9,13},{13,9},{2,6},{6,2},{1... | collective-permute-start | bytes 2359304 | tf_op jit(solution)/shard_map/ppermute | solution.py:672
  121.2 0.7 collective-permute-start.22
  121.9 5.6 %shard_map.118 = (f32[512,1536]{1,0:T(8,128)S(1)}, f32[8,128]{1,0:T(8,128)S(1)}) custom-call(s32[1]{0:T(128)} %bitcast.refs_0_, f32[128,512]{1,0:T(8,128)S(1)} %add.22.refs_1_, f32[32,512]{1,0:T(8,128)S(1)} %get-tuple-element.67.refs_2_.refs_1_, bf16[2048,1536]{1,0:T(8,128)(2,1)S(1)} %bitcast.18, f32[512,1536]{1,0:T(8,128)S(1)} %get-tuple-element.68.refs_4_, ...), custom_call_target="tpu_custom_call" | custom-call | flops 64424508 | bytes 157286 | tf_op jit(solution)/shard_map/pallas_call | solution.py:53
  127.5 5.8 %collective-permute-done.18.refs_2_ = bf16[256,1536]{1,0:T(8,128)(2,1)S(1)} collective-permute-done((bf16[256,1536]{1,0:T(8,128)(2,1)S(1)}, bf16[256,1536]{1,0:T(8,128)(2,1)S(1)}, u32[]{:S(2)}, u32[]{:S(2)}) %collective-permute-start.18) | collective-permute-done | bytes 786464 | tf_op jit(solution)/shard_map/ppermute | solution.py:672
  133.3 0.4 shard_map.119
  133.7 4.3 %collective-permute-start.19 = (bf16[256,1536]{1,0:T(8,128)(2,1)S(1)}, bf16[256,1536]{1,0:T(8,128)(2,1)S(1)}, u32[]{:S(2)}, u32[]{:S(2)}) collective-permute-start(bf16[256,1536]{1,0:T(8,128)(2,1)S(1)} %get-tuple-element.96.refs_15_), channel_id=1, source_target_pairs={{0,4},{4,0},{8,12},{12,8},{1,5},{5,1},{9,13},{13,9},{2,6},{6,2},{1... | collective-permute-start | bytes 2359304 | tf_op jit(solution)/shard_map/ppermute | solution.py:672
  138.1 0.9 collective-permute-start.20
  139.0 4.1 %shard_map.120 = (f32[128,512]{1,0:T(8,128)S(1)}, f32[8,128]{1,0:T(8,128)S(1)}) custom-call(s32[1]{0:T(128)} %bitcast.refs_0_, bf16[2048,1536]{1,0:T(8,128)(2,1)S(1)} %bitcast.19, f32[32,512]{1,0:T(8,128)S(1)} %get-tuple-element.67.refs_2_.refs_1_, f32[128,512]{1,0:T(8,128)S(1)} %get-tuple-element.100.refs_3_, ...), custom_call_target="tpu_custom_call", output_to_operand_aliasing={{0}: (3, {})} | custom-call | flops 64424508 | bytes 157286 | tf_op jit(solution)/shard_map/pallas_call | solution.py:53
  143.1 0.1 collective-permute-start.23
  143.2 1.5 collective-permute-done.23
  144.8 1.5 collective-permute-start.24
  146.3 15.9 %shard_map.121 = (bf16[2048,1536]{1,0:T(8,128)(2,1)}, f32[8,128]{1,0:T(8,128)S(1)}) custom-call(s32[1]{0:T(128)} %bitcast.refs_0_, f32[128,512]{1,0:T(8,128)S(1)} %add.22.refs_1_, f32[32,512]{1,0:T(8,128)S(1)} %get-tuple-element.67.refs_2_.refs_1_, bf16[512,1536]{1,0:T(8,128)(2,1)S(1)} %copy-done.2, bf16[256,1536]{1,0:T(8,128)(2,1)S(1)} %get-tuple-element.72.refs_4_, ...), custom_call_target="tpu_custom_call" | custom-call | flops 257698032 | bytes 251658 | tf_op jit(solution)/shard_map/pallas_call | solution.py:53
  162.3 1.1 shard_map.122
  163.3 0.1 shard_map.123
  163.4 3.0 %collective-permute-start.25 = (bf16[2,512]{1,0:T(2,128)(2,1)S(1)}, bf16[2,512]{1,0:T(2,128)(2,1)S(1)}, u32[]{:S(2)}, u32[]{:S(2)}) collective-permute-start(bf16[2,512]{1,0:T(2,128)(2,1)S(1)} %get-tuple-element.111), channel_id=1, source_target_pairs={{0,12},{4,0},{8,4},{12,8},{1,13},{5,1},{9,5},{13,9},{2,14},{6,2},{... | collective-permute-start | bytes 6152 | tf_op jit(solution)/shard_map/ppermute | solution.py:692
  166.4 1.8 %collective-permute-start.26 = (bf16[2,512]{1,0:T(2,128)(2,1)S(1)}, bf16[2,512]{1,0:T(2,128)(2,1)S(1)}, u32[]{:S(2)}, u32[]{:S(2)}) collective-permute-start(bf16[2,512]{1,0:T(2,128)(2,1)S(1)} %get-tuple-element.112), channel_id=1, source_target_pairs={{0,8},{4,12},{8,0},{12,4},{1,9},{5,13},{9,1},{13,5},{2,10},{6,14},... | collective-permute-start | bytes 6152 | tf_op jit(solution)/shard_map/ppermute | solution.py:692
  168.2 5.5 %shard_map.124 = (bf16[2048,256]{1,0:T(8,128)(2,1)}, f32[8,128]{1,0:T(8,128)S(1)}) custom-call(f32[128,512]{1,0:T(8,128)S(1)} %add.24.refs_0_, f32[32,512]{1,0:T(8,128)S(1)} %get-tuple-element.67.refs_2_.refs_1_, bf16[528,256]{1,0:T(8,128)(2,1)S(1)} %copy-done.7, bf16[528,256]{1,0:T(8,128)(2,1)S(1)} %collective-permute-done.refs_1_.refs_3_, ...), custom_call_target="tpu_custom_call" | custom-call | flops 42949672 | bytes 41943 | tf_op jit(solution)/shard_map/pallas_call | solution.py:53
  173.7 1.0 shard_map.125
  174.7 0.6 fusion
  (49 shorter events, 0.3 us)
Async XLA Ops:
  0.6 17.6 %collective-permute-start.3 = (bf16[512,256]{1,0:T(8,128)(2,1)}, bf16[512,256]{1,0:T(8,128)(2,1)S(1)}, u32[]{:S(2)}, u32[]{:S(2)}) collective-permute-start(bf16[512,256]{1,0:T(8,128)(2,1)} %refs_1_.1), channel_id=1, source_target_pairs={{0,1},{1,0},{2,3},{3,2},{4,5},{5,4},{6,7},{7,6},{8,9},{9,8},{10,11... | collective-permute-start | bytes 786440 | tf_op jit(solution)/shard_map/ppermute | solution.py:631
  2.9 18.6 %collective-permute-start = (bf16[528,256]{1,0:T(8,128)(2,1)}, bf16[528,256]{1,0:T(8,128)(2,1)S(1)}, u32[]{:S(2)}, u32[]{:S(2)}) collective-permute-start(bf16[528,256]{1,0:T(8,128)(2,1)} %get-tuple-element.60.refs_2_), channel_id=1, source_target_pairs={{0,4},{4,8},{8,12},{12,0},{1,5},{5,9},{9,13},{13,1},{2,6},{6,10},{... | collective-permute-start | bytes 811016 | tf_op jit(solution)/shard_map/ppermute | solution.py:628
  5.5 21.1 %collective-permute-start.1 = (bf16[528,256]{1,0:T(8,128)(2,1)}, bf16[528,256]{1,0:T(8,128)(2,1)S(1)}, u32[]{:S(2)}, u32[]{:S(2)}) collective-permute-start(bf16[528,256]{1,0:T(8,128)(2,1)} %get-tuple-element.60.refs_2_), channel_id=1, source_target_pairs={{0,8},{4,12},{8,0},{12,4},{1,9},{5,13},{9,1},{13,5},{2,10},{6,14},... | collective-permute-start | bytes 811016 | tf_op jit(solution)/shard_map/ppermute | solution.py:628
  8.0 18.5 %collective-permute-start.2 = (bf16[528,256]{1,0:T(8,128)(2,1)}, bf16[528,256]{1,0:T(8,128)(2,1)}, u32[]{:S(2)}, u32[]{:S(2)}) collective-permute-start(bf16[528,256]{1,0:T(8,128)(2,1)} %get-tuple-element.60.refs_2_), channel_id=1, source_target_pairs={{0,12},{4,0},{8,4},{12,8},{1,13},{5,1},{9,5},{13,9},{2,14},{6,2},{... | collective-permute-start | bytes 811016 | tf_op jit(solution)/shard_map/ppermute | solution.py:628
  9.4 2.8 %copy-start = (bf16[128,16,1536]{2,1,0:T(8,128)(2,1)S(1)}, bf16[128,16,1536]{2,1,0:T(8,128)(2,1)}, u32[]{:S(2)}) copy-start(bf16[128,16,1536]{2,1,0:T(8,128)(2,1)} %param.10) | copy-start | bytes 18874372
  12.2 1.4 copy-start.1
  13.6 0.7 copy-start.8
  14.3 3.9 %copy-start.4 = (bf16[512,256]{1,0:T(8,128)(2,1)S(1)}, bf16[512,256]{1,0:T(8,128)(2,1)}, u32[]{:S(2)}) copy-start(bf16[512,256]{1,0:T(8,128)(2,1)} %refs_1_.1) | copy-start | bytes 786436
  18.3 2.5 %copy-start.5 = (bf16[512,256]{1,0:T(8,128)(2,1)}, bf16[512,256]{1,0:T(8,128)(2,1)S(1)}, u32[]{:S(2)}) copy-start(bf16[512,256]{1,0:T(8,128)(2,1)S(1)} %collective-permute-done.3.refs_2_) | copy-start | bytes 786436
  19.2 15.9 %collective-permute-start.4 = (bf16[1024,256]{1,0:T(8,128)(2,1)}, bf16[1024,256]{1,0:T(8,128)(2,1)}, u32[]{:S(2)}, u32[]{:S(2)}) collective-permute-start(bf16[1024,256]{1,0:T(8,128)(2,1)} %pad_maximum_fusion), channel_id=1, source_target_pairs={{0,2},{1,3},{2,0},{3,1},{4,6},{5,7},{6,4},{7,5},{8,10},{9,11},{10,... | collective-permute-start | bytes 1572872 | tf_op jit(solution)/shard_map/ppermute | solution.py:631
  20.8 41.0 %collective-permute-start.7 = (bf16[256,1536]{1,0:T(8,128)(2,1)S(1)}, bf16[256,1536]{1,0:T(8,128)(2,1)S(1)}, u32[]{:S(2)}, u32[]{:S(2)}) collective-permute-start(bf16[256,1536]{1,0:T(8,128)(2,1)S(1)} %get-tuple-element.69), channel_id=1, source_target_pairs={{4,8},{8,4},{5,9},{9,5},{6,10},{10,6},{7,11},{11,7},{20,24},{24,20... | collective-permute-start | bytes 2359304 | tf_op jit(solution)/shard_map/ppermute | solution.py:645
  21.5 13.5 %copy-start.6 = (bf16[512,256]{1,0:T(8,128)(2,1)S(1)}, bf16[512,256]{1,0:T(8,128)(2,1)}, u32[]{:S(2)}) copy-start(bf16[512,256]{1,0:T(8,128)(2,1)} %copy-done.5) | copy-start | bytes 786436
  21.5 40.2 %collective-permute-start.8 = (bf16[256,1536]{1,0:T(8,128)(2,1)S(1)}, bf16[256,1536]{1,0:T(8,128)(2,1)S(1)}, u32[]{:S(2)}, u32[]{:S(2)}) collective-permute-start(bf16[256,1536]{1,0:T(8,128)(2,1)S(1)} %get-tuple-element.69), channel_id=1, source_target_pairs={{0,4},{4,0},{8,12},{12,8},{1,5},{5,1},{9,13},{13,9},{2,6},{6,2},{1... | collective-permute-start | bytes 2359304 | tf_op jit(solution)/shard_map/ppermute | solution.py:645
  26.6 41.7 %collective-permute-start.11 = (bf16[256,1536]{1,0:T(8,128)(2,1)S(1)}, bf16[256,1536]{1,0:T(8,128)(2,1)S(1)}, u32[]{:S(2)}, u32[]{:S(2)}) collective-permute-start(bf16[256,1536]{1,0:T(8,128)(2,1)S(1)} %get-tuple-element.77), channel_id=1, source_target_pairs={{4,8},{8,4},{5,9},{9,5},{6,10},{10,6},{7,11},{11,7},{20,24},{24,20... | collective-permute-start | bytes 2359304 | tf_op jit(solution)/shard_map/ppermute | solution.py:645
  27.3 41.0 %collective-permute-start.12 = (bf16[256,1536]{1,0:T(8,128)(2,1)S(1)}, bf16[256,1536]{1,0:T(8,128)(2,1)S(1)}, u32[]{:S(2)}, u32[]{:S(2)}) collective-permute-start(bf16[256,1536]{1,0:T(8,128)(2,1)S(1)} %get-tuple-element.77), channel_id=1, source_target_pairs={{0,4},{4,0},{8,12},{12,8},{1,5},{5,1},{9,13},{13,9},{2,6},{6,2},{1... | collective-permute-start | bytes 2359304 | tf_op jit(solution)/shard_map/ppermute | solution.py:645
  35.0 1.9 %copy-start.3 = (bf16[1536,1024]{1,0:T(8,128)(2,1)S(1)}, bf16[1536,1024]{1,0:T(8,128)(2,1)}, u32[]{:S(2)}) copy-start(bf16[1536,1024]{1,0:T(8,128)(2,1)} %refs_4_.3) | copy-start | bytes 9437188
  36.9 3.6 %copy-start.7 = (bf16[528,256]{1,0:T(8,128)(2,1)S(1)}, bf16[528,256]{1,0:T(8,128)(2,1)}, u32[]{:S(2)}) copy-start(bf16[528,256]{1,0:T(8,128)(2,1)} %get-tuple-element.60.refs_2_) | copy-start | bytes 811012
  36.9 3.6 %copy-start.9 = (bf16[128,16,256]{2,1,0:T(8,128)(2,1)S(1)}, bf16[128,16,256]{2,1,0:T(8,128)(2,1)}, u32[]{:S(2)}) copy-start(bf16[128,16,256]{2,1,0:T(8,128)(2,1)} %param.11) | copy-start | bytes 3145732
  40.5 15.9 %slice-start = ((s8[6291456]{0:T(1024)(128)(4,1)}), s8[4194304]{0:T(1024)(128)(4,1)S(1)}, s32[]{:S(2)}) async-start(s8[6291456]{0:T(1024)(128)(4,1)} %bitcast.11), calls=%async_computation | async-start | bytes 8388608
  40.5 15.9 %slice-start.1 = ((s8[6291456]{0:T(1024)(128)(4,1)}), s8[2097152]{0:T(1024)(128)(4,1)S(1)}, s32[]{:S(2)}) async-start(s8[6291456]{0:T(1024)(128)(4,1)} %bitcast.11), calls=%async_computation.1 | async-start | bytes 4194304
  46.3 1.6 collective-permute-start.5
  48.0 8.4 %collective-permute-start.6 = (f32[128,512]{1,0:T(8,128)S(1)}, f32[128,512]{1,0:T(8,128)S(1)}, u32[]{:S(2)}, u32[]{:S(2)}) collective-permute-start(f32[128,512]{1,0:T(8,128)S(1)} %add.21), channel_id=1, source_target_pairs={{0,2},{1,3},{2,0},{3,1},{4,6},{5,7},{6,4},{7,5},{8,10},{9,11},{10,... | collective-permute-start | bytes 786440 | tf_op jit(solution)/shard_map/ppermute | solution.py:620
  62.2 20.5 %collective-permute-start.10 = (bf16[256,1536]{1,0:T(8,128)(2,1)S(1)}, bf16[256,1536]{1,0:T(8,128)(2,1)S(1)}, u32[]{:S(2)}, u32[]{:S(2)}) collective-permute-start(bf16[256,1536]{1,0:T(8,128)(2,1)S(1)} %get-tuple-element.73.refs_6_.refs_5_), channel_id=1, source_target_pairs={{0,4},{4,0},{8,12},{12,8},{1,5},{5,1},{9,13},{13,9},{2,6},{6,2},{1... | collective-permute-start | bytes 2359304 | tf_op jit(solution)/shard_map/ppermute | solution.py:672
  62.3 20.5 %collective-permute-start.9 = (bf16[256,1536]{1,0:T(8,128)(2,1)S(1)}, bf16[256,1536]{1,0:T(8,128)(2,1)S(1)}, u32[]{:S(2)}, u32[]{:S(2)}) collective-permute-start(bf16[256,1536]{1,0:T(8,128)(2,1)S(1)} %get-tuple-element.72.refs_4_), channel_id=1, source_target_pairs={{4,8},{8,4},{5,9},{9,5},{6,10},{10,6},{7,11},{11,7},{20,24},{24,20... | collective-permute-start | bytes 2359304 | tf_op jit(solution)/shard_map/ppermute | solution.py:672
  68.7 27.7 %collective-permute-start.15 = (bf16[256,1536]{1,0:T(8,128)(2,1)S(1)}, bf16[256,1536]{1,0:T(8,128)(2,1)S(1)}, u32[]{:S(2)}, u32[]{:S(2)}) collective-permute-start(bf16[256,1536]{1,0:T(8,128)(2,1)S(1)} %get-tuple-element.79.refs_5_.refs_6_), channel_id=1, source_target_pairs={{4,8},{8,4},{5,9},{9,5},{6,10},{10,6},{7,11},{11,7},{20,24},{24,20... | collective-permute-start | bytes 2359304 | tf_op jit(solution)/shard_map/ppermute | solution.py:672
  69.4 30.1 %collective-permute-start.16 = (bf16[256,1536]{1,0:T(8,128)(2,1)S(1)}, bf16[256,1536]{1,0:T(8,128)(2,1)S(1)}, u32[]{:S(2)}, u32[]{:S(2)}) collective-permute-start(bf16[256,1536]{1,0:T(8,128)(2,1)S(1)} %get-tuple-element.87.refs_7_), channel_id=1, source_target_pairs={{0,4},{4,0},{8,12},{12,8},{1,5},{5,1},{9,13},{13,9},{2,6},{6,2},{1... | collective-permute-start | bytes 2359304 | tf_op jit(solution)/shard_map/ppermute | solution.py:672
  83.3 28.6 %collective-permute-start.13 = (bf16[256,1536]{1,0:T(8,128)(2,1)S(1)}, bf16[256,1536]{1,0:T(8,128)(2,1)S(1)}, u32[]{:S(2)}, u32[]{:S(2)}) collective-permute-start(bf16[256,1536]{1,0:T(8,128)(2,1)S(1)} %get-tuple-element.82.refs_4_.refs_8_), channel_id=1, source_target_pairs={{4,8},{8,4},{5,9},{9,5},{6,10},{10,6},{7,11},{11,7},{20,24},{24,20... | collective-permute-start | bytes 2359304 | tf_op jit(solution)/shard_map/ppermute | solution.py:672
  84.1 32.4 %collective-permute-start.14 = (bf16[256,1536]{1,0:T(8,128)(2,1)S(1)}, bf16[256,1536]{1,0:T(8,128)(2,1)S(1)}, u32[]{:S(2)}, u32[]{:S(2)}) collective-permute-start(bf16[256,1536]{1,0:T(8,128)(2,1)S(1)} %get-tuple-element.83.refs_6_.refs_9_), channel_id=1, source_target_pairs={{0,4},{4,0},{8,12},{12,8},{1,5},{5,1},{9,13},{13,9},{2,6},{6,2},{1... | collective-permute-start | bytes 2359304 | tf_op jit(solution)/shard_map/ppermute | solution.py:672
  100.0 27.5 %collective-permute-start.17 = (bf16[256,1536]{1,0:T(8,128)(2,1)S(1)}, bf16[256,1536]{1,0:T(8,128)(2,1)S(1)}, u32[]{:S(2)}, u32[]{:S(2)}) collective-permute-start(bf16[256,1536]{1,0:T(8,128)(2,1)S(1)} %get-tuple-element.89.refs_5_.refs_10_), channel_id=1, source_target_pairs={{4,8},{8,4},{5,9},{9,5},{6,10},{10,6},{7,11},{11,7},{20,24},{24,20... | collective-permute-start | bytes 2359304 | tf_op jit(solution)/shard_map/ppermute | solution.py:672
  100.7 32.6 %collective-permute-start.18 = (bf16[256,1536]{1,0:T(8,128)(2,1)S(1)}, bf16[256,1536]{1,0:T(8,128)(2,1)S(1)}, u32[]{:S(2)}, u32[]{:S(2)}) collective-permute-start(bf16[256,1536]{1,0:T(8,128)(2,1)S(1)} %get-tuple-element.94.refs_7_.refs_11_), channel_id=1, source_target_pairs={{0,4},{4,0},{8,12},{12,8},{1,5},{5,1},{9,13},{13,9},{2,6},{6,2},{1... | collective-permute-start | bytes 2359304 | tf_op jit(solution)/shard_map/ppermute | solution.py:672
  116.9 45.4 %collective-permute-start.21 = (bf16[256,1536]{1,0:T(8,128)(2,1)S(1)}, bf16[256,1536]{1,0:T(8,128)(2,1)S(1)}, u32[]{:S(2)}, u32[]{:S(2)}) collective-permute-start(bf16[256,1536]{1,0:T(8,128)(2,1)S(1)} %get-tuple-element.98.refs_13_), channel_id=1, source_target_pairs={{0,4},{4,0},{8,12},{12,8},{1,5},{5,1},{9,13},{13,9},{2,6},{6,2},{1... | collective-permute-start | bytes 2359304 | tf_op jit(solution)/shard_map/ppermute | solution.py:672
  121.2 41.1 %collective-permute-start.22 = (bf16[256,1536]{1,0:T(8,128)(2,1)S(1)}, bf16[256,1536]{1,0:T(8,128)(2,1)S(1)}, u32[]{:S(2)}, u32[]{:S(2)}) collective-permute-start(bf16[256,1536]{1,0:T(8,128)(2,1)S(1)} %get-tuple-element.99.refs_4_.refs_12_), channel_id=1, source_target_pairs={{4,8},{8,4},{5,9},{9,5},{6,10},{10,6},{7,11},{11,7},{20,24},{24,20... | collective-permute-start | bytes 2359304 | tf_op jit(solution)/shard_map/ppermute | solution.py:672
  133.7 39.9 %collective-permute-start.19 = (bf16[256,1536]{1,0:T(8,128)(2,1)S(1)}, bf16[256,1536]{1,0:T(8,128)(2,1)S(1)}, u32[]{:S(2)}, u32[]{:S(2)}) collective-permute-start(bf16[256,1536]{1,0:T(8,128)(2,1)S(1)} %get-tuple-element.96.refs_15_), channel_id=1, source_target_pairs={{0,4},{4,0},{8,12},{12,8},{1,5},{5,1},{9,13},{13,9},{2,6},{6,2},{1... | collective-permute-start | bytes 2359304 | tf_op jit(solution)/shard_map/ppermute | solution.py:672
  138.1 35.6 %collective-permute-start.20 = (bf16[256,1536]{1,0:T(8,128)(2,1)S(1)}, bf16[256,1536]{1,0:T(8,128)(2,1)S(1)}, u32[]{:S(2)}, u32[]{:S(2)}) collective-permute-start(bf16[256,1536]{1,0:T(8,128)(2,1)S(1)} %get-tuple-element.97.refs_5_.refs_14_), channel_id=1, source_target_pairs={{4,8},{8,4},{5,9},{9,5},{6,10},{10,6},{7,11},{11,7},{20,24},{24,20... | collective-permute-start | bytes 2359304 | tf_op jit(solution)/shard_map/ppermute | solution.py:672
  139.0 7.3 %copy-start.2 = (bf16[512,1536]{1,0:T(8,128)(2,1)S(1)}, bf16[512,1536]{1,0:T(8,128)(2,1)}, u32[]{:S(2)}) copy-start(bf16[512,1536]{1,0:T(8,128)(2,1)} %refs_3_.3) | copy-start | bytes 4718596
  143.1 1.6 collective-permute-start.23
  144.8 17.4 %collective-permute-start.24 = (f32[128,512]{1,0:T(8,128)S(1)}, f32[128,512]{1,0:T(8,128)S(1)}, u32[]{:S(2)}, u32[]{:S(2)}) collective-permute-start(f32[128,512]{1,0:T(8,128)S(1)} %add.23), channel_id=1, source_target_pairs={{0,2},{1,3},{2,0},{3,1},{4,6},{5,7},{6,4},{7,5},{8,10},{9,11},{10,... | collective-permute-start | bytes 786440 | tf_op jit(solution)/shard_map/ppermute | solution.py:620
  163.4 11.3 %collective-permute-start.25 = (bf16[2,512]{1,0:T(2,128)(2,1)S(1)}, bf16[2,512]{1,0:T(2,128)(2,1)S(1)}, u32[]{:S(2)}, u32[]{:S(2)}) collective-permute-start(bf16[2,512]{1,0:T(2,128)(2,1)S(1)} %get-tuple-element.111), channel_id=1, source_target_pairs={{0,12},{4,0},{8,4},{12,8},{1,13},{5,1},{9,5},{13,9},{2,14},{6,2},{... | collective-permute-start | bytes 6152 | tf_op jit(solution)/shard_map/ppermute | solution.py:692
  166.4 8.3 %collective-permute-start.26 = (bf16[2,512]{1,0:T(2,128)(2,1)S(1)}, bf16[2,512]{1,0:T(2,128)(2,1)S(1)}, u32[]{:S(2)}, u32[]{:S(2)}) collective-permute-start(bf16[2,512]{1,0:T(2,128)(2,1)S(1)} %get-tuple-element.112), channel_id=1, source_target_pairs={{0,8},{4,12},{8,0},{12,4},{1,9},{5,13},{9,1},{13,5},{2,10},{6,14},... | collective-permute-start | bytes 6152 | tf_op jit(solution)/shard_map/ppermute | solution.py:692
  168.2 6.5 %collective-permute-start.27 = (bf16[2,512]{1,0:T(2,128)(2,1)S(1)}, bf16[2,512]{1,0:T(2,128)(2,1)S(1)}, u32[]{:S(2)}, u32[]{:S(2)}) collective-permute-start(bf16[2,512]{1,0:T(2,128)(2,1)S(1)} %get-tuple-element.113), channel_id=1, source_target_pairs={{0,4},{4,8},{8,12},{12,0},{1,5},{5,9},{9,13},{13,1},{2,6},{6,10},{... | collective-permute-start | bytes 6152 | tf_op jit(solution)/shard_map/ppermute | solution.py:692

commit v7 on v6

--- a/solution.py
+++ b/solution.py
@@ -640,7 +640,7 @@
     low, token = project_in(pos, size, [(-1, True)], down, aux_own, low, [inputs], 1, rank)
 
     sent, tokens = zip(
-        *[pin(inputs[c * half : (c + 1) * half], [token] if c == 0 else blocks[1:]) for c in range(CHUNKS)]
+        *[pin(inputs[c * half : (c + 1) * half], [token]) for c in range(CHUNKS)]
     )
     got = [[lax.ppermute(sent[c], "dp", p) for p in (pairs_a, pairs_b)] for c in range(CHUNKS)]
 

time: 176 us -> 173 us (0.983)
  starting transfers between devices: 63.1 us -> 55.2 us
  local copies, waits for them, and re-layouts: 6.96 us -> 9.65 us
    ppermute x4, starting transfers between devices: 12.9 us -> 4.72 us  [per_device(): lax.ppermute(sent[c], 'dp', p)]
    ppermute x2, waiting for transfers between devices: 0.01 us -> 2.46 us  [per_device(): lax.ppermute(rows, 'mp', [(i, i ^ bit) for i in range(shares)])]
    slice x1, local copies, waits for them, and re-layouts: 0.1 us -> 2.35 us  [per_device(): inputs[c * half:(c + 1) * half]]
    unnamed x24 -> x22, local copies, waits for them, and re-layouts: 6.84 us -> 7.28 us
  transfers between devices with their start and end apart: 28 -> 28, of which waited for: 8 -> 8; matrix products, arithmetic and copies ran while one was open for 1% -> 2% of each run, Pallas kernels for 43% -> 44%
where the time goes in v7:
time: 173 us; the launch traced here: 172 us
  Pallas kernels  75 us (43%)
  starting transfers between devices  55.2 us (32%)
  waiting for transfers between devices  28.8 us (17%)
  local copies, waits for them, and re-layouts  9.65 us (6%)
  other arithmetic  2.53 us (1%)
    pallas_call x24, Pallas kernels, call(): return lambda *arrays: call_it(*arrays, *after)  75 us
    ppermute x6, starting transfers between devices, per_device(): lax.ppermute(to_a, 'dp', pairs_a)  29.4 us
    ppermute x6, waiting for transfers between devices, per_device(): lax.ppermute(to_a, 'dp', pairs_a)  16.4 us
    ppermute x4, waiting for transfers between devices, exchange(): lax.ppermute(part, 'mp', [(i, i ^ bit) for i in range(shares)])  9.88 us
    unnamed x22, local copies, waits for them, and re-layouts  7.28 us
    ppermute x3, starting transfers between devices, per_device(): lax.ppermute(block, 'dp', [(i, (i + s) % size) for i in range(size)])  6.53 us
    ppermute x3, starting transfers between devices, per_device(): lax.ppermute(gate_rows[s], 'dp', [(i, (i - s) % size) for i in range(size)])  4.76 us
    ppermute x4, starting transfers between devices, per_device(): lax.ppermute(sent[c], 'dp', p)  4.72 us
  transfers between devices with their start and end apart: 28, of which 8 were waited for; matrix products, arithmetic and copies ran while one was open for 2% of the time, Pallas kernels for 44%

profile of v7, /device:TPU:0, one launch (start us, length us, event | category | flops | bytes accessed | tf_op | source)
XLA Modules:
  0.0 172.3 jit_solution(12774561132231337462)
XLA Ops:
  0.6 0.5 collective-permute-start.3
  1.1 1.7 shard_map.102
  2.9 2.6 %collective-permute-start = (bf16[528,256]{1,0:T(8,128)(2,1)}, bf16[528,256]{1,0:T(8,128)(2,1)}, u32[]{:S(2)}, u32[]{:S(2)}) collective-permute-start(bf16[528,256]{1,0:T(8,128)(2,1)} %get-tuple-element.60.refs_2_), channel_id=1, source_target_pairs={{0,4},{4,8},{8,12},{12,0},{1,5},{5,9},{9,13},{13,1},{2,6},{6,10},{... | collective-permute-start | bytes 811016 | tf_op jit(solution)/shard_map/ppermute | solution.py:628
  5.5 2.6 %collective-permute-start.1 = (bf16[528,256]{1,0:T(8,128)(2,1)}, bf16[528,256]{1,0:T(8,128)(2,1)}, u32[]{:S(2)}, u32[]{:S(2)}) collective-permute-start(bf16[528,256]{1,0:T(8,128)(2,1)} %get-tuple-element.60.refs_2_), channel_id=1, source_target_pairs={{0,8},{4,12},{8,0},{12,4},{1,9},{5,13},{9,1},{13,5},{2,10},{6,14},... | collective-permute-start | bytes 811016 | tf_op jit(solution)/shard_map/ppermute | solution.py:628
  8.0 1.3 collective-permute-start.2
  9.4 1.8 %pad_maximum_fusion = bf16[1024,256]{1,0:T(8,128)(2,1)} fusion(bf16[512,256]{1,0:T(8,128)(2,1)S(1)} %collective-permute-done.3.refs_2_, bf16[512,256]{1,0:T(8,128)(2,1)} %refs_1_.1), kind=kLoop, calls=%fused_computation | loop fusion | flops 1048576 | bytes 1048576 | tf_op jit(solution)/shard_map/concatenate | solution.py:633
  11.2 0.7 copy-done.4
  11.9 1.5 collective-permute-start.4
  13.4 2.4 %fusion.1 = (bf16[256,1536]{1,0:T(8,128)(2,1)S(1)}, bf16[256,1536]{1,0:T(8,128)(2,1)}) fusion(bf16[512,1536]{1,0:T(8,128)(2,1)} %refs_3_.3), kind=kLoop, calls=%fused_computation.3 | loop fusion | bytes 3145728 | tf_op jit(solution)/shard_map/slice | solution.py:643
  15.8 2.8 %copy-done = bf16[128,16,1536]{2,1,0:T(8,128)(2,1)S(1)} copy-done((bf16[128,16,1536]{2,1,0:T(8,128)(2,1)S(1)}, bf16[128,16,1536]{2,1,0:T(8,128)(2,1)}, u32[]{:S(2)}) %copy-start) | copy-done | bytes 6291480
  18.6 3.9 %shard_map.103 = (f32[128,512]{1,0:T(8,128)S(1)}, f32[8,128]{1,0:T(8,128)S(1)}) custom-call(s32[1]{0:T(128)} %bitcast.refs_0_, bf16[2048,1536]{1,0:T(8,128)(2,1)S(1)} %bitcast.10, f32[8,512]{1,0:T(8,128)S(1)} %copy-done.7, f32[128,512]{1,0:T(8,128)S(1)} %broadcast_in_dim.3.refs_3_, bf16[512,1536]{1,0:T(8,128)(2,1)S(1)} %copy-done.1), custom_call_target="tpu_custom_call", output_to_operand_aliasing={{0}: (3, {})} | custom-call | flops 64424508 | bytes 157286 | tf_op jit(solution)/shard_map/pallas_call | solution.py:53
  22.5 0.7 collective-permute-start.7
  23.2 2.5 %collective-permute-done.4.refs_3_ = bf16[1024,256]{1,0:T(8,128)(2,1)} collective-permute-done((bf16[1024,256]{1,0:T(8,128)(2,1)}, bf16[1024,256]{1,0:T(8,128)(2,1)}, u32[]{:S(2)}, u32[]{:S(2)}) %collective-permute-start.4) | collective-permute-done | bytes 524320 | tf_op jit(solution)/shard_map/ppermute | solution.py:631
  25.7 0.7 collective-permute-start.8
  26.3 1.9 %copy-done.2 = bf16[1536,1024]{1,0:T(8,128)(2,1)S(1)} copy-done((bf16[1536,1024]{1,0:T(8,128)(2,1)S(1)}, bf16[1536,1024]{1,0:T(8,128)(2,1)}, u32[]{:S(2)}) %copy-start.2) | copy-done | bytes 3145752
  28.2 0.9 copy-done.3
  29.2 0.9 copy-done.5
  30.1 3.6 %shard_map.104 = (f32[512,1536]{1,0:T(8,128)S(1)}, f32[8,128]{1,0:T(8,128)S(1)}) custom-call(s32[1]{0:T(128)} %bitcast.4.refs_0_, bf16[512,256]{1,0:T(8,128)(2,1)S(1)} %copy-done.3, bf16[512,256]{1,0:T(8,128)(2,1)S(1)} %copy-done.5, bf16[1024,256]{1,0:T(8,128)(2,1)} %collective-permute-done.4.refs_3_, bf16[1536,1024]{1,0:T(8,128)(2,1)S(1)} %copy-done.2, ...), custom_call_target="tpu_custom_call" | custom-call | flops 32212254 | bytes 62914 | tf_op jit(solution)/shard_map/pallas_call | solution.py:53
  33.7 0.7 collective-permute-start.11
  34.5 2.6 %collective-permute-start.12 = (bf16[256,1536]{1,0:T(8,128)(2,1)S(1)}, bf16[256,1536]{1,0:T(8,128)(2,1)S(1)}, u32[]{:S(2)}, u32[]{:S(2)}) collective-permute-start(bf16[256,1536]{1,0:T(8,128)(2,1)S(1)} %get-tuple-element.77), channel_id=1, source_target_pairs={{0,4},{4,0},{8,12},{12,8},{1,5},{5,1},{9,13},{13,9},{2,6},{6,2},{1... | collective-permute-start | bytes 2359304 | tf_op jit(solution)/shard_map/ppermute | solution.py:645
  37.1 5.9 %shard_map.107 = (f32[128,512]{1,0:T(8,128)S(1)}, f32[32,512]{1,0:T(8,128)S(1)}, f32[8,128]{1,0:T(8,128)}) custom-call(s32[1]{0:T(128)} %bitcast.refs_0_, bf16[2048,256]{1,0:T(8,128)(2,1)S(1)} %bitcast.20, bf16[528,256]{1,0:T(8,128)(2,1)S(1)} %copy-done.6, bf16[528,256]{1,0:T(8,128)(2,1)} %collective-permute-done.refs_3_, ...), custom_call_target="tpu_custom_call" | custom-call | flops 10737418240 | bytes 10485760 | tf_op jit(solution)/shard_map/pallas_call | solution.py:53
  43.0 0.1 collective-permute-start.5
  43.1 1.5 collective-permute-done.5
  44.7 1.6 collective-permute-start.6
  46.2 6.8 %collective-permute-done.6 = f32[128,512]{1,0:T(8,128)S(1)} collective-permute-done((f32[128,512]{1,0:T(8,128)S(1)}, f32[128,512]{1,0:T(8,128)S(1)}, u32[]{:S(2)}, u32[]{:S(2)}) %collective-permute-start.6) | collective-permute-done | bytes 262176 | tf_op jit(solution)/shard_map/ppermute | solution.py:620
  53.1 5.3 %shard_map.108 = (bf16[512,1536]{1,0:T(8,128)(2,1)S(1)}, f32[8,128]{1,0:T(8,128)S(1)}) custom-call(s32[1]{0:T(128)} %bitcast.refs_0_, f32[128,512]{1,0:T(8,128)S(1)} %add.22.refs_1_, f32[32,512]{1,0:T(8,128)S(1)} %get-tuple-element.67.refs_2_.refs_1_, bf16[2048,1536]{1,0:T(8,128)(2,1)S(1)} %bitcast.13), custom_call_target="tpu_custom_call" | custom-call | flops 64424508 | bytes 157286 | tf_op jit(solution)/shard_map/pallas_call | solution.py:53
  58.4 0.4 shard_map.109
  58.9 0.1 collective-permute-start.10
  59.0 0.7 collective-permute-start.9
  59.7 5.3 %shard_map.110 = (bf16[512,1536]{1,0:T(8,128)(2,1)S(1)}, f32[8,128]{1,0:T(8,128)S(1)}) custom-call(s32[1]{0:T(128)} %bitcast.refs_0_, f32[128,512]{1,0:T(8,128)S(1)} %add.22.refs_1_, f32[32,512]{1,0:T(8,128)S(1)} %get-tuple-element.67.refs_2_.refs_1_, bf16[2048,1536]{1,0:T(8,128)(2,1)S(1)} %bitcast.14, f32[8,128]{1,0:T(8,128)S(1)} %get-tuple-element.74.refs_4_), custom_call_target="tpu_custom_call" | custom-call | flops 64424508 | bytes 157286 | tf_op jit(solution)/shard_map/pallas_call | solution.py:53
  65.0 0.4 shard_map.111
  65.4 0.7 collective-permute-start.15
  66.1 6.1 %collective-permute-start.16 = (bf16[256,1536]{1,0:T(8,128)(2,1)S(1)}, bf16[256,1536]{1,0:T(8,128)(2,1)S(1)}, u32[]{:S(2)}, u32[]{:S(2)}) collective-permute-start(bf16[256,1536]{1,0:T(8,128)(2,1)S(1)} %get-tuple-element.87.refs_7_), channel_id=1, source_target_pairs={{0,4},{4,0},{8,12},{12,8},{1,5},{5,1},{9,13},{13,9},{2,6},{6,2},{1... | collective-permute-start | bytes 2359304 | tf_op jit(solution)/shard_map/ppermute | solution.py:672
  72.3 3.9 %shard_map.112 = (f32[128,512]{1,0:T(8,128)S(1)}, f32[8,128]{1,0:T(8,128)S(1)}) custom-call(s32[1]{0:T(128)} %bitcast.refs_0_, bf16[2048,1536]{1,0:T(8,128)(2,1)S(1)} %bitcast.15, f32[32,512]{1,0:T(8,128)S(1)} %get-tuple-element.67.refs_2_.refs_1_, f32[128,512]{1,0:T(8,128)S(1)} %get-tuple-element.76.refs_3_, ...), custom_call_target="tpu_custom_call", output_to_operand_aliasing={{0}: (3, {})} | custom-call | flops 64424508 | bytes 157286 | tf_op jit(solution)/shard_map/pallas_call | solution.py:53
  76.2 3.2 %collective-permute-done.10.refs_2_ = bf16[256,1536]{1,0:T(8,128)(2,1)S(1)} collective-permute-done((bf16[256,1536]{1,0:T(8,128)(2,1)S(1)}, bf16[256,1536]{1,0:T(8,128)(2,1)S(1)}, u32[]{:S(2)}, u32[]{:S(2)}) %collective-permute-start.10) | collective-permute-done | bytes 786464 | tf_op jit(solution)/shard_map/ppermute | solution.py:672
  79.4 0.6 shard_map.113
  80.0 0.7 collective-permute-start.13
  80.8 7.2 %collective-permute-start.14 = (bf16[256,1536]{1,0:T(8,128)(2,1)S(1)}, bf16[256,1536]{1,0:T(8,128)(2,1)S(1)}, u32[]{:S(2)}, u32[]{:S(2)}) collective-permute-start(bf16[256,1536]{1,0:T(8,128)(2,1)S(1)} %get-tuple-element.83.refs_6_.refs_9_), channel_id=1, source_target_pairs={{0,4},{4,0},{8,12},{12,8},{1,5},{5,1},{9,13},{13,9},{2,6},{6,2},{1... | collective-permute-start | bytes 2359304 | tf_op jit(solution)/shard_map/ppermute | solution.py:672
  87.9 5.2 %shard_map.114 = (bf16[512,1536]{1,0:T(8,128)(2,1)S(1)}, f32[8,128]{1,0:T(8,128)S(1)}) custom-call(s32[1]{0:T(128)} %bitcast.refs_0_, f32[128,512]{1,0:T(8,128)S(1)} %add.22.refs_1_, f32[32,512]{1,0:T(8,128)S(1)} %get-tuple-element.67.refs_2_.refs_1_, bf16[2048,1536]{1,0:T(8,128)(2,1)S(1)} %bitcast.16, f32[8,128]{1,0:T(8,128)S(1)} %get-tuple-element.84.refs_4_), custom_call_target="tpu_custom_call" | custom-call | flops 64424508 | bytes 157286 | tf_op jit(solution)/shard_map/pallas_call | solution.py:53
  93.2 3.1 %collective-permute-done.16.refs_2_ = bf16[256,1536]{1,0:T(8,128)(2,1)S(1)} collective-permute-done((bf16[256,1536]{1,0:T(8,128)(2,1)S(1)}, bf16[256,1536]{1,0:T(8,128)(2,1)S(1)}, u32[]{:S(2)}, u32[]{:S(2)}) %collective-permute-start.16) | collective-permute-done | bytes 786464 | tf_op jit(solution)/shard_map/ppermute | solution.py:672
  96.3 0.4 shard_map.115
  96.7 0.7 collective-permute-start.17
  97.4 7.2 %collective-permute-start.18 = (bf16[256,1536]{1,0:T(8,128)(2,1)S(1)}, bf16[256,1536]{1,0:T(8,128)(2,1)S(1)}, u32[]{:S(2)}, u32[]{:S(2)}) collective-permute-start(bf16[256,1536]{1,0:T(8,128)(2,1)S(1)} %get-tuple-element.94.refs_7_.refs_11_), channel_id=1, source_target_pairs={{0,4},{4,0},{8,12},{12,8},{1,5},{5,1},{9,13},{13,9},{2,6},{6,2},{1... | collective-permute-start | bytes 2359304 | tf_op jit(solution)/shard_map/ppermute | solution.py:672
  104.6 4.1 %shard_map.116 = (f32[128,512]{1,0:T(8,128)S(1)}, f32[8,128]{1,0:T(8,128)S(1)}) custom-call(s32[1]{0:T(128)} %bitcast.refs_0_, bf16[2048,1536]{1,0:T(8,128)(2,1)S(1)} %bitcast.17, f32[32,512]{1,0:T(8,128)S(1)} %get-tuple-element.67.refs_2_.refs_1_, f32[128,512]{1,0:T(8,128)S(1)} %get-tuple-element.86.refs_3_, ...), custom_call_target="tpu_custom_call", output_to_operand_aliasing={{0}: (3, {})} | custom-call | flops 64424508 | bytes 157286 | tf_op jit(solution)/shard_map/pallas_call | solution.py:53
  108.7 4.4 %collective-permute-done.14.refs_2_ = bf16[256,1536]{1,0:T(8,128)(2,1)S(1)} collective-permute-done((bf16[256,1536]{1,0:T(8,128)(2,1)S(1)}, bf16[256,1536]{1,0:T(8,128)(2,1)S(1)}, u32[]{:S(2)}, u32[]{:S(2)}) %collective-permute-start.14) | collective-permute-done | bytes 786464 | tf_op jit(solution)/shard_map/ppermute | solution.py:672
  113.1 0.4 shard_map.117
  113.6 4.4 %collective-permute-start.21 = (bf16[256,1536]{1,0:T(8,128)(2,1)S(1)}, bf16[256,1536]{1,0:T(8,128)(2,1)S(1)}, u32[]{:S(2)}, u32[]{:S(2)}) collective-permute-start(bf16[256,1536]{1,0:T(8,128)(2,1)S(1)} %get-tuple-element.98.refs_13_), channel_id=1, source_target_pairs={{0,4},{4,0},{8,12},{12,8},{1,5},{5,1},{9,13},{13,9},{2,6},{6,2},{1... | collective-permute-start | bytes 2359304 | tf_op jit(solution)/shard_map/ppermute | solution.py:672
  118.0 0.7 collective-permute-start.22
  118.7 5.6 %shard_map.118 = (f32[512,1536]{1,0:T(8,128)S(1)}, f32[8,128]{1,0:T(8,128)S(1)}) custom-call(s32[1]{0:T(128)} %bitcast.refs_0_, f32[128,512]{1,0:T(8,128)S(1)} %add.22.refs_1_, f32[32,512]{1,0:T(8,128)S(1)} %get-tuple-element.67.refs_2_.refs_1_, bf16[2048,1536]{1,0:T(8,128)(2,1)S(1)} %bitcast.18, f32[512,1536]{1,0:T(8,128)S(1)} %get-tuple-element.68.refs_4_, ...), custom_call_target="tpu_custom_call" | custom-call | flops 64424508 | bytes 157286 | tf_op jit(solution)/shard_map/pallas_call | solution.py:53
  124.3 5.7 %collective-permute-done.18.refs_2_ = bf16[256,1536]{1,0:T(8,128)(2,1)S(1)} collective-permute-done((bf16[256,1536]{1,0:T(8,128)(2,1)S(1)}, bf16[256,1536]{1,0:T(8,128)(2,1)S(1)}, u32[]{:S(2)}, u32[]{:S(2)}) %collective-permute-start.18) | collective-permute-done | bytes 786464 | tf_op jit(solution)/shard_map/ppermute | solution.py:672
  130.0 0.4 shard_map.119
  130.4 4.4 %collective-permute-start.19 = (bf16[256,1536]{1,0:T(8,128)(2,1)S(1)}, bf16[256,1536]{1,0:T(8,128)(2,1)S(1)}, u32[]{:S(2)}, u32[]{:S(2)}) collective-permute-start(bf16[256,1536]{1,0:T(8,128)(2,1)S(1)} %get-tuple-element.96.refs_15_), channel_id=1, source_target_pairs={{0,4},{4,0},{8,12},{12,8},{1,5},{5,1},{9,13},{13,9},{2,6},{6,2},{1... | collective-permute-start | bytes 2359304 | tf_op jit(solution)/shard_map/ppermute | solution.py:672
  134.8 0.9 collective-permute-start.20
  135.8 4.1 %shard_map.120 = (f32[128,512]{1,0:T(8,128)S(1)}, f32[8,128]{1,0:T(8,128)S(1)}) custom-call(s32[1]{0:T(128)} %bitcast.refs_0_, bf16[2048,1536]{1,0:T(8,128)(2,1)S(1)} %bitcast.19, f32[32,512]{1,0:T(8,128)S(1)} %get-tuple-element.67.refs_2_.refs_1_, f32[128,512]{1,0:T(8,128)S(1)} %get-tuple-element.100.refs_3_, ...), custom_call_target="tpu_custom_call", output_to_operand_aliasing={{0}: (3, {})} | custom-call | flops 64424508 | bytes 157286 | tf_op jit(solution)/shard_map/pallas_call | solution.py:53
  140.0 1.5 collective-permute-done.23
  141.6 1.6 collective-permute-start.24
  143.1 15.9 %shard_map.121 = (bf16[2048,1536]{1,0:T(8,128)(2,1)}, f32[8,128]{1,0:T(8,128)S(1)}) custom-call(s32[1]{0:T(128)} %bitcast.refs_0_, f32[128,512]{1,0:T(8,128)S(1)} %add.22.refs_1_, f32[32,512]{1,0:T(8,128)S(1)} %get-tuple-element.67.refs_2_.refs_1_, bf16[512,1536]{1,0:T(8,128)(2,1)S(1)} %copy-done.1, bf16[256,1536]{1,0:T(8,128)(2,1)S(1)} %get-tuple-element.72.refs_4_, ...), custom_call_target="tpu_custom_call" | custom-call | flops 257698032 | bytes 251658 | tf_op jit(solution)/shard_map/pallas_call | solution.py:53
  159.1 1.0 shard_map.122
  160.2 2.9 %collective-permute-start.25 = (bf16[2,512]{1,0:T(2,128)(2,1)S(1)}, bf16[2,512]{1,0:T(2,128)(2,1)S(1)}, u32[]{:S(2)}, u32[]{:S(2)}) collective-permute-start(bf16[2,512]{1,0:T(2,128)(2,1)S(1)} %get-tuple-element.111), channel_id=1, source_target_pairs={{0,12},{4,0},{8,4},{12,8},{1,13},{5,1},{9,5},{13,9},{2,14},{6,2},{... | collective-permute-start | bytes 6152 | tf_op jit(solution)/shard_map/ppermute | solution.py:692
  163.0 1.8 %collective-permute-start.26 = (bf16[2,512]{1,0:T(2,128)(2,1)S(1)}, bf16[2,512]{1,0:T(2,128)(2,1)S(1)}, u32[]{:S(2)}, u32[]{:S(2)}) collective-permute-start(bf16[2,512]{1,0:T(2,128)(2,1)S(1)} %get-tuple-element.112), channel_id=1, source_target_pairs={{0,8},{4,12},{8,0},{12,4},{1,9},{5,13},{9,1},{13,5},{2,10},{6,14},... | collective-permute-start | bytes 6152 | tf_op jit(solution)/shard_map/ppermute | solution.py:692
  164.8 0.1 collective-permute-start.27
  164.9 5.7 %shard_map.124 = (bf16[2048,256]{1,0:T(8,128)(2,1)}, f32[8,128]{1,0:T(8,128)S(1)}) custom-call(f32[128,512]{1,0:T(8,128)S(1)} %add.24.refs_0_, f32[32,512]{1,0:T(8,128)S(1)} %get-tuple-element.67.refs_2_.refs_1_, bf16[528,256]{1,0:T(8,128)(2,1)S(1)} %copy-done.6, bf16[528,256]{1,0:T(8,128)(2,1)} %collective-permute-done.refs_3_, ...), custom_call_target="tpu_custom_call" | custom-call | flops 42949672 | bytes 41943 | tf_op jit(solution)/shard_map/pallas_call | solution.py:53
  170.6 1.1 shard_map.125
  171.7 0.6 fusion
  (47 shorter events, 0.4 us)
Async XLA Ops:
  0.6 8.8 %collective-permute-start.3 = (bf16[512,256]{1,0:T(8,128)(2,1)}, bf16[512,256]{1,0:T(8,128)(2,1)S(1)}, u32[]{:S(2)}, u32[]{:S(2)}) collective-permute-start(bf16[512,256]{1,0:T(8,128)(2,1)} %refs_1_.1), channel_id=1, source_target_pairs={{0,1},{1,0},{2,3},{3,2},{4,5},{5,4},{6,7},{7,6},{8,9},{9,8},{10,11... | collective-permute-start | bytes 786440 | tf_op jit(solution)/shard_map/ppermute | solution.py:631
  2.9 30.9 %collective-permute-start = (bf16[528,256]{1,0:T(8,128)(2,1)}, bf16[528,256]{1,0:T(8,128)(2,1)}, u32[]{:S(2)}, u32[]{:S(2)}) collective-permute-start(bf16[528,256]{1,0:T(8,128)(2,1)} %get-tuple-element.60.refs_2_), channel_id=1, source_target_pairs={{0,4},{4,8},{8,12},{12,0},{1,5},{5,9},{9,13},{13,1},{2,6},{6,10},{... | collective-permute-start | bytes 811016 | tf_op jit(solution)/shard_map/ppermute | solution.py:628
  5.5 29.0 %collective-permute-start.1 = (bf16[528,256]{1,0:T(8,128)(2,1)}, bf16[528,256]{1,0:T(8,128)(2,1)}, u32[]{:S(2)}, u32[]{:S(2)}) collective-permute-start(bf16[528,256]{1,0:T(8,128)(2,1)} %get-tuple-element.60.refs_2_), channel_id=1, source_target_pairs={{0,8},{4,12},{8,0},{12,4},{1,9},{5,13},{9,1},{13,5},{2,10},{6,14},... | collective-permute-start | bytes 811016 | tf_op jit(solution)/shard_map/ppermute | solution.py:628
  8.0 29.0 %collective-permute-start.2 = (bf16[528,256]{1,0:T(8,128)(2,1)}, bf16[528,256]{1,0:T(8,128)(2,1)}, u32[]{:S(2)}, u32[]{:S(2)}) collective-permute-start(bf16[528,256]{1,0:T(8,128)(2,1)} %get-tuple-element.60.refs_2_), channel_id=1, source_target_pairs={{0,12},{4,0},{8,4},{12,8},{1,13},{5,1},{9,5},{13,9},{2,14},{6,2},{... | collective-permute-start | bytes 811016 | tf_op jit(solution)/shard_map/ppermute | solution.py:628
  11.2 0.7 copy-start.4
  11.9 3.9 %copy-start.1 = (bf16[512,1536]{1,0:T(8,128)(2,1)S(1)}, bf16[512,1536]{1,0:T(8,128)(2,1)}, u32[]{:S(2)}) copy-start(bf16[512,1536]{1,0:T(8,128)(2,1)} %refs_3_.3) | copy-start | bytes 4718596
  11.9 3.9 %copy-start.7 = (f32[8,512]{1,0:T(8,128)S(1)}, f32[8,512]{1,0:T(8,128)}, u32[]{:S(2)}) copy-start(f32[8,512]{1,0:T(8,128)} %get-tuple-element.61.refs_2_) | copy-start | bytes 49156
  11.9 13.8 %collective-permute-start.4 = (bf16[1024,256]{1,0:T(8,128)(2,1)}, bf16[1024,256]{1,0:T(8,128)(2,1)}, u32[]{:S(2)}, u32[]{:S(2)}) collective-permute-start(bf16[1024,256]{1,0:T(8,128)(2,1)} %pad_maximum_fusion), channel_id=1, source_target_pairs={{0,2},{1,3},{2,0},{3,1},{4,6},{5,7},{6,4},{7,5},{8,10},{9,11},{10,... | collective-permute-start | bytes 1572872 | tf_op jit(solution)/shard_map/ppermute | solution.py:631
  15.8 2.8 %copy-start = (bf16[128,16,1536]{2,1,0:T(8,128)(2,1)S(1)}, bf16[128,16,1536]{2,1,0:T(8,128)(2,1)}, u32[]{:S(2)}) copy-start(bf16[128,16,1536]{2,1,0:T(8,128)(2,1)} %param.10) | copy-start | bytes 18874372
  22.5 35.9 %collective-permute-start.7 = (bf16[256,1536]{1,0:T(8,128)(2,1)}, bf16[256,1536]{1,0:T(8,128)(2,1)S(1)}, u32[]{:S(2)}, u32[]{:S(2)}) collective-permute-start(bf16[256,1536]{1,0:T(8,128)(2,1)} %get-tuple-element.69), channel_id=1, source_target_pairs={{4,8},{8,4},{5,9},{9,5},{6,10},{10,6},{7,11},{11,7},{20,24},{24,20... | collective-permute-start | bytes 2359304 | tf_op jit(solution)/shard_map/ppermute | solution.py:645
  25.7 32.8 %collective-permute-start.8 = (bf16[256,1536]{1,0:T(8,128)(2,1)}, bf16[256,1536]{1,0:T(8,128)(2,1)S(1)}, u32[]{:S(2)}, u32[]{:S(2)}) collective-permute-start(bf16[256,1536]{1,0:T(8,128)(2,1)} %get-tuple-element.69), channel_id=1, source_target_pairs={{0,4},{4,0},{8,12},{12,8},{1,5},{5,1},{9,13},{13,9},{2,6},{6,2},{1... | collective-permute-start | bytes 2359304 | tf_op jit(solution)/shard_map/ppermute | solution.py:645
  26.3 1.9 %copy-start.2 = (bf16[1536,1024]{1,0:T(8,128)(2,1)S(1)}, bf16[1536,1024]{1,0:T(8,128)(2,1)}, u32[]{:S(2)}) copy-start(bf16[1536,1024]{1,0:T(8,128)(2,1)} %refs_4_.3) | copy-start | bytes 9437188
  28.2 0.9 copy-start.3
  29.2 0.9 copy-start.5
  30.1 7.0 %copy-start.6 = (bf16[528,256]{1,0:T(8,128)(2,1)S(1)}, bf16[528,256]{1,0:T(8,128)(2,1)}, u32[]{:S(2)}) copy-start(bf16[528,256]{1,0:T(8,128)(2,1)} %get-tuple-element.60.refs_2_) | copy-start | bytes 811012
  30.1 7.0 %copy-start.8 = (bf16[128,16,256]{2,1,0:T(8,128)(2,1)S(1)}, bf16[128,16,256]{2,1,0:T(8,128)(2,1)}, u32[]{:S(2)}) copy-start(bf16[128,16,256]{2,1,0:T(8,128)(2,1)} %param.11) | copy-start | bytes 3145732
  33.7 31.2 %collective-permute-start.11 = (bf16[256,1536]{1,0:T(8,128)(2,1)S(1)}, bf16[256,1536]{1,0:T(8,128)(2,1)S(1)}, u32[]{:S(2)}, u32[]{:S(2)}) collective-permute-start(bf16[256,1536]{1,0:T(8,128)(2,1)S(1)} %get-tuple-element.77), channel_id=1, source_target_pairs={{4,8},{8,4},{5,9},{9,5},{6,10},{10,6},{7,11},{11,7},{20,24},{24,20... | collective-permute-start | bytes 2359304 | tf_op jit(solution)/shard_map/ppermute | solution.py:645
  34.5 30.5 %collective-permute-start.12 = (bf16[256,1536]{1,0:T(8,128)(2,1)S(1)}, bf16[256,1536]{1,0:T(8,128)(2,1)S(1)}, u32[]{:S(2)}, u32[]{:S(2)}) collective-permute-start(bf16[256,1536]{1,0:T(8,128)(2,1)S(1)} %get-tuple-element.77), channel_id=1, source_target_pairs={{0,4},{4,0},{8,12},{12,8},{1,5},{5,1},{9,13},{13,9},{2,6},{6,2},{1... | collective-permute-start | bytes 2359304 | tf_op jit(solution)/shard_map/ppermute | solution.py:645
  37.1 16.0 %slice-start = ((s8[6291456]{0:T(1024)(128)(4,1)}), s8[4194304]{0:T(1024)(128)(4,1)S(1)}, s32[]{:S(2)}) async-start(s8[6291456]{0:T(1024)(128)(4,1)} %bitcast.11), calls=%async_computation | async-start | bytes 8388608
  37.1 16.0 %slice-start.1 = ((s8[6291456]{0:T(1024)(128)(4,1)}), s8[2097152]{0:T(1024)(128)(4,1)S(1)}, s32[]{:S(2)}) async-start(s8[6291456]{0:T(1024)(128)(4,1)} %bitcast.11), calls=%async_computation.1 | async-start | bytes 4194304
  43.0 1.6 collective-permute-start.5
  44.7 8.4 %collective-permute-start.6 = (f32[128,512]{1,0:T(8,128)S(1)}, f32[128,512]{1,0:T(8,128)S(1)}, u32[]{:S(2)}, u32[]{:S(2)}) collective-permute-start(f32[128,512]{1,0:T(8,128)S(1)} %add.21), channel_id=1, source_target_pairs={{0,2},{1,3},{2,0},{3,1},{4,6},{5,7},{6,4},{7,5},{8,10},{9,11},{10,... | collective-permute-start | bytes 786440 | tf_op jit(solution)/shard_map/ppermute | solution.py:620
  58.9 20.5 %collective-permute-start.10 = (bf16[256,1536]{1,0:T(8,128)(2,1)S(1)}, bf16[256,1536]{1,0:T(8,128)(2,1)S(1)}, u32[]{:S(2)}, u32[]{:S(2)}) collective-permute-start(bf16[256,1536]{1,0:T(8,128)(2,1)S(1)} %get-tuple-element.73.refs_6_.refs_5_), channel_id=1, source_target_pairs={{0,4},{4,0},{8,12},{12,8},{1,5},{5,1},{9,13},{13,9},{2,6},{6,2},{1... | collective-permute-start | bytes 2359304 | tf_op jit(solution)/shard_map/ppermute | solution.py:672
  59.0 20.5 %collective-permute-start.9 = (bf16[256,1536]{1,0:T(8,128)(2,1)S(1)}, bf16[256,1536]{1,0:T(8,128)(2,1)S(1)}, u32[]{:S(2)}, u32[]{:S(2)}) collective-permute-start(bf16[256,1536]{1,0:T(8,128)(2,1)S(1)} %get-tuple-element.72.refs_4_), channel_id=1, source_target_pairs={{4,8},{8,4},{5,9},{9,5},{6,10},{10,6},{7,11},{11,7},{20,24},{24,20... | collective-permute-start | bytes 2359304 | tf_op jit(solution)/shard_map/ppermute | solution.py:672
  65.4 27.8 %collective-permute-start.15 = (bf16[256,1536]{1,0:T(8,128)(2,1)S(1)}, bf16[256,1536]{1,0:T(8,128)(2,1)S(1)}, u32[]{:S(2)}, u32[]{:S(2)}) collective-permute-start(bf16[256,1536]{1,0:T(8,128)(2,1)S(1)} %get-tuple-element.79.refs_5_.refs_6_), channel_id=1, source_target_pairs={{4,8},{8,4},{5,9},{9,5},{6,10},{10,6},{7,11},{11,7},{20,24},{24,20... | collective-permute-start | bytes 2359304 | tf_op jit(solution)/shard_map/ppermute | solution.py:672
  66.1 30.1 %collective-permute-start.16 = (bf16[256,1536]{1,0:T(8,128)(2,1)S(1)}, bf16[256,1536]{1,0:T(8,128)(2,1)S(1)}, u32[]{:S(2)}, u32[]{:S(2)}) collective-permute-start(bf16[256,1536]{1,0:T(8,128)(2,1)S(1)} %get-tuple-element.87.refs_7_), channel_id=1, source_target_pairs={{0,4},{4,0},{8,12},{12,8},{1,5},{5,1},{9,13},{13,9},{2,6},{6,2},{1... | collective-permute-start | bytes 2359304 | tf_op jit(solution)/shard_map/ppermute | solution.py:672
  80.0 28.7 %collective-permute-start.13 = (bf16[256,1536]{1,0:T(8,128)(2,1)S(1)}, bf16[256,1536]{1,0:T(8,128)(2,1)S(1)}, u32[]{:S(2)}, u32[]{:S(2)}) collective-permute-start(bf16[256,1536]{1,0:T(8,128)(2,1)S(1)} %get-tuple-element.82.refs_4_.refs_8_), channel_id=1, source_target_pairs={{4,8},{8,4},{5,9},{9,5},{6,10},{10,6},{7,11},{11,7},{20,24},{24,20... | collective-permute-start | bytes 2359304 | tf_op jit(solution)/shard_map/ppermute | solution.py:672
  80.8 32.4 %collective-permute-start.14 = (bf16[256,1536]{1,0:T(8,128)(2,1)S(1)}, bf16[256,1536]{1,0:T(8,128)(2,1)S(1)}, u32[]{:S(2)}, u32[]{:S(2)}) collective-permute-start(bf16[256,1536]{1,0:T(8,128)(2,1)S(1)} %get-tuple-element.83.refs_6_.refs_9_), channel_id=1, source_target_pairs={{0,4},{4,0},{8,12},{12,8},{1,5},{5,1},{9,13},{13,9},{2,6},{6,2},{1... | collective-permute-start | bytes 2359304 | tf_op jit(solution)/shard_map/ppermute | solution.py:672
  96.7 27.6 %collective-permute-start.17 = (bf16[256,1536]{1,0:T(8,128)(2,1)S(1)}, bf16[256,1536]{1,0:T(8,128)(2,1)S(1)}, u32[]{:S(2)}, u32[]{:S(2)}) collective-permute-start(bf16[256,1536]{1,0:T(8,128)(2,1)S(1)} %get-tuple-element.89.refs_5_.refs_10_), channel_id=1, source_target_pairs={{4,8},{8,4},{5,9},{9,5},{6,10},{10,6},{7,11},{11,7},{20,24},{24,20... | collective-permute-start | bytes 2359304 | tf_op jit(solution)/shard_map/ppermute | solution.py:672
  97.4 32.6 %collective-permute-start.18 = (bf16[256,1536]{1,0:T(8,128)(2,1)S(1)}, bf16[256,1536]{1,0:T(8,128)(2,1)S(1)}, u32[]{:S(2)}, u32[]{:S(2)}) collective-permute-start(bf16[256,1536]{1,0:T(8,128)(2,1)S(1)} %get-tuple-element.94.refs_7_.refs_11_), channel_id=1, source_target_pairs={{0,4},{4,0},{8,12},{12,8},{1,5},{5,1},{9,13},{13,9},{2,6},{6,2},{1... | collective-permute-start | bytes 2359304 | tf_op jit(solution)/shard_map/ppermute | solution.py:672
  113.6 45.5 %collective-permute-start.21 = (bf16[256,1536]{1,0:T(8,128)(2,1)S(1)}, bf16[256,1536]{1,0:T(8,128)(2,1)S(1)}, u32[]{:S(2)}, u32[]{:S(2)}) collective-permute-start(bf16[256,1536]{1,0:T(8,128)(2,1)S(1)} %get-tuple-element.98.refs_13_), channel_id=1, source_target_pairs={{0,4},{4,0},{8,12},{12,8},{1,5},{5,1},{9,13},{13,9},{2,6},{6,2},{1... | collective-permute-start | bytes 2359304 | tf_op jit(solution)/shard_map/ppermute | solution.py:672
  118.0 41.1 %collective-permute-start.22 = (bf16[256,1536]{1,0:T(8,128)(2,1)S(1)}, bf16[256,1536]{1,0:T(8,128)(2,1)S(1)}, u32[]{:S(2)}, u32[]{:S(2)}) collective-permute-start(bf16[256,1536]{1,0:T(8,128)(2,1)S(1)} %get-tuple-element.99.refs_4_.refs_12_), channel_id=1, source_target_pairs={{4,8},{8,4},{5,9},{9,5},{6,10},{10,6},{7,11},{11,7},{20,24},{24,20... | collective-permute-start | bytes 2359304 | tf_op jit(solution)/shard_map/ppermute | solution.py:672
  130.4 40.2 %collective-permute-start.19 = (bf16[256,1536]{1,0:T(8,128)(2,1)S(1)}, bf16[256,1536]{1,0:T(8,128)(2,1)S(1)}, u32[]{:S(2)}, u32[]{:S(2)}) collective-permute-start(bf16[256,1536]{1,0:T(8,128)(2,1)S(1)} %get-tuple-element.96.refs_15_), channel_id=1, source_target_pairs={{0,4},{4,0},{8,12},{12,8},{1,5},{5,1},{9,13},{13,9},{2,6},{6,2},{1... | collective-permute-start | bytes 2359304 | tf_op jit(solution)/shard_map/ppermute | solution.py:672
  134.8 35.7 %collective-permute-start.20 = (bf16[256,1536]{1,0:T(8,128)(2,1)S(1)}, bf16[256,1536]{1,0:T(8,128)(2,1)S(1)}, u32[]{:S(2)}, u32[]{:S(2)}) collective-permute-start(bf16[256,1536]{1,0:T(8,128)(2,1)S(1)} %get-tuple-element.97.refs_5_.refs_14_), channel_id=1, source_target_pairs={{4,8},{8,4},{5,9},{9,5},{6,10},{10,6},{7,11},{11,7},{20,24},{24,20... | collective-permute-start | bytes 2359304 | tf_op jit(solution)/shard_map/ppermute | solution.py:672
  139.9 1.6 collective-permute-start.23
  141.6 17.5 %collective-permute-start.24 = (f32[128,512]{1,0:T(8,128)S(1)}, f32[128,512]{1,0:T(8,128)S(1)}, u32[]{:S(2)}, u32[]{:S(2)}) collective-permute-start(f32[128,512]{1,0:T(8,128)S(1)} %add.23), channel_id=1, source_target_pairs={{0,2},{1,3},{2,0},{3,1},{4,6},{5,7},{6,4},{7,5},{8,10},{9,11},{10,... | collective-permute-start | bytes 786440 | tf_op jit(solution)/shard_map/ppermute | solution.py:620
  160.2 11.5 %collective-permute-start.25 = (bf16[2,512]{1,0:T(2,128)(2,1)S(1)}, bf16[2,512]{1,0:T(2,128)(2,1)S(1)}, u32[]{:S(2)}, u32[]{:S(2)}) collective-permute-start(bf16[2,512]{1,0:T(2,128)(2,1)S(1)} %get-tuple-element.111), channel_id=1, source_target_pairs={{0,12},{4,0},{8,4},{12,8},{1,13},{5,1},{9,5},{13,9},{2,14},{6,2},{... | collective-permute-start | bytes 6152 | tf_op jit(solution)/shard_map/ppermute | solution.py:692
  163.0 8.6 %collective-permute-start.26 = (bf16[2,512]{1,0:T(2,128)(2,1)S(1)}, bf16[2,512]{1,0:T(2,128)(2,1)S(1)}, u32[]{:S(2)}, u32[]{:S(2)}) collective-permute-start(bf16[2,512]{1,0:T(2,128)(2,1)S(1)} %get-tuple-element.112), channel_id=1, source_target_pairs={{0,8},{4,12},{8,0},{12,4},{1,9},{5,13},{9,1},{13,5},{2,10},{6,14},... | collective-permute-start | bytes 6152 | tf_op jit(solution)/shard_map/ppermute | solution.py:692
  164.8 6.8 %collective-permute-start.27 = (bf16[2,512]{1,0:T(2,128)(2,1)S(1)}, bf16[2,512]{1,0:T(2,128)(2,1)S(1)}, u32[]{:S(2)}, u32[]{:S(2)}) collective-permute-start(bf16[2,512]{1,0:T(2,128)(2,1)S(1)} %get-tuple-element.113), channel_id=1, source_target_pairs={{0,4},{4,8},{8,12},{12,0},{1,5},{5,9},{9,13},{13,1},{2,6},{6,10},{... | collective-permute-start | bytes 6152 | tf_op jit(solution)/shard_map/ppermute | solution.py:692

commit v8 on v7

--- a/solution.py
+++ b/solution.py
@@ -16,7 +16,7 @@
 STEP_IN = 1024
 STEP_ROWS = 512
 STEP_DOWN = 1024
-STEP_UP = 512
+STEP_UP = 1024
 
 
 def call(body, out_shape, *, grid=None, in_specs=None, out_specs=None, scratch=(), prefetch=0,
@@ -566,6 +566,7 @@
         scratch=[pltpu.VMEM((slots * count, width), BF), pltpu.VMEM((2, rank, slots * count), F32)],
         flops=2 * slots * count * total * width,
         moved=2 * (total * width + slots * count * width),
+        vmem=24,
         after=after,
     )(*arrays)
 

time: 173 us -> 173 us (level)
  transfers between devices with their start and end apart: 28 -> 28, of which waited for: 8 -> 8; matrix products, arithmetic and copies ran while one was open for 2% -> 3% of each run, Pallas kernels for 44% -> 43%
where the time goes in v8:
time: 173 us; the launch traced here: 172 us
  Pallas kernels  74.9 us (43%)
  starting transfers between devices  55.2 us (32%)
  waiting for transfers between devices  28.8 us (17%)
  local copies, waits for them, and re-layouts  9.65 us (6%)
  other arithmetic  2.53 us (1%)
    pallas_call x24, Pallas kernels, call(): return lambda *arrays: call_it(*arrays, *after)  74.9 us
    ppermute x6, starting transfers between devices, per_device(): lax.ppermute(to_a, 'dp', pairs_a)  29.4 us
    ppermute x6, waiting for transfers between devices, per_device(): lax.ppermute(to_a, 'dp', pairs_a)  16.4 us
    ppermute x4, waiting for transfers between devices, exchange(): lax.ppermute(part, 'mp', [(i, i ^ bit) for i in range(shares)])  9.88 us
    unnamed x22, local copies, waits for them, and re-layouts  7.28 us
    ppermute x3, starting transfers between devices, per_device(): lax.ppermute(block, 'dp', [(i, (i + s) % size) for i in range(size)])  6.53 us
    ppermute x3, starting transfers between devices, per_device(): lax.ppermute(gate_rows[s], 'dp', [(i, (i - s) % size) for i in range(size)])  4.76 us
    ppermute x4, starting transfers between devices, per_device(): lax.ppermute(sent[c], 'dp', p)  4.72 us
  transfers between devices with their start and end apart: 28, of which 8 were waited for; matrix products, arithmetic and copies ran while one was open for 3% of the time, Pallas kernels for 43%

profile of v8, /device:TPU:0, one launch (start us, length us, event | category | flops | bytes accessed | tf_op | source)
XLA Modules:
  0.0 172.1 jit_solution(10590206809481727893)
XLA Ops:
  0.6 0.5 collective-permute-start.3
  1.1 1.7 shard_map.102
  2.9 2.6 %collective-permute-start = (bf16[528,256]{1,0:T(8,128)(2,1)}, bf16[528,256]{1,0:T(8,128)(2,1)}, u32[]{:S(2)}, u32[]{:S(2)}) collective-permute-start(bf16[528,256]{1,0:T(8,128)(2,1)} %get-tuple-element.60.refs_2_), channel_id=1, source_target_pairs={{0,4},{4,8},{8,12},{12,0},{1,5},{5,9},{9,13},{13,1},{2,6},{6,10},{... | collective-permute-start | bytes 811016 | tf_op jit(solution)/shard_map/ppermute | solution.py:629
  5.5 2.6 %collective-permute-start.1 = (bf16[528,256]{1,0:T(8,128)(2,1)}, bf16[528,256]{1,0:T(8,128)(2,1)}, u32[]{:S(2)}, u32[]{:S(2)}) collective-permute-start(bf16[528,256]{1,0:T(8,128)(2,1)} %get-tuple-element.60.refs_2_), channel_id=1, source_target_pairs={{0,8},{4,12},{8,0},{12,4},{1,9},{5,13},{9,1},{13,5},{2,10},{6,14},... | collective-permute-start | bytes 811016 | tf_op jit(solution)/shard_map/ppermute | solution.py:629
  8.0 1.3 collective-permute-start.2
  9.4 1.8 %pad_maximum_fusion = bf16[1024,256]{1,0:T(8,128)(2,1)} fusion(bf16[512,256]{1,0:T(8,128)(2,1)S(1)} %collective-permute-done.3.refs_2_, bf16[512,256]{1,0:T(8,128)(2,1)} %refs_1_.1), kind=kLoop, calls=%fused_computation | loop fusion | flops 1048576 | bytes 1048576 | tf_op jit(solution)/shard_map/concatenate | solution.py:634
  11.2 0.7 copy-done.4
  11.9 1.5 collective-permute-start.4
  13.4 2.4 %fusion.1 = (bf16[256,1536]{1,0:T(8,128)(2,1)S(1)}, bf16[256,1536]{1,0:T(8,128)(2,1)}) fusion(bf16[512,1536]{1,0:T(8,128)(2,1)} %refs_3_.3), kind=kLoop, calls=%fused_computation.3 | loop fusion | bytes 3145728 | tf_op jit(solution)/shard_map/slice | solution.py:644
  15.8 2.8 %copy-done = bf16[128,16,1536]{2,1,0:T(8,128)(2,1)S(1)} copy-done((bf16[128,16,1536]{2,1,0:T(8,128)(2,1)S(1)}, bf16[128,16,1536]{2,1,0:T(8,128)(2,1)}, u32[]{:S(2)}) %copy-start) | copy-done | bytes 6291480
  18.6 3.9 %shard_map.103 = (f32[128,512]{1,0:T(8,128)S(1)}, f32[8,128]{1,0:T(8,128)S(1)}) custom-call(s32[1]{0:T(128)} %bitcast.refs_0_, bf16[2048,1536]{1,0:T(8,128)(2,1)S(1)} %bitcast.10, f32[8,512]{1,0:T(8,128)S(1)} %copy-done.7, f32[128,512]{1,0:T(8,128)S(1)} %broadcast_in_dim.3.refs_3_, bf16[512,1536]{1,0:T(8,128)(2,1)S(1)} %copy-done.1), custom_call_target="tpu_custom_call", output_to_operand_aliasing={{0}: (3, {})} | custom-call | flops 64424508 | bytes 157286 | tf_op jit(solution)/shard_map/pallas_call | solution.py:53
  22.5 0.7 collective-permute-start.7
  23.2 2.5 %collective-permute-done.4.refs_3_ = bf16[1024,256]{1,0:T(8,128)(2,1)} collective-permute-done((bf16[1024,256]{1,0:T(8,128)(2,1)}, bf16[1024,256]{1,0:T(8,128)(2,1)}, u32[]{:S(2)}, u32[]{:S(2)}) %collective-permute-start.4) | collective-permute-done | bytes 524320 | tf_op jit(solution)/shard_map/ppermute | solution.py:632
  25.7 0.7 collective-permute-start.8
  26.3 1.9 %copy-done.2 = bf16[1536,1024]{1,0:T(8,128)(2,1)S(1)} copy-done((bf16[1536,1024]{1,0:T(8,128)(2,1)S(1)}, bf16[1536,1024]{1,0:T(8,128)(2,1)}, u32[]{:S(2)}) %copy-start.2) | copy-done | bytes 3145752
  28.2 0.9 copy-done.3
  29.2 0.9 copy-done.5
  30.1 3.6 %shard_map.104 = (f32[512,1536]{1,0:T(8,128)S(1)}, f32[8,128]{1,0:T(8,128)S(1)}) custom-call(s32[1]{0:T(128)} %bitcast.4.refs_0_, bf16[512,256]{1,0:T(8,128)(2,1)S(1)} %copy-done.3, bf16[512,256]{1,0:T(8,128)(2,1)S(1)} %copy-done.5, bf16[1024,256]{1,0:T(8,128)(2,1)} %collective-permute-done.4.refs_3_, bf16[1536,1024]{1,0:T(8,128)(2,1)S(1)} %copy-done.2, ...), custom_call_target="tpu_custom_call" | custom-call | flops 32212254 | bytes 62914 | tf_op jit(solution)/shard_map/pallas_call | solution.py:53
  33.7 0.7 collective-permute-start.11
  34.5 2.6 %collective-permute-start.12 = (bf16[256,1536]{1,0:T(8,128)(2,1)S(1)}, bf16[256,1536]{1,0:T(8,128)(2,1)S(1)}, u32[]{:S(2)}, u32[]{:S(2)}) collective-permute-start(bf16[256,1536]{1,0:T(8,128)(2,1)S(1)} %get-tuple-element.77), channel_id=1, source_target_pairs={{0,4},{4,0},{8,12},{12,8},{1,5},{5,1},{9,13},{13,9},{2,6},{6,2},{1... | collective-permute-start | bytes 2359304 | tf_op jit(solution)/shard_map/ppermute | solution.py:646
  37.1 5.9 %shard_map.107 = (f32[128,512]{1,0:T(8,128)S(1)}, f32[32,512]{1,0:T(8,128)S(1)}, f32[8,128]{1,0:T(8,128)}) custom-call(s32[1]{0:T(128)} %bitcast.refs_0_, bf16[2048,256]{1,0:T(8,128)(2,1)S(1)} %bitcast.20, bf16[528,256]{1,0:T(8,128)(2,1)S(1)} %copy-done.6, bf16[528,256]{1,0:T(8,128)(2,1)} %collective-permute-done.refs_3_, ...), custom_call_target="tpu_custom_call" | custom-call | flops 10737418240 | bytes 10485760 | tf_op jit(solution)/shard_map/pallas_call | solution.py:53
  43.0 0.1 collective-permute-start.5
  43.1 1.5 collective-permute-done.5
  44.7 1.6 collective-permute-start.6
  46.2 6.8 %collective-permute-done.6 = f32[128,512]{1,0:T(8,128)S(1)} collective-permute-done((f32[128,512]{1,0:T(8,128)S(1)}, f32[128,512]{1,0:T(8,128)S(1)}, u32[]{:S(2)}, u32[]{:S(2)}) %collective-permute-start.6) | collective-permute-done | bytes 262176 | tf_op jit(solution)/shard_map/ppermute | solution.py:621
  53.1 5.3 %shard_map.108 = (bf16[512,1536]{1,0:T(8,128)(2,1)S(1)}, f32[8,128]{1,0:T(8,128)S(1)}) custom-call(s32[1]{0:T(128)} %bitcast.refs_0_, f32[128,512]{1,0:T(8,128)S(1)} %add.22.refs_1_, f32[32,512]{1,0:T(8,128)S(1)} %get-tuple-element.67.refs_2_.refs_1_, bf16[2048,1536]{1,0:T(8,128)(2,1)S(1)} %bitcast.13), custom_call_target="tpu_custom_call" | custom-call | flops 64424508 | bytes 157286 | tf_op jit(solution)/shard_map/pallas_call | solution.py:53
  58.4 0.4 shard_map.109
  58.9 0.1 collective-permute-start.10
  59.0 0.7 collective-permute-start.9
  59.7 5.3 %shard_map.110 = (bf16[512,1536]{1,0:T(8,128)(2,1)S(1)}, f32[8,128]{1,0:T(8,128)S(1)}) custom-call(s32[1]{0:T(128)} %bitcast.refs_0_, f32[128,512]{1,0:T(8,128)S(1)} %add.22.refs_1_, f32[32,512]{1,0:T(8,128)S(1)} %get-tuple-element.67.refs_2_.refs_1_, bf16[2048,1536]{1,0:T(8,128)(2,1)S(1)} %bitcast.14, f32[8,128]{1,0:T(8,128)S(1)} %get-tuple-element.74.refs_4_), custom_call_target="tpu_custom_call" | custom-call | flops 64424508 | bytes 157286 | tf_op jit(solution)/shard_map/pallas_call | solution.py:53
  65.0 0.4 shard_map.111
  65.4 0.7 collective-permute-start.15
  66.1 6.1 %collective-permute-start.16 = (bf16[256,1536]{1,0:T(8,128)(2,1)S(1)}, bf16[256,1536]{1,0:T(8,128)(2,1)S(1)}, u32[]{:S(2)}, u32[]{:S(2)}) collective-permute-start(bf16[256,1536]{1,0:T(8,128)(2,1)S(1)} %get-tuple-element.87.refs_7_), channel_id=1, source_target_pairs={{0,4},{4,0},{8,12},{12,8},{1,5},{5,1},{9,13},{13,9},{2,6},{6,2},{1... | collective-permute-start | bytes 2359304 | tf_op jit(solution)/shard_map/ppermute | solution.py:673
  72.3 3.9 %shard_map.112 = (f32[128,512]{1,0:T(8,128)S(1)}, f32[8,128]{1,0:T(8,128)S(1)}) custom-call(s32[1]{0:T(128)} %bitcast.refs_0_, bf16[2048,1536]{1,0:T(8,128)(2,1)S(1)} %bitcast.15, f32[32,512]{1,0:T(8,128)S(1)} %get-tuple-element.67.refs_2_.refs_1_, f32[128,512]{1,0:T(8,128)S(1)} %get-tuple-element.76.refs_3_, ...), custom_call_target="tpu_custom_call", output_to_operand_aliasing={{0}: (3, {})} | custom-call | flops 64424508 | bytes 157286 | tf_op jit(solution)/shard_map/pallas_call | solution.py:53
  76.2 3.2 %collective-permute-done.10.refs_2_ = bf16[256,1536]{1,0:T(8,128)(2,1)S(1)} collective-permute-done((bf16[256,1536]{1,0:T(8,128)(2,1)S(1)}, bf16[256,1536]{1,0:T(8,128)(2,1)S(1)}, u32[]{:S(2)}, u32[]{:S(2)}) %collective-permute-start.10) | collective-permute-done | bytes 786464 | tf_op jit(solution)/shard_map/ppermute | solution.py:673
  79.4 0.6 shard_map.113
  80.0 0.7 collective-permute-start.13
  80.8 7.2 %collective-permute-start.14 = (bf16[256,1536]{1,0:T(8,128)(2,1)S(1)}, bf16[256,1536]{1,0:T(8,128)(2,1)S(1)}, u32[]{:S(2)}, u32[]{:S(2)}) collective-permute-start(bf16[256,1536]{1,0:T(8,128)(2,1)S(1)} %get-tuple-element.83.refs_6_.refs_9_), channel_id=1, source_target_pairs={{0,4},{4,0},{8,12},{12,8},{1,5},{5,1},{9,13},{13,9},{2,6},{6,2},{1... | collective-permute-start | bytes 2359304 | tf_op jit(solution)/shard_map/ppermute | solution.py:673
  87.9 5.2 %shard_map.114 = (bf16[512,1536]{1,0:T(8,128)(2,1)S(1)}, f32[8,128]{1,0:T(8,128)S(1)}) custom-call(s32[1]{0:T(128)} %bitcast.refs_0_, f32[128,512]{1,0:T(8,128)S(1)} %add.22.refs_1_, f32[32,512]{1,0:T(8,128)S(1)} %get-tuple-element.67.refs_2_.refs_1_, bf16[2048,1536]{1,0:T(8,128)(2,1)S(1)} %bitcast.16, f32[8,128]{1,0:T(8,128)S(1)} %get-tuple-element.84.refs_4_), custom_call_target="tpu_custom_call" | custom-call | flops 64424508 | bytes 157286 | tf_op jit(solution)/shard_map/pallas_call | solution.py:53
  93.2 3.1 %collective-permute-done.16.refs_2_ = bf16[256,1536]{1,0:T(8,128)(2,1)S(1)} collective-permute-done((bf16[256,1536]{1,0:T(8,128)(2,1)S(1)}, bf16[256,1536]{1,0:T(8,128)(2,1)S(1)}, u32[]{:S(2)}, u32[]{:S(2)}) %collective-permute-start.16) | collective-permute-done | bytes 786464 | tf_op jit(solution)/shard_map/ppermute | solution.py:673
  96.3 0.4 shard_map.115
  96.7 0.7 collective-permute-start.17
  97.4 7.2 %collective-permute-start.18 = (bf16[256,1536]{1,0:T(8,128)(2,1)S(1)}, bf16[256,1536]{1,0:T(8,128)(2,1)S(1)}, u32[]{:S(2)}, u32[]{:S(2)}) collective-permute-start(bf16[256,1536]{1,0:T(8,128)(2,1)S(1)} %get-tuple-element.94.refs_7_.refs_11_), channel_id=1, source_target_pairs={{0,4},{4,0},{8,12},{12,8},{1,5},{5,1},{9,13},{13,9},{2,6},{6,2},{1... | collective-permute-start | bytes 2359304 | tf_op jit(solution)/shard_map/ppermute | solution.py:673
  104.6 4.1 %shard_map.116 = (f32[128,512]{1,0:T(8,128)S(1)}, f32[8,128]{1,0:T(8,128)S(1)}) custom-call(s32[1]{0:T(128)} %bitcast.refs_0_, bf16[2048,1536]{1,0:T(8,128)(2,1)S(1)} %bitcast.17, f32[32,512]{1,0:T(8,128)S(1)} %get-tuple-element.67.refs_2_.refs_1_, f32[128,512]{1,0:T(8,128)S(1)} %get-tuple-element.86.refs_3_, ...), custom_call_target="tpu_custom_call", output_to_operand_aliasing={{0}: (3, {})} | custom-call | flops 64424508 | bytes 157286 | tf_op jit(solution)/shard_map/pallas_call | solution.py:53
  108.7 4.4 %collective-permute-done.14.refs_2_ = bf16[256,1536]{1,0:T(8,128)(2,1)S(1)} collective-permute-done((bf16[256,1536]{1,0:T(8,128)(2,1)S(1)}, bf16[256,1536]{1,0:T(8,128)(2,1)S(1)}, u32[]{:S(2)}, u32[]{:S(2)}) %collective-permute-start.14) | collective-permute-done | bytes 786464 | tf_op jit(solution)/shard_map/ppermute | solution.py:673
  113.1 0.4 shard_map.117
  113.6 4.4 %collective-permute-start.21 = (bf16[256,1536]{1,0:T(8,128)(2,1)S(1)}, bf16[256,1536]{1,0:T(8,128)(2,1)S(1)}, u32[]{:S(2)}, u32[]{:S(2)}) collective-permute-start(bf16[256,1536]{1,0:T(8,128)(2,1)S(1)} %get-tuple-element.98.refs_13_), channel_id=1, source_target_pairs={{0,4},{4,0},{8,12},{12,8},{1,5},{5,1},{9,13},{13,9},{2,6},{6,2},{1... | collective-permute-start | bytes 2359304 | tf_op jit(solution)/shard_map/ppermute | solution.py:673
  118.0 0.7 collective-permute-start.22
  118.7 5.6 %shard_map.118 = (f32[512,1536]{1,0:T(8,128)S(1)}, f32[8,128]{1,0:T(8,128)S(1)}) custom-call(s32[1]{0:T(128)} %bitcast.refs_0_, f32[128,512]{1,0:T(8,128)S(1)} %add.22.refs_1_, f32[32,512]{1,0:T(8,128)S(1)} %get-tuple-element.67.refs_2_.refs_1_, bf16[2048,1536]{1,0:T(8,128)(2,1)S(1)} %bitcast.18, f32[512,1536]{1,0:T(8,128)S(1)} %get-tuple-element.68.refs_4_, ...), custom_call_target="tpu_custom_call" | custom-call | flops 64424508 | bytes 157286 | tf_op jit(solution)/shard_map/pallas_call | solution.py:53
  124.3 5.7 %collective-permute-done.18.refs_2_ = bf16[256,1536]{1,0:T(8,128)(2,1)S(1)} collective-permute-done((bf16[256,1536]{1,0:T(8,128)(2,1)S(1)}, bf16[256,1536]{1,0:T(8,128)(2,1)S(1)}, u32[]{:S(2)}, u32[]{:S(2)}) %collective-permute-start.18) | collective-permute-done | bytes 786464 | tf_op jit(solution)/shard_map/ppermute | solution.py:673
  130.0 0.4 shard_map.119
  130.4 4.4 %collective-permute-start.19 = (bf16[256,1536]{1,0:T(8,128)(2,1)S(1)}, bf16[256,1536]{1,0:T(8,128)(2,1)S(1)}, u32[]{:S(2)}, u32[]{:S(2)}) collective-permute-start(bf16[256,1536]{1,0:T(8,128)(2,1)S(1)} %get-tuple-element.96.refs_15_), channel_id=1, source_target_pairs={{0,4},{4,0},{8,12},{12,8},{1,5},{5,1},{9,13},{13,9},{2,6},{6,2},{1... | collective-permute-start | bytes 2359304 | tf_op jit(solution)/shard_map/ppermute | solution.py:673
  134.8 0.9 collective-permute-start.20
  135.8 4.1 %shard_map.120 = (f32[128,512]{1,0:T(8,128)S(1)}, f32[8,128]{1,0:T(8,128)S(1)}) custom-call(s32[1]{0:T(128)} %bitcast.refs_0_, bf16[2048,1536]{1,0:T(8,128)(2,1)S(1)} %bitcast.19, f32[32,512]{1,0:T(8,128)S(1)} %get-tuple-element.67.refs_2_.refs_1_, f32[128,512]{1,0:T(8,128)S(1)} %get-tuple-element.100.refs_3_, ...), custom_call_target="tpu_custom_call", output_to_operand_aliasing={{0}: (3, {})} | custom-call | flops 64424508 | bytes 157286 | tf_op jit(solution)/shard_map/pallas_call | solution.py:53
  140.0 1.5 collective-permute-done.23
  141.6 1.6 collective-permute-start.24
  143.1 15.9 %shard_map.121 = (bf16[2048,1536]{1,0:T(8,128)(2,1)}, f32[8,128]{1,0:T(8,128)S(1)}) custom-call(s32[1]{0:T(128)} %bitcast.refs_0_, f32[128,512]{1,0:T(8,128)S(1)} %add.22.refs_1_, f32[32,512]{1,0:T(8,128)S(1)} %get-tuple-element.67.refs_2_.refs_1_, bf16[512,1536]{1,0:T(8,128)(2,1)S(1)} %copy-done.1, bf16[256,1536]{1,0:T(8,128)(2,1)S(1)} %get-tuple-element.72.refs_4_, ...), custom_call_target="tpu_custom_call" | custom-call | flops 257698032 | bytes 251658 | tf_op jit(solution)/shard_map/pallas_call | solution.py:53
  159.1 1.0 shard_map.122
  160.2 2.9 %collective-permute-start.25 = (bf16[2,512]{1,0:T(2,128)(2,1)S(1)}, bf16[2,512]{1,0:T(2,128)(2,1)S(1)}, u32[]{:S(2)}, u32[]{:S(2)}) collective-permute-start(bf16[2,512]{1,0:T(2,128)(2,1)S(1)} %get-tuple-element.111), channel_id=1, source_target_pairs={{0,12},{4,0},{8,4},{12,8},{1,13},{5,1},{9,5},{13,9},{2,14},{6,2},{... | collective-permute-start | bytes 6152 | tf_op jit(solution)/shard_map/ppermute | solution.py:693
  163.0 1.8 %collective-permute-start.26 = (bf16[2,512]{1,0:T(2,128)(2,1)S(1)}, bf16[2,512]{1,0:T(2,128)(2,1)S(1)}, u32[]{:S(2)}, u32[]{:S(2)}) collective-permute-start(bf16[2,512]{1,0:T(2,128)(2,1)S(1)} %get-tuple-element.112), channel_id=1, source_target_pairs={{0,8},{4,12},{8,0},{12,4},{1,9},{5,13},{9,1},{13,5},{2,10},{6,14},... | collective-permute-start | bytes 6152 | tf_op jit(solution)/shard_map/ppermute | solution.py:693
  164.8 0.1 collective-permute-start.27
  164.9 5.5 %shard_map.124 = (bf16[2048,256]{1,0:T(8,128)(2,1)}, f32[8,128]{1,0:T(8,128)S(1)}) custom-call(f32[128,512]{1,0:T(8,128)S(1)} %add.24.refs_0_, f32[32,512]{1,0:T(8,128)S(1)} %get-tuple-element.67.refs_2_.refs_1_, bf16[528,256]{1,0:T(8,128)(2,1)S(1)} %copy-done.6, bf16[528,256]{1,0:T(8,128)(2,1)} %collective-permute-done.refs_3_, ...), custom_call_target="tpu_custom_call" | custom-call | flops 42949672 | bytes 41943 | tf_op jit(solution)/shard_map/pallas_call | solution.py:53
  170.4 1.1 shard_map.125
  171.5 0.6 fusion
  (47 shorter events, 0.4 us)
Async XLA Ops:
  0.6 8.8 %collective-permute-start.3 = (bf16[512,256]{1,0:T(8,128)(2,1)}, bf16[512,256]{1,0:T(8,128)(2,1)S(1)}, u32[]{:S(2)}, u32[]{:S(2)}) collective-permute-start(bf16[512,256]{1,0:T(8,128)(2,1)} %refs_1_.1), channel_id=1, source_target_pairs={{0,1},{1,0},{2,3},{3,2},{4,5},{5,4},{6,7},{7,6},{8,9},{9,8},{10,11... | collective-permute-start | bytes 786440 | tf_op jit(solution)/shard_map/ppermute | solution.py:632
  2.9 30.9 %collective-permute-start = (bf16[528,256]{1,0:T(8,128)(2,1)}, bf16[528,256]{1,0:T(8,128)(2,1)}, u32[]{:S(2)}, u32[]{:S(2)}) collective-permute-start(bf16[528,256]{1,0:T(8,128)(2,1)} %get-tuple-element.60.refs_2_), channel_id=1, source_target_pairs={{0,4},{4,8},{8,12},{12,0},{1,5},{5,9},{9,13},{13,1},{2,6},{6,10},{... | collective-permute-start | bytes 811016 | tf_op jit(solution)/shard_map/ppermute | solution.py:629
  5.5 29.0 %collective-permute-start.1 = (bf16[528,256]{1,0:T(8,128)(2,1)}, bf16[528,256]{1,0:T(8,128)(2,1)}, u32[]{:S(2)}, u32[]{:S(2)}) collective-permute-start(bf16[528,256]{1,0:T(8,128)(2,1)} %get-tuple-element.60.refs_2_), channel_id=1, source_target_pairs={{0,8},{4,12},{8,0},{12,4},{1,9},{5,13},{9,1},{13,5},{2,10},{6,14},... | collective-permute-start | bytes 811016 | tf_op jit(solution)/shard_map/ppermute | solution.py:629
  8.0 29.0 %collective-permute-start.2 = (bf16[528,256]{1,0:T(8,128)(2,1)}, bf16[528,256]{1,0:T(8,128)(2,1)}, u32[]{:S(2)}, u32[]{:S(2)}) collective-permute-start(bf16[528,256]{1,0:T(8,128)(2,1)} %get-tuple-element.60.refs_2_), channel_id=1, source_target_pairs={{0,12},{4,0},{8,4},{12,8},{1,13},{5,1},{9,5},{13,9},{2,14},{6,2},{... | collective-permute-start | bytes 811016 | tf_op jit(solution)/shard_map/ppermute | solution.py:629
  11.2 0.7 copy-start.4
  11.9 3.9 %copy-start.1 = (bf16[512,1536]{1,0:T(8,128)(2,1)S(1)}, bf16[512,1536]{1,0:T(8,128)(2,1)}, u32[]{:S(2)}) copy-start(bf16[512,1536]{1,0:T(8,128)(2,1)} %refs_3_.3) | copy-start | bytes 4718596
  11.9 3.9 %copy-start.7 = (f32[8,512]{1,0:T(8,128)S(1)}, f32[8,512]{1,0:T(8,128)}, u32[]{:S(2)}) copy-start(f32[8,512]{1,0:T(8,128)} %get-tuple-element.61.refs_2_) | copy-start | bytes 49156
  11.9 13.8 %collective-permute-start.4 = (bf16[1024,256]{1,0:T(8,128)(2,1)}, bf16[1024,256]{1,0:T(8,128)(2,1)}, u32[]{:S(2)}, u32[]{:S(2)}) collective-permute-start(bf16[1024,256]{1,0:T(8,128)(2,1)} %pad_maximum_fusion), channel_id=1, source_target_pairs={{0,2},{1,3},{2,0},{3,1},{4,6},{5,7},{6,4},{7,5},{8,10},{9,11},{10,... | collective-permute-start | bytes 1572872 | tf_op jit(solution)/shard_map/ppermute | solution.py:632
  15.8 2.8 %copy-start = (bf16[128,16,1536]{2,1,0:T(8,128)(2,1)S(1)}, bf16[128,16,1536]{2,1,0:T(8,128)(2,1)}, u32[]{:S(2)}) copy-start(bf16[128,16,1536]{2,1,0:T(8,128)(2,1)} %param.10) | copy-start | bytes 18874372
  22.5 35.9 %collective-permute-start.7 = (bf16[256,1536]{1,0:T(8,128)(2,1)}, bf16[256,1536]{1,0:T(8,128)(2,1)S(1)}, u32[]{:S(2)}, u32[]{:S(2)}) collective-permute-start(bf16[256,1536]{1,0:T(8,128)(2,1)} %get-tuple-element.69), channel_id=1, source_target_pairs={{4,8},{8,4},{5,9},{9,5},{6,10},{10,6},{7,11},{11,7},{20,24},{24,20... | collective-permute-start | bytes 2359304 | tf_op jit(solution)/shard_map/ppermute | solution.py:646
  25.7 32.8 %collective-permute-start.8 = (bf16[256,1536]{1,0:T(8,128)(2,1)}, bf16[256,1536]{1,0:T(8,128)(2,1)S(1)}, u32[]{:S(2)}, u32[]{:S(2)}) collective-permute-start(bf16[256,1536]{1,0:T(8,128)(2,1)} %get-tuple-element.69), channel_id=1, source_target_pairs={{0,4},{4,0},{8,12},{12,8},{1,5},{5,1},{9,13},{13,9},{2,6},{6,2},{1... | collective-permute-start | bytes 2359304 | tf_op jit(solution)/shard_map/ppermute | solution.py:646
  26.3 1.9 %copy-start.2 = (bf16[1536,1024]{1,0:T(8,128)(2,1)S(1)}, bf16[1536,1024]{1,0:T(8,128)(2,1)}, u32[]{:S(2)}) copy-start(bf16[1536,1024]{1,0:T(8,128)(2,1)} %refs_4_.3) | copy-start | bytes 9437188
  28.2 0.9 copy-start.3
  29.2 0.9 copy-start.5
  30.1 7.0 %copy-start.6 = (bf16[528,256]{1,0:T(8,128)(2,1)S(1)}, bf16[528,256]{1,0:T(8,128)(2,1)}, u32[]{:S(2)}) copy-start(bf16[528,256]{1,0:T(8,128)(2,1)} %get-tuple-element.60.refs_2_) | copy-start | bytes 811012
  30.1 7.0 %copy-start.8 = (bf16[128,16,256]{2,1,0:T(8,128)(2,1)S(1)}, bf16[128,16,256]{2,1,0:T(8,128)(2,1)}, u32[]{:S(2)}) copy-start(bf16[128,16,256]{2,1,0:T(8,128)(2,1)} %param.11) | copy-start | bytes 3145732
  33.7 31.2 %collective-permute-start.11 = (bf16[256,1536]{1,0:T(8,128)(2,1)S(1)}, bf16[256,1536]{1,0:T(8,128)(2,1)S(1)}, u32[]{:S(2)}, u32[]{:S(2)}) collective-permute-start(bf16[256,1536]{1,0:T(8,128)(2,1)S(1)} %get-tuple-element.77), channel_id=1, source_target_pairs={{4,8},{8,4},{5,9},{9,5},{6,10},{10,6},{7,11},{11,7},{20,24},{24,20... | collective-permute-start | bytes 2359304 | tf_op jit(solution)/shard_map/ppermute | solution.py:646
  34.5 30.5 %collective-permute-start.12 = (bf16[256,1536]{1,0:T(8,128)(2,1)S(1)}, bf16[256,1536]{1,0:T(8,128)(2,1)S(1)}, u32[]{:S(2)}, u32[]{:S(2)}) collective-permute-start(bf16[256,1536]{1,0:T(8,128)(2,1)S(1)} %get-tuple-element.77), channel_id=1, source_target_pairs={{0,4},{4,0},{8,12},{12,8},{1,5},{5,1},{9,13},{13,9},{2,6},{6,2},{1... | collective-permute-start | bytes 2359304 | tf_op jit(solution)/shard_map/ppermute | solution.py:646
  37.1 16.0 %slice-start = ((s8[6291456]{0:T(1024)(128)(4,1)}), s8[4194304]{0:T(1024)(128)(4,1)S(1)}, s32[]{:S(2)}) async-start(s8[6291456]{0:T(1024)(128)(4,1)} %bitcast.11), calls=%async_computation | async-start | bytes 8388608
  37.1 16.0 %slice-start.1 = ((s8[6291456]{0:T(1024)(128)(4,1)}), s8[2097152]{0:T(1024)(128)(4,1)S(1)}, s32[]{:S(2)}) async-start(s8[6291456]{0:T(1024)(128)(4,1)} %bitcast.11), calls=%async_computation.1 | async-start | bytes 4194304
  43.0 1.6 collective-permute-start.5
  44.7 8.4 %collective-permute-start.6 = (f32[128,512]{1,0:T(8,128)S(1)}, f32[128,512]{1,0:T(8,128)S(1)}, u32[]{:S(2)}, u32[]{:S(2)}) collective-permute-start(f32[128,512]{1,0:T(8,128)S(1)} %add.21), channel_id=1, source_target_pairs={{0,2},{1,3},{2,0},{3,1},{4,6},{5,7},{6,4},{7,5},{8,10},{9,11},{10,... | collective-permute-start | bytes 786440 | tf_op jit(solution)/shard_map/ppermute | solution.py:621
  58.9 20.5 %collective-permute-start.10 = (bf16[256,1536]{1,0:T(8,128)(2,1)S(1)}, bf16[256,1536]{1,0:T(8,128)(2,1)S(1)}, u32[]{:S(2)}, u32[]{:S(2)}) collective-permute-start(bf16[256,1536]{1,0:T(8,128)(2,1)S(1)} %get-tuple-element.73.refs_6_.refs_5_), channel_id=1, source_target_pairs={{0,4},{4,0},{8,12},{12,8},{1,5},{5,1},{9,13},{13,9},{2,6},{6,2},{1... | collective-permute-start | bytes 2359304 | tf_op jit(solution)/shard_map/ppermute | solution.py:673
  59.0 20.5 %collective-permute-start.9 = (bf16[256,1536]{1,0:T(8,128)(2,1)S(1)}, bf16[256,1536]{1,0:T(8,128)(2,1)S(1)}, u32[]{:S(2)}, u32[]{:S(2)}) collective-permute-start(bf16[256,1536]{1,0:T(8,128)(2,1)S(1)} %get-tuple-element.72.refs_4_), channel_id=1, source_target_pairs={{4,8},{8,4},{5,9},{9,5},{6,10},{10,6},{7,11},{11,7},{20,24},{24,20... | collective-permute-start | bytes 2359304 | tf_op jit(solution)/shard_map/ppermute | solution.py:673
  65.4 27.8 %collective-permute-start.15 = (bf16[256,1536]{1,0:T(8,128)(2,1)S(1)}, bf16[256,1536]{1,0:T(8,128)(2,1)S(1)}, u32[]{:S(2)}, u32[]{:S(2)}) collective-permute-start(bf16[256,1536]{1,0:T(8,128)(2,1)S(1)} %get-tuple-element.79.refs_5_.refs_6_), channel_id=1, source_target_pairs={{4,8},{8,4},{5,9},{9,5},{6,10},{10,6},{7,11},{11,7},{20,24},{24,20... | collective-permute-start | bytes 2359304 | tf_op jit(solution)/shard_map/ppermute | solution.py:673
  66.1 30.1 %collective-permute-start.16 = (bf16[256,1536]{1,0:T(8,128)(2,1)S(1)}, bf16[256,1536]{1,0:T(8,128)(2,1)S(1)}, u32[]{:S(2)}, u32[]{:S(2)}) collective-permute-start(bf16[256,1536]{1,0:T(8,128)(2,1)S(1)} %get-tuple-element.87.refs_7_), channel_id=1, source_target_pairs={{0,4},{4,0},{8,12},{12,8},{1,5},{5,1},{9,13},{13,9},{2,6},{6,2},{1... | collective-permute-start | bytes 2359304 | tf_op jit(solution)/shard_map/ppermute | solution.py:673
  80.0 28.7 %collective-permute-start.13 = (bf16[256,1536]{1,0:T(8,128)(2,1)S(1)}, bf16[256,1536]{1,0:T(8,128)(2,1)S(1)}, u32[]{:S(2)}, u32[]{:S(2)}) collective-permute-start(bf16[256,1536]{1,0:T(8,128)(2,1)S(1)} %get-tuple-element.82.refs_4_.refs_8_), channel_id=1, source_target_pairs={{4,8},{8,4},{5,9},{9,5},{6,10},{10,6},{7,11},{11,7},{20,24},{24,20... | collective-permute-start | bytes 2359304 | tf_op jit(solution)/shard_map/ppermute | solution.py:673
  80.8 32.4 %collective-permute-start.14 = (bf16[256,1536]{1,0:T(8,128)(2,1)S(1)}, bf16[256,1536]{1,0:T(8,128)(2,1)S(1)}, u32[]{:S(2)}, u32[]{:S(2)}) collective-permute-start(bf16[256,1536]{1,0:T(8,128)(2,1)S(1)} %get-tuple-element.83.refs_6_.refs_9_), channel_id=1, source_target_pairs={{0,4},{4,0},{8,12},{12,8},{1,5},{5,1},{9,13},{13,9},{2,6},{6,2},{1... | collective-permute-start | bytes 2359304 | tf_op jit(solution)/shard_map/ppermute | solution.py:673
  96.7 27.6 %collective-permute-start.17 = (bf16[256,1536]{1,0:T(8,128)(2,1)S(1)}, bf16[256,1536]{1,0:T(8,128)(2,1)S(1)}, u32[]{:S(2)}, u32[]{:S(2)}) collective-permute-start(bf16[256,1536]{1,0:T(8,128)(2,1)S(1)} %get-tuple-element.89.refs_5_.refs_10_), channel_id=1, source_target_pairs={{4,8},{8,4},{5,9},{9,5},{6,10},{10,6},{7,11},{11,7},{20,24},{24,20... | collective-permute-start | bytes 2359304 | tf_op jit(solution)/shard_map/ppermute | solution.py:673
  97.4 32.6 %collective-permute-start.18 = (bf16[256,1536]{1,0:T(8,128)(2,1)S(1)}, bf16[256,1536]{1,0:T(8,128)(2,1)S(1)}, u32[]{:S(2)}, u32[]{:S(2)}) collective-permute-start(bf16[256,1536]{1,0:T(8,128)(2,1)S(1)} %get-tuple-element.94.refs_7_.refs_11_), channel_id=1, source_target_pairs={{0,4},{4,0},{8,12},{12,8},{1,5},{5,1},{9,13},{13,9},{2,6},{6,2},{1... | collective-permute-start | bytes 2359304 | tf_op jit(solution)/shard_map/ppermute | solution.py:673
  113.6 45.5 %collective-permute-start.21 = (bf16[256,1536]{1,0:T(8,128)(2,1)S(1)}, bf16[256,1536]{1,0:T(8,128)(2,1)S(1)}, u32[]{:S(2)}, u32[]{:S(2)}) collective-permute-start(bf16[256,1536]{1,0:T(8,128)(2,1)S(1)} %get-tuple-element.98.refs_13_), channel_id=1, source_target_pairs={{0,4},{4,0},{8,12},{12,8},{1,5},{5,1},{9,13},{13,9},{2,6},{6,2},{1... | collective-permute-start | bytes 2359304 | tf_op jit(solution)/shard_map/ppermute | solution.py:673
  118.0 41.1 %collective-permute-start.22 = (bf16[256,1536]{1,0:T(8,128)(2,1)S(1)}, bf16[256,1536]{1,0:T(8,128)(2,1)S(1)}, u32[]{:S(2)}, u32[]{:S(2)}) collective-permute-start(bf16[256,1536]{1,0:T(8,128)(2,1)S(1)} %get-tuple-element.99.refs_4_.refs_12_), channel_id=1, source_target_pairs={{4,8},{8,4},{5,9},{9,5},{6,10},{10,6},{7,11},{11,7},{20,24},{24,20... | collective-permute-start | bytes 2359304 | tf_op jit(solution)/shard_map/ppermute | solution.py:673
  130.4 40.0 %collective-permute-start.19 = (bf16[256,1536]{1,0:T(8,128)(2,1)S(1)}, bf16[256,1536]{1,0:T(8,128)(2,1)S(1)}, u32[]{:S(2)}, u32[]{:S(2)}) collective-permute-start(bf16[256,1536]{1,0:T(8,128)(2,1)S(1)} %get-tuple-element.96.refs_15_), channel_id=1, source_target_pairs={{0,4},{4,0},{8,12},{12,8},{1,5},{5,1},{9,13},{13,9},{2,6},{6,2},{1... | collective-permute-start | bytes 2359304 | tf_op jit(solution)/shard_map/ppermute | solution.py:673
  134.8 35.6 %collective-permute-start.20 = (bf16[256,1536]{1,0:T(8,128)(2,1)S(1)}, bf16[256,1536]{1,0:T(8,128)(2,1)S(1)}, u32[]{:S(2)}, u32[]{:S(2)}) collective-permute-start(bf16[256,1536]{1,0:T(8,128)(2,1)S(1)} %get-tuple-element.97.refs_5_.refs_14_), channel_id=1, source_target_pairs={{4,8},{8,4},{5,9},{9,5},{6,10},{10,6},{7,11},{11,7},{20,24},{24,20... | collective-permute-start | bytes 2359304 | tf_op jit(solution)/shard_map/ppermute | solution.py:673
  139.9 1.6 collective-permute-start.23
  141.6 17.5 %collective-permute-start.24 = (f32[128,512]{1,0:T(8,128)S(1)}, f32[128,512]{1,0:T(8,128)S(1)}, u32[]{:S(2)}, u32[]{:S(2)}) collective-permute-start(f32[128,512]{1,0:T(8,128)S(1)} %add.23), channel_id=1, source_target_pairs={{0,2},{1,3},{2,0},{3,1},{4,6},{5,7},{6,4},{7,5},{8,10},{9,11},{10,... | collective-permute-start | bytes 786440 | tf_op jit(solution)/shard_map/ppermute | solution.py:621
  160.2 11.3 %collective-permute-start.25 = (bf16[2,512]{1,0:T(2,128)(2,1)S(1)}, bf16[2,512]{1,0:T(2,128)(2,1)S(1)}, u32[]{:S(2)}, u32[]{:S(2)}) collective-permute-start(bf16[2,512]{1,0:T(2,128)(2,1)S(1)} %get-tuple-element.111), channel_id=1, source_target_pairs={{0,12},{4,0},{8,4},{12,8},{1,13},{5,1},{9,5},{13,9},{2,14},{6,2},{... | collective-permute-start | bytes 6152 | tf_op jit(solution)/shard_map/ppermute | solution.py:693
  163.0 8.4 %collective-permute-start.26 = (bf16[2,512]{1,0:T(2,128)(2,1)S(1)}, bf16[2,512]{1,0:T(2,128)(2,1)S(1)}, u32[]{:S(2)}, u32[]{:S(2)}) collective-permute-start(bf16[2,512]{1,0:T(2,128)(2,1)S(1)} %get-tuple-element.112), channel_id=1, source_target_pairs={{0,8},{4,12},{8,0},{12,4},{1,9},{5,13},{9,1},{13,5},{2,10},{6,14},... | collective-permute-start | bytes 6152 | tf_op jit(solution)/shard_map/ppermute | solution.py:693
  164.8 6.7 %collective-permute-start.27 = (bf16[2,512]{1,0:T(2,128)(2,1)S(1)}, bf16[2,512]{1,0:T(2,128)(2,1)S(1)}, u32[]{:S(2)}, u32[]{:S(2)}) collective-permute-start(bf16[2,512]{1,0:T(2,128)(2,1)S(1)} %get-tuple-element.113), channel_id=1, source_target_pairs={{0,4},{4,8},{8,12},{12,0},{1,5},{5,9},{9,13},{13,1},{2,6},{6,10},{... | collective-permute-start | bytes 6152 | tf_op jit(solution)/shard_map/ppermute | solution.py:693
